TPU v7x, 32 devices: a whole 2x2x4 slice. The times are simulated.
32 devices in a mesh: sample: 4 (over y, x), gz: 8 (over z, core).
Axes of the slice: x: 2, y: 2, z: 4, core: 2. Of those that a mesh axis runs over, the one named last changes fastest.
Arguments:
- cubes: bfloat16 [8, 32, 32, 1024], P('sample', 'gz'), may hold values from -6 to 6
- weight_a: bfloat16 [27, 2048], replicated, may hold values from -0.21875 to 0.21875
- weight_b: bfloat16 [27, 8192], replicated, may hold values from -0.15625 to 0.15625
- cotangent: bfloat16 [8, 8, 8, 1024], P('sample', 'gz'), may hold values from -6 to 6
Outputs:
- input_grad: bfloat16 [8, 32, 32, 1024], P('sample', 'gz')
- weight_grad_a: float32 [27, 2048], replicated
- weight_grad_b: float32 [27, 8192], replicated
All inputs are finite; a program needn't handle non-finite values.
Results may differ from a plain program's by a relative error of at most 0.012.
Values may be sent and summed in bfloat16 or wider, within the bound.
No kernel may reach another device: no remote copies, remote signals or barrier semaphores. Data moves between devices by JAX's collectives and lax.ppermute only.
A program may use at most 192 MiB of HBM per device.

v0:
```python
import jax
import jax.numpy as jnp
from jax import lax
from jax.experimental import pallas as pl
from jax.experimental.pallas import tpu as pltpu
from jax.sharding import PartitionSpec as P

C1 = 32
C2 = 64
C3 = 128
SIDE = 32
ZD = 4
HALO = 3
TERMS_B = 27 * 64
TERMS_A = 14 * 32
BF = jnp.bfloat16
F32 = jnp.float32
AXES = ("sample", "gz")
VMEM = pl.BlockSpec(memory_space=pltpu.VMEM)
SMEM = pl.BlockSpec(memory_space=pltpu.SMEM)
ANY = pl.BlockSpec(memory_space=pl.ANY)


def dot(a, b):
    return jnp.dot(a, b, preferred_element_type=F32)


def dot_t(a, b):
    return lax.dot_general(a, b, (((0,), (0,)), ((), ())), preferred_element_type=F32)


def row_picker(variants, stride, columns):
    shape = (variants * 16, columns)
    row = lax.broadcasted_iota(jnp.int32, shape, 0)
    col = lax.broadcasted_iota(jnp.int32, shape, 1)
    return jnp.where(col == stride * (row % 16) + row // 16 - 1, 1.0, 0.0).astype(BF)


def rows_at(block, before, total):
    rows, lanes = block.shape
    parts = []
    if before:
        parts.append(jnp.zeros((before, lanes), block.dtype))
    parts.append(block)
    if total - before - rows:
        parts.append(jnp.zeros((total - before - rows, lanes), block.dtype))
    return jnp.concatenate(parts, axis=0) if len(parts) > 1 else block


def lanes_below(shape, bound):
    return lax.broadcasted_iota(jnp.int32, shape, 1) < bound


def halves(left, right):
    return jnp.where(lanes_below(left.shape, 64), left.astype(F32), right.astype(F32)).astype(BF)


def spread_input(target, b, zz, plane, picker):
    plane = jnp.concatenate([jnp.zeros((32, 32), BF), plane, jnp.zeros((32, 96), BF)], axis=1)
    moved = dot(picker, plane).astype(BF)
    for v in range(4):
        target[b, zz, v] = moved[16 * v : 16 * v + 16]


def prepare_kernel(cubes, wa, wb, wbt, xs, ta, tb, tbt):
    picker = row_picker(4, 2, 32)
    for b in range(cubes.shape[0]):
        for z in range(ZD):
            spread_input(xs, b, HALO + z, cubes[b, z], picker)
    for d in range(9):
        block = wa[d]
        for px in range(2):
            ta[256 * d : 256 * d + 256, 128 * px : 128 * px + 128] = halves(
                rows_at(block, 32 * px, 256), rows_at(block, 64 + 32 * px, 256)
            )
        block = wb[d]
        for e in range(2):
            tb[256 * d : 256 * d + 256, 128 * e : 128 * e + 128] = rows_at(block, 64 * e, 256)
        block = wbt[d]
        for e in range(2):
            tbt[768 * d : 768 * d + 768, 128 * e : 128 * e + 128] = halves(
                rows_at(block, 256 * e, 768), rows_at(block, 256 * e + 128, 768)
            )


def forward_kernel(where, own, recv_a, recv_b, ta, tb, cot, xs, dsl, pools, grad_b, pooled):
    del own
    cube_count = xs.shape[0]
    even = where[0] % 2 == 0
    picker = row_picker(4, 2, 32)
    for b in range(cube_count):
        for z in range(HALO):
            from_a, from_b = recv_a[b, z].astype(F32), recv_b[b, z].astype(F32)
            spread_input(xs, b, z, jnp.where(even, from_b, from_a).astype(BF), picker)
            spread_input(xs, b, HALO + ZD + z, jnp.where(even, from_a, from_b).astype(BF), picker)

    low = jnp.where(where[0] == 0, 0.0, 1.0)
    high = jnp.where(where[0] == where[1] - 1, 0.0, 1.0)
    rows = cube_count * 8 * 16

    def group(g, carry):
        lanes = pl.ds(pl.multiple_of(128 * g, 128), 256)
        stacks = []
        for p in range(2):
            stacks.append(
                jnp.concatenate(
                    [
                        xs[:, dz : dz + 8, p + dy, :, lanes].reshape(rows, 256)
                        for dz in range(3)
                        for dy in range(3)
                    ],
                    axis=1,
                )
            )
        pre = dot(jnp.concatenate(stacks, axis=0), ta[...])
        squash = jax.nn.sigmoid(pre)
        act = pre * squash
        slope = (squash + act * (1.0 - squash)).astype(BF).reshape(2, cube_count, 8, 16, 256)
        for p in range(2):
            dsl[:, :, p, :, pl.ds(pl.multiple_of(256 * g, 256), 256)] = slope[p][:, 1:7]
        act = act.reshape(2, cube_count, 4, 2, 16, 256)
        act = act[0] + act[1]
        act = act[:, :, 0] + act[:, :, 1]
        act = (act[..., :128] + act[..., 128:]) * 0.125
        out = pl.ds(pl.multiple_of(128 * g, 128), 128)
        for z in range(4):
            part = act[:, z]
            if z == 0:
                part = part * low
            if z == 3:
                part = part * high
            pooled[:, z, :, out] = part.astype(BF)
        return carry

    lax.fori_loop(0, 8, group, 0)

    shifter = row_picker(3, 1, 16)
    for b in range(cube_count):
        for z in range(4):
            plane = jnp.concatenate([jnp.zeros((16, 64), BF), pooled[b, z], jnp.zeros((16, 64), BF)], axis=1)
            moved = dot(shifter, plane).astype(BF)
            for v in range(3):
                pools[b, z, v] = moved[16 * v : 16 * v + 16]

    rows_b = cube_count * 2 * 16
    columns = []
    for dz in range(3):
        for dy in range(3):
            columns.append(
                jnp.concatenate(
                    [
                        pools[:, dz : dz + 2, dy, :, 128 * g : 128 * g + 256].reshape(rows_b, 256)
                        for g in range(8)
                    ],
                    axis=0,
                )
            )
    pre_b = dot(jnp.concatenate(columns, axis=1), tb[...])
    squash = jax.nn.sigmoid(pre_b)
    slope_b = squash + pre_b * squash * (1.0 - squash)
    for g in range(8):
        part = slope_b[rows_b * g : rows_b * g + rows_b].reshape(cube_count, 2, 16, 256)
        up = cot[:, :, 128 * g : 128 * g + 128].astype(F32) * 0.125
        for z in range(2):
            for e in range(2):
                at = 256 * g + 128 * e
                grad_b[:, z, :, at : at + 128] = (up * part[:, z, :, 128 * e : 128 * e + 128]).astype(BF)


def terms_b_kernel(pools, grad_b, out):
    cube_count = grad_b.shape[0]
    rows_b = cube_count * 2 * 16
    grads = jnp.concatenate(
        [grad_b[:, :, :, 256 * g : 256 * g + 256].reshape(rows_b, 256) for g in range(8)], axis=0
    )
    for dz in range(3):
        for dy in range(3):
            windows = jnp.concatenate(
                [
                    pools[:, dz : dz + 2, dy, :, 128 * g : 128 * g + 256].reshape(rows_b, 256)
                    for g in range(8)
                ],
                axis=0,
            )
            full = dot_t(windows, grads)
            for dx in range(3):
                at = 64 * (9 * dz + 3 * dy + dx)
                term = full[64 * dx : 64 * dx + 64, :128] + full[64 * dx + 64 : 64 * dx + 128, 128:]
                out[at : at + 64] = term.astype(BF)


def backward_kernel(where, grad_b, recv_a, recv_b, tbt, dsl, xs, terms_b, ga_out, out, gs, ga, gpool, acc, sem):
    cube_count = grad_b.shape[0]
    even = where[0] % 2 == 0
    shifter = row_picker(3, 1, 16)

    def spread_plane(b, zz, plane):
        moved = dot(shifter, plane).astype(BF)
        for v in range(3):
            gs[b, zz, v, :, 128:2176] = moved[16 * v : 16 * v + 16]
            gs[b, zz, v, :, :128] = jnp.zeros((16, 128), BF)
            gs[b, zz, v, :, 2176:] = jnp.zeros((16, 128), BF)

    for b in range(cube_count):
        for z in range(2):
            spread_plane(b, 2 + z, grad_b[b, z])
            from_a, from_b = recv_a[b, z].astype(F32), recv_b[b, z].astype(F32)
            spread_plane(b, z, jnp.where(even, from_b, from_a).astype(BF))
            spread_plane(b, 4 + z, jnp.where(even, from_a, from_b).astype(BF))

    low = jnp.where(where[0] == 0, 0.0, 0.125)
    high = jnp.where(where[0] == where[1] - 1, 0.0, 0.125)
    rows = cube_count * 4 * 16
    columns = []
    for dz in range(3):
        for dy in range(3):
            columns.append(
                jnp.concatenate(
                    [gs[:, dz : dz + 4, dy, :, 512 * q : 512 * q + 768].reshape(rows, 768) for q in range(4)],
                    axis=0,
                )
            )
    back = dot(jnp.concatenate(columns, axis=1), tbt[...])
    for q in range(4):
        part = back[rows * q : rows * q + rows].reshape(cube_count, 4, 16, 256)
        for z in range(4):
            scale = low if z == 0 else high if z == 3 else 0.125
            gpool[:, z, :, 256 * q : 256 * q + 256] = part[:, z] * scale

    acc[...] = jnp.zeros_like(acc)
    ga[:, :, :, :, :128] = jnp.zeros((cube_count, 6, 4, 16, 128), BF)
    ga[:, :, :, :, 2176:] = jnp.zeros((cube_count, 6, 4, 16, 128), BF)
    rows_a = cube_count * 6 * 16
    own = cube_count * 4 * 16
    place = lax.broadcasted_iota(jnp.int32, (rows_a, 128), 0) % 16

    def group(g, carry):
        lanes = pl.ds(pl.multiple_of(128 * g, 128), 128)
        up = gpool[:, :, :, lanes]
        up = jnp.concatenate(
            [up[:, 0:1], up[:, 1:2], up[:, 1:2], up[:, 2:3], up[:, 2:3], up[:, 3:4]], axis=1
        ).reshape(rows_a, 128)
        sides = []
        for p in range(2):
            pair = []
            for px in range(2):
                at = pl.ds(pl.multiple_of(256 * g + 128 * px, 128), 128)
                grad = up * dsl[:, :, p, :, at].astype(F32).reshape(rows_a, 128)
                to = pl.ds(pl.multiple_of(256 * g + 128 * px + 128, 128), 128)
                kept = grad.astype(BF).reshape(cube_count, 6, 16, 128)
                ga[:, :, 1 + p, :, to] = kept
                pair.append(kept[:, 1:5].reshape(own, 128))
                if p == 1:
                    moved = jnp.where(place == 0, 0.0, pltpu.roll(grad, 1, 0))
                else:
                    moved = jnp.where(place == 15, 0.0, pltpu.roll(grad, rows_a - 1, 0))
                ga[:, :, 0 if p else 3, :, to] = moved.astype(BF).reshape(cube_count, 6, 16, 128)
            sides.append(jnp.concatenate(pair, axis=1))
        grads = jnp.concatenate(sides, axis=0)
        wide = pl.ds(pl.multiple_of(128 * g, 128), 256)
        windows = jnp.concatenate(
            [
                jnp.concatenate(
                    [
                        xs[:, HALO - 1 + dz : HALO + 3 + dz, p + dy, :, wide].reshape(own, 256)
                        for dz in range(3)
                        for dy in range(3)
                    ],
                    axis=1,
                )
                for p in range(2)
            ],
            axis=0,
        )
        acc[...] += dot_t(grads, windows)
        return carry

    lax.fori_loop(0, 8, group, 0)

    leave = pltpu.make_async_copy(ga, ga_out, sem)
    leave.start()
    out[:TERMS_B] = terms_b[...]
    pending = None
    for d in range(9):
        full = acc[:, 256 * d : 256 * d + 256].T
        for dx in range(3):
            left = full[32 * dx : 32 * dx + 32, :128] + full[32 * dx + 32 : 32 * dx + 64, 128:]
            right = full[32 * dx + 64 : 32 * dx + 96, :128] + full[32 * dx + 96 : 32 * dx + 128, 128:]
            mask = lanes_below((32, 128), 64)
            merged = jnp.where(mask, left, right)
            total = merged + pltpu.roll(merged, 64, 1)
            at = 3 * d + dx
            if at % 2 == 0:
                pending = total
            else:
                to = TERMS_B + 16 * (at - 1)
                out[to : to + 32] = jnp.where(mask, pending, total).astype(BF)
    out[TERMS_B + 416 : TERMS_B + TERMS_A] = pending.astype(BF)
    out[TERMS_B + TERMS_A :] = jnp.zeros((out.shape[0] - TERMS_B - TERMS_A, 128), BF)
    leave.wait()


RANKS = (-3, -1, 0, 2, 1, 3, 4, 6, 5, 7, 8, 10)


def input_kernel(ga_in, wat, out, tat, ga, sem):
    arrive = pltpu.make_async_copy(ga_in, ga, sem)
    arrive.start()
    cube_count = ga.shape[0]
    lane = lax.broadcasted_iota(jnp.int32, (64, 128), 1)
    for d in range(9):
        block = wat[d].astype(F32)
        turned = [block if s == 0 else pltpu.roll(block, 32 * s, 1) for s in range(4)]
        for slot, rank in enumerate(RANKS):
            for half in range(2):
                start = 32 * (rank - 1 - 4 * half)
                keep = (lane >= start) & (lane < start + 96)
                value = jnp.where(keep, turned[(rank - 1) % 4], 0.0).astype(BF)
                tat[768 * d + 64 * slot : 768 * d + 64 * slot + 64, 128 * half : 128 * half + 128] = value

    arrive.wait()
    rows = cube_count * ZD * 16
    sides = []
    for p in range(2):
        columns = []
        for dz in range(3):
            for dy in range(3):
                columns.append(
                    jnp.concatenate(
                        [
                            ga[:, dz : dz + ZD, p + dy, :, 512 * q : 512 * q + 768].reshape(rows, 768)
                            for q in range(4)
                        ],
                        axis=0,
                    )
                )
        sides.append(dot(jnp.concatenate(columns, axis=1), tat[...]).astype(BF).reshape(4, cube_count, ZD, 16, 256))
    row = lax.broadcasted_iota(jnp.int32, (32, 32), 0)
    col = lax.broadcasted_iota(jnp.int32, (32, 32), 1)
    mixer = jnp.where(col == row // 2 + 16 * (row % 2), 1.0, 0.0).astype(BF)
    for b in range(cube_count):
        for z in range(ZD):
            for q in range(4):
                both = jnp.concatenate([sides[0][q, b, z], sides[1][q, b, z]], axis=0)
                out[b, z, :, 256 * q : 256 * q + 256] = dot(mixer, both).astype(BF)


def call(kernel, args, outs, scratch, flops, smem=0, any_in=(), any_out=(), aliases=None):
    specs = [SMEM if i < smem else ANY if i in any_in else VMEM for i in range(len(args))]
    return pl.pallas_call(
        kernel,
        out_shape=[jax.ShapeDtypeStruct(shape, dtype) for shape, dtype in outs],
        in_specs=specs,
        out_specs=[ANY if i in any_out else VMEM for i in range(len(outs))],
        scratch_shapes=scratch,
        input_output_aliases=aliases or {},
        compiler_params=pltpu.CompilerParams(vmem_limit_bytes=28 * 1024 * 1024),
        cost_estimate=pl.CostEstimate(flops=flops, bytes_accessed=1_000_000, transcendentals=0),
    )(*args)


def swap(first, second, count):
    pairs_a = [(i, i ^ 1) for i in range(count)]
    pairs_b = [(i, ((i + 1) ^ 1) - 1) for i in range(1, count - 1)]
    return lax.ppermute(first, "gz", pairs_a), lax.ppermute(second, "gz", pairs_b)


def gather_kernel(pieces, out):
    mine = jnp.sum(pieces[...].astype(F32), axis=0).astype(BF)
    for i in range(out.shape[0]):
        out[i] = mine


def total_of(partial, count):
    rows, lanes = partial.shape
    shape = (count, rows // count, lanes)
    pieces = lax.all_to_all(partial.reshape(shape), AXES, 0, 0)
    (copies,) = call(gather_kernel, [pieces], [(shape, BF)], [], 1_000_000)
    return lax.all_to_all(copies, AXES, 0, 0).reshape(rows, lanes)


def shards(cubes, weight_a, weight_b, cotangent):
    cube_count = cubes.shape[0]
    ring = lax.axis_size("gz")
    count = lax.axis_size("sample") * ring
    me = lax.axis_index("gz")
    where = jnp.stack([me, jnp.int32(ring)]).astype(jnp.int32)
    odd = me % 2
    first = lax.dynamic_slice_in_dim(cubes, 1 - odd, HALO, axis=1)
    second = lax.dynamic_slice_in_dim(cubes, odd, HALO, axis=1)
    recv_a, recv_b = swap(first, second, ring)

    wa = weight_a.reshape(9, 96, C2)
    wa2 = jnp.concatenate([wa, wa], axis=-1)
    wb = weight_b.reshape(9, 192, C3)
    wbt = weight_b.reshape(3, 3, 3, C2, C3)[::-1, ::-1, ::-1].transpose(0, 1, 2, 4, 3).reshape(9, 384, C2)
    wbt2 = jnp.concatenate([wbt, wbt], axis=-1)
    wat = weight_a.reshape(3, 3, 3, C1, C2)[::-1, ::-1].transpose(0, 1, 4, 2, 3).reshape(9, C2, 96)
    wat = jnp.pad(wat, ((0, 0), (0, 0), (0, 32)))
    cot = jnp.repeat(cotangent.reshape(cube_count, SIDE // 4, SIDE // 4 * C3), 2, axis=1)

    own_xs, ta, tb, tbt = call(
        prepare_kernel,
        [cubes, wa2, wb, wbt2],
        [
            ((cube_count, ZD + 2 * HALO, 4, 16, 1152), BF),
            ((2304, 256), BF),
            ((2304, 256), BF),
            ((6912, 256), BF),
        ],
        [],
        1_000_000_000,
    )
    xs, dsl, pools, grad_b = call(
        forward_kernel,
        [where, own_xs, recv_a, recv_b, ta, tb, cot],
        [
            ((cube_count, ZD + 2 * HALO, 4, 16, 1152), BF),
            ((cube_count, 6, 2, 16, 2048), BF),
            ((cube_count, 4, 3, 16, 1152), BF),
            ((cube_count, 2, 16, 2048), BF),
        ],
        [pltpu.VMEM((cube_count, 4, 16, 1024), BF)],
        8_000_000_000,
        smem=1,
        aliases={1: 0},
    )
    back_a, back_b = swap(grad_b, grad_b, ring)
    (terms_b,) = call(terms_b_kernel, [pools, grad_b], [((TERMS_B, 128), BF)], [], 1_000_000_000)
    rows = -(-(TERMS_B + TERMS_A) // (8 * count)) * 8 * count
    rows = -(-rows // (16 * count)) * 16 * count if count > 32 else rows
    ga, partial = call(
        backward_kernel,
        [where, grad_b, back_a, back_b, tbt, dsl, xs, terms_b],
        [((cube_count, 6, 4, 16, 2304), BF), ((rows, 128), BF)],
        [
            pltpu.VMEM((cube_count, 6, 3, 16, 2304), BF),
            pltpu.VMEM((cube_count, 6, 4, 16, 2304), BF),
            pltpu.VMEM((cube_count, 4, 16, 1024), F32),
            pltpu.VMEM((256, 2304), F32),
            pltpu.SemaphoreType.DMA,
        ],
        6_000_000_000,
        smem=1,
        any_out=(0,),
    )
    (input_grad,) = call(
        input_kernel,
        [ga, wat],
        [((cube_count, ZD, SIDE, SIDE * C1), BF)],
        [
            pltpu.VMEM((6912, 256), BF),
            pltpu.VMEM((cube_count, 6, 4, 16, 2304), BF),
            pltpu.SemaphoreType.DMA,
        ],
        4_000_000_000,
        any_in=(0,),
    )
    scale = 1.0 / (cube_count * lax.axis_size("sample"))
    total = total_of(partial, count)
    total_b = total[:TERMS_B].astype(F32).reshape(27, C2 * C3) * scale
    total_a = total[TERMS_B : TERMS_B + TERMS_A].astype(F32).reshape(14, C1, 2, C2).transpose(0, 2, 1, 3)
    total_a = total_a.reshape(28, C1 * C2)[:27] * scale
    return input_grad, total_a, total_b


def solution(mesh):
    in_specs = (P("sample", "gz", None, None), P(), P(), P("sample", "gz", None, None))
    out_specs = (P("sample", "gz", None, None), P(), P())
    return jax.shard_map(shards, mesh=mesh, in_specs=in_specs, out_specs=out_specs, check_vma=False)
```

profile of v0, /device:TPU:0, one launch (start us, length us, event | category | flops | bytes accessed | tf_op | source)
XLA Modules:
  0.0 89.3 jit_solution(15768741955314272362)
XLA Ops:
  0.7 2.1 %constant_dynamic-slice_fusion = (bf16[2,3,32,1024]{3,2,1,0:T(8,128)(2,1)}, bf16[2,3,32,1024]{3,2,1,0:T(8,128)(2,1)}) fusion(bf16[2,4,32,1024]{3,2,1,0:T(8,128)(2,1)} %cubes.1, s32[]{:T(128)S(6)} %select_n.15, s32[]{:T(128)S(6)} %select_n.14), kind=kLoop, calls=%fused_computation.6 | loop fusion | bytes 1572872 | tf_op jit(solution)/shard_map/dynamic_slice | solution.py:390
  2.8 0.5 collective-permute-start
  3.2 0.7 collective-permute-start.1
  3.9 1.2 %reshape.50 = bf16[9,96,64]{2,1,0:T(8,128)(2,1)S(1)} reshape(bf16[27,2048]{1,0:T(8,128)(2,1)} %param.5) | data formatting | bytes 221184 | tf_op jit(solution)/shard_map/reshape | solution.py:393
  5.1 0.1 pad_maximum_fusion.1.wa
  5.2 0.3 reshape.51.wb
  5.5 0.1 copy.14
  5.6 1.2 %copy.11 = bf16[3,3,3,64,128]{3,4,2,1,0:T(8,128)(2,1)} copy(bf16[3,3,3,64,128]{4,3,2,1,0:T(8,128)(2,1)S(1)} %bitcast.23) | data formatting | bytes 884736 | tf_op jit(solution)/shard_map/reshape | solution.py:396
  6.9 1.3 %rev.6 = bf16[3,3,3,64,128]{3,4,2,1,0:T(8,128)(2,1)S(1)} reverse(bf16[3,3,3,64,128]{3,4,2,1,0:T(8,128)(2,1)} %copy.11), dimensions={0,1,2} | reverse | bytes 884736 | tf_op jit(solution)/shard_map/rev | solution.py:396
  8.3 0.5 pad_maximum_fusion.wbt
  8.8 1.3 %shard_map.67 = (bf16[2,10,4,16,1152]{4,3,2,1,0:T(8,128)(2,1)S(1)}, bf16[2304,256]{1,0:T(8,128)(2,1)S(1)}, bf16[2304,256]{1,0:T(8,128)(2,1)S(1)}, bf16[6912,256]{1,0:T(8,128)(2,1)S(1)}) custom-call(bf16[2,4,32,1024]{3,2,1,0:T(8,128)(2,1)S(1)} %copy-done, bf16[9,96,128]{2,1,0:T(8,128)(2,1)S(1)} %pad_maximum_fusion.1.wa, bf16[9,192,128]{2,1,0:T(8,128)(2,1)S(1)} %reshape.51.wb, ...), custom_call_target="tpu_custom_call" | custom-call | flops 1000000000 | bytes 1000000 | tf_op jit(solution)/shard_map/pallas_call | solution.py:350
  10.0 0.1 pad_add_fusion.where
  10.1 8.9 %shard_map.68 = (bf16[2,10,4,16,1152]{4,3,2,1,0:T(8,128)(2,1)S(1)}, bf16[2,6,2,16,2048]{4,3,2,1,0:T(8,128)(2,1)S(1)}, bf16[2,4,3,16,1152]{4,3,2,1,0:T(8,128)(2,1)S(1)}, bf16[2,2,16,2048]{3,2,1,0:T(8,128)(2,1)S(1)}) custom-call(s32[2]{0:T(128)S(1)} %pad_add_fusion.where, ...), custom_call_target="tpu_custom_call", output_to_operand_aliasing={{0}: (1, {})} | custom-call | flops 8000000000 | bytes 1000000 | tf_op jit(solution)/shard_map/pallas_call | solution.py:350
  19.0 4.0 %collective-permute-start.2 = (bf16[2,2,16,2048]{3,2,1,0:T(8,128)(2,1)S(1)}, bf16[2,2,16,2048]{3,2,1,0:T(8,128)(2,1)S(1)}, u32[]{:S(2)}, u32[]{:S(2)}) collective-permute-start(bf16[2,2,16,2048]{3,2,1,0:T(8,128)(2,1)S(1)} %get-tuple-element.16.grad_b), channel_id=1, source_target_pairs={{0,1},{1,0},{2,3},{3,2},{4,5},{5,4},{6,7},{7,6},{8,9},{9,8},{10,11... | collective-permute-start | bytes 786440 | tf_op jit(solution)/shard_map/ppermute | solution.py:365
  23.0 0.7 collective-permute-start.3
  23.7 0.8 shard_map.69.terms_b
  24.6 9.4 %shard_map.70 = (bf16[2,6,4,16,2304]{4,3,2,1,0:T(8,128)(2,1)S(1)}, bf16[2304,128]{1,0:T(8,128)(2,1)S(1)}) custom-call(s32[2]{0:T(128)S(1)} %pad_add_fusion.where, bf16[2,2,16,2048]{3,2,1,0:T(8,128)(2,1)S(1)} %get-tuple-element.16.grad_b, bf16[2,2,16,2048]{3,2,1,0:T(8,128)(2,1)S(1)} %collective-permute-done.2.recv_a, ...), custom_call_target="tpu_custom_call" | custom-call | flops 6000000000 | bytes 1000000 | tf_op jit(solution)/shard_map/pallas_call | solution.py:350
  34.0 29.0 %all_to_all.10.pieces = bf16[32,72,128]{2,1,0:T(8,128)(2,1)S(1)} all-to-all(bf16[32,72,128]{2,1,0:T(8,128)(2,1)S(1)} %bitcast.19), channel_id=1, replica_groups=mesh['sample'=4,'gz'=8] {'sample','gz'}, dimensions={0} | all-to-all | bytes 1179648 | tf_op jit(solution)/shard_map/all_to_all | solution.py:377
  63.1 0.9 %shard_map.72 = bf16[32,72,128]{2,1,0:T(8,128)(2,1)} custom-call(bf16[32,72,128]{2,1,0:T(8,128)(2,1)S(1)} %all_to_all.10.pieces), custom_call_target="tpu_custom_call" | custom-call | flops 1000000 | bytes 1000000 | tf_op jit(solution)/shard_map/pallas_call | solution.py:350
  64.0 3.5 %all-to-all-start.1 = ((bf16[32,72,128]{2,1,0:T(8,128)(2,1)}), bf16[32,72,128]{2,1,0:T(8,128)(2,1)}, u32[]{:S(2)}, u32[]{:S(2)}) async-start(bf16[32,72,128]{2,1,0:T(8,128)(2,1)} %shard_map.72), calls=%async_computation.1 | async-start | bytes 1179648 | tf_op jit(solution)/shard_map/all_to_all | solution.py:379
  67.5 1.8 %reshape.56 = bf16[3,3,3,32,64]{4,3,2,1,0:T(8,128)(2,1)} reshape(bf16[27,2048]{1,0:T(8,128)(2,1)} %param.5) | data formatting | bytes 221184 | tf_op jit(solution)/shard_map/reshape | solution.py:398
  69.3 1.6 %rev.7 = bf16[3,3,3,32,64]{4,3,2,1,0:T(8,128)(2,1)} reverse(bf16[3,3,3,32,64]{4,3,2,1,0:T(8,128)(2,1)} %reshape.56), dimensions={0,1} | reverse | bytes 221184 | tf_op jit(solution)/shard_map/rev | solution.py:398
  71.0 1.7 %copy.12 = bf16[9,64,96]{2,1,0:T(8,128)(2,1)} copy(bf16[9,64,96]{1,2,0:T(8,128)(2,1)} %bitcast.25) | data formatting | bytes 221184 | tf_op jit(solution)/shard_map/reshape | solution.py:398
  72.7 0.9 %pad.4.wat = bf16[9,64,128]{2,1,0:T(8,128)(2,1)S(1)} pad(bf16[9,64,96]{2,1,0:T(8,128)(2,1)} %copy.12, bf16[]{:T(256)} %constant.28.clone.1), padding=0_0x0_0x0_32 | pad | bytes 258050 | tf_op jit(solution)/shard_map/jit(_pad)/pad | solution.py:399
  73.6 5.7 %shard_map.71 = bf16[2,4,32,1024]{3,2,1,0:T(8,128)(2,1)} custom-call(bf16[2,6,4,16,2304]{4,3,2,1,0:T(8,128)(2,1)S(1)} %get-tuple-element.21.ga_in, bf16[9,64,128]{2,1,0:T(8,128)(2,1)S(1)} %pad.4.wat), custom_call_target="tpu_custom_call" | custom-call | flops 4000000000 | bytes 1000000 | tf_op jit(solution)/shard_map/pallas_call | solution.py:350
  79.4 5.7 %all-to-all-done.1 = bf16[32,72,128]{2,1,0:T(8,128)(2,1)} async-done(((bf16[32,72,128]{2,1,0:T(8,128)(2,1)}), bf16[32,72,128]{2,1,0:T(8,128)(2,1)}, u32[]{:S(2)}, u32[]{:S(2)}) %all-to-all-start.1) | async-done | bytes 589856 | tf_op jit(solution)/shard_map/all_to_all | solution.py:379
  85.0 1.1 %convert_multiply_fusion = f32[24,72,128]{2,1,0:T(8,128)S(1)} fusion(bf16[32,72,128]{2,1,0:T(8,128)(2,1)} %all-to-all-done.1), kind=kLoop, calls=%fused_computation.1 | loop fusion | flops 442368 | bytes 1327104 | tf_op jit(solution)/shard_map/mul | solution.py:461
  86.1 1.1 %mul.19 = f32[27,8192]{1,0:T(8,128)} reshape(f32[24,72,128]{2,1,0:T(8,128)S(1)} %convert_multiply_fusion) | data formatting | bytes 1769472 | tf_op jit(solution)/shard_map/mul | solution.py:461
  87.3 0.9 %slice.17 = bf16[448,128]{1,0:T(8,128)(2,1)S(1)} slice(bf16[2304,128]{1,0:T(8,128)(2,1)} %bitcast.7), slice={[1728:2176], [0:128]} | slice | bytes 229376 | tf_op jit(solution)/shard_map/slice | solution.py:462
  88.2 0.1 reshape.60
  88.3 0.2 reshape.61
  88.6 0.7 convert_multiply_fusion.1
  (14 shorter events, 0.2 us)
Async XLA Ops:
  0.6 4.6 %copy-start.1 = (bf16[27,8192]{1,0:T(8,128)(2,1)S(1)}, bf16[27,8192]{1,0:T(8,128)(2,1)}, u32[]{:S(2)}) copy-start(bf16[27,8192]{1,0:T(8,128)(2,1)} %param.6) | copy-start | bytes 1327108
  2.8 7.4 %collective-permute-start = (bf16[2,3,32,1024]{3,2,1,0:T(8,128)(2,1)}, bf16[2,3,32,1024]{3,2,1,0:T(8,128)(2,1)S(1)}, u32[]{:S(2)}, u32[]{:S(2)}) collective-permute-start(bf16[2,3,32,1024]{3,2,1,0:T(8,128)(2,1)} %get-tuple-element.24), channel_id=1, source_target_pairs={{0,1},{1,0},{2,3},{3,2},{4,5},{5,4},{6,7},{7,6},{8,9},{9,8},{10,11... | collective-permute-start | bytes 1179656 | tf_op jit(solution)/shard_map/ppermute | solution.py:365
  3.2 6.9 %collective-permute-start.1 = (bf16[2,3,32,1024]{3,2,1,0:T(8,128)(2,1)}, bf16[2,3,32,1024]{3,2,1,0:T(8,128)(2,1)S(1)}, u32[]{:S(2)}, u32[]{:S(2)}) collective-permute-start(bf16[2,3,32,1024]{3,2,1,0:T(8,128)(2,1)} %get-tuple-element.23), channel_id=1, source_target_pairs={{1,2},{2,1},{3,4},{4,3},{5,6},{6,5},{9,10},{10,9},{11,12},{12,11},... | collective-permute-start | bytes 1179656 | tf_op jit(solution)/shard_map/ppermute | solution.py:365
  5.6 2.5 %copy-start.2 = (bf16[2,1,8,1024]{3,2,1,0:T(8,128)(2,1)S(1)}, bf16[2,1,8,1024]{3,2,1,0:T(8,128)(2,1)}, u32[]{:S(2)}) copy-start(bf16[2,1,8,1024]{3,2,1,0:T(8,128)(2,1)} %param.7) | copy-start | bytes 98308
  6.9 1.9 %copy-start = (bf16[2,4,32,1024]{3,2,1,0:T(8,128)(2,1)S(1)}, bf16[2,4,32,1024]{3,2,1,0:T(8,128)(2,1)}, u32[]{:S(2)}) copy-start(bf16[2,4,32,1024]{3,2,1,0:T(8,128)(2,1)} %cubes.1) | copy-start | bytes 1572868
  19.0 5.5 %collective-permute-start.2 = (bf16[2,2,16,2048]{3,2,1,0:T(8,128)(2,1)S(1)}, bf16[2,2,16,2048]{3,2,1,0:T(8,128)(2,1)S(1)}, u32[]{:S(2)}, u32[]{:S(2)}) collective-permute-start(bf16[2,2,16,2048]{3,2,1,0:T(8,128)(2,1)S(1)} %get-tuple-element.16.grad_b), channel_id=1, source_target_pairs={{0,1},{1,0},{2,3},{3,2},{4,5},{5,4},{6,7},{7,6},{8,9},{9,8},{10,11... | collective-permute-start | bytes 786440 | tf_op jit(solution)/shard_map/ppermute | solution.py:365
  23.0 1.5 %collective-permute-start.3 = (bf16[2,2,16,2048]{3,2,1,0:T(8,128)(2,1)S(1)}, bf16[2,2,16,2048]{3,2,1,0:T(8,128)(2,1)S(1)}, u32[]{:S(2)}, u32[]{:S(2)}) collective-permute-start(bf16[2,2,16,2048]{3,2,1,0:T(8,128)(2,1)S(1)} %get-tuple-element.16.grad_b), channel_id=1, source_target_pairs={{1,2},{2,1},{3,4},{4,3},{5,6},{6,5},{9,10},{10,9},{11,12},{12,11},... | collective-permute-start | bytes 786440 | tf_op jit(solution)/shard_map/ppermute | solution.py:365
  64.0 21.1 %all-to-all-start.1 = ((bf16[32,72,128]{2,1,0:T(8,128)(2,1)}), bf16[32,72,128]{2,1,0:T(8,128)(2,1)}, u32[]{:S(2)}, u32[]{:S(2)}) async-start(bf16[32,72,128]{2,1,0:T(8,128)(2,1)} %shard_map.72), calls=%async_computation.1 | async-start | bytes 1179648 | tf_op jit(solution)/shard_map/all_to_all | solution.py:379
where the time goes:
time: 89.7 us; the launch traced here: 89.3 us
  blocking collectives  29 us (32%)
  Pallas kernels  27.1 us (30%)
  local copies, waits for them, and re-layouts  14.8 us (16%)
  starting transfers between devices  9.27 us (10%)
  waiting for transfers between devices  5.69 us (6%)
  other arithmetic  2.49 us (3%)
    all_to_all x1, blocking collectives, total_of(): pieces = lax.all_to_all(partial.reshape(shape), AXES, 0, 0)  29 us
    pallas_call x6, Pallas kernels, call(): pl.pallas_call(kernel, out_shape=[jax.ShapeDtypeStruct(shape, dtype) for...  27.1 us
    all_to_all x1, waiting for transfers between devices, total_of(): return lax.all_to_all(copies, AXES, 0, 0).reshape(rows, lanes)  5.68 us
    ppermute x2, starting transfers between devices, swap(): lax.ppermute(first, 'gz', pairs_a)  4.43 us
    reshape x2, local copies, waits for them, and re-layouts, shards(): weight_a.reshape(3, 3, 3, C1, C2)[::-1, ::-1].transpose(0, 1, 4, 2, 3)  3.57 us
    all_to_all x1, starting transfers between devices, total_of(): return lax.all_to_all(copies, AXES, 0, 0).reshape(rows, lanes)  3.5 us
    dynamic_slice x1, local copies, waits for them, and re-layouts, shards(): second = lax.dynamic_slice_in_dim(cubes, odd, HALO, axis=1)  2.1 us
  transfers between devices with their start and end apart: 5, of which 1 were waited for; matrix products, arithmetic and copies ran while one was open for 12% of the time, Pallas kernels for 9%

commit v1 on v0

--- a/solution.py
+++ b/solution.py
@@ -11,8 +11,8 @@
 SIDE = 32
 ZD = 4
 HALO = 3
-TERMS_B = 27 * 64
-TERMS_A = 14 * 32
+ROWS_B = C1 * 2 * 28
+ROWS_A = C1 // 2 * 28
 BF = jnp.bfloat16
 F32 = jnp.float32
 AXES = ("sample", "gz")
@@ -27,6 +27,10 @@
 
 def dot_t(a, b):
     return lax.dot_general(a, b, (((0,), (0,)), ((), ())), preferred_element_type=F32)
+
+
+def sigmoid(v):
+    return pl.reciprocal(1.0 + jnp.exp(-v), approx=True)
 
 
 def row_picker(variants, stride, columns):
@@ -52,7 +56,7 @@
 
 
 def halves(left, right):
-    return jnp.where(lanes_below(left.shape, 64), left.astype(F32), right.astype(F32)).astype(BF)
+    return jnp.where(lanes_below(left.shape, 64), left, right).astype(BF)
 
 
 def spread_input(target, b, zz, plane, picker):
@@ -62,23 +66,30 @@
         target[b, zz, v] = moved[16 * v : 16 * v + 16]
 
 
-def prepare_kernel(cubes, wa, wb, wbt, xs, ta, tb, tbt):
+def prepare_kernel(cubes, wa, wb, xs, ta, tb, tbt, wat):
     picker = row_picker(4, 2, 32)
     for b in range(cubes.shape[0]):
         for z in range(ZD):
             spread_input(xs, b, HALO + z, cubes[b, z], picker)
     for d in range(9):
-        block = wa[d]
+        block = wa[d].astype(F32)
+        block = jnp.concatenate([block, block], axis=1)
         for px in range(2):
             ta[256 * d : 256 * d + 256, 128 * px : 128 * px + 128] = halves(
                 rows_at(block, 32 * px, 256), rows_at(block, 64 + 32 * px, 256)
             )
+        wat[8 - d] = rows_at(block, 0, 128).T[:64].astype(BF)
         block = wb[d]
         for e in range(2):
             tb[256 * d : 256 * d + 256, 128 * e : 128 * e + 128] = rows_at(block, 64 * e, 256)
-        block = wbt[d]
+        turned = []
+        for dx in (2, 1, 0):
+            part = block[64 * dx : 64 * dx + 64].astype(F32)
+            turned.append(jnp.concatenate([part, part], axis=0).T)
+        block = jnp.concatenate(turned, axis=0)
+        to = 768 * (8 - d)
         for e in range(2):
-            tbt[768 * d : 768 * d + 768, 128 * e : 128 * e + 128] = halves(
+            tbt[to : to + 768, 128 * e : 128 * e + 128] = halves(
                 rows_at(block, 256 * e, 768), rows_at(block, 256 * e + 128, 768)
             )
 
@@ -90,9 +101,11 @@
     picker = row_picker(4, 2, 32)
     for b in range(cube_count):
         for z in range(HALO):
-            from_a, from_b = recv_a[b, z].astype(F32), recv_b[b, z].astype(F32)
-            spread_input(xs, b, z, jnp.where(even, from_b, from_a).astype(BF), picker)
-            spread_input(xs, b, HALO + ZD + z, jnp.where(even, from_a, from_b).astype(BF), picker)
+            far = ZD - HALO + z
+            below = jnp.where(even, recv_b[b, far].astype(F32), recv_a[b, far].astype(F32)).astype(BF)
+            above = jnp.where(even, recv_a[b, z].astype(F32), recv_b[b, z].astype(F32)).astype(BF)
+            spread_input(xs, b, z, below, picker)
+            spread_input(xs, b, HALO + ZD + z, above, picker)
 
     low = jnp.where(where[0] == 0, 0.0, 1.0)
     high = jnp.where(where[0] == where[1] - 1, 0.0, 1.0)
@@ -113,7 +126,7 @@
                 )
             )
         pre = dot(jnp.concatenate(stacks, axis=0), ta[...])
-        squash = jax.nn.sigmoid(pre)
+        squash = sigmoid(pre)
         act = pre * squash
         slope = (squash + act * (1.0 - squash)).astype(BF).reshape(2, cube_count, 8, 16, 256)
         for p in range(2):
@@ -156,23 +169,28 @@
                 )
             )
     pre_b = dot(jnp.concatenate(columns, axis=1), tb[...])
-    squash = jax.nn.sigmoid(pre_b)
+    squash = sigmoid(pre_b)
     slope_b = squash + pre_b * squash * (1.0 - squash)
+    row = lax.broadcasted_iota(jnp.int32, (16, 8), 0)
+    twice = jnp.where(row // 2 == lax.broadcasted_iota(jnp.int32, (16, 8), 1), 0.125, 0.0).astype(BF)
+    ups = [dot(twice, cot[b, 0]) for b in range(cube_count)]
     for g in range(8):
         part = slope_b[rows_b * g : rows_b * g + rows_b].reshape(cube_count, 2, 16, 256)
-        up = cot[:, :, 128 * g : 128 * g + 128].astype(F32) * 0.125
+        up = jnp.stack([ups[b][:, 128 * g : 128 * g + 128] for b in range(cube_count)])
         for z in range(2):
             for e in range(2):
                 at = 256 * g + 128 * e
                 grad_b[:, z, :, at : at + 128] = (up * part[:, z, :, 128 * e : 128 * e + 128]).astype(BF)
 
 
-def terms_b_kernel(pools, grad_b, out):
+def terms_b_kernel(where, pools, grad_b, *rest):
+    outs, terms = rest[:-1], rest[-1]
     cube_count = grad_b.shape[0]
     rows_b = cube_count * 2 * 16
     grads = jnp.concatenate(
         [grad_b[:, :, :, 256 * g : 256 * g + 256].reshape(rows_b, 256) for g in range(8)], axis=0
     )
+    terms[pl.ds(27, C2, stride=28), :] = jnp.zeros((C2, 128), F32)
     for dz in range(3):
         for dy in range(3):
             windows = jnp.concatenate(
@@ -184,12 +202,53 @@
             )
             full = dot_t(windows, grads)
             for dx in range(3):
-                at = 64 * (9 * dz + 3 * dy + dx)
                 term = full[64 * dx : 64 * dx + 64, :128] + full[64 * dx + 64 : 64 * dx + 128, 128:]
-                out[at : at + 64] = term.astype(BF)
-
-
-def backward_kernel(where, grad_b, recv_a, recv_b, tbt, dsl, xs, terms_b, ga_out, out, gs, ga, gpool, acc, sem):
+                terms[pl.ds(9 * dz + 3 * dy + dx, C2, stride=28), :] = term
+    share = ROWS_B // len(outs)
+    for k, out in enumerate(outs):
+        chunk = where[2] ^ k
+        out[...] = terms[pl.ds(pl.multiple_of(chunk * share, 8), share), :].astype(BF)
+
+
+def scatter_b_kernel(*refs):
+    parts, out = refs[1:-1], refs[-1]
+    total = parts[0][...].astype(F32)
+    for part in parts[1:]:
+        total = total + part[...].astype(F32)
+    out[...] = total.reshape(out.shape).astype(BF)
+
+
+def exchange_kernel(after, pieces_b, pieces_a, out):
+    del after
+    mine = jnp.concatenate(
+        [jnp.sum(pieces_b[...].astype(F32), axis=0), jnp.sum(pieces_a[...].astype(F32), axis=0)], axis=0
+    ).astype(BF)
+    for i in range(out.shape[0]):
+        out[i] = mine
+
+
+def collect_kernel(pieces, out):
+    count, rows, lanes = pieces.shape
+    piece = out.shape[0] - ROWS_A * out.shape[0] // (ROWS_A + ROWS_B)
+    piece = piece // count
+    parts = pieces[...].astype(F32)
+    whole = jnp.concatenate([parts[:, :piece].reshape(count * piece, lanes), jnp.sum(parts[:, piece:], axis=0)], axis=0)
+    out[...] = whole.astype(BF)
+
+
+def finish_kernel(where, scale, *refs):
+    parts, out_a, out_b, whole = refs[:-3], refs[-3], refs[-2], refs[-1]
+    for k, part in enumerate(parts):
+        whole[where[2] ^ k] = part[...].astype(F32)
+    for rows, width, base, out in ((ROWS_B, C2, 0, out_b), (ROWS_A, C1 // 2, ROWS_B // len(parts), out_a)):
+        each = width // len(parts)
+        for i in range(width):
+            start = base + 28 * (i % each)
+            out[:, 128 * i : 128 * i + 128] = whole[i // each, start : start + 27] * scale[0]
+
+
+def backward_kernel(where, grad_b, recv_a, recv_b, tbt, dsl, xs, after, ga_out, out, gs, ga, gpool, acc, term, terms, sem):
+    del after
     cube_count = grad_b.shape[0]
     even = where[0] % 2 == 0
     shifter = row_picker(3, 1, 16)
@@ -279,24 +338,20 @@
 
     leave = pltpu.make_async_copy(ga, ga_out, sem)
     leave.start()
-    out[:TERMS_B] = terms_b[...]
-    pending = None
+    terms[pl.ds(27, C1 // 2, stride=28), :] = jnp.zeros((C1 // 2, 128), F32)
+    mask = lanes_below((32, 128), 64)
     for d in range(9):
         full = acc[:, 256 * d : 256 * d + 256].T
         for dx in range(3):
             left = full[32 * dx : 32 * dx + 32, :128] + full[32 * dx + 32 : 32 * dx + 64, 128:]
             right = full[32 * dx + 64 : 32 * dx + 96, :128] + full[32 * dx + 96 : 32 * dx + 128, 128:]
-            mask = lanes_below((32, 128), 64)
             merged = jnp.where(mask, left, right)
-            total = merged + pltpu.roll(merged, 64, 1)
-            at = 3 * d + dx
-            if at % 2 == 0:
-                pending = total
-            else:
-                to = TERMS_B + 16 * (at - 1)
-                out[to : to + 32] = jnp.where(mask, pending, total).astype(BF)
-    out[TERMS_B + 416 : TERMS_B + TERMS_A] = pending.astype(BF)
-    out[TERMS_B + TERMS_A :] = jnp.zeros((out.shape[0] - TERMS_B - TERMS_A, 128), BF)
+            slot = (3 * d + dx) % 4
+            term[slot] = merged + pltpu.roll(merged, 64, 1)
+            evens = term[slot, pl.ds(0, C1 // 2, stride=2), :]
+            odds = term[slot, pl.ds(1, C1 // 2, stride=2), :]
+            terms[pl.ds(3 * d + dx, C1 // 2, stride=28), :] = jnp.where(mask[:16], evens, odds)
+    out[...] = terms[...].reshape(out.shape).astype(BF)
     leave.wait()
 
 
@@ -365,55 +420,35 @@
     return lax.ppermute(first, "gz", pairs_a), lax.ppermute(second, "gz", pairs_b)
 
 
-def gather_kernel(pieces, out):
-    mine = jnp.sum(pieces[...].astype(F32), axis=0).astype(BF)
-    for i in range(out.shape[0]):
-        out[i] = mine
-
-
-def total_of(partial, count):
-    rows, lanes = partial.shape
-    shape = (count, rows // count, lanes)
-    pieces = lax.all_to_all(partial.reshape(shape), AXES, 0, 0)
-    (copies,) = call(gather_kernel, [pieces], [(shape, BF)], [], 1_000_000)
-    return lax.all_to_all(copies, AXES, 0, 0).reshape(rows, lanes)
+def swap_samples(parts, count):
+    return [
+        lax.ppermute(part, "sample", [(i, i ^ k) for i in range(count)]) for k, part in enumerate(parts) if k
+    ]
 
 
 def shards(cubes, weight_a, weight_b, cotangent):
     cube_count = cubes.shape[0]
     ring = lax.axis_size("gz")
-    count = lax.axis_size("sample") * ring
-    me = lax.axis_index("gz")
-    where = jnp.stack([me, jnp.int32(ring)]).astype(jnp.int32)
-    odd = me % 2
-    first = lax.dynamic_slice_in_dim(cubes, 1 - odd, HALO, axis=1)
-    second = lax.dynamic_slice_in_dim(cubes, odd, HALO, axis=1)
-    recv_a, recv_b = swap(first, second, ring)
-
-    wa = weight_a.reshape(9, 96, C2)
-    wa2 = jnp.concatenate([wa, wa], axis=-1)
-    wb = weight_b.reshape(9, 192, C3)
-    wbt = weight_b.reshape(3, 3, 3, C2, C3)[::-1, ::-1, ::-1].transpose(0, 1, 2, 4, 3).reshape(9, 384, C2)
-    wbt2 = jnp.concatenate([wbt, wbt], axis=-1)
-    wat = weight_a.reshape(3, 3, 3, C1, C2)[::-1, ::-1].transpose(0, 1, 4, 2, 3).reshape(9, C2, 96)
-    wat = jnp.pad(wat, ((0, 0), (0, 0), (0, 32)))
-    cot = jnp.repeat(cotangent.reshape(cube_count, SIDE // 4, SIDE // 4 * C3), 2, axis=1)
-
-    own_xs, ta, tb, tbt = call(
+    samples = lax.axis_size("sample")
+    where = jnp.stack([lax.axis_index("gz"), jnp.int32(ring), lax.axis_index("sample")]).astype(jnp.int32)
+    recv_a, recv_b = swap(cubes, cubes, ring)
+
+    own_xs, ta, tb, tbt, wat = call(
         prepare_kernel,
-        [cubes, wa2, wb, wbt2],
+        [cubes, weight_a.reshape(9, 96, C2), weight_b.reshape(9, 192, C3)],
         [
             ((cube_count, ZD + 2 * HALO, 4, 16, 1152), BF),
             ((2304, 256), BF),
             ((2304, 256), BF),
             ((6912, 256), BF),
+            ((9, C2, 128), BF),
         ],
         [],
         1_000_000_000,
     )
     xs, dsl, pools, grad_b = call(
         forward_kernel,
-        [where, own_xs, recv_a, recv_b, ta, tb, cot],
+        [where, own_xs, recv_a, recv_b, ta, tb, cotangent],
         [
             ((cube_count, ZD + 2 * HALO, 4, 16, 1152), BF),
             ((cube_count, 6, 2, 16, 2048), BF),
@@ -426,24 +461,44 @@
         aliases={1: 0},
     )
     back_a, back_b = swap(grad_b, grad_b, ring)
-    (terms_b,) = call(terms_b_kernel, [pools, grad_b], [((TERMS_B, 128), BF)], [], 1_000_000_000)
-    rows = -(-(TERMS_B + TERMS_A) // (8 * count)) * 8 * count
-    rows = -(-rows // (16 * count)) * 16 * count if count > 32 else rows
-    ga, partial = call(
+    share_b, share_a = ROWS_B // samples, ROWS_A // samples
+    parts_b = call(
+        terms_b_kernel,
+        [where, pools, grad_b],
+        [((share_b, 128), BF)] * samples,
+        [pltpu.VMEM((ROWS_B, 128), F32)],
+        1_000_000_000,
+        smem=1,
+    )
+    others_b = swap_samples(parts_b, samples)
+    ga, partial_a = call(
         backward_kernel,
-        [where, grad_b, back_a, back_b, tbt, dsl, xs, terms_b],
-        [((cube_count, 6, 4, 16, 2304), BF), ((rows, 128), BF)],
+        [where, grad_b, back_a, back_b, tbt, dsl, xs, parts_b[0]],
+        [((cube_count, 6, 4, 16, 2304), BF), ((samples, share_a, 128), BF)],
         [
             pltpu.VMEM((cube_count, 6, 3, 16, 2304), BF),
             pltpu.VMEM((cube_count, 6, 4, 16, 2304), BF),
             pltpu.VMEM((cube_count, 4, 16, 1024), F32),
             pltpu.VMEM((256, 2304), F32),
+            pltpu.VMEM((4, C1, 128), F32),
+            pltpu.VMEM((ROWS_A, 128), F32),
             pltpu.SemaphoreType.DMA,
         ],
         6_000_000_000,
         smem=1,
+        any_in=(7,),
         any_out=(0,),
     )
+    (scattered_b,) = call(
+        scatter_b_kernel,
+        [partial_a, parts_b[0], *others_b],
+        [((ring, share_b // ring, 128), BF)],
+        [],
+        1_000_000,
+        any_in=(0,),
+    )
+    pieces_a = lax.all_to_all(partial_a, "sample", 0, 0)
+    pieces_b = lax.all_to_all(scattered_b, "gz", 0, 0)
     (input_grad,) = call(
         input_kernel,
         [ga, wat],
@@ -456,11 +511,25 @@
         4_000_000_000,
         any_in=(0,),
     )
-    scale = 1.0 / (cube_count * lax.axis_size("sample"))
-    total = total_of(partial, count)
-    total_b = total[:TERMS_B].astype(F32).reshape(27, C2 * C3) * scale
-    total_a = total[TERMS_B : TERMS_B + TERMS_A].astype(F32).reshape(14, C1, 2, C2).transpose(0, 2, 1, 3)
-    total_a = total_a.reshape(28, C1 * C2)[:27] * scale
+    (copies,) = call(
+        exchange_kernel,
+        [input_grad, pieces_b, pieces_a],
+        [((ring, share_b // ring + share_a, 128), BF)],
+        [],
+        1_000_000,
+        any_in=(0,),
+    )
+    pieces = lax.all_to_all(copies, "gz", 0, 0)
+    (mine,) = call(collect_kernel, [pieces], [((share_b + share_a, 128), BF)], [], 1_000_000)
+    scale = jnp.full((1,), 1.0 / (cube_count * samples), F32)
+    total_a, total_b = call(
+        finish_kernel,
+        [where, scale, mine, *swap_samples([mine] * samples, samples)],
+        [((27, C1 * C2), F32), ((27, C2 * C3), F32)],
+        [pltpu.VMEM((samples, share_b + share_a, 128), F32)],
+        1_000_000,
+        smem=2,
+    )
     return input_grad, total_a, total_b
 
 

time: 89.7 us -> 91.8 us (1.023)
  starting transfers between devices: 9.27 us -> 25.7 us
  blocking collectives: 29 us -> 16.4 us
  local copies, waits for them, and re-layouts: 14.8 us -> 8.28 us
  waiting for transfers between devices: 5.69 us -> 9.57 us
  Pallas kernels: 27.1 us -> 30.4 us
  other arithmetic: 2.49 us -> 0.08 us
    all_to_all x1, blocking collectives: 29 us -> 16.4 us  [shards(): pieces = lax.all_to_all(copies, 'gz', 0, 0)]
    ppermute x0 -> x6, starting transfers between devices: none -> 7.11 us  [swap_samples(): lax.ppermute(part, 'sample', [(i, i ^ k) for i in range(count)])]
    unnamed x8 -> x10, local copies, waits for them, and re-layouts: 0.16 us -> 5.83 us
    ppermute x0 -> x6, waiting for transfers between devices: none -> 5.31 us  [swap_samples(): lax.ppermute(part, 'sample', [(i, i ^ k) for i in range(count)])]
    ppermute x2, starting transfers between devices: 4.43 us -> 9.61 us  [swap(): lax.ppermute(first, 'gz', pairs_a)]
    reshape x9 -> x2, local copies, waits for them, and re-layouts: 6.62 us -> 2.45 us  [the longest x1 1.3 us: shards(): weight_b.reshape(9, 192, C3)]
    all_to_all x1 -> x2, starting transfers between devices: 3.5 us -> 7.6 us  [the longest x1 3.89 us: shards(): pieces_b = lax.all_to_all(scattered_b, 'gz', 0, 0)]
    pallas_call x6 -> x9, Pallas kernels: 27.1 us -> 30.4 us  [call(): pl.pallas_call(kernel, out_shape=[jax.ShapeDtypeStruct(shape, dtype) for...]
  transfers between devices with their start and end apart: 5 -> 12, of which waited for: 1 -> 3; matrix products, arithmetic and copies ran while one was open for 12% -> 3% of each run, Pallas kernels for 9% -> 21%
where the time goes in v1:
time: 91.8 us; the launch traced here: 91.2 us
  Pallas kernels  30.4 us (33%)
  starting transfers between devices  25.7 us (28%)
  blocking collectives  16.4 us (18%)
  waiting for transfers between devices  9.57 us (10%)
  local copies, waits for them, and re-layouts  8.28 us (9%)
    pallas_call x9, Pallas kernels, call(): pl.pallas_call(kernel, out_shape=[jax.ShapeDtypeStruct(shape, dtype) for...  30.4 us
    all_to_all x1, blocking collectives, shards(): pieces = lax.all_to_all(copies, 'gz', 0, 0)  16.4 us
    ppermute x2, starting transfers between devices, swap(): lax.ppermute(first, 'gz', pairs_a)  9.61 us
    ppermute x6, starting transfers between devices, swap_samples(): lax.ppermute(part, 'sample', [(i, i ^ k) for i in range(count)])  7.11 us
    unnamed x10, local copies, waits for them, and re-layouts  5.83 us
    ppermute x6, waiting for transfers between devices, swap_samples(): lax.ppermute(part, 'sample', [(i, i ^ k) for i in range(count)])  5.31 us
    all_to_all x1, waiting for transfers between devices, shards(): pieces_a = lax.all_to_all(partial_a, 'sample', 0, 0)  4.25 us
    all_to_all x1, starting transfers between devices, shards(): pieces_b = lax.all_to_all(scattered_b, 'gz', 0, 0)  3.89 us
  transfers between devices with their start and end apart: 12, of which 3 were waited for; matrix products, arithmetic and copies ran while one was open for 3% of the time, Pallas kernels for 21%

profile of v1, /device:TPU:0, one launch (start us, length us, event | category | flops | bytes accessed | tf_op | source)
XLA Modules:
  0.0 91.2 jit_solution(6700203132492978616)
XLA Ops:
  0.6 0.7 collective-permute-start.1
  1.3 4.4 %collective-permute-start = (bf16[2,4,32,1024]{3,2,1,0:T(8,128)(2,1)}, bf16[2,4,32,1024]{3,2,1,0:T(8,128)(2,1)S(1)}, u32[]{:S(2)}, u32[]{:S(2)}) collective-permute-start(bf16[2,4,32,1024]{3,2,1,0:T(8,128)(2,1)} %cubes.1), channel_id=1, source_target_pairs={{0,1},{1,0},{2,3},{3,2},{4,5},{5,4},{6,7},{7,6},{8,9},{9,8},{10,11... | collective-permute-start | bytes 1572872 | tf_op jit(solution)/shard_map/ppermute | solution.py:420
  5.8 1.1 %reshape.12.wa = bf16[9,96,64]{2,1,0:T(8,128)(2,1)S(1)} reshape(bf16[27,2048]{1,0:T(8,128)(2,1)} %param.5) | data formatting | bytes 221184 | tf_op jit(solution)/shard_map/reshape | solution.py:438
  6.9 1.3 %reshape.13.wb = bf16[9,192,128]{2,1,0:T(8,128)(2,1)S(1)} reshape(bf16[27,8192]{1,0:T(8,128)(2,1)} %param.6) | data formatting | bytes 884736 | tf_op jit(solution)/shard_map/reshape | solution.py:438
  8.2 1.0 %copy-done.1 = bf16[2,4,32,1024]{3,2,1,0:T(8,128)(2,1)S(1)} copy-done((bf16[2,4,32,1024]{3,2,1,0:T(8,128)(2,1)S(1)}, bf16[2,4,32,1024]{3,2,1,0:T(8,128)(2,1)}, u32[]{:S(2)}) %copy-start.1) | copy-done | bytes 524312
  9.3 1.2 %shard_map.67 = (bf16[2,10,4,16,1152]{4,3,2,1,0:T(8,128)(2,1)S(1)}, bf16[2304,256]{1,0:T(8,128)(2,1)S(1)}, bf16[2304,256]{1,0:T(8,128)(2,1)S(1)}, bf16[6912,256]{1,0:T(8,128)(2,1)S(1)}, bf16[9,64,128]{2,1,0:T(8,128)(2,1)S(1)}) custom-call(bf16[2,4,32,1024]{3,2,1,0:T(8,128)(2,1)S(1)} %copy-done.1, bf16[9,96,64]{2,1,0:T(8,128)(2,1)S(1)} %reshape.12.wa, ...), custom_call_target="tpu_custom_call" | custom-call | flops 1000000000 | bytes 1000000 | tf_op jit(solution)/shard_map/pallas_call | solution.py:405
  10.5 0.1 pad_add_fusion.where
  10.6 9.4 %shard_map.68 = (bf16[2,10,4,16,1152]{4,3,2,1,0:T(8,128)(2,1)S(1)}, bf16[2,6,2,16,2048]{4,3,2,1,0:T(8,128)(2,1)S(1)}, bf16[2,4,3,16,1152]{4,3,2,1,0:T(8,128)(2,1)S(1)}, bf16[2,2,16,2048]{3,2,1,0:T(8,128)(2,1)S(1)}) custom-call(s32[3]{0:T(128)S(1)} %pad_add_fusion.where, ...), custom_call_target="tpu_custom_call", output_to_operand_aliasing={{0}: (1, {})} | custom-call | flops 8000000000 | bytes 1000000 | tf_op jit(solution)/shard_map/pallas_call | solution.py:405
  20.0 0.7 collective-permute-start.3
  20.6 5.2 %collective-permute-start.2 = (bf16[2,2,16,2048]{3,2,1,0:T(8,128)(2,1)S(1)}, bf16[2,2,16,2048]{3,2,1,0:T(8,128)(2,1)S(1)}, u32[]{:S(2)}, u32[]{:S(2)}) collective-permute-start(bf16[2,2,16,2048]{3,2,1,0:T(8,128)(2,1)S(1)} %get-tuple-element.23.grad_b), channel_id=1, source_target_pairs={{0,1},{1,0},{2,3},{3,2},{4,5},{5,4},{6,7},{7,6},{8,9},{9,8},{10,11... | collective-permute-start | bytes 786440 | tf_op jit(solution)/shard_map/ppermute | solution.py:420
  25.8 1.4 %shard_map.69 = (bf16[448,128]{1,0:T(8,128)(2,1)S(1)}, bf16[448,128]{1,0:T(8,128)(2,1)S(1)}, bf16[448,128]{1,0:T(8,128)(2,1)S(1)}, bf16[448,128]{1,0:T(8,128)(2,1)S(1)}) custom-call(s32[3]{0:T(128)S(1)} %pad_add_fusion.where, bf16[2,4,3,16,1152]{4,3,2,1,0:T(8,128)(2,1)S(1)} %get-tuple-element.27.pools, bf16[2,2,16,2048]{3,2,1,0:T(8,128)(2,1)S(1)} %get-tuple-element.23.grad_b), custom_call_target="tpu_custom_call" | custom-call | flops 1000000000 | bytes 1000000 | tf_op jit(solution)/shard_map/pallas_call | solution.py:405
  27.3 1.5 %collective-permute-start.4 = (bf16[448,128]{1,0:T(8,128)(2,1)S(1)}, bf16[448,128]{1,0:T(8,128)(2,1)S(1)}, u32[]{:S(2)}, u32[]{:S(2)}) collective-permute-start(bf16[448,128]{1,0:T(8,128)(2,1)S(1)} %get-tuple-element.32), channel_id=1, source_target_pairs={{0,8},{8,0},{16,24},{24,16},{1,9},{9,1},{17,25},{25,17},{2,10},{10... | collective-permute-start | bytes 344072 | tf_op jit(solution)/shard_map/ppermute | solution.py:425
  28.8 1.5 %collective-permute-start.5 = (bf16[448,128]{1,0:T(8,128)(2,1)S(1)}, bf16[448,128]{1,0:T(8,128)(2,1)S(1)}, u32[]{:S(2)}, u32[]{:S(2)}) collective-permute-start(bf16[448,128]{1,0:T(8,128)(2,1)S(1)} %get-tuple-element.33), channel_id=1, source_target_pairs={{0,16},{8,24},{16,0},{24,8},{1,17},{9,25},{17,1},{25,9},{2,18},{10... | collective-permute-start | bytes 344072 | tf_op jit(solution)/shard_map/ppermute | solution.py:425
  30.4 0.5 collective-permute-start.6
  30.8 10.1 %shard_map.70 = (bf16[2,6,4,16,2304]{4,3,2,1,0:T(8,128)(2,1)S(1)}, bf16[4,112,128]{2,1,0:T(8,128)(2,1)}) custom-call(s32[3]{0:T(128)S(1)} %pad_add_fusion.where, bf16[2,2,16,2048]{3,2,1,0:T(8,128)(2,1)S(1)} %get-tuple-element.23.grad_b, bf16[2,2,16,2048]{3,2,1,0:T(8,128)(2,1)S(1)} %collective-permute-done.2.recv_a, ...), custom_call_target="tpu_custom_call" | custom-call | flops 6000000000 | bytes 1000000 | tf_op jit(solution)/shard_map/pallas_call | solution.py:405
  41.0 1.8 %copy-done.3 = bf16[2,6,4,16,2304]{4,3,2,1,0:T(8,128)(2,1)} copy-done((bf16[2,6,4,16,2304]{4,3,2,1,0:T(8,128)(2,1)}, bf16[2,6,4,16,2304]{4,3,2,1,0:T(8,128)(2,1)S(1)}, u32[]{:S(2)}) %copy-start.3) | copy-done | bytes 3538968
  42.7 3.7 %all-to-all-start.1 = ((bf16[4,112,128]{2,1,0:T(8,128)(2,1)}), bf16[4,112,128]{2,1,0:T(8,128)(2,1)S(1)}, u32[]{:S(2)}, u32[]{:S(2)}) async-start(bf16[4,112,128]{2,1,0:T(8,128)(2,1)} %get-tuple-element.31.refs_0_), calls=%async_computation.1 | async-start | bytes 229376 | tf_op jit(solution)/shard_map/all_to_all | solution.py:500
  46.5 0.7 shard_map.72
  47.2 4.3 %all-to-all-done.1.pieces_a = bf16[4,112,128]{2,1,0:T(8,128)(2,1)S(1)} async-done(((bf16[4,112,128]{2,1,0:T(8,128)(2,1)}), bf16[4,112,128]{2,1,0:T(8,128)(2,1)S(1)}, u32[]{:S(2)}, u32[]{:S(2)}) %all-to-all-start.1) | async-done | bytes 114720 | tf_op jit(solution)/shard_map/all_to_all | solution.py:500
  51.4 3.9 %all-to-all-start = ((bf16[8,56,128]{2,1,0:T(8,128)(2,1)}), bf16[8,56,128]{2,1,0:T(8,128)(2,1)S(1)}, u32[]{:S(2)}, u32[]{:S(2)}) async-start(bf16[8,56,128]{2,1,0:T(8,128)(2,1)} %shard_map.72), calls=%async_computation | async-start | bytes 229376 | tf_op jit(solution)/shard_map/all_to_all | solution.py:501
  55.3 2.0 %copy-done.4 = bf16[2,6,4,16,2304]{4,3,2,1,0:T(8,128)(2,1)S(1)} copy-done((bf16[2,6,4,16,2304]{4,3,2,1,0:T(8,128)(2,1)S(1)}, bf16[2,6,4,16,2304]{4,3,2,1,0:T(8,128)(2,1)}, u32[]{:S(2)}) %copy-start.4) | copy-done | bytes 3538968
  57.3 5.7 %shard_map.71.after = bf16[2,4,32,1024]{3,2,1,0:T(8,128)(2,1)} custom-call(bf16[2,6,4,16,2304]{4,3,2,1,0:T(8,128)(2,1)S(1)} %copy-done.4, bf16[9,64,128]{2,1,0:T(8,128)(2,1)S(1)} %get-tuple-element.30.wat), custom_call_target="tpu_custom_call" | custom-call | flops 4000000000 | bytes 1000000 | tf_op jit(solution)/shard_map/pallas_call | solution.py:405
  63.0 0.0 copy-start
  63.1 1.0 %copy-done = bf16[2,4,32,1024]{3,2,1,0:T(8,128)(2,1)S(1)} copy-done((bf16[2,4,32,1024]{3,2,1,0:T(8,128)(2,1)S(1)}, bf16[2,4,32,1024]{3,2,1,0:T(8,128)(2,1)}, u32[]{:S(2)}) %copy-start) | copy-done | bytes 524312
  64.1 16.4 %all_to_all.15.pieces = bf16[8,168,128]{2,1,0:T(8,128)(2,1)S(1)} all-to-all(bf16[8,168,128]{2,1,0:T(8,128)(2,1)S(1)} %shard_map.73), channel_id=1, replica_groups=mesh['sample'=4,'gz'=8] {'gz'}, dimensions={0} | all-to-all | bytes 688128 | tf_op jit(solution)/shard_map/all_to_all | solution.py:522
  80.5 0.1 shard_map.74.refs_0_
  80.6 0.7 collective-permute-start.9
  81.3 1.7 %collective-permute-start.8 = (bf16[560,128]{1,0:T(8,128)(2,1)S(1)}, bf16[560,128]{1,0:T(8,128)(2,1)S(1)}, u32[]{:S(2)}, u32[]{:S(2)}) collective-permute-start(bf16[560,128]{1,0:T(8,128)(2,1)S(1)} %shard_map.74.refs_0_), channel_id=1, source_target_pairs={{0,16},{8,24},{16,0},{24,8},{1,17},{9,25},{17,1},{25,9},{2,18},{10... | collective-permute-start | bytes 430088 | tf_op jit(solution)/shard_map/ppermute | solution.py:425
  83.0 1.2 %collective-permute-start.7 = (bf16[560,128]{1,0:T(8,128)(2,1)S(1)}, bf16[560,128]{1,0:T(8,128)(2,1)S(1)}, u32[]{:S(2)}, u32[]{:S(2)}) collective-permute-start(bf16[560,128]{1,0:T(8,128)(2,1)S(1)} %shard_map.74.refs_0_), channel_id=1, source_target_pairs={{0,8},{8,0},{16,24},{24,16},{1,9},{9,1},{17,25},{25,17},{2,10},{10... | collective-permute-start | bytes 430088 | tf_op jit(solution)/shard_map/ppermute | solution.py:425
  84.1 4.1 %collective-permute-done.9.refs_3_ = bf16[560,128]{1,0:T(8,128)(2,1)S(1)} collective-permute-done((bf16[560,128]{1,0:T(8,128)(2,1)S(1)}, bf16[560,128]{1,0:T(8,128)(2,1)S(1)}, u32[]{:S(2)}, u32[]{:S(2)}) %collective-permute-start.9) | collective-permute-done | bytes 143392 | tf_op jit(solution)/shard_map/ppermute | solution.py:425
  88.2 1.2 %collective-permute-done.8.refs_2_ = bf16[560,128]{1,0:T(8,128)(2,1)S(1)} collective-permute-done((bf16[560,128]{1,0:T(8,128)(2,1)S(1)}, bf16[560,128]{1,0:T(8,128)(2,1)S(1)}, u32[]{:S(2)}, u32[]{:S(2)}) %collective-permute-start.8) | collective-permute-done | bytes 143392 | tf_op jit(solution)/shard_map/ppermute | solution.py:425
  89.4 1.7 %shard_map.75 = (f32[27,2048]{1,0:T(8,128)}, f32[27,8192]{1,0:T(8,128)}) custom-call(s32[3]{0:T(128)S(1)} %pad_add_fusion.where, f32[1]{0:T(128)} %constant.11.clone.1.scale, bf16[560,128]{1,0:T(8,128)(2,1)S(1)} %shard_map.74.refs_0_, bf16[560,128]{1,0:T(8,128)(2,1)S(1)} %collective-permute-done.7.refs_1_, ...), custom_call_target="tpu_custom_call" | custom-call | flops 1000000 | bytes 1000000 | tf_op jit(solution)/shard_map/pallas_call | solution.py:405
  (15 shorter events, 0.1 us)
Async XLA Ops:
  0.6 10.0 %copy-start.2 = (bf16[2,1,8,1024]{3,2,1,0:T(8,128)(2,1)S(1)}, bf16[2,1,8,1024]{3,2,1,0:T(8,128)(2,1)}, u32[]{:S(2)}) copy-start(bf16[2,1,8,1024]{3,2,1,0:T(8,128)(2,1)} %cot.1) | copy-start | bytes 98308
  0.6 10.0 %collective-permute-start.1 = (bf16[2,4,32,1024]{3,2,1,0:T(8,128)(2,1)}, bf16[2,4,32,1024]{3,2,1,0:T(8,128)(2,1)S(1)}, u32[]{:S(2)}, u32[]{:S(2)}) collective-permute-start(bf16[2,4,32,1024]{3,2,1,0:T(8,128)(2,1)} %cubes.1), channel_id=1, source_target_pairs={{1,2},{2,1},{3,4},{4,3},{5,6},{6,5},{9,10},{10,9},{11,12},{12,11},... | collective-permute-start | bytes 1572872 | tf_op jit(solution)/shard_map/ppermute | solution.py:420
  1.3 9.3 %collective-permute-start = (bf16[2,4,32,1024]{3,2,1,0:T(8,128)(2,1)}, bf16[2,4,32,1024]{3,2,1,0:T(8,128)(2,1)S(1)}, u32[]{:S(2)}, u32[]{:S(2)}) collective-permute-start(bf16[2,4,32,1024]{3,2,1,0:T(8,128)(2,1)} %cubes.1), channel_id=1, source_target_pairs={{0,1},{1,0},{2,3},{3,2},{4,5},{5,4},{6,7},{7,6},{8,9},{9,8},{10,11... | collective-permute-start | bytes 1572872 | tf_op jit(solution)/shard_map/ppermute | solution.py:420
  8.2 1.0 %copy-start.1 = (bf16[2,4,32,1024]{3,2,1,0:T(8,128)(2,1)S(1)}, bf16[2,4,32,1024]{3,2,1,0:T(8,128)(2,1)}, u32[]{:S(2)}) copy-start(bf16[2,4,32,1024]{3,2,1,0:T(8,128)(2,1)} %cubes.1) | copy-start | bytes 1572868
  20.0 10.9 %collective-permute-start.3 = (bf16[2,2,16,2048]{3,2,1,0:T(8,128)(2,1)S(1)}, bf16[2,2,16,2048]{3,2,1,0:T(8,128)(2,1)S(1)}, u32[]{:S(2)}, u32[]{:S(2)}) collective-permute-start(bf16[2,2,16,2048]{3,2,1,0:T(8,128)(2,1)S(1)} %get-tuple-element.23.grad_b), channel_id=1, source_target_pairs={{1,2},{2,1},{3,4},{4,3},{5,6},{6,5},{9,10},{10,9},{11,12},{12,11},... | collective-permute-start | bytes 786440 | tf_op jit(solution)/shard_map/ppermute | solution.py:420
  20.6 10.2 %collective-permute-start.2 = (bf16[2,2,16,2048]{3,2,1,0:T(8,128)(2,1)S(1)}, bf16[2,2,16,2048]{3,2,1,0:T(8,128)(2,1)S(1)}, u32[]{:S(2)}, u32[]{:S(2)}) collective-permute-start(bf16[2,2,16,2048]{3,2,1,0:T(8,128)(2,1)S(1)} %get-tuple-element.23.grad_b), channel_id=1, source_target_pairs={{0,1},{1,0},{2,3},{3,2},{4,5},{5,4},{6,7},{7,6},{8,9},{9,8},{10,11... | collective-permute-start | bytes 786440 | tf_op jit(solution)/shard_map/ppermute | solution.py:420
  27.3 19.2 %collective-permute-start.4 = (bf16[448,128]{1,0:T(8,128)(2,1)S(1)}, bf16[448,128]{1,0:T(8,128)(2,1)S(1)}, u32[]{:S(2)}, u32[]{:S(2)}) collective-permute-start(bf16[448,128]{1,0:T(8,128)(2,1)S(1)} %get-tuple-element.32), channel_id=1, source_target_pairs={{0,8},{8,0},{16,24},{24,16},{1,9},{9,1},{17,25},{25,17},{2,10},{10... | collective-permute-start | bytes 344072 | tf_op jit(solution)/shard_map/ppermute | solution.py:425
  28.8 17.6 %collective-permute-start.5 = (bf16[448,128]{1,0:T(8,128)(2,1)S(1)}, bf16[448,128]{1,0:T(8,128)(2,1)S(1)}, u32[]{:S(2)}, u32[]{:S(2)}) collective-permute-start(bf16[448,128]{1,0:T(8,128)(2,1)S(1)} %get-tuple-element.33), channel_id=1, source_target_pairs={{0,16},{8,24},{16,0},{24,8},{1,17},{9,25},{17,1},{25,9},{2,18},{10... | collective-permute-start | bytes 344072 | tf_op jit(solution)/shard_map/ppermute | solution.py:425
  30.4 16.1 %collective-permute-start.6 = (bf16[448,128]{1,0:T(8,128)(2,1)S(1)}, bf16[448,128]{1,0:T(8,128)(2,1)S(1)}, u32[]{:S(2)}, u32[]{:S(2)}) collective-permute-start(bf16[448,128]{1,0:T(8,128)(2,1)S(1)} %get-tuple-element.34), channel_id=1, source_target_pairs={{0,24},{8,16},{16,8},{24,0},{1,25},{9,17},{17,9},{25,1},{2,26},{10... | collective-permute-start | bytes 344072 | tf_op jit(solution)/shard_map/ppermute | solution.py:425
  41.0 1.8 %copy-start.3 = (bf16[2,6,4,16,2304]{4,3,2,1,0:T(8,128)(2,1)}, bf16[2,6,4,16,2304]{4,3,2,1,0:T(8,128)(2,1)S(1)}, u32[]{:S(2)}) copy-start(bf16[2,6,4,16,2304]{4,3,2,1,0:T(8,128)(2,1)S(1)} %get-tuple-element.29.ga_in) | copy-start | bytes 10616836
  42.7 8.7 %all-to-all-start.1 = ((bf16[4,112,128]{2,1,0:T(8,128)(2,1)}), bf16[4,112,128]{2,1,0:T(8,128)(2,1)S(1)}, u32[]{:S(2)}, u32[]{:S(2)}) async-start(bf16[4,112,128]{2,1,0:T(8,128)(2,1)} %get-tuple-element.31.refs_0_), calls=%async_computation.1 | async-start | bytes 229376 | tf_op jit(solution)/shard_map/all_to_all | solution.py:500
  51.4 11.6 %all-to-all-start = ((bf16[8,56,128]{2,1,0:T(8,128)(2,1)}), bf16[8,56,128]{2,1,0:T(8,128)(2,1)S(1)}, u32[]{:S(2)}, u32[]{:S(2)}) async-start(bf16[8,56,128]{2,1,0:T(8,128)(2,1)} %shard_map.72), calls=%async_computation | async-start | bytes 229376 | tf_op jit(solution)/shard_map/all_to_all | solution.py:501
  55.3 2.0 %copy-start.4 = (bf16[2,6,4,16,2304]{4,3,2,1,0:T(8,128)(2,1)S(1)}, bf16[2,6,4,16,2304]{4,3,2,1,0:T(8,128)(2,1)}, u32[]{:S(2)}) copy-start(bf16[2,6,4,16,2304]{4,3,2,1,0:T(8,128)(2,1)} %copy-done.3) | copy-start | bytes 10616836
  63.0 1.0 %copy-start = (bf16[2,4,32,1024]{3,2,1,0:T(8,128)(2,1)S(1)}, bf16[2,4,32,1024]{3,2,1,0:T(8,128)(2,1)}, u32[]{:S(2)}) copy-start(bf16[2,4,32,1024]{3,2,1,0:T(8,128)(2,1)} %shard_map.71.after) | copy-start | bytes 1572868
  80.6 7.6 %collective-permute-start.9 = (bf16[560,128]{1,0:T(8,128)(2,1)S(1)}, bf16[560,128]{1,0:T(8,128)(2,1)S(1)}, u32[]{:S(2)}, u32[]{:S(2)}) collective-permute-start(bf16[560,128]{1,0:T(8,128)(2,1)S(1)} %shard_map.74.refs_0_), channel_id=1, source_target_pairs={{0,24},{8,16},{16,8},{24,0},{1,25},{9,17},{17,9},{25,1},{2,26},{10... | collective-permute-start | bytes 430088 | tf_op jit(solution)/shard_map/ppermute | solution.py:425
  81.3 8.2 %collective-permute-start.8 = (bf16[560,128]{1,0:T(8,128)(2,1)S(1)}, bf16[560,128]{1,0:T(8,128)(2,1)S(1)}, u32[]{:S(2)}, u32[]{:S(2)}) collective-permute-start(bf16[560,128]{1,0:T(8,128)(2,1)S(1)} %shard_map.74.refs_0_), channel_id=1, source_target_pairs={{0,16},{8,24},{16,0},{24,8},{1,17},{9,25},{17,1},{25,9},{2,18},{10... | collective-permute-start | bytes 430088 | tf_op jit(solution)/shard_map/ppermute | solution.py:425
  83.0 6.5 %collective-permute-start.7 = (bf16[560,128]{1,0:T(8,128)(2,1)S(1)}, bf16[560,128]{1,0:T(8,128)(2,1)S(1)}, u32[]{:S(2)}, u32[]{:S(2)}) collective-permute-start(bf16[560,128]{1,0:T(8,128)(2,1)S(1)} %shard_map.74.refs_0_), channel_id=1, source_target_pairs={{0,8},{8,0},{16,24},{24,16},{1,9},{9,1},{17,25},{25,17},{2,10},{10... | collective-permute-start | bytes 430088 | tf_op jit(solution)/shard_map/ppermute | solution.py:425

commit v2 on v1

--- a/solution.py
+++ b/solution.py
@@ -15,7 +15,6 @@
 ROWS_A = C1 // 2 * 28
 BF = jnp.bfloat16
 F32 = jnp.float32
-AXES = ("sample", "gz")
 VMEM = pl.BlockSpec(memory_space=pltpu.VMEM)
 SMEM = pl.BlockSpec(memory_space=pltpu.SMEM)
 ANY = pl.BlockSpec(memory_space=pl.ANY)
@@ -210,44 +209,56 @@
         out[...] = terms[pl.ds(pl.multiple_of(chunk * share, 8), share), :].astype(BF)
 
 
-def scatter_b_kernel(*refs):
-    parts, out = refs[1:-1], refs[-1]
-    total = parts[0][...].astype(F32)
-    for part in parts[1:]:
-        total = total + part[...].astype(F32)
-    out[...] = total.reshape(out.shape).astype(BF)
-
-
-def exchange_kernel(after, pieces_b, pieces_a, out):
+def tree(parts):
+    while len(parts) > 1:
+        parts = [left + right for left, right in zip(parts[::2], parts[1::2])]
+    return parts[0]
+
+
+def halve_kernel(where, after, *refs):
     del after
+    parts, keep, send = refs[:-2], refs[-2], refs[-1]
+    count = len(parts) // 2
     mine = jnp.concatenate(
-        [jnp.sum(pieces_b[...].astype(F32), axis=0), jnp.sum(pieces_a[...].astype(F32), axis=0)], axis=0
-    ).astype(BF)
-    for i in range(out.shape[0]):
-        out[i] = mine
-
-
-def collect_kernel(pieces, out):
-    count, rows, lanes = pieces.shape
-    piece = out.shape[0] - ROWS_A * out.shape[0] // (ROWS_A + ROWS_B)
-    piece = piece // count
-    parts = pieces[...].astype(F32)
-    whole = jnp.concatenate([parts[:, :piece].reshape(count * piece, lanes), jnp.sum(parts[:, piece:], axis=0)], axis=0)
-    out[...] = whole.astype(BF)
-
-
-def finish_kernel(where, scale, *refs):
-    parts, out_a, out_b, whole = refs[:-3], refs[-3], refs[-2], refs[-1]
+        [
+            tree([part[...].astype(F32) for part in parts[:count]]),
+            tree([part[...].astype(F32) for part in parts[count:]]),
+        ],
+        axis=0,
+    )
+    half = keep.shape[0]
+    low = where[0] % 2 == 0
+    keep[...] = jnp.where(low, mine[:half], mine[half:]).astype(BF)
+    send[...] = jnp.where(low, mine[half:], mine[:half]).astype(BF)
+
+
+def add_kernel(after, *refs):
+    del after
+    parts, out = refs[:-1], refs[-1]
+    out[...] = tree([part[...].astype(F32) for part in parts]).astype(BF)
+
+
+def stack_kernel(where, *refs):
+    parts, out = refs[:-1], refs[-1]
     for k, part in enumerate(parts):
-        whole[where[2] ^ k] = part[...].astype(F32)
-    for rows, width, base, out in ((ROWS_B, C2, 0, out_b), (ROWS_A, C1 // 2, ROWS_B // len(parts), out_a)):
-        each = width // len(parts)
+        out[where[2] ^ k] = part[...]
+
+
+def finish_kernel(where, scale, own, other, out_a, out_b, whole):
+    core = where[0] % 2
+    whole[core] = own[...].astype(F32)
+    whole[1 - core] = other[...].astype(F32)
+    count, half = own.shape[0], own.shape[1]
+    for width, base, out in ((C2, 0, out_b), (C1 // 2, ROWS_B // count, out_a)):
+        each = width // count
         for i in range(width):
             start = base + 28 * (i % each)
-            out[:, 128 * i : 128 * i + 128] = whole[i // each, start : start + 27] * scale[0]
-
-
-def backward_kernel(where, grad_b, recv_a, recv_b, tbt, dsl, xs, after, ga_out, out, gs, ga, gpool, acc, term, terms, sem):
+            piece = whole[start // half, i // each, start % half : start % half + 27]
+            out[:, 128 * i : 128 * i + 128] = piece * scale[0]
+
+
+def backward_kernel(where, grad_b, recv_a, recv_b, tbt, dsl, xs, after, ga, *rest):
+    outs, (gs, gpool, acc, term, terms) = rest[:-5], rest[-5:]
     del after
     cube_count = grad_b.shape[0]
     even = where[0] % 2 == 0
@@ -336,8 +347,6 @@
 
     lax.fori_loop(0, 8, group, 0)
 
-    leave = pltpu.make_async_copy(ga, ga_out, sem)
-    leave.start()
     terms[pl.ds(27, C1 // 2, stride=28), :] = jnp.zeros((C1 // 2, 128), F32)
     mask = lanes_below((32, 128), 64)
     for d in range(9):
@@ -351,17 +360,16 @@
             evens = term[slot, pl.ds(0, C1 // 2, stride=2), :]
             odds = term[slot, pl.ds(1, C1 // 2, stride=2), :]
             terms[pl.ds(3 * d + dx, C1 // 2, stride=28), :] = jnp.where(mask[:16], evens, odds)
-    out[...] = terms[...].reshape(out.shape).astype(BF)
-    leave.wait()
+    share = ROWS_A // len(outs)
+    for k, out in enumerate(outs):
+        chunk = where[2] ^ k
+        out[...] = terms[pl.ds(pl.multiple_of(chunk * share, 8), share), :].astype(BF)
 
 
 RANKS = (-3, -1, 0, 2, 1, 3, 4, 6, 5, 7, 8, 10)
 
 
-def input_kernel(ga_in, wat, out, tat, ga, sem):
-    arrive = pltpu.make_async_copy(ga_in, ga, sem)
-    arrive.start()
-    cube_count = ga.shape[0]
+def mirror_kernel(wat, tat):
     lane = lax.broadcasted_iota(jnp.int32, (64, 128), 1)
     for d in range(9):
         block = wat[d].astype(F32)
@@ -373,8 +381,9 @@
                 value = jnp.where(keep, turned[(rank - 1) % 4], 0.0).astype(BF)
                 tat[768 * d + 64 * slot : 768 * d + 64 * slot + 64, 128 * half : 128 * half + 128] = value
 
-    arrive.wait()
-    rows = cube_count * ZD * 16
+
+def one_cube(b, ga, tat, out, token, block, sem):
+    rows = ZD * 16
     sides = []
     for p in range(2):
         columns = []
@@ -382,22 +391,36 @@
             for dy in range(3):
                 columns.append(
                     jnp.concatenate(
-                        [
-                            ga[:, dz : dz + ZD, p + dy, :, 512 * q : 512 * q + 768].reshape(rows, 768)
-                            for q in range(4)
-                        ],
+                        [ga[b, dz : dz + ZD, p + dy, :, 512 * q : 512 * q + 768].reshape(rows, 768) for q in range(4)],
                         axis=0,
                     )
                 )
-        sides.append(dot(jnp.concatenate(columns, axis=1), tat[...]).astype(BF).reshape(4, cube_count, ZD, 16, 256))
+        sides.append(jnp.concatenate(columns, axis=1))
+    both = dot(jnp.concatenate(sides, axis=0), tat[...]).astype(BF).reshape(2, 4, ZD, 16, 256)
     row = lax.broadcasted_iota(jnp.int32, (32, 32), 0)
     col = lax.broadcasted_iota(jnp.int32, (32, 32), 1)
     mixer = jnp.where(col == row // 2 + 16 * (row % 2), 1.0, 0.0).astype(BF)
-    for b in range(cube_count):
-        for z in range(ZD):
-            for q in range(4):
-                both = jnp.concatenate([sides[0][q, b, z], sides[1][q, b, z]], axis=0)
-                out[b, z, :, 256 * q : 256 * q + 256] = dot(mixer, both).astype(BF)
+    for z in range(ZD):
+        for q in range(4):
+            pair = jnp.concatenate([both[0, q, z], both[1, q, z]], axis=0)
+            block[z, :, 256 * q : 256 * q + 256] = dot(mixer, pair).astype(BF)
+    leave = pltpu.make_async_copy(block, out.at[b], sem)
+    leave.start()
+    token[...] = jnp.zeros_like(token)
+    leave.wait()
+
+
+def first_cube_kernel(ga, wat, out, tat, token, block, sem):
+    mirror_kernel(wat, tat)
+    one_cube(0, ga, tat, out, token, block, sem)
+
+
+def later_cube_kernel(b):
+    def kernel(before, ga, tat, out, token, block, sem):
+        del before
+        one_cube(b, ga, tat, out, token, block, sem)
+
+    return kernel
 
 
 def call(kernel, args, outs, scratch, flops, smem=0, any_in=(), any_out=(), aliases=None):
@@ -420,9 +443,10 @@
     return lax.ppermute(first, "gz", pairs_a), lax.ppermute(second, "gz", pairs_b)
 
 
-def swap_samples(parts, count):
+def swap_along(parts, axis, step):
+    count = lax.axis_size(axis)
     return [
-        lax.ppermute(part, "sample", [(i, i ^ k) for i in range(count)]) for k, part in enumerate(parts) if k
+        lax.ppermute(part, axis, [(i, i ^ (k * step)) for i in range(count)]) for k, part in enumerate(parts) if k
     ]
 
 
@@ -470,63 +494,58 @@
         1_000_000_000,
         smem=1,
     )
-    others_b = swap_samples(parts_b, samples)
-    ga, partial_a = call(
+    others_b = swap_along(parts_b, "sample", 1)
+    ga, *parts_a = call(
         backward_kernel,
         [where, grad_b, back_a, back_b, tbt, dsl, xs, parts_b[0]],
-        [((cube_count, 6, 4, 16, 2304), BF), ((samples, share_a, 128), BF)],
+        [((cube_count, 6, 4, 16, 2304), BF)] + [((share_a, 128), BF)] * samples,
         [
             pltpu.VMEM((cube_count, 6, 3, 16, 2304), BF),
-            pltpu.VMEM((cube_count, 6, 4, 16, 2304), BF),
             pltpu.VMEM((cube_count, 4, 16, 1024), F32),
             pltpu.VMEM((256, 2304), F32),
             pltpu.VMEM((4, C1, 128), F32),
             pltpu.VMEM((ROWS_A, 128), F32),
-            pltpu.SemaphoreType.DMA,
         ],
         6_000_000_000,
         smem=1,
-        any_in=(7,),
-        any_out=(0,),
-    )
-    (scattered_b,) = call(
-        scatter_b_kernel,
-        [partial_a, parts_b[0], *others_b],
-        [((ring, share_b // ring, 128), BF)],
-        [],
-        1_000_000,
-        any_in=(0,),
-    )
-    pieces_a = lax.all_to_all(partial_a, "sample", 0, 0)
-    pieces_b = lax.all_to_all(scattered_b, "gz", 0, 0)
-    (input_grad,) = call(
-        input_kernel,
-        [ga, wat],
-        [((cube_count, ZD, SIDE, SIDE * C1), BF)],
-        [
-            pltpu.VMEM((6912, 256), BF),
-            pltpu.VMEM((cube_count, 6, 4, 16, 2304), BF),
-            pltpu.SemaphoreType.DMA,
-        ],
-        4_000_000_000,
-        any_in=(0,),
-    )
-    (copies,) = call(
-        exchange_kernel,
-        [input_grad, pieces_b, pieces_a],
-        [((ring, share_b // ring + share_a, 128), BF)],
-        [],
-        1_000_000,
-        any_in=(0,),
-    )
-    pieces = lax.all_to_all(copies, "gz", 0, 0)
-    (mine,) = call(collect_kernel, [pieces], [((share_b + share_a, 128), BF)], [], 1_000_000)
+    )
+    others_a = swap_along(parts_a, "sample", 1)
+    whole = ((cube_count, ZD, SIDE, SIDE * C1), BF)
+    token = ((8, 128), F32)
+    block = [pltpu.VMEM((ZD, SIDE, SIDE * C1), BF), pltpu.SemaphoreType.DMA]
+    input_grad, tat, done = call(
+        first_cube_kernel, [ga, wat], [whole, ((6912, 256), BF), token], block, 2_000_000_000, any_out=(0,)
+    )
+    half = (share_b + share_a) // 2
+    small = [((half, 128), BF)]
+    keep, send = call(
+        halve_kernel, [where, done, parts_b[0], *others_b, parts_a[0], *others_a], small * 2, [], 1_000_000, smem=1
+    )
+    (keep,) = call(add_kernel, [done, keep, *swap_along([send] * 2, "gz", 1)], small, [], 1_000_000)
+    others = swap_along([keep] * (ring // 2), "gz", 2)
+    for b in range(1, cube_count):
+        input_grad, done = call(
+            later_cube_kernel(b),
+            [input_grad, ga, tat],
+            [whole, token],
+            block,
+            2_000_000_000,
+            any_in=(0,),
+            any_out=(0,),
+            aliases={0: 0},
+        )
+    (keep,) = call(add_kernel, [done, keep, *others], small, [], 1_000_000)
+    shape = (samples, half, 128)
+    (own,) = call(
+        stack_kernel, [where, keep, *swap_along([keep] * samples, "sample", 1)], [(shape, BF)], [], 1_000_000, smem=1
+    )
+    (other,) = swap_along([own] * 2, "gz", 1)
     scale = jnp.full((1,), 1.0 / (cube_count * samples), F32)
     total_a, total_b = call(
         finish_kernel,
-        [where, scale, mine, *swap_samples([mine] * samples, samples)],
+        [where, scale, own, other],
         [((27, C1 * C2), F32), ((27, C2 * C3), F32)],
-        [pltpu.VMEM((samples, share_b + share_a, 128), F32)],
+        [pltpu.VMEM((2, *shape), F32)],
         1_000_000,
         smem=2,
     )

time: 91.8 us -> 70.6 us (0.77)
  blocking collectives: 16.4 us -> 0 us
  local copies, waits for them, and re-layouts: 8.28 us -> 3.49 us
    all_to_all x1 -> x0, blocking collectives: 16.4 us -> none  [shards(): pieces = lax.all_to_all(copies, 'gz', 0, 0)]
    ppermute x6 -> x14, starting transfers between devices: 7.11 us -> 15.3 us  [swap_along(): lax.ppermute(part, axis, [(i, i ^ k * step) for i in range(count)])]
    all_to_all x2 -> x0, starting transfers between devices: 7.6 us -> none  [the longest x1 3.89 us: shards(): pieces_b = lax.all_to_all(scattered_b, 'gz', 0, 0)]
    unnamed x10 -> x4, local copies, waits for them, and re-layouts: 5.83 us -> 1.04 us
    all_to_all x2 -> x0, waiting for transfers between devices: 4.25 us -> none  [the longest x1 4.25 us: shards(): pieces_a = lax.all_to_all(partial_a, 'sample', 0, 0)]
    ppermute x6 -> x14, waiting for transfers between devices: 5.31 us -> 9.16 us  [swap_along(): lax.ppermute(part, axis, [(i, i ^ k * step) for i in range(count)])]
    pallas_call x9 -> x11, Pallas kernels: 30.4 us -> 30.4 us  [call(): pl.pallas_call(kernel, out_shape=[jax.ShapeDtypeStruct(shape, dtype) for...]
  transfers between devices with their start and end apart: 12 -> 18, of which waited for: 3 -> 6; matrix products, arithmetic and copies ran while one was open for 3% -> 4% of each run, Pallas kernels for 21% -> 26%
where the time goes in v2:
time: 70.6 us; the launch traced here: 70.3 us
  Pallas kernels  30.4 us (43%)
  starting transfers between devices  26.4 us (37%)
  waiting for transfers between devices  9.17 us (13%)
  local copies, waits for them, and re-layouts  3.49 us (5%)
  between operations  0.81 us (1%)
    pallas_call x11, Pallas kernels, call(): pl.pallas_call(kernel, out_shape=[jax.ShapeDtypeStruct(shape, dtype) for...  30.4 us
    ppermute x14, starting transfers between devices, swap_along(): lax.ppermute(part, axis, [(i, i ^ k * step) for i in range(count)])  15.3 us
    ppermute x2, starting transfers between devices, swap(): lax.ppermute(first, 'gz', pairs_a)  9.6 us
    ppermute x14, waiting for transfers between devices, swap_along(): lax.ppermute(part, axis, [(i, i ^ k * step) for i in range(count)])  9.16 us
    ppermute x2, starting transfers between devices, swap(): lax.ppermute(second, 'gz', pairs_b)  1.55 us
  transfers between devices with their start and end apart: 18, of which 6 were waited for; matrix products, arithmetic and copies ran while one was open for 4% of the time, Pallas kernels for 26%

profile of v2, /device:TPU:0, one launch (start us, length us, event | category | flops | bytes accessed | tf_op | source)
XLA Modules:
  0.0 70.3 jit_solution(169370019970854674)
XLA Ops:
  0.6 0.7 collective-permute-start.1
  1.3 4.4 %collective-permute-start = (bf16[2,4,32,1024]{3,2,1,0:T(8,128)(2,1)}, bf16[2,4,32,1024]{3,2,1,0:T(8,128)(2,1)S(1)}, u32[]{:S(2)}, u32[]{:S(2)}) collective-permute-start(bf16[2,4,32,1024]{3,2,1,0:T(8,128)(2,1)} %cubes.1), channel_id=1, source_target_pairs={{0,1},{1,0},{2,3},{3,2},{4,5},{5,4},{6,7},{7,6},{8,9},{9,8},{10,11... | collective-permute-start | bytes 1572872 | tf_op jit(solution)/shard_map/ppermute | solution.py:443
  5.8 1.1 %reshape.12.wa = bf16[9,96,64]{2,1,0:T(8,128)(2,1)S(1)} reshape(bf16[27,2048]{1,0:T(8,128)(2,1)} %param.5) | data formatting | bytes 221184 | tf_op jit(solution)/shard_map/reshape | solution.py:462
  6.9 1.3 %reshape.13.wb = bf16[9,192,128]{2,1,0:T(8,128)(2,1)S(1)} reshape(bf16[27,8192]{1,0:T(8,128)(2,1)} %param.6) | data formatting | bytes 884736 | tf_op jit(solution)/shard_map/reshape | solution.py:462
  8.2 1.0 %copy-done = bf16[2,4,32,1024]{3,2,1,0:T(8,128)(2,1)S(1)} copy-done((bf16[2,4,32,1024]{3,2,1,0:T(8,128)(2,1)S(1)}, bf16[2,4,32,1024]{3,2,1,0:T(8,128)(2,1)}, u32[]{:S(2)}) %copy-start) | copy-done | bytes 524312
  9.3 1.2 %shard_map.67 = (bf16[2,10,4,16,1152]{4,3,2,1,0:T(8,128)(2,1)S(1)}, bf16[2304,256]{1,0:T(8,128)(2,1)S(1)}, bf16[2304,256]{1,0:T(8,128)(2,1)S(1)}, bf16[6912,256]{1,0:T(8,128)(2,1)S(1)}, bf16[9,64,128]{2,1,0:T(8,128)(2,1)S(1)}) custom-call(bf16[2,4,32,1024]{3,2,1,0:T(8,128)(2,1)S(1)} %copy-done, bf16[9,96,64]{2,1,0:T(8,128)(2,1)S(1)} %reshape.12.wa, ...), custom_call_target="tpu_custom_call" | custom-call | flops 1000000000 | bytes 1000000 | tf_op jit(solution)/shard_map/pallas_call | solution.py:428
  10.6 9.3 %shard_map.68 = (bf16[2,10,4,16,1152]{4,3,2,1,0:T(8,128)(2,1)S(1)}, bf16[2,6,2,16,2048]{4,3,2,1,0:T(8,128)(2,1)S(1)}, bf16[2,4,3,16,1152]{4,3,2,1,0:T(8,128)(2,1)S(1)}, bf16[2,2,16,2048]{3,2,1,0:T(8,128)(2,1)S(1)}) custom-call(s32[3]{0:T(128)S(1)} %pad_add_fusion.where, ...), custom_call_target="tpu_custom_call", output_to_operand_aliasing={{0}: (1, {})} | custom-call | flops 8000000000 | bytes 1000000 | tf_op jit(solution)/shard_map/pallas_call | solution.py:428
  20.0 0.9 %collective-permute-start.3 = (bf16[2,2,16,2048]{3,2,1,0:T(8,128)(2,1)S(1)}, bf16[2,2,16,2048]{3,2,1,0:T(8,128)(2,1)S(1)}, u32[]{:S(2)}, u32[]{:S(2)}) collective-permute-start(bf16[2,2,16,2048]{3,2,1,0:T(8,128)(2,1)S(1)} %get-tuple-element.33.grad_b), channel_id=1, source_target_pairs={{1,2},{2,1},{3,4},{4,3},{5,6},{6,5},{9,10},{10,9},{11,12},{12,11},... | collective-permute-start | bytes 786440 | tf_op jit(solution)/shard_map/ppermute | solution.py:443
  20.8 5.2 %collective-permute-start.2 = (bf16[2,2,16,2048]{3,2,1,0:T(8,128)(2,1)S(1)}, bf16[2,2,16,2048]{3,2,1,0:T(8,128)(2,1)S(1)}, u32[]{:S(2)}, u32[]{:S(2)}) collective-permute-start(bf16[2,2,16,2048]{3,2,1,0:T(8,128)(2,1)S(1)} %get-tuple-element.33.grad_b), channel_id=1, source_target_pairs={{0,1},{1,0},{2,3},{3,2},{4,5},{5,4},{6,7},{7,6},{8,9},{9,8},{10,11... | collective-permute-start | bytes 786440 | tf_op jit(solution)/shard_map/ppermute | solution.py:443
  26.0 1.4 %shard_map.69 = (bf16[448,128]{1,0:T(8,128)(2,1)S(1)}, bf16[448,128]{1,0:T(8,128)(2,1)S(1)}, bf16[448,128]{1,0:T(8,128)(2,1)S(1)}, bf16[448,128]{1,0:T(8,128)(2,1)S(1)}) custom-call(s32[3]{0:T(128)S(1)} %pad_add_fusion.where, bf16[2,4,3,16,1152]{4,3,2,1,0:T(8,128)(2,1)S(1)} %get-tuple-element.37.pools, bf16[2,2,16,2048]{3,2,1,0:T(8,128)(2,1)S(1)} %get-tuple-element.33.grad_b), custom_call_target="tpu_custom_call" | custom-call | flops 1000000000 | bytes 1000000 | tf_op jit(solution)/shard_map/pallas_call | solution.py:428
  27.4 1.5 %collective-permute-start.4 = (bf16[448,128]{1,0:T(8,128)(2,1)S(1)}, bf16[448,128]{1,0:T(8,128)(2,1)S(1)}, u32[]{:S(2)}, u32[]{:S(2)}) collective-permute-start(bf16[448,128]{1,0:T(8,128)(2,1)S(1)} %get-tuple-element.46), channel_id=1, source_target_pairs={{0,8},{8,0},{16,24},{24,16},{1,9},{9,1},{17,25},{25,17},{2,10},{10... | collective-permute-start | bytes 344072 | tf_op jit(solution)/shard_map/ppermute | solution.py:449
  29.0 1.5 %collective-permute-start.5 = (bf16[448,128]{1,0:T(8,128)(2,1)S(1)}, bf16[448,128]{1,0:T(8,128)(2,1)S(1)}, u32[]{:S(2)}, u32[]{:S(2)}) collective-permute-start(bf16[448,128]{1,0:T(8,128)(2,1)S(1)} %get-tuple-element.47), channel_id=1, source_target_pairs={{0,16},{8,24},{16,0},{24,8},{1,17},{9,25},{17,1},{25,9},{2,18},{10... | collective-permute-start | bytes 344072 | tf_op jit(solution)/shard_map/ppermute | solution.py:449
  30.5 0.5 collective-permute-start.6
  31.0 9.1 %shard_map.70 = (bf16[2,6,4,16,2304]{4,3,2,1,0:T(8,128)(2,1)S(1)}, bf16[112,128]{1,0:T(8,128)(2,1)S(1)}, bf16[112,128]{1,0:T(8,128)(2,1)S(1)}, bf16[112,128]{1,0:T(8,128)(2,1)S(1)}, bf16[112,128]{1,0:T(8,128)(2,1)S(1)}) custom-call(s32[3]{0:T(128)S(1)} %pad_add_fusion.where, bf16[2,2,16,2048]{3,2,1,0:T(8,128)(2,1)S(1)} %get-tuple-element.33.grad_b, ...), custom_call_target="tpu_custom_call" | custom-call | flops 6000000000 | bytes 1000000 | tf_op jit(solution)/shard_map/pallas_call | solution.py:428
  40.1 1.6 %collective-permute-start.7 = (bf16[112,128]{1,0:T(8,128)(2,1)S(1)}, bf16[112,128]{1,0:T(8,128)(2,1)S(1)}, u32[]{:S(2)}, u32[]{:S(2)}) collective-permute-start(bf16[112,128]{1,0:T(8,128)(2,1)S(1)} %get-tuple-element.50), channel_id=1, source_target_pairs={{0,8},{8,0},{16,24},{24,16},{1,9},{9,1},{17,25},{25,17},{2,10},{10... | collective-permute-start | bytes 86024 | tf_op jit(solution)/shard_map/ppermute | solution.py:449
  41.6 1.5 %collective-permute-start.8 = (bf16[112,128]{1,0:T(8,128)(2,1)S(1)}, bf16[112,128]{1,0:T(8,128)(2,1)S(1)}, u32[]{:S(2)}, u32[]{:S(2)}) collective-permute-start(bf16[112,128]{1,0:T(8,128)(2,1)S(1)} %get-tuple-element.51), channel_id=1, source_target_pairs={{0,16},{8,24},{16,0},{24,8},{1,17},{9,25},{17,1},{25,9},{2,18},{10... | collective-permute-start | bytes 86024 | tf_op jit(solution)/shard_map/ppermute | solution.py:449
  43.6 3.3 %shard_map.71 = (bf16[2,4,32,1024]{3,2,1,0:T(8,128)(2,1)}, bf16[6912,256]{1,0:T(8,128)(2,1)S(1)}, f32[8,128]{1,0:T(8,128)S(1)}) custom-call(bf16[2,6,4,16,2304]{4,3,2,1,0:T(8,128)(2,1)S(1)} %get-tuple-element.39.ga, bf16[9,64,128]{2,1,0:T(8,128)(2,1)S(1)} %get-tuple-element.40.wat), custom_call_target="tpu_custom_call" | custom-call | flops 2000000000 | bytes 1000000 | tf_op jit(solution)/shard_map/pallas_call | solution.py:428
  47.0 0.9 %collective-permute-done.9.refs_7_ = bf16[112,128]{1,0:T(8,128)(2,1)S(1)} collective-permute-done((bf16[112,128]{1,0:T(8,128)(2,1)S(1)}, bf16[112,128]{1,0:T(8,128)(2,1)S(1)}, u32[]{:S(2)}, u32[]{:S(2)}) %collective-permute-start.9) | collective-permute-done | bytes 28704 | tf_op jit(solution)/shard_map/ppermute | solution.py:449
  47.9 0.6 shard_map.73
  48.6 1.2 %collective-permute-done.10.refs_1_ = bf16[280,128]{1,0:T(8,128)(2,1)S(1)} collective-permute-done((bf16[280,128]{1,0:T(8,128)(2,1)S(1)}, bf16[280,128]{1,0:T(8,128)(2,1)S(1)}, u32[]{:S(2)}, u32[]{:S(2)}) %collective-permute-start.10) | collective-permute-done | bytes 71712 | tf_op jit(solution)/shard_map/ppermute | solution.py:449
  49.9 2.5 %collective-permute-start.13 = (bf16[280,128]{1,0:T(8,128)(2,1)S(1)}, bf16[280,128]{1,0:T(8,128)(2,1)S(1)}, u32[]{:S(2)}, u32[]{:S(2)}) collective-permute-start(bf16[280,128]{1,0:T(8,128)(2,1)S(1)} %shard_map.74.refs_0_), channel_id=1, source_target_pairs={{0,6},{1,7},{2,4},{3,5},{4,2},{5,3},{6,0},{7,1},{8,14},{9,15},{10,... | collective-permute-start | bytes 215048 | tf_op jit(solution)/shard_map/ppermute | solution.py:449
  52.4 0.6 collective-permute-start.12
  53.0 1.4 %collective-permute-start.11 = (bf16[280,128]{1,0:T(8,128)(2,1)S(1)}, bf16[280,128]{1,0:T(8,128)(2,1)S(1)}, u32[]{:S(2)}, u32[]{:S(2)}) collective-permute-start(bf16[280,128]{1,0:T(8,128)(2,1)S(1)} %shard_map.74.refs_0_), channel_id=1, source_target_pairs={{0,2},{1,3},{2,0},{3,1},{4,6},{5,7},{6,4},{7,5},{8,10},{9,11},{10,... | collective-permute-start | bytes 215048 | tf_op jit(solution)/shard_map/ppermute | solution.py:449
  54.4 3.0 %shard_map.72 = (bf16[2,4,32,1024]{3,2,1,0:T(8,128)(2,1)}, f32[8,128]{1,0:T(8,128)S(1)}) custom-call(bf16[2,4,32,1024]{3,2,1,0:T(8,128)(2,1)} %get-tuple-element.41.before, bf16[2,6,4,16,2304]{4,3,2,1,0:T(8,128)(2,1)S(1)} %get-tuple-element.39.ga, bf16[6912,256]{1,0:T(8,128)(2,1)S(1)} %get-tuple-element.42.tat), custom_call_target="tpu_custom_call", output_to_operand_aliasing={{0}: (0, {})} | custom-call | flops 2000000000 | bytes 1000000 | tf_op jit(solution)/shard_map/pallas_call | solution.py:428
  57.4 2.5 %collective-permute-done.12.refs_2_ = bf16[280,128]{1,0:T(8,128)(2,1)S(1)} collective-permute-done((bf16[280,128]{1,0:T(8,128)(2,1)S(1)}, bf16[280,128]{1,0:T(8,128)(2,1)S(1)}, u32[]{:S(2)}, u32[]{:S(2)}) %collective-permute-start.12) | collective-permute-done | bytes 71712 | tf_op jit(solution)/shard_map/ppermute | solution.py:449
  59.9 1.6 %collective-permute-start.16 = (bf16[280,128]{1,0:T(8,128)(2,1)S(1)}, bf16[280,128]{1,0:T(8,128)(2,1)S(1)}, u32[]{:S(2)}, u32[]{:S(2)}) collective-permute-start(bf16[280,128]{1,0:T(8,128)(2,1)S(1)} %shard_map.75.refs_0_), channel_id=1, source_target_pairs={{0,24},{8,16},{16,8},{24,0},{1,25},{9,17},{17,9},{25,1},{2,26},{10... | collective-permute-start | bytes 215048 | tf_op jit(solution)/shard_map/ppermute | solution.py:449
  61.5 0.5 collective-permute-start.15
  62.0 1.5 %collective-permute-start.14 = (bf16[280,128]{1,0:T(8,128)(2,1)S(1)}, bf16[280,128]{1,0:T(8,128)(2,1)S(1)}, u32[]{:S(2)}, u32[]{:S(2)}) collective-permute-start(bf16[280,128]{1,0:T(8,128)(2,1)S(1)} %shard_map.75.refs_0_), channel_id=1, source_target_pairs={{0,8},{8,0},{16,24},{24,16},{1,9},{9,1},{17,25},{25,17},{2,10},{10... | collective-permute-start | bytes 215048 | tf_op jit(solution)/shard_map/ppermute | solution.py:449
  63.5 2.5 %collective-permute-done.16.refs_3_ = bf16[280,128]{1,0:T(8,128)(2,1)S(1)} collective-permute-done((bf16[280,128]{1,0:T(8,128)(2,1)S(1)}, bf16[280,128]{1,0:T(8,128)(2,1)S(1)}, u32[]{:S(2)}, u32[]{:S(2)}) %collective-permute-start.16) | collective-permute-done | bytes 71712 | tf_op jit(solution)/shard_map/ppermute | solution.py:449
  66.4 0.6 shard_map.76.own
  67.0 1.6 %collective-permute-done.17.other = bf16[4,280,128]{2,1,0:T(8,128)(2,1)S(1)} collective-permute-done((bf16[4,280,128]{2,1,0:T(8,128)(2,1)S(1)}, bf16[4,280,128]{2,1,0:T(8,128)(2,1)S(1)}, u32[]{:S(2)}, u32[]{:S(2)}) %collective-permute-start.17) | collective-permute-done | bytes 286752 | tf_op jit(solution)/shard_map/ppermute | solution.py:449
  68.6 1.7 %shard_map.77 = (f32[27,2048]{1,0:T(8,128)}, f32[27,8192]{1,0:T(8,128)}) custom-call(s32[3]{0:T(128)S(1)} %pad_add_fusion.where, f32[1]{0:T(128)} %constant.11.clone.1.scale, bf16[4,280,128]{2,1,0:T(8,128)(2,1)S(1)} %shard_map.76.own, bf16[4,280,128]{2,1,0:T(8,128)(2,1)S(1)} %collective-permute-done.17.other), custom_call_target="tpu_custom_call" | custom-call | flops 1000000 | bytes 1000000 | tf_op jit(solution)/shard_map/pallas_call | solution.py:428
  (22 shorter events, 1.2 us)
Async XLA Ops:
  0.6 10.0 %copy-start.1 = (bf16[2,1,8,1024]{3,2,1,0:T(8,128)(2,1)S(1)}, bf16[2,1,8,1024]{3,2,1,0:T(8,128)(2,1)}, u32[]{:S(2)}) copy-start(bf16[2,1,8,1024]{3,2,1,0:T(8,128)(2,1)} %cot.1) | copy-start | bytes 98308
  0.6 10.0 %collective-permute-start.1 = (bf16[2,4,32,1024]{3,2,1,0:T(8,128)(2,1)}, bf16[2,4,32,1024]{3,2,1,0:T(8,128)(2,1)S(1)}, u32[]{:S(2)}, u32[]{:S(2)}) collective-permute-start(bf16[2,4,32,1024]{3,2,1,0:T(8,128)(2,1)} %cubes.1), channel_id=1, source_target_pairs={{1,2},{2,1},{3,4},{4,3},{5,6},{6,5},{9,10},{10,9},{11,12},{12,11},... | collective-permute-start | bytes 1572872 | tf_op jit(solution)/shard_map/ppermute | solution.py:443
  1.3 9.3 %collective-permute-start = (bf16[2,4,32,1024]{3,2,1,0:T(8,128)(2,1)}, bf16[2,4,32,1024]{3,2,1,0:T(8,128)(2,1)S(1)}, u32[]{:S(2)}, u32[]{:S(2)}) collective-permute-start(bf16[2,4,32,1024]{3,2,1,0:T(8,128)(2,1)} %cubes.1), channel_id=1, source_target_pairs={{0,1},{1,0},{2,3},{3,2},{4,5},{5,4},{6,7},{7,6},{8,9},{9,8},{10,11... | collective-permute-start | bytes 1572872 | tf_op jit(solution)/shard_map/ppermute | solution.py:443
  8.2 1.0 %copy-start = (bf16[2,4,32,1024]{3,2,1,0:T(8,128)(2,1)S(1)}, bf16[2,4,32,1024]{3,2,1,0:T(8,128)(2,1)}, u32[]{:S(2)}) copy-start(bf16[2,4,32,1024]{3,2,1,0:T(8,128)(2,1)} %cubes.1) | copy-start | bytes 1572868
  20.0 11.0 %collective-permute-start.3 = (bf16[2,2,16,2048]{3,2,1,0:T(8,128)(2,1)S(1)}, bf16[2,2,16,2048]{3,2,1,0:T(8,128)(2,1)S(1)}, u32[]{:S(2)}, u32[]{:S(2)}) collective-permute-start(bf16[2,2,16,2048]{3,2,1,0:T(8,128)(2,1)S(1)} %get-tuple-element.33.grad_b), channel_id=1, source_target_pairs={{1,2},{2,1},{3,4},{4,3},{5,6},{6,5},{9,10},{10,9},{11,12},{12,11},... | collective-permute-start | bytes 786440 | tf_op jit(solution)/shard_map/ppermute | solution.py:443
  20.8 10.2 %collective-permute-start.2 = (bf16[2,2,16,2048]{3,2,1,0:T(8,128)(2,1)S(1)}, bf16[2,2,16,2048]{3,2,1,0:T(8,128)(2,1)S(1)}, u32[]{:S(2)}, u32[]{:S(2)}) collective-permute-start(bf16[2,2,16,2048]{3,2,1,0:T(8,128)(2,1)S(1)} %get-tuple-element.33.grad_b), channel_id=1, source_target_pairs={{0,1},{1,0},{2,3},{3,2},{4,5},{5,4},{6,7},{7,6},{8,9},{9,8},{10,11... | collective-permute-start | bytes 786440 | tf_op jit(solution)/shard_map/ppermute | solution.py:443
  27.4 15.7 %collective-permute-start.4 = (bf16[448,128]{1,0:T(8,128)(2,1)S(1)}, bf16[448,128]{1,0:T(8,128)(2,1)S(1)}, u32[]{:S(2)}, u32[]{:S(2)}) collective-permute-start(bf16[448,128]{1,0:T(8,128)(2,1)S(1)} %get-tuple-element.46), channel_id=1, source_target_pairs={{0,8},{8,0},{16,24},{24,16},{1,9},{9,1},{17,25},{25,17},{2,10},{10... | collective-permute-start | bytes 344072 | tf_op jit(solution)/shard_map/ppermute | solution.py:449
  29.0 18.0 %collective-permute-start.5 = (bf16[448,128]{1,0:T(8,128)(2,1)S(1)}, bf16[448,128]{1,0:T(8,128)(2,1)S(1)}, u32[]{:S(2)}, u32[]{:S(2)}) collective-permute-start(bf16[448,128]{1,0:T(8,128)(2,1)S(1)} %get-tuple-element.47), channel_id=1, source_target_pairs={{0,16},{8,24},{16,0},{24,8},{1,17},{9,25},{17,1},{25,9},{2,18},{10... | collective-permute-start | bytes 344072 | tf_op jit(solution)/shard_map/ppermute | solution.py:449
  30.5 16.4 %collective-permute-start.6 = (bf16[448,128]{1,0:T(8,128)(2,1)S(1)}, bf16[448,128]{1,0:T(8,128)(2,1)S(1)}, u32[]{:S(2)}, u32[]{:S(2)}) collective-permute-start(bf16[448,128]{1,0:T(8,128)(2,1)S(1)} %get-tuple-element.48), channel_id=1, source_target_pairs={{0,24},{8,16},{16,8},{24,0},{1,25},{9,17},{17,9},{25,1},{2,26},{10... | collective-permute-start | bytes 344072 | tf_op jit(solution)/shard_map/ppermute | solution.py:449
  40.1 6.9 %collective-permute-start.7 = (bf16[112,128]{1,0:T(8,128)(2,1)S(1)}, bf16[112,128]{1,0:T(8,128)(2,1)S(1)}, u32[]{:S(2)}, u32[]{:S(2)}) collective-permute-start(bf16[112,128]{1,0:T(8,128)(2,1)S(1)} %get-tuple-element.50), channel_id=1, source_target_pairs={{0,8},{8,0},{16,24},{24,16},{1,9},{9,1},{17,25},{25,17},{2,10},{10... | collective-permute-start | bytes 86024 | tf_op jit(solution)/shard_map/ppermute | solution.py:449
  41.6 5.4 %collective-permute-start.8 = (bf16[112,128]{1,0:T(8,128)(2,1)S(1)}, bf16[112,128]{1,0:T(8,128)(2,1)S(1)}, u32[]{:S(2)}, u32[]{:S(2)}) collective-permute-start(bf16[112,128]{1,0:T(8,128)(2,1)S(1)} %get-tuple-element.51), channel_id=1, source_target_pairs={{0,16},{8,24},{16,0},{24,8},{1,17},{9,25},{17,1},{25,9},{2,18},{10... | collective-permute-start | bytes 86024 | tf_op jit(solution)/shard_map/ppermute | solution.py:449
  43.2 4.8 %collective-permute-start.9 = (bf16[112,128]{1,0:T(8,128)(2,1)S(1)}, bf16[112,128]{1,0:T(8,128)(2,1)S(1)}, u32[]{:S(2)}, u32[]{:S(2)}) collective-permute-start(bf16[112,128]{1,0:T(8,128)(2,1)S(1)} %get-tuple-element.52), channel_id=1, source_target_pairs={{0,24},{8,16},{16,8},{24,0},{1,25},{9,17},{17,9},{25,1},{2,26},{10... | collective-permute-start | bytes 86024 | tf_op jit(solution)/shard_map/ppermute | solution.py:449
  48.6 1.3 %collective-permute-start.10 = (bf16[280,128]{1,0:T(8,128)(2,1)S(1)}, bf16[280,128]{1,0:T(8,128)(2,1)S(1)}, u32[]{:S(2)}, u32[]{:S(2)}) collective-permute-start(bf16[280,128]{1,0:T(8,128)(2,1)S(1)} %get-tuple-element.54), channel_id=1, source_target_pairs={{0,1},{1,0},{2,3},{3,2},{4,5},{5,4},{6,7},{7,6},{8,9},{9,8},{10,11... | collective-permute-start | bytes 215048 | tf_op jit(solution)/shard_map/ppermute | solution.py:449
  49.9 7.5 %collective-permute-start.13 = (bf16[280,128]{1,0:T(8,128)(2,1)S(1)}, bf16[280,128]{1,0:T(8,128)(2,1)S(1)}, u32[]{:S(2)}, u32[]{:S(2)}) collective-permute-start(bf16[280,128]{1,0:T(8,128)(2,1)S(1)} %shard_map.74.refs_0_), channel_id=1, source_target_pairs={{0,6},{1,7},{2,4},{3,5},{4,2},{5,3},{6,0},{7,1},{8,14},{9,15},{10,... | collective-permute-start | bytes 215048 | tf_op jit(solution)/shard_map/ppermute | solution.py:449
  52.4 7.5 %collective-permute-start.12 = (bf16[280,128]{1,0:T(8,128)(2,1)S(1)}, bf16[280,128]{1,0:T(8,128)(2,1)S(1)}, u32[]{:S(2)}, u32[]{:S(2)}) collective-permute-start(bf16[280,128]{1,0:T(8,128)(2,1)S(1)} %shard_map.74.refs_0_), channel_id=1, source_target_pairs={{0,4},{1,5},{2,6},{3,7},{4,0},{5,1},{6,2},{7,3},{8,12},{9,13},{10,... | collective-permute-start | bytes 215048 | tf_op jit(solution)/shard_map/ppermute | solution.py:449
  53.0 6.9 %collective-permute-start.11 = (bf16[280,128]{1,0:T(8,128)(2,1)S(1)}, bf16[280,128]{1,0:T(8,128)(2,1)S(1)}, u32[]{:S(2)}, u32[]{:S(2)}) collective-permute-start(bf16[280,128]{1,0:T(8,128)(2,1)S(1)} %shard_map.74.refs_0_), channel_id=1, source_target_pairs={{0,2},{1,3},{2,0},{3,1},{4,6},{5,7},{6,4},{7,5},{8,10},{9,11},{10,... | collective-permute-start | bytes 215048 | tf_op jit(solution)/shard_map/ppermute | solution.py:449
  59.9 6.1 %collective-permute-start.16 = (bf16[280,128]{1,0:T(8,128)(2,1)S(1)}, bf16[280,128]{1,0:T(8,128)(2,1)S(1)}, u32[]{:S(2)}, u32[]{:S(2)}) collective-permute-start(bf16[280,128]{1,0:T(8,128)(2,1)S(1)} %shard_map.75.refs_0_), channel_id=1, source_target_pairs={{0,24},{8,16},{16,8},{24,0},{1,25},{9,17},{17,9},{25,1},{2,26},{10... | collective-permute-start | bytes 215048 | tf_op jit(solution)/shard_map/ppermute | solution.py:449
  61.5 4.8 %collective-permute-start.15 = (bf16[280,128]{1,0:T(8,128)(2,1)S(1)}, bf16[280,128]{1,0:T(8,128)(2,1)S(1)}, u32[]{:S(2)}, u32[]{:S(2)}) collective-permute-start(bf16[280,128]{1,0:T(8,128)(2,1)S(1)} %shard_map.75.refs_0_), channel_id=1, source_target_pairs={{0,16},{8,24},{16,0},{24,8},{1,17},{9,25},{17,1},{25,9},{2,18},{10... | collective-permute-start | bytes 215048 | tf_op jit(solution)/shard_map/ppermute | solution.py:449
  62.0 4.3 %collective-permute-start.14 = (bf16[280,128]{1,0:T(8,128)(2,1)S(1)}, bf16[280,128]{1,0:T(8,128)(2,1)S(1)}, u32[]{:S(2)}, u32[]{:S(2)}) collective-permute-start(bf16[280,128]{1,0:T(8,128)(2,1)S(1)} %shard_map.75.refs_0_), channel_id=1, source_target_pairs={{0,8},{8,0},{16,24},{24,16},{1,9},{9,1},{17,25},{25,17},{2,10},{10... | collective-permute-start | bytes 215048 | tf_op jit(solution)/shard_map/ppermute | solution.py:449
  66.9 1.6 %collective-permute-start.17 = (bf16[4,280,128]{2,1,0:T(8,128)(2,1)S(1)}, bf16[4,280,128]{2,1,0:T(8,128)(2,1)S(1)}, u32[]{:S(2)}, u32[]{:S(2)}) collective-permute-start(bf16[4,280,128]{2,1,0:T(8,128)(2,1)S(1)} %shard_map.76.own), channel_id=1, source_target_pairs={{0,1},{1,0},{2,3},{3,2},{4,5},{5,4},{6,7},{7,6},{8,9},{9,8},{10,11... | collective-permute-start | bytes 860168 | tf_op jit(solution)/shard_map/ppermute | solution.py:449

commit v3 on v2

--- a/solution.py
+++ b/solution.py
@@ -65,7 +65,21 @@
         target[b, zz, v] = moved[16 * v : 16 * v + 16]
 
 
-def prepare_kernel(cubes, wa, wb, xs, ta, tb, tbt, wat):
+RANKS = (-3, -1, 0, 2, 1, 3, 4, 6, 5, 7, 8, 10)
+
+
+def mirror(d, block, tat):
+    lane = lax.broadcasted_iota(jnp.int32, (64, 128), 1)
+    turned = [block if s == 0 else pltpu.roll(block, 32 * s, 1) for s in range(4)]
+    for slot, rank in enumerate(RANKS):
+        for half in range(2):
+            start = 32 * (rank - 1 - 4 * half)
+            keep = (lane >= start) & (lane < start + 96)
+            value = jnp.where(keep, turned[(rank - 1) % 4], 0.0).astype(BF)
+            tat[768 * d + 64 * slot : 768 * d + 64 * slot + 64, 128 * half : 128 * half + 128] = value
+
+
+def prepare_kernel(cubes, wa, wb, xs, ta, tb, tbt, tat):
     picker = row_picker(4, 2, 32)
     for b in range(cubes.shape[0]):
         for z in range(ZD):
@@ -77,7 +91,7 @@
             ta[256 * d : 256 * d + 256, 128 * px : 128 * px + 128] = halves(
                 rows_at(block, 32 * px, 256), rows_at(block, 64 + 32 * px, 256)
             )
-        wat[8 - d] = rows_at(block, 0, 128).T[:64].astype(BF)
+        mirror(8 - d, rows_at(block, 0, 128).T[:64], tat)
         block = wb[d]
         for e in range(2):
             tb[256 * d : 256 * d + 256, 128 * e : 128 * e + 128] = rows_at(block, 64 * e, 256)
@@ -93,7 +107,7 @@
             )
 
 
-def forward_kernel(where, own, recv_a, recv_b, ta, tb, cot, xs, dsl, pools, grad_b, pooled):
+def forward_kernel(where, own, recv_a, recv_b, ta, tb, cot, xs, dsl, pools, grad_b, pooled, pre_even, pre_odd):
     del own
     cube_count = xs.shape[0]
     even = where[0] % 2 == 0
@@ -110,8 +124,8 @@
     high = jnp.where(where[0] == where[1] - 1, 0.0, 1.0)
     rows = cube_count * 8 * 16
 
-    def group(g, carry):
-        lanes = pl.ds(pl.multiple_of(128 * g, 128), 256)
+    def product(g, target):
+        lanes = pl.ds(128 * g if isinstance(g, int) else pl.multiple_of(128 * g, 128), 256)
         stacks = []
         for p in range(2):
             stacks.append(
@@ -124,17 +138,21 @@
                     axis=1,
                 )
             )
-        pre = dot(jnp.concatenate(stacks, axis=0), ta[...])
+        target[...] = dot(jnp.concatenate(stacks, axis=0), ta[...])
+
+    def pool(g, source):
+        pre = source[...]
         squash = sigmoid(pre)
         act = pre * squash
         slope = (squash + act * (1.0 - squash)).astype(BF).reshape(2, cube_count, 8, 16, 256)
         for p in range(2):
-            dsl[:, :, p, :, pl.ds(pl.multiple_of(256 * g, 256), 256)] = slope[p][:, 1:7]
+            to = pl.ds(256 * g if isinstance(g, int) else pl.multiple_of(256 * g, 256), 256)
+            dsl[:, :, p, :, to] = slope[p][:, 1:7]
         act = act.reshape(2, cube_count, 4, 2, 16, 256)
         act = act[0] + act[1]
         act = act[:, :, 0] + act[:, :, 1]
         act = (act[..., :128] + act[..., 128:]) * 0.125
-        out = pl.ds(pl.multiple_of(128 * g, 128), 128)
+        out = pl.ds(128 * g if isinstance(g, int) else pl.multiple_of(128 * g, 128), 128)
         for z in range(4):
             part = act[:, z]
             if z == 0:
@@ -142,9 +160,19 @@
             if z == 3:
                 part = part * high
             pooled[:, z, :, out] = part.astype(BF)
+
+    def pair(i, carry):
+        product(2 * i + 1, pre_odd)
+        pool(2 * i, pre_even)
+        product(2 * i + 2, pre_even)
+        pool(2 * i + 1, pre_odd)
         return carry
 
-    lax.fori_loop(0, 8, group, 0)
+    product(0, pre_even)
+    lax.fori_loop(0, 3, pair, 0)
+    product(7, pre_odd)
+    pool(6, pre_even)
+    pool(7, pre_odd)
 
     shifter = row_picker(3, 1, 16)
     for b in range(cube_count):
@@ -258,7 +286,7 @@
 
 
 def backward_kernel(where, grad_b, recv_a, recv_b, tbt, dsl, xs, after, ga, *rest):
-    outs, (gs, gpool, acc, term, terms) = rest[:-5], rest[-5:]
+    outs, (gs, gpool, turned, term, terms) = rest[:-5], rest[-5:]
     del after
     cube_count = grad_b.shape[0]
     even = where[0] % 2 == 0
@@ -297,7 +325,6 @@
             scale = low if z == 0 else high if z == 3 else 0.125
             gpool[:, z, :, 256 * q : 256 * q + 256] = part[:, z] * scale
 
-    acc[...] = jnp.zeros_like(acc)
     ga[:, :, :, :, :128] = jnp.zeros((cube_count, 6, 4, 16, 128), BF)
     ga[:, :, :, :, 2176:] = jnp.zeros((cube_count, 6, 4, 16, 128), BF)
     rows_a = cube_count * 6 * 16
@@ -310,47 +337,36 @@
         up = jnp.concatenate(
             [up[:, 0:1], up[:, 1:2], up[:, 1:2], up[:, 2:3], up[:, 2:3], up[:, 3:4]], axis=1
         ).reshape(rows_a, 128)
-        sides = []
         for p in range(2):
-            pair = []
             for px in range(2):
                 at = pl.ds(pl.multiple_of(256 * g + 128 * px, 128), 128)
                 grad = up * dsl[:, :, p, :, at].astype(F32).reshape(rows_a, 128)
                 to = pl.ds(pl.multiple_of(256 * g + 128 * px + 128, 128), 128)
                 kept = grad.astype(BF).reshape(cube_count, 6, 16, 128)
                 ga[:, :, 1 + p, :, to] = kept
-                pair.append(kept[:, 1:5].reshape(own, 128))
+                turned[g, 128 * px : 128 * px + 128, own * p : own * p + own] = kept[:, 1:5].reshape(own, 128).T
                 if p == 1:
                     moved = jnp.where(place == 0, 0.0, pltpu.roll(grad, 1, 0))
                 else:
                     moved = jnp.where(place == 15, 0.0, pltpu.roll(grad, rows_a - 1, 0))
                 ga[:, :, 0 if p else 3, :, to] = moved.astype(BF).reshape(cube_count, 6, 16, 128)
-            sides.append(jnp.concatenate(pair, axis=1))
-        grads = jnp.concatenate(sides, axis=0)
-        wide = pl.ds(pl.multiple_of(128 * g, 128), 256)
+        return carry
+
+    lax.fori_loop(0, 8, group, 0)
+
+    terms[pl.ds(27, C1 // 2, stride=28), :] = jnp.zeros((C1 // 2, 128), F32)
+    mask = lanes_below((32, 128), 64)
+    for d in range(9):
+        dz, dy = d // 3, d % 3
         windows = jnp.concatenate(
             [
-                jnp.concatenate(
-                    [
-                        xs[:, HALO - 1 + dz : HALO + 3 + dz, p + dy, :, wide].reshape(own, 256)
-                        for dz in range(3)
-                        for dy in range(3)
-                    ],
-                    axis=1,
-                )
+                xs[:, HALO - 1 + dz : HALO + 3 + dz, p + dy, :, 128 * g : 128 * g + 256].reshape(own, 256)
+                for g in range(8)
                 for p in range(2)
             ],
             axis=0,
         )
-        acc[...] += dot_t(grads, windows)
-        return carry
-
-    lax.fori_loop(0, 8, group, 0)
-
-    terms[pl.ds(27, C1 // 2, stride=28), :] = jnp.zeros((C1 // 2, 128), F32)
-    mask = lanes_below((32, 128), 64)
-    for d in range(9):
-        full = acc[:, 256 * d : 256 * d + 256].T
+        full = dot(jnp.concatenate([turned[g] for g in range(8)], axis=1), windows).T
         for dx in range(3):
             left = full[32 * dx : 32 * dx + 32, :128] + full[32 * dx + 32 : 32 * dx + 64, 128:]
             right = full[32 * dx + 64 : 32 * dx + 96, :128] + full[32 * dx + 96 : 32 * dx + 128, 128:]
@@ -366,23 +382,7 @@
         out[...] = terms[pl.ds(pl.multiple_of(chunk * share, 8), share), :].astype(BF)
 
 
-RANKS = (-3, -1, 0, 2, 1, 3, 4, 6, 5, 7, 8, 10)
-
-
-def mirror_kernel(wat, tat):
-    lane = lax.broadcasted_iota(jnp.int32, (64, 128), 1)
-    for d in range(9):
-        block = wat[d].astype(F32)
-        turned = [block if s == 0 else pltpu.roll(block, 32 * s, 1) for s in range(4)]
-        for slot, rank in enumerate(RANKS):
-            for half in range(2):
-                start = 32 * (rank - 1 - 4 * half)
-                keep = (lane >= start) & (lane < start + 96)
-                value = jnp.where(keep, turned[(rank - 1) % 4], 0.0).astype(BF)
-                tat[768 * d + 64 * slot : 768 * d + 64 * slot + 64, 128 * half : 128 * half + 128] = value
-
-
-def one_cube(b, ga, tat, out, token, block, sem):
+def one_cube(b, ga, tat, out, landed):
     rows = ZD * 16
     sides = []
     for p in range(2):
@@ -403,24 +403,34 @@
     for z in range(ZD):
         for q in range(4):
             pair = jnp.concatenate([both[0, q, z], both[1, q, z]], axis=0)
-            block[z, :, 256 * q : 256 * q + 256] = dot(mixer, pair).astype(BF)
-    leave = pltpu.make_async_copy(block, out.at[b], sem)
-    leave.start()
+            out[z, :, 256 * q : 256 * q + 256] = dot(mixer, pair).astype(BF)
+        if landed is not None:
+            landed(z)
+
+
+def early_cube_kernel(b):
+    def kernel(ga, tat, out):
+        one_cube(b, ga, tat, out, None)
+
+    return kernel
+
+
+def last_cube_kernel(ga, tat, *rest):
+    early, (out, token, block, sems) = rest[:-4], rest[-4:]
+    last = len(early)
+    copies = [pltpu.make_async_copy(cube, out.at[b], sems.at[b]) for b, cube in enumerate(early)]
+    for copy in copies:
+        copy.start()
+
+    def landed(z):
+        copy = pltpu.make_async_copy(block.at[z], out.at[last, z], sems.at[last + z])
+        copy.start()
+        copies.append(copy)
+
+    one_cube(last, ga, tat, block, landed)
     token[...] = jnp.zeros_like(token)
-    leave.wait()
-
-
-def first_cube_kernel(ga, wat, out, tat, token, block, sem):
-    mirror_kernel(wat, tat)
-    one_cube(0, ga, tat, out, token, block, sem)
-
-
-def later_cube_kernel(b):
-    def kernel(before, ga, tat, out, token, block, sem):
-        del before
-        one_cube(b, ga, tat, out, token, block, sem)
-
-    return kernel
+    for copy in copies:
+        copy.wait()
 
 
 def call(kernel, args, outs, scratch, flops, smem=0, any_in=(), any_out=(), aliases=None):
@@ -457,7 +467,7 @@
     where = jnp.stack([lax.axis_index("gz"), jnp.int32(ring), lax.axis_index("sample")]).astype(jnp.int32)
     recv_a, recv_b = swap(cubes, cubes, ring)
 
-    own_xs, ta, tb, tbt, wat = call(
+    own_xs, ta, tb, tbt, tat = call(
         prepare_kernel,
         [cubes, weight_a.reshape(9, 96, C2), weight_b.reshape(9, 192, C3)],
         [
@@ -465,7 +475,7 @@
             ((2304, 256), BF),
             ((2304, 256), BF),
             ((6912, 256), BF),
-            ((9, C2, 128), BF),
+            ((6912, 256), BF),
         ],
         [],
         1_000_000_000,
@@ -479,7 +489,7 @@
             ((cube_count, 4, 3, 16, 1152), BF),
             ((cube_count, 2, 16, 2048), BF),
         ],
-        [pltpu.VMEM((cube_count, 4, 16, 1024), BF)],
+        [pltpu.VMEM((cube_count, 4, 16, 1024), BF)] + [pltpu.VMEM((cube_count * 256, 256), F32)] * 2,
         8_000_000_000,
         smem=1,
         aliases={1: 0},
@@ -502,7 +512,7 @@
         [
             pltpu.VMEM((cube_count, 6, 3, 16, 2304), BF),
             pltpu.VMEM((cube_count, 4, 16, 1024), F32),
-            pltpu.VMEM((256, 2304), F32),
+            pltpu.VMEM((8, 256, cube_count * 128), BF),
             pltpu.VMEM((4, C1, 128), F32),
             pltpu.VMEM((ROWS_A, 128), F32),
         ],
@@ -510,30 +520,25 @@
         smem=1,
     )
     others_a = swap_along(parts_a, "sample", 1)
-    whole = ((cube_count, ZD, SIDE, SIDE * C1), BF)
-    token = ((8, 128), F32)
-    block = [pltpu.VMEM((ZD, SIDE, SIDE * C1), BF), pltpu.SemaphoreType.DMA]
-    input_grad, tat, done = call(
-        first_cube_kernel, [ga, wat], [whole, ((6912, 256), BF), token], block, 2_000_000_000, any_out=(0,)
-    )
+    cube = (ZD, SIDE, SIDE * C1)
+    early = [
+        call(early_cube_kernel(b), [ga, tat], [(cube, BF)], [], 2_000_000_000)[0] for b in range(cube_count - 1)
+    ]
     half = (share_b + share_a) // 2
     small = [((half, 128), BF)]
     keep, send = call(
-        halve_kernel, [where, done, parts_b[0], *others_b, parts_a[0], *others_a], small * 2, [], 1_000_000, smem=1
-    )
-    (keep,) = call(add_kernel, [done, keep, *swap_along([send] * 2, "gz", 1)], small, [], 1_000_000)
+        halve_kernel, [where, early[0], parts_b[0], *others_b, parts_a[0], *others_a], small * 2, [], 1_000_000, smem=1
+    )
+    (keep,) = call(add_kernel, [where, keep, *swap_along([send] * 2, "gz", 1)], small, [], 1_000_000, smem=1)
     others = swap_along([keep] * (ring // 2), "gz", 2)
-    for b in range(1, cube_count):
-        input_grad, done = call(
-            later_cube_kernel(b),
-            [input_grad, ga, tat],
-            [whole, token],
-            block,
-            2_000_000_000,
-            any_in=(0,),
-            any_out=(0,),
-            aliases={0: 0},
-        )
+    input_grad, done = call(
+        last_cube_kernel,
+        [ga, tat, *early],
+        [((cube_count, *cube), BF), ((8, 128), F32)],
+        [pltpu.VMEM(cube, BF), pltpu.SemaphoreType.DMA((cube_count - 1 + ZD,))],
+        2_000_000_000,
+        any_out=(0,),
+    )
     (keep,) = call(add_kernel, [done, keep, *others], small, [], 1_000_000)
     shape = (samples, half, 128)
     (own,) = call(

time: 70.6 us -> 73.6 us (1.042)
  Pallas kernels: 30.4 us -> 33.3 us
  starting transfers between devices: 26.4 us -> 25.3 us
  waiting for transfers between devices: 9.17 us -> 10.2 us
    pallas_call x11, Pallas kernels: 30.4 us -> 33.3 us  [call(): pl.pallas_call(kernel, out_shape=[jax.ShapeDtypeStruct(shape, dtype) for...]
    ppermute x2, starting transfers between devices: 9.6 us -> 8.52 us  [swap(): lax.ppermute(first, 'gz', pairs_a)]
    ppermute x14, waiting for transfers between devices: 9.16 us -> 10.2 us  [swap_along(): lax.ppermute(part, axis, [(i, i ^ k * step) for i in range(count)])]
  transfers between devices with their start and end apart: 18 -> 18, of which waited for: 6 -> 7; matrix products, arithmetic and copies ran while one was open for 4% -> 3% of each run, Pallas kernels for 26% -> 27%
where the time goes in v3:
time: 73.6 us; the launch traced here: 73.3 us
  Pallas kernels  33.3 us (45%)
  starting transfers between devices  25.3 us (34%)
  waiting for transfers between devices  10.2 us (14%)
  local copies, waits for them, and re-layouts  3.49 us (5%)
  between operations  0.82 us (1%)
    pallas_call x11, Pallas kernels, call(): pl.pallas_call(kernel, out_shape=[jax.ShapeDtypeStruct(shape, dtype) for...  33.3 us
    ppermute x14, starting transfers between devices, swap_along(): lax.ppermute(part, axis, [(i, i ^ k * step) for i in range(count)])  15.3 us
    ppermute x14, waiting for transfers between devices, swap_along(): lax.ppermute(part, axis, [(i, i ^ k * step) for i in range(count)])  10.2 us
    ppermute x2, starting transfers between devices, swap(): lax.ppermute(first, 'gz', pairs_a)  8.52 us
    ppermute x2, starting transfers between devices, swap(): lax.ppermute(second, 'gz', pairs_b)  1.55 us
  transfers between devices with their start and end apart: 18, of which 7 were waited for; matrix products, arithmetic and copies ran while one was open for 3% of the time, Pallas kernels for 27%

profile of v3, /device:TPU:0, one launch (start us, length us, event | category | flops | bytes accessed | tf_op | source)
XLA Modules:
  0.0 73.3 jit_solution(6851173147778388487)
XLA Ops:
  0.6 0.7 collective-permute-start.1
  1.3 4.4 %collective-permute-start = (bf16[2,4,32,1024]{3,2,1,0:T(8,128)(2,1)}, bf16[2,4,32,1024]{3,2,1,0:T(8,128)(2,1)S(1)}, u32[]{:S(2)}, u32[]{:S(2)}) collective-permute-start(bf16[2,4,32,1024]{3,2,1,0:T(8,128)(2,1)} %cubes.1), channel_id=1, source_target_pairs={{0,1},{1,0},{2,3},{3,2},{4,5},{5,4},{6,7},{7,6},{8,9},{9,8},{10,11... | collective-permute-start | bytes 1572872 | tf_op jit(solution)/shard_map/ppermute | solution.py:453
  5.8 1.1 %reshape.12.wa = bf16[9,96,64]{2,1,0:T(8,128)(2,1)S(1)} reshape(bf16[27,2048]{1,0:T(8,128)(2,1)} %param.5) | data formatting | bytes 221184 | tf_op jit(solution)/shard_map/reshape | solution.py:472
  6.9 1.3 %reshape.13.wb = bf16[9,192,128]{2,1,0:T(8,128)(2,1)S(1)} reshape(bf16[27,8192]{1,0:T(8,128)(2,1)} %param.6) | data formatting | bytes 884736 | tf_op jit(solution)/shard_map/reshape | solution.py:472
  8.2 1.0 %copy-done = bf16[2,4,32,1024]{3,2,1,0:T(8,128)(2,1)S(1)} copy-done((bf16[2,4,32,1024]{3,2,1,0:T(8,128)(2,1)S(1)}, bf16[2,4,32,1024]{3,2,1,0:T(8,128)(2,1)}, u32[]{:S(2)}) %copy-start) | copy-done | bytes 524312
  9.3 2.3 %shard_map.67 = (bf16[2,10,4,16,1152]{4,3,2,1,0:T(8,128)(2,1)S(1)}, bf16[2304,256]{1,0:T(8,128)(2,1)S(1)}, bf16[2304,256]{1,0:T(8,128)(2,1)S(1)}, bf16[6912,256]{1,0:T(8,128)(2,1)S(1)}, bf16[6912,256]{1,0:T(8,128)(2,1)S(1)}) custom-call(bf16[2,4,32,1024]{3,2,1,0:T(8,128)(2,1)S(1)} %copy-done, bf16[9,96,64]{2,1,0:T(8,128)(2,1)S(1)} %reshape.12.wa, ...), custom_call_target="tpu_custom_call" | custom-call | flops 1000000000 | bytes 1000000 | tf_op jit(solution)/shard_map/pallas_call | solution.py:438
  11.7 10.0 %shard_map.68 = (bf16[2,10,4,16,1152]{4,3,2,1,0:T(8,128)(2,1)S(1)}, bf16[2,6,2,16,2048]{4,3,2,1,0:T(8,128)(2,1)S(1)}, bf16[2,4,3,16,1152]{4,3,2,1,0:T(8,128)(2,1)S(1)}, bf16[2,2,16,2048]{3,2,1,0:T(8,128)(2,1)S(1)}) custom-call(s32[3]{0:T(128)S(1)} %pad_add_fusion.where.after, ...), custom_call_target="tpu_custom_call", output_to_operand_aliasing={{0}: (1, {})} | custom-call | flops 8000000000 | bytes 1000000 | tf_op jit(solution)/shard_map/pallas_call | solution.py:438
  21.7 0.9 %collective-permute-start.3 = (bf16[2,2,16,2048]{3,2,1,0:T(8,128)(2,1)S(1)}, bf16[2,2,16,2048]{3,2,1,0:T(8,128)(2,1)S(1)}, u32[]{:S(2)}, u32[]{:S(2)}) collective-permute-start(bf16[2,2,16,2048]{3,2,1,0:T(8,128)(2,1)S(1)} %get-tuple-element.30.grad_b), channel_id=1, source_target_pairs={{1,2},{2,1},{3,4},{4,3},{5,6},{6,5},{9,10},{10,9},{11,12},{12,11},... | collective-permute-start | bytes 786440 | tf_op jit(solution)/shard_map/ppermute | solution.py:453
  22.5 4.1 %collective-permute-start.2 = (bf16[2,2,16,2048]{3,2,1,0:T(8,128)(2,1)S(1)}, bf16[2,2,16,2048]{3,2,1,0:T(8,128)(2,1)S(1)}, u32[]{:S(2)}, u32[]{:S(2)}) collective-permute-start(bf16[2,2,16,2048]{3,2,1,0:T(8,128)(2,1)S(1)} %get-tuple-element.30.grad_b), channel_id=1, source_target_pairs={{0,1},{1,0},{2,3},{3,2},{4,5},{5,4},{6,7},{7,6},{8,9},{9,8},{10,11... | collective-permute-start | bytes 786440 | tf_op jit(solution)/shard_map/ppermute | solution.py:453
  26.6 1.4 %shard_map.69 = (bf16[448,128]{1,0:T(8,128)(2,1)S(1)}, bf16[448,128]{1,0:T(8,128)(2,1)S(1)}, bf16[448,128]{1,0:T(8,128)(2,1)S(1)}, bf16[448,128]{1,0:T(8,128)(2,1)S(1)}) custom-call(s32[3]{0:T(128)S(1)} %pad_add_fusion.where.after, bf16[2,4,3,16,1152]{4,3,2,1,0:T(8,128)(2,1)S(1)} %get-tuple-element.34.pools, ...), custom_call_target="tpu_custom_call" | custom-call | flops 1000000000 | bytes 1000000 | tf_op jit(solution)/shard_map/pallas_call | solution.py:438
  28.1 1.6 %collective-permute-start.4 = (bf16[448,128]{1,0:T(8,128)(2,1)S(1)}, bf16[448,128]{1,0:T(8,128)(2,1)S(1)}, u32[]{:S(2)}, u32[]{:S(2)}) collective-permute-start(bf16[448,128]{1,0:T(8,128)(2,1)S(1)} %get-tuple-element.40), channel_id=1, source_target_pairs={{0,8},{8,0},{16,24},{24,16},{1,9},{9,1},{17,25},{25,17},{2,10},{10... | collective-permute-start | bytes 344072 | tf_op jit(solution)/shard_map/ppermute | solution.py:459
  29.6 1.5 %collective-permute-start.5 = (bf16[448,128]{1,0:T(8,128)(2,1)S(1)}, bf16[448,128]{1,0:T(8,128)(2,1)S(1)}, u32[]{:S(2)}, u32[]{:S(2)}) collective-permute-start(bf16[448,128]{1,0:T(8,128)(2,1)S(1)} %get-tuple-element.41), channel_id=1, source_target_pairs={{0,16},{8,24},{16,0},{24,8},{1,17},{9,25},{17,1},{25,9},{2,18},{10... | collective-permute-start | bytes 344072 | tf_op jit(solution)/shard_map/ppermute | solution.py:459
  31.6 10.9 %shard_map.70 = (bf16[2,6,4,16,2304]{4,3,2,1,0:T(8,128)(2,1)S(1)}, bf16[112,128]{1,0:T(8,128)(2,1)S(1)}, bf16[112,128]{1,0:T(8,128)(2,1)S(1)}, bf16[112,128]{1,0:T(8,128)(2,1)S(1)}, bf16[112,128]{1,0:T(8,128)(2,1)S(1)}) custom-call(s32[3]{0:T(128)S(1)} %pad_add_fusion.where.after, bf16[2,2,16,2048]{3,2,1,0:T(8,128)(2,1)S(1)} %get-tuple-element.30.grad_b, ...), custom_call_target="tpu_custom_call" | custom-call | flops 6000000000 | bytes 1000000 | tf_op jit(solution)/shard_map/pallas_call | solution.py:438
  42.5 1.6 %collective-permute-start.7 = (bf16[112,128]{1,0:T(8,128)(2,1)S(1)}, bf16[112,128]{1,0:T(8,128)(2,1)S(1)}, u32[]{:S(2)}, u32[]{:S(2)}) collective-permute-start(bf16[112,128]{1,0:T(8,128)(2,1)S(1)} %get-tuple-element.44), channel_id=1, source_target_pairs={{0,8},{8,0},{16,24},{24,16},{1,9},{9,1},{17,25},{25,17},{2,10},{10... | collective-permute-start | bytes 86024 | tf_op jit(solution)/shard_map/ppermute | solution.py:459
  44.1 1.5 %collective-permute-start.8 = (bf16[112,128]{1,0:T(8,128)(2,1)S(1)}, bf16[112,128]{1,0:T(8,128)(2,1)S(1)}, u32[]{:S(2)}, u32[]{:S(2)}) collective-permute-start(bf16[112,128]{1,0:T(8,128)(2,1)S(1)} %get-tuple-element.45), channel_id=1, source_target_pairs={{0,16},{8,24},{16,0},{24,8},{1,17},{9,25},{17,1},{25,9},{2,18},{10... | collective-permute-start | bytes 86024 | tf_op jit(solution)/shard_map/ppermute | solution.py:459
  46.1 2.3 %shard_map.71.rest_0_.after = bf16[4,32,1024]{2,1,0:T(8,128)(2,1)S(1)} custom-call(bf16[2,6,4,16,2304]{4,3,2,1,0:T(8,128)(2,1)S(1)} %get-tuple-element.36.ga, bf16[6912,256]{1,0:T(8,128)(2,1)S(1)} %get-tuple-element.37.tat), custom_call_target="tpu_custom_call" | custom-call | flops 2000000000 | bytes 1000000 | tf_op jit(solution)/shard_map/pallas_call | solution.py:438
  48.4 2.0 %collective-permute-done.9.refs_7_ = bf16[112,128]{1,0:T(8,128)(2,1)S(1)} collective-permute-done((bf16[112,128]{1,0:T(8,128)(2,1)S(1)}, bf16[112,128]{1,0:T(8,128)(2,1)S(1)}, u32[]{:S(2)}, u32[]{:S(2)}) %collective-permute-start.9) | collective-permute-done | bytes 28704 | tf_op jit(solution)/shard_map/ppermute | solution.py:459
  50.4 0.6 shard_map.73
  51.1 1.2 %collective-permute-done.10.refs_1_ = bf16[280,128]{1,0:T(8,128)(2,1)S(1)} collective-permute-done((bf16[280,128]{1,0:T(8,128)(2,1)S(1)}, bf16[280,128]{1,0:T(8,128)(2,1)S(1)}, u32[]{:S(2)}, u32[]{:S(2)}) %collective-permute-start.10) | collective-permute-done | bytes 71712 | tf_op jit(solution)/shard_map/ppermute | solution.py:459
  52.3 0.6 shard_map.74.refs_0_
  52.9 2.5 %collective-permute-start.13 = (bf16[280,128]{1,0:T(8,128)(2,1)S(1)}, bf16[280,128]{1,0:T(8,128)(2,1)S(1)}, u32[]{:S(2)}, u32[]{:S(2)}) collective-permute-start(bf16[280,128]{1,0:T(8,128)(2,1)S(1)} %shard_map.74.refs_0_), channel_id=1, source_target_pairs={{0,6},{1,7},{2,4},{3,5},{4,2},{5,3},{6,0},{7,1},{8,14},{9,15},{10,... | collective-permute-start | bytes 215048 | tf_op jit(solution)/shard_map/ppermute | solution.py:459
  55.4 0.6 collective-permute-start.12
  56.0 1.4 %collective-permute-start.11 = (bf16[280,128]{1,0:T(8,128)(2,1)S(1)}, bf16[280,128]{1,0:T(8,128)(2,1)S(1)}, u32[]{:S(2)}, u32[]{:S(2)}) collective-permute-start(bf16[280,128]{1,0:T(8,128)(2,1)S(1)} %shard_map.74.refs_0_), channel_id=1, source_target_pairs={{0,2},{1,3},{2,0},{3,1},{4,6},{5,7},{6,4},{7,5},{8,10},{9,11},{10,... | collective-permute-start | bytes 215048 | tf_op jit(solution)/shard_map/ppermute | solution.py:459
  57.4 3.0 %shard_map.72 = (bf16[2,4,32,1024]{3,2,1,0:T(8,128)(2,1)}, f32[8,128]{1,0:T(8,128)S(1)}) custom-call(bf16[2,6,4,16,2304]{4,3,2,1,0:T(8,128)(2,1)S(1)} %get-tuple-element.36.ga, bf16[6912,256]{1,0:T(8,128)(2,1)S(1)} %get-tuple-element.37.tat, bf16[4,32,1024]{2,1,0:T(8,128)(2,1)S(1)} %shard_map.71.rest_0_.after), custom_call_target="tpu_custom_call" | custom-call | flops 2000000000 | bytes 1000000 | tf_op jit(solution)/shard_map/pallas_call | solution.py:438
  60.3 2.6 %collective-permute-done.12.refs_2_ = bf16[280,128]{1,0:T(8,128)(2,1)S(1)} collective-permute-done((bf16[280,128]{1,0:T(8,128)(2,1)S(1)}, bf16[280,128]{1,0:T(8,128)(2,1)S(1)}, u32[]{:S(2)}, u32[]{:S(2)}) %collective-permute-start.12) | collective-permute-done | bytes 71712 | tf_op jit(solution)/shard_map/ppermute | solution.py:459
  63.5 1.5 %collective-permute-start.15 = (bf16[280,128]{1,0:T(8,128)(2,1)S(1)}, bf16[280,128]{1,0:T(8,128)(2,1)S(1)}, u32[]{:S(2)}, u32[]{:S(2)}) collective-permute-start(bf16[280,128]{1,0:T(8,128)(2,1)S(1)} %shard_map.75.refs_0_), channel_id=1, source_target_pairs={{0,16},{8,24},{16,0},{24,8},{1,17},{9,25},{17,1},{25,9},{2,18},{10... | collective-permute-start | bytes 215048 | tf_op jit(solution)/shard_map/ppermute | solution.py:459
  65.0 1.5 %collective-permute-start.14 = (bf16[280,128]{1,0:T(8,128)(2,1)S(1)}, bf16[280,128]{1,0:T(8,128)(2,1)S(1)}, u32[]{:S(2)}, u32[]{:S(2)}) collective-permute-start(bf16[280,128]{1,0:T(8,128)(2,1)S(1)} %shard_map.75.refs_0_), channel_id=1, source_target_pairs={{0,8},{8,0},{16,24},{24,16},{1,9},{9,1},{17,25},{25,17},{2,10},{10... | collective-permute-start | bytes 215048 | tf_op jit(solution)/shard_map/ppermute | solution.py:459
  66.5 1.9 %collective-permute-done.16.refs_3_ = bf16[280,128]{1,0:T(8,128)(2,1)S(1)} collective-permute-done((bf16[280,128]{1,0:T(8,128)(2,1)S(1)}, bf16[280,128]{1,0:T(8,128)(2,1)S(1)}, u32[]{:S(2)}, u32[]{:S(2)}) %collective-permute-start.16) | collective-permute-done | bytes 71712 | tf_op jit(solution)/shard_map/ppermute | solution.py:459
  68.6 0.7 collective-permute-done.14.refs_1_
  69.3 0.6 shard_map.76.own
  70.0 1.6 %collective-permute-done.17.other = bf16[4,280,128]{2,1,0:T(8,128)(2,1)S(1)} collective-permute-done((bf16[4,280,128]{2,1,0:T(8,128)(2,1)S(1)}, bf16[4,280,128]{2,1,0:T(8,128)(2,1)S(1)}, u32[]{:S(2)}, u32[]{:S(2)}) %collective-permute-start.17) | collective-permute-done | bytes 286752 | tf_op jit(solution)/shard_map/ppermute | solution.py:459
  71.5 1.7 %shard_map.77 = (f32[27,2048]{1,0:T(8,128)}, f32[27,8192]{1,0:T(8,128)}) custom-call(s32[3]{0:T(128)S(1)} %pad_add_fusion.where.after, f32[1]{0:T(128)} %constant.11.clone.1.scale, bf16[4,280,128]{2,1,0:T(8,128)(2,1)S(1)} %shard_map.76.own, bf16[4,280,128]{2,1,0:T(8,128)(2,1)S(1)} %collective-permute-done.17.other), custom_call_target="tpu_custom_call" | custom-call | flops 1000000 | bytes 1000000 | tf_op jit(solution)/shard_map/pallas_call | solution.py:438
  (22 shorter events, 2.0 us)
Async XLA Ops:
  0.6 11.1 %copy-start.1 = (bf16[2,1,8,1024]{3,2,1,0:T(8,128)(2,1)S(1)}, bf16[2,1,8,1024]{3,2,1,0:T(8,128)(2,1)}, u32[]{:S(2)}) copy-start(bf16[2,1,8,1024]{3,2,1,0:T(8,128)(2,1)} %cot.1) | copy-start | bytes 98308
  0.6 11.0 %collective-permute-start.1 = (bf16[2,4,32,1024]{3,2,1,0:T(8,128)(2,1)}, bf16[2,4,32,1024]{3,2,1,0:T(8,128)(2,1)S(1)}, u32[]{:S(2)}, u32[]{:S(2)}) collective-permute-start(bf16[2,4,32,1024]{3,2,1,0:T(8,128)(2,1)} %cubes.1), channel_id=1, source_target_pairs={{1,2},{2,1},{3,4},{4,3},{5,6},{6,5},{9,10},{10,9},{11,12},{12,11},... | collective-permute-start | bytes 1572872 | tf_op jit(solution)/shard_map/ppermute | solution.py:453
  1.3 10.3 %collective-permute-start = (bf16[2,4,32,1024]{3,2,1,0:T(8,128)(2,1)}, bf16[2,4,32,1024]{3,2,1,0:T(8,128)(2,1)S(1)}, u32[]{:S(2)}, u32[]{:S(2)}) collective-permute-start(bf16[2,4,32,1024]{3,2,1,0:T(8,128)(2,1)} %cubes.1), channel_id=1, source_target_pairs={{0,1},{1,0},{2,3},{3,2},{4,5},{5,4},{6,7},{7,6},{8,9},{9,8},{10,11... | collective-permute-start | bytes 1572872 | tf_op jit(solution)/shard_map/ppermute | solution.py:453
  8.2 1.0 %copy-start = (bf16[2,4,32,1024]{3,2,1,0:T(8,128)(2,1)S(1)}, bf16[2,4,32,1024]{3,2,1,0:T(8,128)(2,1)}, u32[]{:S(2)}) copy-start(bf16[2,4,32,1024]{3,2,1,0:T(8,128)(2,1)} %cubes.1) | copy-start | bytes 1572868
  21.7 10.0 %collective-permute-start.3 = (bf16[2,2,16,2048]{3,2,1,0:T(8,128)(2,1)S(1)}, bf16[2,2,16,2048]{3,2,1,0:T(8,128)(2,1)S(1)}, u32[]{:S(2)}, u32[]{:S(2)}) collective-permute-start(bf16[2,2,16,2048]{3,2,1,0:T(8,128)(2,1)S(1)} %get-tuple-element.30.grad_b), channel_id=1, source_target_pairs={{1,2},{2,1},{3,4},{4,3},{5,6},{6,5},{9,10},{10,9},{11,12},{12,11},... | collective-permute-start | bytes 786440 | tf_op jit(solution)/shard_map/ppermute | solution.py:453
  22.5 9.1 %collective-permute-start.2 = (bf16[2,2,16,2048]{3,2,1,0:T(8,128)(2,1)S(1)}, bf16[2,2,16,2048]{3,2,1,0:T(8,128)(2,1)S(1)}, u32[]{:S(2)}, u32[]{:S(2)}) collective-permute-start(bf16[2,2,16,2048]{3,2,1,0:T(8,128)(2,1)S(1)} %get-tuple-element.30.grad_b), channel_id=1, source_target_pairs={{0,1},{1,0},{2,3},{3,2},{4,5},{5,4},{6,7},{7,6},{8,9},{9,8},{10,11... | collective-permute-start | bytes 786440 | tf_op jit(solution)/shard_map/ppermute | solution.py:453
  28.1 17.6 %collective-permute-start.4 = (bf16[448,128]{1,0:T(8,128)(2,1)S(1)}, bf16[448,128]{1,0:T(8,128)(2,1)S(1)}, u32[]{:S(2)}, u32[]{:S(2)}) collective-permute-start(bf16[448,128]{1,0:T(8,128)(2,1)S(1)} %get-tuple-element.40), channel_id=1, source_target_pairs={{0,8},{8,0},{16,24},{24,16},{1,9},{9,1},{17,25},{25,17},{2,10},{10... | collective-permute-start | bytes 344072 | tf_op jit(solution)/shard_map/ppermute | solution.py:459
  29.6 18.7 %collective-permute-start.5 = (bf16[448,128]{1,0:T(8,128)(2,1)S(1)}, bf16[448,128]{1,0:T(8,128)(2,1)S(1)}, u32[]{:S(2)}, u32[]{:S(2)}) collective-permute-start(bf16[448,128]{1,0:T(8,128)(2,1)S(1)} %get-tuple-element.41), channel_id=1, source_target_pairs={{0,16},{8,24},{16,0},{24,8},{1,17},{9,25},{17,1},{25,9},{2,18},{10... | collective-permute-start | bytes 344072 | tf_op jit(solution)/shard_map/ppermute | solution.py:459
  31.1 17.2 %collective-permute-start.6 = (bf16[448,128]{1,0:T(8,128)(2,1)S(1)}, bf16[448,128]{1,0:T(8,128)(2,1)S(1)}, u32[]{:S(2)}, u32[]{:S(2)}) collective-permute-start(bf16[448,128]{1,0:T(8,128)(2,1)S(1)} %get-tuple-element.42), channel_id=1, source_target_pairs={{0,24},{8,16},{16,8},{24,0},{1,25},{9,17},{17,9},{25,1},{2,26},{10... | collective-permute-start | bytes 344072 | tf_op jit(solution)/shard_map/ppermute | solution.py:459
  42.5 5.9 %collective-permute-start.7 = (bf16[112,128]{1,0:T(8,128)(2,1)S(1)}, bf16[112,128]{1,0:T(8,128)(2,1)S(1)}, u32[]{:S(2)}, u32[]{:S(2)}) collective-permute-start(bf16[112,128]{1,0:T(8,128)(2,1)S(1)} %get-tuple-element.44), channel_id=1, source_target_pairs={{0,8},{8,0},{16,24},{24,16},{1,9},{9,1},{17,25},{25,17},{2,10},{10... | collective-permute-start | bytes 86024 | tf_op jit(solution)/shard_map/ppermute | solution.py:459
  44.1 4.3 %collective-permute-start.8 = (bf16[112,128]{1,0:T(8,128)(2,1)S(1)}, bf16[112,128]{1,0:T(8,128)(2,1)S(1)}, u32[]{:S(2)}, u32[]{:S(2)}) collective-permute-start(bf16[112,128]{1,0:T(8,128)(2,1)S(1)} %get-tuple-element.45), channel_id=1, source_target_pairs={{0,16},{8,24},{16,0},{24,8},{1,17},{9,25},{17,1},{25,9},{2,18},{10... | collective-permute-start | bytes 86024 | tf_op jit(solution)/shard_map/ppermute | solution.py:459
  45.6 4.8 %collective-permute-start.9 = (bf16[112,128]{1,0:T(8,128)(2,1)S(1)}, bf16[112,128]{1,0:T(8,128)(2,1)S(1)}, u32[]{:S(2)}, u32[]{:S(2)}) collective-permute-start(bf16[112,128]{1,0:T(8,128)(2,1)S(1)} %get-tuple-element.46), channel_id=1, source_target_pairs={{0,24},{8,16},{16,8},{24,0},{1,25},{9,17},{17,9},{25,1},{2,26},{10... | collective-permute-start | bytes 86024 | tf_op jit(solution)/shard_map/ppermute | solution.py:459
  51.0 1.3 %collective-permute-start.10 = (bf16[280,128]{1,0:T(8,128)(2,1)S(1)}, bf16[280,128]{1,0:T(8,128)(2,1)S(1)}, u32[]{:S(2)}, u32[]{:S(2)}) collective-permute-start(bf16[280,128]{1,0:T(8,128)(2,1)S(1)} %get-tuple-element.48), channel_id=1, source_target_pairs={{0,1},{1,0},{2,3},{3,2},{4,5},{5,4},{6,7},{7,6},{8,9},{9,8},{10,11... | collective-permute-start | bytes 215048 | tf_op jit(solution)/shard_map/ppermute | solution.py:459
  52.9 7.4 %collective-permute-start.13 = (bf16[280,128]{1,0:T(8,128)(2,1)S(1)}, bf16[280,128]{1,0:T(8,128)(2,1)S(1)}, u32[]{:S(2)}, u32[]{:S(2)}) collective-permute-start(bf16[280,128]{1,0:T(8,128)(2,1)S(1)} %shard_map.74.refs_0_), channel_id=1, source_target_pairs={{0,6},{1,7},{2,4},{3,5},{4,2},{5,3},{6,0},{7,1},{8,14},{9,15},{10,... | collective-permute-start | bytes 215048 | tf_op jit(solution)/shard_map/ppermute | solution.py:459
  55.4 7.5 %collective-permute-start.12 = (bf16[280,128]{1,0:T(8,128)(2,1)S(1)}, bf16[280,128]{1,0:T(8,128)(2,1)S(1)}, u32[]{:S(2)}, u32[]{:S(2)}) collective-permute-start(bf16[280,128]{1,0:T(8,128)(2,1)S(1)} %shard_map.74.refs_0_), channel_id=1, source_target_pairs={{0,4},{1,5},{2,6},{3,7},{4,0},{5,1},{6,2},{7,3},{8,12},{9,13},{10,... | collective-permute-start | bytes 215048 | tf_op jit(solution)/shard_map/ppermute | solution.py:459
  56.0 6.9 %collective-permute-start.11 = (bf16[280,128]{1,0:T(8,128)(2,1)S(1)}, bf16[280,128]{1,0:T(8,128)(2,1)S(1)}, u32[]{:S(2)}, u32[]{:S(2)}) collective-permute-start(bf16[280,128]{1,0:T(8,128)(2,1)S(1)} %shard_map.74.refs_0_), channel_id=1, source_target_pairs={{0,2},{1,3},{2,0},{3,1},{4,6},{5,7},{6,4},{7,5},{8,10},{9,11},{10,... | collective-permute-start | bytes 215048 | tf_op jit(solution)/shard_map/ppermute | solution.py:459
  62.9 5.4 %collective-permute-start.16 = (bf16[280,128]{1,0:T(8,128)(2,1)S(1)}, bf16[280,128]{1,0:T(8,128)(2,1)S(1)}, u32[]{:S(2)}, u32[]{:S(2)}) collective-permute-start(bf16[280,128]{1,0:T(8,128)(2,1)S(1)} %shard_map.75.refs_0_), channel_id=1, source_target_pairs={{0,24},{8,16},{16,8},{24,0},{1,25},{9,17},{17,9},{25,1},{2,26},{10... | collective-permute-start | bytes 215048 | tf_op jit(solution)/shard_map/ppermute | solution.py:459
  63.5 5.1 %collective-permute-start.15 = (bf16[280,128]{1,0:T(8,128)(2,1)S(1)}, bf16[280,128]{1,0:T(8,128)(2,1)S(1)}, u32[]{:S(2)}, u32[]{:S(2)}) collective-permute-start(bf16[280,128]{1,0:T(8,128)(2,1)S(1)} %shard_map.75.refs_0_), channel_id=1, source_target_pairs={{0,16},{8,24},{16,0},{24,8},{1,17},{9,25},{17,1},{25,9},{2,18},{10... | collective-permute-start | bytes 215048 | tf_op jit(solution)/shard_map/ppermute | solution.py:459
  65.0 4.3 %collective-permute-start.14 = (bf16[280,128]{1,0:T(8,128)(2,1)S(1)}, bf16[280,128]{1,0:T(8,128)(2,1)S(1)}, u32[]{:S(2)}, u32[]{:S(2)}) collective-permute-start(bf16[280,128]{1,0:T(8,128)(2,1)S(1)} %shard_map.75.refs_0_), channel_id=1, source_target_pairs={{0,8},{8,0},{16,24},{24,16},{1,9},{9,1},{17,25},{25,17},{2,10},{10... | collective-permute-start | bytes 215048 | tf_op jit(solution)/shard_map/ppermute | solution.py:459
  69.9 1.6 %collective-permute-start.17 = (bf16[4,280,128]{2,1,0:T(8,128)(2,1)S(1)}, bf16[4,280,128]{2,1,0:T(8,128)(2,1)S(1)}, u32[]{:S(2)}, u32[]{:S(2)}) collective-permute-start(bf16[4,280,128]{2,1,0:T(8,128)(2,1)S(1)} %shard_map.76.own), channel_id=1, source_target_pairs={{0,1},{1,0},{2,3},{3,2},{4,5},{5,4},{6,7},{7,6},{8,9},{9,8},{10,11... | collective-permute-start | bytes 860168 | tf_op jit(solution)/shard_map/ppermute | solution.py:459

commit v4 on v3

--- a/solution.py
+++ b/solution.py
@@ -107,7 +107,7 @@
             )
 
 
-def forward_kernel(where, own, recv_a, recv_b, ta, tb, cot, xs, dsl, pools, grad_b, pooled, pre_even, pre_odd):
+def forward_kernel(where, own, recv_a, recv_b, ta, tb, cot, xs, dsl, pools, grad_b, pooled):
     del own
     cube_count = xs.shape[0]
     even = where[0] % 2 == 0
@@ -124,55 +124,44 @@
     high = jnp.where(where[0] == where[1] - 1, 0.0, 1.0)
     rows = cube_count * 8 * 16
 
-    def product(g, target):
-        lanes = pl.ds(128 * g if isinstance(g, int) else pl.multiple_of(128 * g, 128), 256)
+    def groups(i, carry):
         stacks = []
-        for p in range(2):
-            stacks.append(
-                jnp.concatenate(
-                    [
-                        xs[:, dz : dz + 8, p + dy, :, lanes].reshape(rows, 256)
-                        for dz in range(3)
-                        for dy in range(3)
-                    ],
-                    axis=1,
+        for j in range(2):
+            lanes = pl.ds(pl.multiple_of(256 * i + 128 * j, 128), 256)
+            for p in range(2):
+                stacks.append(
+                    jnp.concatenate(
+                        [
+                            xs[:, dz : dz + 8, p + dy, :, lanes].reshape(rows, 256)
+                            for dz in range(3)
+                            for dy in range(3)
+                        ],
+                        axis=1,
+                    )
                 )
-            )
-        target[...] = dot(jnp.concatenate(stacks, axis=0), ta[...])
-
-    def pool(g, source):
-        pre = source[...]
+        pre = dot(jnp.concatenate(stacks, axis=0), ta[...])
         squash = sigmoid(pre)
         act = pre * squash
-        slope = (squash + act * (1.0 - squash)).astype(BF).reshape(2, cube_count, 8, 16, 256)
-        for p in range(2):
-            to = pl.ds(256 * g if isinstance(g, int) else pl.multiple_of(256 * g, 256), 256)
-            dsl[:, :, p, :, to] = slope[p][:, 1:7]
-        act = act.reshape(2, cube_count, 4, 2, 16, 256)
-        act = act[0] + act[1]
-        act = act[:, :, 0] + act[:, :, 1]
-        act = (act[..., :128] + act[..., 128:]) * 0.125
-        out = pl.ds(128 * g if isinstance(g, int) else pl.multiple_of(128 * g, 128), 128)
-        for z in range(4):
-            part = act[:, z]
-            if z == 0:
-                part = part * low
-            if z == 3:
-                part = part * high
-            pooled[:, z, :, out] = part.astype(BF)
-
-    def pair(i, carry):
-        product(2 * i + 1, pre_odd)
-        pool(2 * i, pre_even)
-        product(2 * i + 2, pre_even)
-        pool(2 * i + 1, pre_odd)
+        slope = (squash + act * (1.0 - squash)).astype(BF).reshape(2, 2, cube_count, 8, 16, 256)
+        act = act.reshape(2, 2, cube_count, 4, 2, 16, 256)
+        for j in range(2):
+            for p in range(2):
+                to = pl.ds(pl.multiple_of(512 * i + 256 * j, 256), 256)
+                dsl[:, :, p, :, to] = slope[j, p][:, 1:7]
+            part = act[j, 0] + act[j, 1]
+            part = part[:, :, 0] + part[:, :, 1]
+            part = (part[..., :128] + part[..., 128:]) * 0.125
+            out = pl.ds(pl.multiple_of(256 * i + 128 * j, 128), 128)
+            for z in range(4):
+                plane = part[:, z]
+                if z == 0:
+                    plane = plane * low
+                if z == 3:
+                    plane = plane * high
+                pooled[:, z, :, out] = plane.astype(BF)
         return carry
 
-    product(0, pre_even)
-    lax.fori_loop(0, 3, pair, 0)
-    product(7, pre_odd)
-    pool(6, pre_even)
-    pool(7, pre_odd)
+    lax.fori_loop(0, 4, groups, 0)
 
     shifter = row_picker(3, 1, 16)
     for b in range(cube_count):
@@ -210,8 +199,7 @@
                 grad_b[:, z, :, at : at + 128] = (up * part[:, z, :, 128 * e : 128 * e + 128]).astype(BF)
 
 
-def terms_b_kernel(where, pools, grad_b, *rest):
-    outs, terms = rest[:-1], rest[-1]
+def terms_b_kernel(pools, grad_b, terms):
     cube_count = grad_b.shape[0]
     rows_b = cube_count * 2 * 16
     grads = jnp.concatenate(
@@ -231,10 +219,6 @@
             for dx in range(3):
                 term = full[64 * dx : 64 * dx + 64, :128] + full[64 * dx + 64 : 64 * dx + 128, 128:]
                 terms[pl.ds(9 * dz + 3 * dy + dx, C2, stride=28), :] = term
-    share = ROWS_B // len(outs)
-    for k, out in enumerate(outs):
-        chunk = where[2] ^ k
-        out[...] = terms[pl.ds(pl.multiple_of(chunk * share, 8), share), :].astype(BF)
 
 
 def tree(parts):
@@ -243,21 +227,10 @@
     return parts[0]
 
 
-def halve_kernel(where, after, *refs):
-    del after
-    parts, keep, send = refs[:-2], refs[-2], refs[-1]
-    count = len(parts) // 2
-    mine = jnp.concatenate(
-        [
-            tree([part[...].astype(F32) for part in parts[:count]]),
-            tree([part[...].astype(F32) for part in parts[count:]]),
-        ],
-        axis=0,
-    )
-    half = keep.shape[0]
-    low = where[0] % 2 == 0
-    keep[...] = jnp.where(low, mine[:half], mine[half:]).astype(BF)
-    send[...] = jnp.where(low, mine[half:], mine[:half]).astype(BF)
+def scatter_kernel(where, keep, recv, *outs):
+    for k, out in enumerate(outs):
+        part = where[2] ^ k
+        out[...] = (keep[part].astype(F32) + recv[part].astype(F32)).astype(BF)
 
 
 def add_kernel(after, *refs):
@@ -276,18 +249,16 @@
     core = where[0] % 2
     whole[core] = own[...].astype(F32)
     whole[1 - core] = other[...].astype(F32)
-    count, half = own.shape[0], own.shape[1]
-    for width, base, out in ((C2, 0, out_b), (C1 // 2, ROWS_B // count, out_a)):
-        each = width // count
+    count = own.shape[0]
+    for width, base, out in ((C2, 0, out_b), (C1 // 2, ROWS_B // (2 * count), out_a)):
+        each = width // (2 * count)
         for i in range(width):
             start = base + 28 * (i % each)
-            piece = whole[start // half, i // each, start % half : start % half + 27]
+            piece = whole[i // each // count, i // each % count, start : start + 27]
             out[:, 128 * i : 128 * i + 128] = piece * scale[0]
 
 
-def backward_kernel(where, grad_b, recv_a, recv_b, tbt, dsl, xs, after, ga, *rest):
-    outs, (gs, gpool, turned, term, terms) = rest[:-5], rest[-5:]
-    del after
+def backward_kernel(where, grad_b, recv_a, recv_b, tbt, dsl, xs, terms_b, ga, keep, send, gs, gpool, acc, term, terms):
     cube_count = grad_b.shape[0]
     even = where[0] % 2 == 0
     shifter = row_picker(3, 1, 16)
@@ -331,42 +302,55 @@
     own = cube_count * 4 * 16
     place = lax.broadcasted_iota(jnp.int32, (rows_a, 128), 0) % 16
 
-    def group(g, carry):
+    def one_group(g):
         lanes = pl.ds(pl.multiple_of(128 * g, 128), 128)
         up = gpool[:, :, :, lanes]
         up = jnp.concatenate(
             [up[:, 0:1], up[:, 1:2], up[:, 1:2], up[:, 2:3], up[:, 2:3], up[:, 3:4]], axis=1
         ).reshape(rows_a, 128)
+        sides = []
         for p in range(2):
+            pair = []
             for px in range(2):
                 at = pl.ds(pl.multiple_of(256 * g + 128 * px, 128), 128)
                 grad = up * dsl[:, :, p, :, at].astype(F32).reshape(rows_a, 128)
                 to = pl.ds(pl.multiple_of(256 * g + 128 * px + 128, 128), 128)
                 kept = grad.astype(BF).reshape(cube_count, 6, 16, 128)
                 ga[:, :, 1 + p, :, to] = kept
-                turned[g, 128 * px : 128 * px + 128, own * p : own * p + own] = kept[:, 1:5].reshape(own, 128).T
+                pair.append(kept[:, 1:5].reshape(own, 128))
                 if p == 1:
                     moved = jnp.where(place == 0, 0.0, pltpu.roll(grad, 1, 0))
                 else:
                     moved = jnp.where(place == 15, 0.0, pltpu.roll(grad, rows_a - 1, 0))
                 ga[:, :, 0 if p else 3, :, to] = moved.astype(BF).reshape(cube_count, 6, 16, 128)
+            sides.append(jnp.concatenate(pair, axis=1))
+        wide = pl.ds(pl.multiple_of(128 * g, 128), 256)
+        windows = [
+            jnp.concatenate(
+                [
+                    xs[:, HALO - 1 + dz : HALO + 3 + dz, p + dy, :, wide].reshape(own, 256)
+                    for dz in range(3)
+                    for dy in range(3)
+                ],
+                axis=1,
+            )
+            for p in range(2)
+        ]
+        return sides, windows
+
+    def groups(i, carry):
+        first, second = one_group(2 * i), one_group(2 * i + 1)
+        grads = jnp.concatenate(first[0] + second[0], axis=0)
+        acc[...] += dot_t(grads, jnp.concatenate(first[1] + second[1], axis=0))
         return carry
 
-    lax.fori_loop(0, 8, group, 0)
+    acc[...] = jnp.zeros_like(acc)
+    lax.fori_loop(0, 4, groups, 0)
 
     terms[pl.ds(27, C1 // 2, stride=28), :] = jnp.zeros((C1 // 2, 128), F32)
     mask = lanes_below((32, 128), 64)
     for d in range(9):
-        dz, dy = d // 3, d % 3
-        windows = jnp.concatenate(
-            [
-                xs[:, HALO - 1 + dz : HALO + 3 + dz, p + dy, :, 128 * g : 128 * g + 256].reshape(own, 256)
-                for g in range(8)
-                for p in range(2)
-            ],
-            axis=0,
-        )
-        full = dot(jnp.concatenate([turned[g] for g in range(8)], axis=1), windows).T
+        full = acc[:, 256 * d : 256 * d + 256].T
         for dx in range(3):
             left = full[32 * dx : 32 * dx + 32, :128] + full[32 * dx + 32 : 32 * dx + 64, 128:]
             right = full[32 * dx + 64 : 32 * dx + 96, :128] + full[32 * dx + 96 : 32 * dx + 128, 128:]
@@ -376,10 +360,20 @@
             evens = term[slot, pl.ds(0, C1 // 2, stride=2), :]
             odds = term[slot, pl.ds(1, C1 // 2, stride=2), :]
             terms[pl.ds(3 * d + dx, C1 // 2, stride=28), :] = jnp.where(mask[:16], evens, odds)
-    share = ROWS_A // len(outs)
-    for k, out in enumerate(outs):
-        chunk = where[2] ^ k
-        out[...] = terms[pl.ds(pl.multiple_of(chunk * share, 8), share), :].astype(BF)
+    low = where[0] % 2 == 0
+    count = keep.shape[0]
+    for part in range(count):
+        sides = []
+        for core in range(2):
+            at = core * count + part
+            rows_b, rows_a = ROWS_B // (2 * count), ROWS_A // (2 * count)
+            sides.append(
+                jnp.concatenate(
+                    [terms_b[rows_b * at : rows_b * at + rows_b], terms[rows_a * at : rows_a * at + rows_a]], axis=0
+                )
+            )
+        keep[part] = jnp.where(low, sides[0], sides[1]).astype(BF)
+        send[part] = jnp.where(low, sides[1], sides[0]).astype(BF)
 
 
 def one_cube(b, ga, tat, out, landed):
@@ -489,48 +483,39 @@
             ((cube_count, 4, 3, 16, 1152), BF),
             ((cube_count, 2, 16, 2048), BF),
         ],
-        [pltpu.VMEM((cube_count, 4, 16, 1024), BF)] + [pltpu.VMEM((cube_count * 256, 256), F32)] * 2,
+        [pltpu.VMEM((cube_count, 4, 16, 1024), BF)],
         8_000_000_000,
         smem=1,
         aliases={1: 0},
     )
     back_a, back_b = swap(grad_b, grad_b, ring)
-    share_b, share_a = ROWS_B // samples, ROWS_A // samples
-    parts_b = call(
-        terms_b_kernel,
-        [where, pools, grad_b],
-        [((share_b, 128), BF)] * samples,
-        [pltpu.VMEM((ROWS_B, 128), F32)],
-        1_000_000_000,
-        smem=1,
-    )
-    others_b = swap_along(parts_b, "sample", 1)
-    ga, *parts_a = call(
+    (terms_b,) = call(terms_b_kernel, [pools, grad_b], [((ROWS_B, 128), F32)], [], 1_000_000_000)
+    piece = (ROWS_A + ROWS_B) // (2 * samples)
+    pieces = ((samples, piece, 128), BF)
+    ga, keep, send = call(
         backward_kernel,
-        [where, grad_b, back_a, back_b, tbt, dsl, xs, parts_b[0]],
-        [((cube_count, 6, 4, 16, 2304), BF)] + [((share_a, 128), BF)] * samples,
+        [where, grad_b, back_a, back_b, tbt, dsl, xs, terms_b],
+        [((cube_count, 6, 4, 16, 2304), BF), pieces, pieces],
         [
             pltpu.VMEM((cube_count, 6, 3, 16, 2304), BF),
             pltpu.VMEM((cube_count, 4, 16, 1024), F32),
-            pltpu.VMEM((8, 256, cube_count * 128), BF),
+            pltpu.VMEM((256, 2304), F32),
             pltpu.VMEM((4, C1, 128), F32),
             pltpu.VMEM((ROWS_A, 128), F32),
         ],
         6_000_000_000,
         smem=1,
     )
-    others_a = swap_along(parts_a, "sample", 1)
+    small = [((piece, 128), BF)]
+    (recv,) = swap_along([send] * 2, "gz", 1)
+    parts = call(scatter_kernel, [where, keep, recv], small * samples, [], 1_000_000, smem=1)
+    others = swap_along(parts, "sample", 1)
     cube = (ZD, SIDE, SIDE * C1)
     early = [
         call(early_cube_kernel(b), [ga, tat], [(cube, BF)], [], 2_000_000_000)[0] for b in range(cube_count - 1)
     ]
-    half = (share_b + share_a) // 2
-    small = [((half, 128), BF)]
-    keep, send = call(
-        halve_kernel, [where, early[0], parts_b[0], *others_b, parts_a[0], *others_a], small * 2, [], 1_000_000, smem=1
-    )
-    (keep,) = call(add_kernel, [where, keep, *swap_along([send] * 2, "gz", 1)], small, [], 1_000_000, smem=1)
-    others = swap_along([keep] * (ring // 2), "gz", 2)
+    (mine,) = call(add_kernel, [early[0], parts[0], *others], small, [], 1_000_000)
+    others = swap_along([mine] * (ring // 2), "gz", 2)
     input_grad, done = call(
         last_cube_kernel,
         [ga, tat, *early],
@@ -539,10 +524,9 @@
         2_000_000_000,
         any_out=(0,),
     )
-    (keep,) = call(add_kernel, [done, keep, *others], small, [], 1_000_000)
-    shape = (samples, half, 128)
+    (mine,) = call(add_kernel, [done, mine, *others], small, [], 1_000_000)
     (own,) = call(
-        stack_kernel, [where, keep, *swap_along([keep] * samples, "sample", 1)], [(shape, BF)], [], 1_000_000, smem=1
+        stack_kernel, [where, mine, *swap_along([mine] * samples, "sample", 1)], [pieces], [], 1_000_000, smem=1
     )
     (other,) = swap_along([own] * 2, "gz", 1)
     scale = jnp.full((1,), 1.0 / (cube_count * samples), F32)
@@ -550,7 +534,7 @@
         finish_kernel,
         [where, scale, own, other],
         [((27, C1 * C2), F32), ((27, C2 * C3), F32)],
-        [pltpu.VMEM((2, *shape), F32)],
+        [pltpu.VMEM((2, samples, piece, 128), F32)],
         1_000_000,
         smem=2,
     )

time: 73.6 us -> 68 us (0.924)
  Pallas kernels: 33.3 us -> 28.5 us
    pallas_call x11, Pallas kernels: 33.3 us -> 28.5 us  [call(): pl.pallas_call(kernel, out_shape=[jax.ShapeDtypeStruct(shape, dtype) for...]
    ppermute x14 -> x11, starting transfers between devices: 15.3 us -> 14.6 us  [swap_along(): lax.ppermute(part, axis, [(i, i ^ k * step) for i in range(count)])]
    ppermute x14 -> x11, waiting for transfers between devices: 10.2 us -> 9.83 us  [swap_along(): lax.ppermute(part, axis, [(i, i ^ k * step) for i in range(count)])]
  transfers between devices with their start and end apart: 18 -> 15, of which waited for: 7 -> 8; matrix products, arithmetic and copies ran while one was open for 3% -> 4% of each run, Pallas kernels for 27% -> 12%
where the time goes in v4:
time: 68 us; the launch traced here: 67.7 us
  Pallas kernels  28.5 us (42%)
  starting transfers between devices  24.7 us (36%)
  waiting for transfers between devices  10.2 us (15%)
  local copies, waits for them, and re-layouts  3.49 us (5%)
  between operations  0.79 us (1%)
    pallas_call x11, Pallas kernels, call(): pl.pallas_call(kernel, out_shape=[jax.ShapeDtypeStruct(shape, dtype) for...  28.5 us
    ppermute x11, starting transfers between devices, swap_along(): lax.ppermute(part, axis, [(i, i ^ k * step) for i in range(count)])  14.6 us
    ppermute x11, waiting for transfers between devices, swap_along(): lax.ppermute(part, axis, [(i, i ^ k * step) for i in range(count)])  9.83 us
    ppermute x2, starting transfers between devices, swap(): lax.ppermute(first, 'gz', pairs_a)  8.52 us
    ppermute x2, starting transfers between devices, swap(): lax.ppermute(second, 'gz', pairs_b)  1.55 us
  transfers between devices with their start and end apart: 15, of which 8 were waited for; matrix products, arithmetic and copies ran while one was open for 4% of the time, Pallas kernels for 12%

profile of v4, /device:TPU:0, one launch (start us, length us, event | category | flops | bytes accessed | tf_op | source)
XLA Modules:
  0.0 67.7 jit_solution(4154648463915406101)
XLA Ops:
  0.6 0.7 %collective-permute-start.1 = (bf16[2,4,32,1024]{3,2,1,0:T(8,128)(2,1)}, bf16[2,4,32,1024]{3,2,1,0:T(8,128)(2,1)S(1)}, u32[]{:S(2)}, u32[]{:S(2)}) collective-permute-start(bf16[2,4,32,1024]{3,2,1,0:T(8,128)(2,1)} %cubes.1), channel_id=1, source_target_pairs={{1,2},{2,1},{3,4},{4,3},{5,6},{6,5},{9,10},{10,9},{11,12},{12,11},... | collective-permute-start | bytes 1572872 | tf_op jit(solution)/shard_map/ppermute | solution.py:447
  1.3 4.4 %collective-permute-start = (bf16[2,4,32,1024]{3,2,1,0:T(8,128)(2,1)}, bf16[2,4,32,1024]{3,2,1,0:T(8,128)(2,1)S(1)}, u32[]{:S(2)}, u32[]{:S(2)}) collective-permute-start(bf16[2,4,32,1024]{3,2,1,0:T(8,128)(2,1)} %cubes.1), channel_id=1, source_target_pairs={{0,1},{1,0},{2,3},{3,2},{4,5},{5,4},{6,7},{7,6},{8,9},{9,8},{10,11... | collective-permute-start | bytes 1572872 | tf_op jit(solution)/shard_map/ppermute | solution.py:447
  5.8 1.1 %reshape.12.wa = bf16[9,96,64]{2,1,0:T(8,128)(2,1)S(1)} reshape(bf16[27,2048]{1,0:T(8,128)(2,1)} %param.5) | data formatting | bytes 221184 | tf_op jit(solution)/shard_map/reshape | solution.py:466
  6.9 1.3 %reshape.13.wb = bf16[9,192,128]{2,1,0:T(8,128)(2,1)S(1)} reshape(bf16[27,8192]{1,0:T(8,128)(2,1)} %param.6) | data formatting | bytes 884736 | tf_op jit(solution)/shard_map/reshape | solution.py:466
  8.2 1.0 %copy-done = bf16[2,4,32,1024]{3,2,1,0:T(8,128)(2,1)S(1)} copy-done((bf16[2,4,32,1024]{3,2,1,0:T(8,128)(2,1)S(1)}, bf16[2,4,32,1024]{3,2,1,0:T(8,128)(2,1)}, u32[]{:S(2)}) %copy-start) | copy-done | bytes 524312
  9.3 2.3 %shard_map.67 = (bf16[2,10,4,16,1152]{4,3,2,1,0:T(8,128)(2,1)S(1)}, bf16[2304,256]{1,0:T(8,128)(2,1)S(1)}, bf16[2304,256]{1,0:T(8,128)(2,1)S(1)}, bf16[6912,256]{1,0:T(8,128)(2,1)S(1)}, bf16[6912,256]{1,0:T(8,128)(2,1)S(1)}) custom-call(bf16[2,4,32,1024]{3,2,1,0:T(8,128)(2,1)S(1)} %copy-done, bf16[9,96,64]{2,1,0:T(8,128)(2,1)S(1)} %reshape.12.wa, ...), custom_call_target="tpu_custom_call" | custom-call | flops 1000000000 | bytes 1000000 | tf_op jit(solution)/shard_map/pallas_call | solution.py:432
  11.7 8.6 %shard_map.68 = (bf16[2,10,4,16,1152]{4,3,2,1,0:T(8,128)(2,1)S(1)}, bf16[2,6,2,16,2048]{4,3,2,1,0:T(8,128)(2,1)S(1)}, bf16[2,4,3,16,1152]{4,3,2,1,0:T(8,128)(2,1)S(1)}, bf16[2,2,16,2048]{3,2,1,0:T(8,128)(2,1)S(1)}) custom-call(s32[3]{0:T(128)S(1)} %pad_add_fusion.where, ...), custom_call_target="tpu_custom_call", output_to_operand_aliasing={{0}: (1, {})} | custom-call | flops 8000000000 | bytes 1000000 | tf_op jit(solution)/shard_map/pallas_call | solution.py:432
  20.3 0.9 %collective-permute-start.3 = (bf16[2,2,16,2048]{3,2,1,0:T(8,128)(2,1)S(1)}, bf16[2,2,16,2048]{3,2,1,0:T(8,128)(2,1)S(1)}, u32[]{:S(2)}, u32[]{:S(2)}) collective-permute-start(bf16[2,2,16,2048]{3,2,1,0:T(8,128)(2,1)S(1)} %get-tuple-element.26.grad_b), channel_id=1, source_target_pairs={{1,2},{2,1},{3,4},{4,3},{5,6},{6,5},{9,10},{10,9},{11,12},{12,11},... | collective-permute-start | bytes 786440 | tf_op jit(solution)/shard_map/ppermute | solution.py:447
  21.1 4.1 %collective-permute-start.2 = (bf16[2,2,16,2048]{3,2,1,0:T(8,128)(2,1)S(1)}, bf16[2,2,16,2048]{3,2,1,0:T(8,128)(2,1)S(1)}, u32[]{:S(2)}, u32[]{:S(2)}) collective-permute-start(bf16[2,2,16,2048]{3,2,1,0:T(8,128)(2,1)S(1)} %get-tuple-element.26.grad_b), channel_id=1, source_target_pairs={{0,1},{1,0},{2,3},{3,2},{4,5},{5,4},{6,7},{7,6},{8,9},{9,8},{10,11... | collective-permute-start | bytes 786440 | tf_op jit(solution)/shard_map/ppermute | solution.py:447
  25.2 0.8 %shard_map.69.terms_b = f32[1792,128]{1,0:T(8,128)S(1)} custom-call(bf16[2,4,3,16,1152]{4,3,2,1,0:T(8,128)(2,1)S(1)} %get-tuple-element.30.pools, bf16[2,2,16,2048]{3,2,1,0:T(8,128)(2,1)S(1)} %get-tuple-element.26.grad_b), custom_call_target="tpu_custom_call" | custom-call | flops 1000000000 | bytes 1000000 | tf_op jit(solution)/shard_map/pallas_call | solution.py:432
  26.4 8.5 %shard_map.70 = (bf16[2,6,4,16,2304]{4,3,2,1,0:T(8,128)(2,1)S(1)}, bf16[4,280,128]{2,1,0:T(8,128)(2,1)S(1)}, bf16[4,280,128]{2,1,0:T(8,128)(2,1)S(1)}) custom-call(s32[3]{0:T(128)S(1)} %pad_add_fusion.where, bf16[2,2,16,2048]{3,2,1,0:T(8,128)(2,1)S(1)} %get-tuple-element.26.grad_b, bf16[2,2,16,2048]{3,2,1,0:T(8,128)(2,1)S(1)} %collective-permute-done.2.recv_a, ...), custom_call_target="tpu_custom_call" | custom-call | flops 6000000000 | bytes 1000000 | tf_op jit(solution)/shard_map/pallas_call | solution.py:432
  34.9 2.7 %collective-permute-start.4 = (bf16[4,280,128]{2,1,0:T(8,128)(2,1)S(1)}, bf16[4,280,128]{2,1,0:T(8,128)(2,1)S(1)}, u32[]{:S(2)}, u32[]{:S(2)}) collective-permute-start(bf16[4,280,128]{2,1,0:T(8,128)(2,1)S(1)} %get-tuple-element.36), channel_id=1, source_target_pairs={{0,1},{1,0},{2,3},{3,2},{4,5},{5,4},{6,7},{7,6},{8,9},{9,8},{10,11... | collective-permute-start | bytes 860168 | tf_op jit(solution)/shard_map/ppermute | solution.py:453
  37.7 1.2 %collective-permute-done.4.recv = bf16[4,280,128]{2,1,0:T(8,128)(2,1)S(1)} collective-permute-done((bf16[4,280,128]{2,1,0:T(8,128)(2,1)S(1)}, bf16[4,280,128]{2,1,0:T(8,128)(2,1)S(1)}, u32[]{:S(2)}, u32[]{:S(2)}) %collective-permute-start.4) | collective-permute-done | bytes 286752 | tf_op jit(solution)/shard_map/ppermute | solution.py:453
  38.9 0.6 shard_map.73
  39.5 1.6 %collective-permute-start.5 = (bf16[280,128]{1,0:T(8,128)(2,1)S(1)}, bf16[280,128]{1,0:T(8,128)(2,1)S(1)}, u32[]{:S(2)}, u32[]{:S(2)}) collective-permute-start(bf16[280,128]{1,0:T(8,128)(2,1)S(1)} %get-tuple-element.38), channel_id=1, source_target_pairs={{0,8},{8,0},{16,24},{24,16},{1,9},{9,1},{17,25},{25,17},{2,10},{10... | collective-permute-start | bytes 215048 | tf_op jit(solution)/shard_map/ppermute | solution.py:453
  41.0 1.5 %collective-permute-start.6 = (bf16[280,128]{1,0:T(8,128)(2,1)S(1)}, bf16[280,128]{1,0:T(8,128)(2,1)S(1)}, u32[]{:S(2)}, u32[]{:S(2)}) collective-permute-start(bf16[280,128]{1,0:T(8,128)(2,1)S(1)} %get-tuple-element.39), channel_id=1, source_target_pairs={{0,16},{8,24},{16,0},{24,8},{1,17},{9,25},{17,1},{25,9},{2,18},{10... | collective-permute-start | bytes 215048 | tf_op jit(solution)/shard_map/ppermute | solution.py:453
  42.6 0.5 collective-permute-start.7
  43.0 2.3 %shard_map.71.rest_0_.after = bf16[4,32,1024]{2,1,0:T(8,128)(2,1)S(1)} custom-call(bf16[2,6,4,16,2304]{4,3,2,1,0:T(8,128)(2,1)S(1)} %get-tuple-element.31.ga, bf16[6912,256]{1,0:T(8,128)(2,1)S(1)} %get-tuple-element.32.tat), custom_call_target="tpu_custom_call" | custom-call | flops 2000000000 | bytes 1000000 | tf_op jit(solution)/shard_map/pallas_call | solution.py:432
  45.4 2.4 %collective-permute-done.7.refs_3_ = bf16[280,128]{1,0:T(8,128)(2,1)S(1)} collective-permute-done((bf16[280,128]{1,0:T(8,128)(2,1)S(1)}, bf16[280,128]{1,0:T(8,128)(2,1)S(1)}, u32[]{:S(2)}, u32[]{:S(2)}) %collective-permute-start.7) | collective-permute-done | bytes 71712 | tf_op jit(solution)/shard_map/ppermute | solution.py:453
  47.8 4.1 %collective-permute-start.10 = (bf16[280,128]{1,0:T(8,128)(2,1)S(1)}, bf16[280,128]{1,0:T(8,128)(2,1)S(1)}, u32[]{:S(2)}, u32[]{:S(2)}) collective-permute-start(bf16[280,128]{1,0:T(8,128)(2,1)S(1)} %shard_map.74.refs_0_), channel_id=1, source_target_pairs={{0,6},{1,7},{2,4},{3,5},{4,2},{5,3},{6,0},{7,1},{8,14},{9,15},{10,... | collective-permute-start | bytes 215048 | tf_op jit(solution)/shard_map/ppermute | solution.py:453
  51.9 0.6 collective-permute-start.8
  52.5 3.0 %shard_map.72 = (bf16[2,4,32,1024]{3,2,1,0:T(8,128)(2,1)}, f32[8,128]{1,0:T(8,128)S(1)}) custom-call(bf16[2,6,4,16,2304]{4,3,2,1,0:T(8,128)(2,1)S(1)} %get-tuple-element.31.ga, bf16[6912,256]{1,0:T(8,128)(2,1)S(1)} %get-tuple-element.32.tat, bf16[4,32,1024]{2,1,0:T(8,128)(2,1)S(1)} %shard_map.71.rest_0_.after), custom_call_target="tpu_custom_call" | custom-call | flops 2000000000 | bytes 1000000 | tf_op jit(solution)/shard_map/pallas_call | solution.py:432
  55.5 1.6 %collective-permute-done.9.refs_2_ = bf16[280,128]{1,0:T(8,128)(2,1)S(1)} collective-permute-done((bf16[280,128]{1,0:T(8,128)(2,1)S(1)}, bf16[280,128]{1,0:T(8,128)(2,1)S(1)}, u32[]{:S(2)}, u32[]{:S(2)}) %collective-permute-start.9) | collective-permute-done | bytes 71712 | tf_op jit(solution)/shard_map/ppermute | solution.py:453
  57.2 0.9 %collective-permute-start.13 = (bf16[280,128]{1,0:T(8,128)(2,1)S(1)}, bf16[280,128]{1,0:T(8,128)(2,1)S(1)}, u32[]{:S(2)}, u32[]{:S(2)}) collective-permute-start(bf16[280,128]{1,0:T(8,128)(2,1)S(1)} %shard_map.75.refs_0_), channel_id=1, source_target_pairs={{0,24},{8,16},{16,8},{24,0},{1,25},{9,17},{17,9},{25,1},{2,26},{10... | collective-permute-start | bytes 215048 | tf_op jit(solution)/shard_map/ppermute | solution.py:453
  58.1 1.3 %collective-permute-start.12 = (bf16[280,128]{1,0:T(8,128)(2,1)S(1)}, bf16[280,128]{1,0:T(8,128)(2,1)S(1)}, u32[]{:S(2)}, u32[]{:S(2)}) collective-permute-start(bf16[280,128]{1,0:T(8,128)(2,1)S(1)} %shard_map.75.refs_0_), channel_id=1, source_target_pairs={{0,16},{8,24},{16,0},{24,8},{1,17},{9,25},{17,1},{25,9},{2,18},{10... | collective-permute-start | bytes 215048 | tf_op jit(solution)/shard_map/ppermute | solution.py:453
  59.4 1.4 %collective-permute-start.11 = (bf16[280,128]{1,0:T(8,128)(2,1)S(1)}, bf16[280,128]{1,0:T(8,128)(2,1)S(1)}, u32[]{:S(2)}, u32[]{:S(2)}) collective-permute-start(bf16[280,128]{1,0:T(8,128)(2,1)S(1)} %shard_map.75.refs_0_), channel_id=1, source_target_pairs={{0,8},{8,0},{16,24},{24,16},{1,9},{9,1},{17,25},{25,17},{2,10},{10... | collective-permute-start | bytes 215048 | tf_op jit(solution)/shard_map/ppermute | solution.py:453
  60.8 1.9 %collective-permute-done.13.refs_3_ = bf16[280,128]{1,0:T(8,128)(2,1)S(1)} collective-permute-done((bf16[280,128]{1,0:T(8,128)(2,1)S(1)}, bf16[280,128]{1,0:T(8,128)(2,1)S(1)}, u32[]{:S(2)}, u32[]{:S(2)}) %collective-permute-start.13) | collective-permute-done | bytes 71712 | tf_op jit(solution)/shard_map/ppermute | solution.py:453
  62.6 0.6 collective-permute-done.12.refs_2_
  63.2 0.5 collective-permute-done.11.refs_1_
  63.7 0.6 shard_map.76.own
  64.4 1.6 %collective-permute-done.14.other = bf16[4,280,128]{2,1,0:T(8,128)(2,1)S(1)} collective-permute-done((bf16[4,280,128]{2,1,0:T(8,128)(2,1)S(1)}, bf16[4,280,128]{2,1,0:T(8,128)(2,1)S(1)}, u32[]{:S(2)}, u32[]{:S(2)}) %collective-permute-start.14) | collective-permute-done | bytes 286752 | tf_op jit(solution)/shard_map/ppermute | solution.py:453
  65.9 1.7 %shard_map.77 = (f32[27,2048]{1,0:T(8,128)}, f32[27,8192]{1,0:T(8,128)}) custom-call(s32[3]{0:T(128)S(1)} %pad_add_fusion.where, f32[1]{0:T(128)} %constant.11.clone.1.scale, bf16[4,280,128]{2,1,0:T(8,128)(2,1)S(1)} %shard_map.76.own, bf16[4,280,128]{2,1,0:T(8,128)(2,1)S(1)} %collective-permute-done.14.other), custom_call_target="tpu_custom_call" | custom-call | flops 1000000 | bytes 1000000 | tf_op jit(solution)/shard_map/pallas_call | solution.py:432
  (16 shorter events, 0.6 us)
Async XLA Ops:
  0.6 11.1 %copy-start.1 = (bf16[2,1,8,1024]{3,2,1,0:T(8,128)(2,1)S(1)}, bf16[2,1,8,1024]{3,2,1,0:T(8,128)(2,1)}, u32[]{:S(2)}) copy-start(bf16[2,1,8,1024]{3,2,1,0:T(8,128)(2,1)} %cot.1) | copy-start | bytes 98308
  0.6 11.0 %collective-permute-start.1 = (bf16[2,4,32,1024]{3,2,1,0:T(8,128)(2,1)}, bf16[2,4,32,1024]{3,2,1,0:T(8,128)(2,1)S(1)}, u32[]{:S(2)}, u32[]{:S(2)}) collective-permute-start(bf16[2,4,32,1024]{3,2,1,0:T(8,128)(2,1)} %cubes.1), channel_id=1, source_target_pairs={{1,2},{2,1},{3,4},{4,3},{5,6},{6,5},{9,10},{10,9},{11,12},{12,11},... | collective-permute-start | bytes 1572872 | tf_op jit(solution)/shard_map/ppermute | solution.py:447
  1.3 10.3 %collective-permute-start = (bf16[2,4,32,1024]{3,2,1,0:T(8,128)(2,1)}, bf16[2,4,32,1024]{3,2,1,0:T(8,128)(2,1)S(1)}, u32[]{:S(2)}, u32[]{:S(2)}) collective-permute-start(bf16[2,4,32,1024]{3,2,1,0:T(8,128)(2,1)} %cubes.1), channel_id=1, source_target_pairs={{0,1},{1,0},{2,3},{3,2},{4,5},{5,4},{6,7},{7,6},{8,9},{9,8},{10,11... | collective-permute-start | bytes 1572872 | tf_op jit(solution)/shard_map/ppermute | solution.py:447
  8.2 1.0 %copy-start = (bf16[2,4,32,1024]{3,2,1,0:T(8,128)(2,1)S(1)}, bf16[2,4,32,1024]{3,2,1,0:T(8,128)(2,1)}, u32[]{:S(2)}) copy-start(bf16[2,4,32,1024]{3,2,1,0:T(8,128)(2,1)} %cubes.1) | copy-start | bytes 1572868
  20.3 5.8 %collective-permute-start.3 = (bf16[2,2,16,2048]{3,2,1,0:T(8,128)(2,1)S(1)}, bf16[2,2,16,2048]{3,2,1,0:T(8,128)(2,1)S(1)}, u32[]{:S(2)}, u32[]{:S(2)}) collective-permute-start(bf16[2,2,16,2048]{3,2,1,0:T(8,128)(2,1)S(1)} %get-tuple-element.26.grad_b), channel_id=1, source_target_pairs={{1,2},{2,1},{3,4},{4,3},{5,6},{6,5},{9,10},{10,9},{11,12},{12,11},... | collective-permute-start | bytes 786440 | tf_op jit(solution)/shard_map/ppermute | solution.py:447
  21.1 5.3 %collective-permute-start.2 = (bf16[2,2,16,2048]{3,2,1,0:T(8,128)(2,1)S(1)}, bf16[2,2,16,2048]{3,2,1,0:T(8,128)(2,1)S(1)}, u32[]{:S(2)}, u32[]{:S(2)}) collective-permute-start(bf16[2,2,16,2048]{3,2,1,0:T(8,128)(2,1)S(1)} %get-tuple-element.26.grad_b), channel_id=1, source_target_pairs={{0,1},{1,0},{2,3},{3,2},{4,5},{5,4},{6,7},{7,6},{8,9},{9,8},{10,11... | collective-permute-start | bytes 786440 | tf_op jit(solution)/shard_map/ppermute | solution.py:447
  34.9 3.9 %collective-permute-start.4 = (bf16[4,280,128]{2,1,0:T(8,128)(2,1)S(1)}, bf16[4,280,128]{2,1,0:T(8,128)(2,1)S(1)}, u32[]{:S(2)}, u32[]{:S(2)}) collective-permute-start(bf16[4,280,128]{2,1,0:T(8,128)(2,1)S(1)} %get-tuple-element.36), channel_id=1, source_target_pairs={{0,1},{1,0},{2,3},{3,2},{4,5},{5,4},{6,7},{7,6},{8,9},{9,8},{10,11... | collective-permute-start | bytes 860168 | tf_op jit(solution)/shard_map/ppermute | solution.py:453
  39.5 5.9 %collective-permute-start.5 = (bf16[280,128]{1,0:T(8,128)(2,1)S(1)}, bf16[280,128]{1,0:T(8,128)(2,1)S(1)}, u32[]{:S(2)}, u32[]{:S(2)}) collective-permute-start(bf16[280,128]{1,0:T(8,128)(2,1)S(1)} %get-tuple-element.38), channel_id=1, source_target_pairs={{0,8},{8,0},{16,24},{24,16},{1,9},{9,1},{17,25},{25,17},{2,10},{10... | collective-permute-start | bytes 215048 | tf_op jit(solution)/shard_map/ppermute | solution.py:453
  41.0 4.3 %collective-permute-start.6 = (bf16[280,128]{1,0:T(8,128)(2,1)S(1)}, bf16[280,128]{1,0:T(8,128)(2,1)S(1)}, u32[]{:S(2)}, u32[]{:S(2)}) collective-permute-start(bf16[280,128]{1,0:T(8,128)(2,1)S(1)} %get-tuple-element.39), channel_id=1, source_target_pairs={{0,16},{8,24},{16,0},{24,8},{1,17},{9,25},{17,1},{25,9},{2,18},{10... | collective-permute-start | bytes 215048 | tf_op jit(solution)/shard_map/ppermute | solution.py:453
  42.6 5.2 %collective-permute-start.7 = (bf16[280,128]{1,0:T(8,128)(2,1)S(1)}, bf16[280,128]{1,0:T(8,128)(2,1)S(1)}, u32[]{:S(2)}, u32[]{:S(2)}) collective-permute-start(bf16[280,128]{1,0:T(8,128)(2,1)S(1)} %get-tuple-element.40), channel_id=1, source_target_pairs={{0,24},{8,16},{16,8},{24,0},{1,25},{9,17},{17,9},{25,1},{2,26},{10... | collective-permute-start | bytes 215048 | tf_op jit(solution)/shard_map/ppermute | solution.py:453
  47.8 7.7 %collective-permute-start.10 = (bf16[280,128]{1,0:T(8,128)(2,1)S(1)}, bf16[280,128]{1,0:T(8,128)(2,1)S(1)}, u32[]{:S(2)}, u32[]{:S(2)}) collective-permute-start(bf16[280,128]{1,0:T(8,128)(2,1)S(1)} %shard_map.74.refs_0_), channel_id=1, source_target_pairs={{0,6},{1,7},{2,4},{3,5},{4,2},{5,3},{6,0},{7,1},{8,14},{9,15},{10,... | collective-permute-start | bytes 215048 | tf_op jit(solution)/shard_map/ppermute | solution.py:453
  51.9 5.3 %collective-permute-start.9 = (bf16[280,128]{1,0:T(8,128)(2,1)S(1)}, bf16[280,128]{1,0:T(8,128)(2,1)S(1)}, u32[]{:S(2)}, u32[]{:S(2)}) collective-permute-start(bf16[280,128]{1,0:T(8,128)(2,1)S(1)} %shard_map.74.refs_0_), channel_id=1, source_target_pairs={{0,4},{1,5},{2,6},{3,7},{4,0},{5,1},{6,2},{7,3},{8,12},{9,13},{10,... | collective-permute-start | bytes 215048 | tf_op jit(solution)/shard_map/ppermute | solution.py:453
  51.9 5.3 %collective-permute-start.8 = (bf16[280,128]{1,0:T(8,128)(2,1)S(1)}, bf16[280,128]{1,0:T(8,128)(2,1)S(1)}, u32[]{:S(2)}, u32[]{:S(2)}) collective-permute-start(bf16[280,128]{1,0:T(8,128)(2,1)S(1)} %shard_map.74.refs_0_), channel_id=1, source_target_pairs={{0,2},{1,3},{2,0},{3,1},{4,6},{5,7},{6,4},{7,5},{8,10},{9,11},{10,... | collective-permute-start | bytes 215048 | tf_op jit(solution)/shard_map/ppermute | solution.py:453
  57.2 5.4 %collective-permute-start.13 = (bf16[280,128]{1,0:T(8,128)(2,1)S(1)}, bf16[280,128]{1,0:T(8,128)(2,1)S(1)}, u32[]{:S(2)}, u32[]{:S(2)}) collective-permute-start(bf16[280,128]{1,0:T(8,128)(2,1)S(1)} %shard_map.75.refs_0_), channel_id=1, source_target_pairs={{0,24},{8,16},{16,8},{24,0},{1,25},{9,17},{17,9},{25,1},{2,26},{10... | collective-permute-start | bytes 215048 | tf_op jit(solution)/shard_map/ppermute | solution.py:453
  58.1 5.1 %collective-permute-start.12 = (bf16[280,128]{1,0:T(8,128)(2,1)S(1)}, bf16[280,128]{1,0:T(8,128)(2,1)S(1)}, u32[]{:S(2)}, u32[]{:S(2)}) collective-permute-start(bf16[280,128]{1,0:T(8,128)(2,1)S(1)} %shard_map.75.refs_0_), channel_id=1, source_target_pairs={{0,16},{8,24},{16,0},{24,8},{1,17},{9,25},{17,1},{25,9},{2,18},{10... | collective-permute-start | bytes 215048 | tf_op jit(solution)/shard_map/ppermute | solution.py:453
  59.4 4.3 %collective-permute-start.11 = (bf16[280,128]{1,0:T(8,128)(2,1)S(1)}, bf16[280,128]{1,0:T(8,128)(2,1)S(1)}, u32[]{:S(2)}, u32[]{:S(2)}) collective-permute-start(bf16[280,128]{1,0:T(8,128)(2,1)S(1)} %shard_map.75.refs_0_), channel_id=1, source_target_pairs={{0,8},{8,0},{16,24},{24,16},{1,9},{9,1},{17,25},{25,17},{2,10},{10... | collective-permute-start | bytes 215048 | tf_op jit(solution)/shard_map/ppermute | solution.py:453
  64.3 1.6 %collective-permute-start.14 = (bf16[4,280,128]{2,1,0:T(8,128)(2,1)S(1)}, bf16[4,280,128]{2,1,0:T(8,128)(2,1)S(1)}, u32[]{:S(2)}, u32[]{:S(2)}) collective-permute-start(bf16[4,280,128]{2,1,0:T(8,128)(2,1)S(1)} %shard_map.76.own), channel_id=1, source_target_pairs={{0,1},{1,0},{2,3},{3,2},{4,5},{5,4},{6,7},{7,6},{8,9},{9,8},{10,11... | collective-permute-start | bytes 860168 | tf_op jit(solution)/shard_map/ppermute | solution.py:453

commit v5 on v4

--- a/solution.py
+++ b/solution.py
@@ -58,6 +58,23 @@
     return jnp.where(lanes_below(left.shape, 64), left, right).astype(BF)
 
 
+def silu(pre):
+    squash = sigmoid(pre)
+    act = pre * squash
+    return act, (squash + act * (1.0 - squash)).astype(BF)
+
+
+def windows_a(xs, spans, p, start):
+    lanes = pl.ds(start if isinstance(start, int) else pl.multiple_of(start, 128), 256)
+    columns = []
+    for dz in range(3):
+        for dy in range(3):
+            parts = [xs[:, first + dz : first + dz + planes, p + dy, :, lanes] for first, planes in spans]
+            whole = jnp.concatenate(parts, axis=1) if len(parts) > 1 else parts[0]
+            columns.append(whole.reshape(whole.shape[0] * whole.shape[1] * 16, 256))
+    return jnp.concatenate(columns, axis=1)
+
+
 def spread_input(target, b, zz, plane, picker):
     plane = jnp.concatenate([jnp.zeros((32, 32), BF), plane, jnp.zeros((32, 96), BF)], axis=1)
     moved = dot(picker, plane).astype(BF)
@@ -79,7 +96,7 @@
             tat[768 * d + 64 * slot : 768 * d + 64 * slot + 64, 128 * half : 128 * half + 128] = value
 
 
-def prepare_kernel(cubes, wa, wb, xs, ta, tb, tbt, tat):
+def prepare_kernel(cubes, wa, wb, xs, ta, tb, tbt, dsl, inner):
     picker = row_picker(4, 2, 32)
     for b in range(cubes.shape[0]):
         for z in range(ZD):
@@ -91,7 +108,6 @@
             ta[256 * d : 256 * d + 256, 128 * px : 128 * px + 128] = halves(
                 rows_at(block, 32 * px, 256), rows_at(block, 64 + 32 * px, 256)
             )
-        mirror(8 - d, rows_at(block, 0, 128).T[:64], tat)
         block = wb[d]
         for e in range(2):
             tb[256 * d : 256 * d + 256, 128 * e : 128 * e + 128] = rows_at(block, 64 * e, 256)
@@ -106,9 +122,25 @@
                 rows_at(block, 256 * e, 768), rows_at(block, 256 * e + 128, 768)
             )
 
-
-def forward_kernel(where, own, recv_a, recv_b, ta, tb, cot, xs, dsl, pools, grad_b, pooled):
-    del own
+    cube_count = cubes.shape[0]
+    pre = dot(
+        jnp.concatenate(
+            [windows_a(xs, ((HALO, 2),), p, 128 * g) for g in range(8) for p in range(2)], axis=0
+        ),
+        ta[...],
+    )
+    act, slope = silu(pre)
+    slope = slope.reshape(8, 2, cube_count, 2, 16, 256)
+    act = act.reshape(8, 2, cube_count, 2, 16, 256)
+    for g in range(8):
+        for p in range(2):
+            dsl[:, 2:4, p, :, 256 * g : 256 * g + 256] = slope[g, p]
+        part = act[g, 0] + act[g, 1]
+        inner[:, :, :, 128 * g : 128 * g + 128] = part[..., :128] + part[..., 128:]
+
+
+def forward_kernel(where, own, own_slope, inner, recv_a, recv_b, ta, tb, cot, xs, dsl, pools, grad_b, pooled):
+    del own, own_slope
     cube_count = xs.shape[0]
     even = where[0] % 2 == 0
     picker = row_picker(4, 2, 32)
@@ -120,48 +152,39 @@
             spread_input(xs, b, z, below, picker)
             spread_input(xs, b, HALO + ZD + z, above, picker)
 
-    low = jnp.where(where[0] == 0, 0.0, 1.0)
-    high = jnp.where(where[0] == where[1] - 1, 0.0, 1.0)
-    rows = cube_count * 8 * 16
+    low = jnp.where(where[0] == 0, 0.0, 0.125)
+    high = jnp.where(where[0] == where[1] - 1, 0.0, 0.125)
 
     def groups(i, carry):
-        stacks = []
-        for j in range(2):
-            lanes = pl.ds(pl.multiple_of(256 * i + 128 * j, 128), 256)
+        pre = dot(
+            jnp.concatenate(
+                [
+                    windows_a(xs, ((0, 3), (HALO + ZD - 2, 3)), p, 512 * i + 128 * j)
+                    for j in range(4)
+                    for p in range(2)
+                ],
+                axis=0,
+            ),
+            ta[...],
+        )
+        act, slope = silu(pre)
+        slope = slope.reshape(4, 2, cube_count, 6, 16, 256)
+        act = act.reshape(4, 2, cube_count, 6, 16, 256)
+        for j in range(4):
             for p in range(2):
-                stacks.append(
-                    jnp.concatenate(
-                        [
-                            xs[:, dz : dz + 8, p + dy, :, lanes].reshape(rows, 256)
-                            for dz in range(3)
-                            for dy in range(3)
-                        ],
-                        axis=1,
-                    )
-                )
-        pre = dot(jnp.concatenate(stacks, axis=0), ta[...])
-        squash = sigmoid(pre)
-        act = pre * squash
-        slope = (squash + act * (1.0 - squash)).astype(BF).reshape(2, 2, cube_count, 8, 16, 256)
-        act = act.reshape(2, 2, cube_count, 4, 2, 16, 256)
-        for j in range(2):
-            for p in range(2):
-                to = pl.ds(pl.multiple_of(512 * i + 256 * j, 256), 256)
-                dsl[:, :, p, :, to] = slope[j, p][:, 1:7]
+                to = pl.ds(pl.multiple_of(1024 * i + 256 * j, 256), 256)
+                dsl[:, 0:2, p, :, to] = slope[j, p][:, 1:3]
+                dsl[:, 4:6, p, :, to] = slope[j, p][:, 3:5]
             part = act[j, 0] + act[j, 1]
-            part = part[:, :, 0] + part[:, :, 1]
-            part = (part[..., :128] + part[..., 128:]) * 0.125
-            out = pl.ds(pl.multiple_of(256 * i + 128 * j, 128), 128)
-            for z in range(4):
-                plane = part[:, z]
-                if z == 0:
-                    plane = plane * low
-                if z == 3:
-                    plane = plane * high
-                pooled[:, z, :, out] = plane.astype(BF)
+            part = part[..., :128] + part[..., 128:]
+            out = pl.ds(pl.multiple_of(512 * i + 128 * j, 128), 128)
+            pooled[:, 0, :, out] = ((part[:, 0] + part[:, 1]) * low).astype(BF)
+            pooled[:, 1, :, out] = ((part[:, 2] + inner[:, 0, :, out]) * 0.125).astype(BF)
+            pooled[:, 2, :, out] = ((part[:, 3] + inner[:, 1, :, out]) * 0.125).astype(BF)
+            pooled[:, 3, :, out] = ((part[:, 4] + part[:, 5]) * high).astype(BF)
         return carry
 
-    lax.fori_loop(0, 4, groups, 0)
+    lax.fori_loop(0, 2, groups, 0)
 
     shifter = row_picker(3, 1, 16)
     for b in range(cube_count):
@@ -199,8 +222,24 @@
                 grad_b[:, z, :, at : at + 128] = (up * part[:, z, :, 128 * e : 128 * e + 128]).astype(BF)
 
 
-def terms_b_kernel(pools, grad_b, terms):
+def spread_grad(target, b, zz, plane, shifter):
+    moved = dot(shifter, plane).astype(BF)
+    for v in range(3):
+        target[b, zz, v, :, 128:2176] = moved[16 * v : 16 * v + 16]
+        target[b, zz, v, :, :128] = jnp.zeros((16, 128), BF)
+        target[b, zz, v, :, 2176:] = jnp.zeros((16, 128), BF)
+
+
+def terms_b_kernel(pools, grad_b, wa, terms, gs, tat):
     cube_count = grad_b.shape[0]
+    shifter = row_picker(3, 1, 16)
+    for b in range(cube_count):
+        for z in range(2):
+            spread_grad(gs, b, 2 + z, grad_b[b, z], shifter)
+    for d in range(9):
+        block = wa[d].astype(F32)
+        block = jnp.concatenate([block, block], axis=1)
+        mirror(8 - d, rows_at(block, 0, 128).T[:64], tat)
     rows_b = cube_count * 2 * 16
     grads = jnp.concatenate(
         [grad_b[:, :, :, 256 * g : 256 * g + 256].reshape(rows_b, 256) for g in range(8)], axis=0
@@ -258,24 +297,17 @@
             out[:, 128 * i : 128 * i + 128] = piece * scale[0]
 
 
-def backward_kernel(where, grad_b, recv_a, recv_b, tbt, dsl, xs, terms_b, ga, keep, send, gs, gpool, acc, term, terms):
-    cube_count = grad_b.shape[0]
+def backward_kernel(where, own, recv_a, recv_b, tbt, dsl, xs, terms_b, ga, keep, send, gs, gpool, acc, term, terms):
+    del own
+    cube_count = recv_a.shape[0]
     even = where[0] % 2 == 0
     shifter = row_picker(3, 1, 16)
 
-    def spread_plane(b, zz, plane):
-        moved = dot(shifter, plane).astype(BF)
-        for v in range(3):
-            gs[b, zz, v, :, 128:2176] = moved[16 * v : 16 * v + 16]
-            gs[b, zz, v, :, :128] = jnp.zeros((16, 128), BF)
-            gs[b, zz, v, :, 2176:] = jnp.zeros((16, 128), BF)
-
     for b in range(cube_count):
         for z in range(2):
-            spread_plane(b, 2 + z, grad_b[b, z])
             from_a, from_b = recv_a[b, z].astype(F32), recv_b[b, z].astype(F32)
-            spread_plane(b, z, jnp.where(even, from_b, from_a).astype(BF))
-            spread_plane(b, 4 + z, jnp.where(even, from_a, from_b).astype(BF))
+            spread_grad(gs, b, z, jnp.where(even, from_b, from_a).astype(BF), shifter)
+            spread_grad(gs, b, 4 + z, jnp.where(even, from_a, from_b).astype(BF), shifter)
 
     low = jnp.where(where[0] == 0, 0.0, 0.125)
     high = jnp.where(where[0] == where[1] - 1, 0.0, 0.125)
@@ -299,7 +331,7 @@
     ga[:, :, :, :, :128] = jnp.zeros((cube_count, 6, 4, 16, 128), BF)
     ga[:, :, :, :, 2176:] = jnp.zeros((cube_count, 6, 4, 16, 128), BF)
     rows_a = cube_count * 6 * 16
-    own = cube_count * 4 * 16
+    own_rows = cube_count * 4 * 16
     place = lax.broadcasted_iota(jnp.int32, (rows_a, 128), 0) % 16
 
     def one_group(g):
@@ -317,31 +349,19 @@
                 to = pl.ds(pl.multiple_of(256 * g + 128 * px + 128, 128), 128)
                 kept = grad.astype(BF).reshape(cube_count, 6, 16, 128)
                 ga[:, :, 1 + p, :, to] = kept
-                pair.append(kept[:, 1:5].reshape(own, 128))
+                pair.append(kept[:, 1:5].reshape(own_rows, 128))
                 if p == 1:
                     moved = jnp.where(place == 0, 0.0, pltpu.roll(grad, 1, 0))
                 else:
                     moved = jnp.where(place == 15, 0.0, pltpu.roll(grad, rows_a - 1, 0))
                 ga[:, :, 0 if p else 3, :, to] = moved.astype(BF).reshape(cube_count, 6, 16, 128)
             sides.append(jnp.concatenate(pair, axis=1))
-        wide = pl.ds(pl.multiple_of(128 * g, 128), 256)
-        windows = [
-            jnp.concatenate(
-                [
-                    xs[:, HALO - 1 + dz : HALO + 3 + dz, p + dy, :, wide].reshape(own, 256)
-                    for dz in range(3)
-                    for dy in range(3)
-                ],
-                axis=1,
-            )
-            for p in range(2)
-        ]
-        return sides, windows
+        return sides, [windows_a(xs, ((HALO - 1, ZD),), p, 128 * g) for p in range(2)]
 
     def groups(i, carry):
         first, second = one_group(2 * i), one_group(2 * i + 1)
         grads = jnp.concatenate(first[0] + second[0], axis=0)
-        acc[...] += dot_t(grads, jnp.concatenate(first[1] + second[1], axis=0))
+        acc[...] += dot_t(jnp.concatenate(first[1] + second[1], axis=0), grads)
         return carry
 
     acc[...] = jnp.zeros_like(acc)
@@ -350,7 +370,7 @@
     terms[pl.ds(27, C1 // 2, stride=28), :] = jnp.zeros((C1 // 2, 128), F32)
     mask = lanes_below((32, 128), 64)
     for d in range(9):
-        full = acc[:, 256 * d : 256 * d + 256].T
+        full = acc[256 * d : 256 * d + 256]
         for dx in range(3):
             left = full[32 * dx : 32 * dx + 32, :128] + full[32 * dx + 32 : 32 * dx + 64, 128:]
             right = full[32 * dx + 64 : 32 * dx + 96, :128] + full[32 * dx + 96 : 32 * dx + 128, 128:]
@@ -461,22 +481,24 @@
     where = jnp.stack([lax.axis_index("gz"), jnp.int32(ring), lax.axis_index("sample")]).astype(jnp.int32)
     recv_a, recv_b = swap(cubes, cubes, ring)
 
-    own_xs, ta, tb, tbt, tat = call(
+    wa = weight_a.reshape(9, 96, C2)
+    own_xs, ta, tb, tbt, own_slope, inner = call(
         prepare_kernel,
-        [cubes, weight_a.reshape(9, 96, C2), weight_b.reshape(9, 192, C3)],
+        [cubes, wa, weight_b.reshape(9, 192, C3)],
         [
             ((cube_count, ZD + 2 * HALO, 4, 16, 1152), BF),
             ((2304, 256), BF),
             ((2304, 256), BF),
             ((6912, 256), BF),
-            ((6912, 256), BF),
+            ((cube_count, 6, 2, 16, 2048), BF),
+            ((cube_count, 2, 16, 1024), F32),
         ],
         [],
         1_000_000_000,
     )
     xs, dsl, pools, grad_b = call(
         forward_kernel,
-        [where, own_xs, recv_a, recv_b, ta, tb, cotangent],
+        [where, own_xs, own_slope, inner, recv_a, recv_b, ta, tb, cotangent],
         [
             ((cube_count, ZD + 2 * HALO, 4, 16, 1152), BF),
             ((cube_count, 6, 2, 16, 2048), BF),
@@ -486,25 +508,28 @@
         [pltpu.VMEM((cube_count, 4, 16, 1024), BF)],
         8_000_000_000,
         smem=1,
-        aliases={1: 0},
+        aliases={1: 0, 2: 1},
     )
     back_a, back_b = swap(grad_b, grad_b, ring)
-    (terms_b,) = call(terms_b_kernel, [pools, grad_b], [((ROWS_B, 128), F32)], [], 1_000_000_000)
+    spread = ((cube_count, 6, 3, 16, 2304), BF)
+    terms_b, own_gs, tat = call(
+        terms_b_kernel, [pools, grad_b, wa], [((ROWS_B, 128), F32), spread, ((6912, 256), BF)], [], 1_000_000_000
+    )
     piece = (ROWS_A + ROWS_B) // (2 * samples)
     pieces = ((samples, piece, 128), BF)
-    ga, keep, send = call(
+    ga, keep, send, _ = call(
         backward_kernel,
-        [where, grad_b, back_a, back_b, tbt, dsl, xs, terms_b],
-        [((cube_count, 6, 4, 16, 2304), BF), pieces, pieces],
+        [where, own_gs, back_a, back_b, tbt, dsl, xs, terms_b],
+        [((cube_count, 6, 4, 16, 2304), BF), pieces, pieces, spread],
         [
-            pltpu.VMEM((cube_count, 6, 3, 16, 2304), BF),
             pltpu.VMEM((cube_count, 4, 16, 1024), F32),
-            pltpu.VMEM((256, 2304), F32),
+            pltpu.VMEM((2304, 256), F32),
             pltpu.VMEM((4, C1, 128), F32),
             pltpu.VMEM((ROWS_A, 128), F32),
         ],
         6_000_000_000,
         smem=1,
+        aliases={1: 3},
     )
     small = [((piece, 128), BF)]
     (recv,) = swap_along([send] * 2, "gz", 1)

time: 68 us -> 65.6 us (0.965)
  Pallas kernels: 28.5 us -> 27.2 us
  starting transfers between devices: 24.7 us -> 23.8 us
    pallas_call x11, Pallas kernels: 28.5 us -> 27.2 us  [call(): pl.pallas_call(kernel, out_shape=[jax.ShapeDtypeStruct(shape, dtype) for...]
    ppermute x11, starting transfers between devices: 14.6 us -> 13.9 us  [swap_along(): lax.ppermute(part, axis, [(i, i ^ k * step) for i in range(count)])]
  transfers between devices with their start and end apart: 15 -> 15, of which waited for: 8 -> 7; matrix products, arithmetic and copies ran while one was open for 4% -> 4% of each run, Pallas kernels for 12% -> 15%
where the time goes in v5:
time: 65.6 us; the launch traced here: 65.3 us
  Pallas kernels  27.2 us (41%)
  starting transfers between devices  23.8 us (36%)
  waiting for transfers between devices  9.86 us (15%)
  local copies, waits for them, and re-layouts  3.49 us (5%)
  between operations  0.8 us (1%)
    pallas_call x11, Pallas kernels, call(): pl.pallas_call(kernel, out_shape=[jax.ShapeDtypeStruct(shape, dtype) for...  27.2 us
    ppermute x11, starting transfers between devices, swap_along(): lax.ppermute(part, axis, [(i, i ^ k * step) for i in range(count)])  13.9 us
    ppermute x11, waiting for transfers between devices, swap_along(): lax.ppermute(part, axis, [(i, i ^ k * step) for i in range(count)])  9.85 us
    ppermute x2, starting transfers between devices, swap(): lax.ppermute(first, 'gz', pairs_a)  8.38 us
    ppermute x2, starting transfers between devices, swap(): lax.ppermute(second, 'gz', pairs_b)  1.55 us
  transfers between devices with their start and end apart: 15, of which 7 were waited for; matrix products, arithmetic and copies ran while one was open for 4% of the time, Pallas kernels for 15%

profile of v5, /device:TPU:0, one launch (start us, length us, event | category | flops | bytes accessed | tf_op | source)
XLA Modules:
  0.0 65.3 jit_solution(17109618909229144130)
XLA Ops:
  0.6 0.7 %collective-permute-start.1 = (bf16[2,4,32,1024]{3,2,1,0:T(8,128)(2,1)}, bf16[2,4,32,1024]{3,2,1,0:T(8,128)(2,1)S(1)}, u32[]{:S(2)}, u32[]{:S(2)}) collective-permute-start(bf16[2,4,32,1024]{3,2,1,0:T(8,128)(2,1)} %cubes.1), channel_id=1, source_target_pairs={{1,2},{2,1},{3,4},{4,3},{5,6},{6,5},{9,10},{10,9},{11,12},{12,11},... | collective-permute-start | bytes 1572872 | tf_op jit(solution)/shard_map/ppermute | solution.py:467
  1.3 4.4 %collective-permute-start = (bf16[2,4,32,1024]{3,2,1,0:T(8,128)(2,1)}, bf16[2,4,32,1024]{3,2,1,0:T(8,128)(2,1)S(1)}, u32[]{:S(2)}, u32[]{:S(2)}) collective-permute-start(bf16[2,4,32,1024]{3,2,1,0:T(8,128)(2,1)} %cubes.1), channel_id=1, source_target_pairs={{0,1},{1,0},{2,3},{3,2},{4,5},{5,4},{6,7},{7,6},{8,9},{9,8},{10,11... | collective-permute-start | bytes 1572872 | tf_op jit(solution)/shard_map/ppermute | solution.py:467
  5.8 1.1 %reshape.12.wa = bf16[9,96,64]{2,1,0:T(8,128)(2,1)S(1)} reshape(bf16[27,2048]{1,0:T(8,128)(2,1)} %param.5) | data formatting | bytes 221184 | tf_op jit(solution)/shard_map/reshape | solution.py:484
  6.9 1.3 %reshape.13.wb = bf16[9,192,128]{2,1,0:T(8,128)(2,1)S(1)} reshape(bf16[27,8192]{1,0:T(8,128)(2,1)} %param.6) | data formatting | bytes 884736 | tf_op jit(solution)/shard_map/reshape | solution.py:487
  8.2 1.0 %copy-done = bf16[2,4,32,1024]{3,2,1,0:T(8,128)(2,1)S(1)} copy-done((bf16[2,4,32,1024]{3,2,1,0:T(8,128)(2,1)S(1)}, bf16[2,4,32,1024]{3,2,1,0:T(8,128)(2,1)}, u32[]{:S(2)}) %copy-start) | copy-done | bytes 524312
  9.3 2.5 %shard_map.67 = (bf16[2,10,4,16,1152]{4,3,2,1,0:T(8,128)(2,1)S(1)}, bf16[2304,256]{1,0:T(8,128)(2,1)S(1)}, bf16[2304,256]{1,0:T(8,128)(2,1)S(1)}, bf16[6912,256]...) custom-call(bf16[2,4,32,1024]{3,2,1,0:T(8,128)(2,1)S(1)} %copy-done, ...), custom_call_target="tpu_custom_call" | custom-call | flops 1000000000 | bytes 1000000 | tf_op jit(solution)/shard_map/pallas_call | solution.py:452
  11.8 7.1 %shard_map.68 = (bf16[2,10,4,16,1152]{4,3,2,1,0:T(8,128)(2,1)S(1)}, bf16[2,6,2,16,2048]{4,3,2,1,0:T(8,128)(2,1)S(1)}, bf16[2,4,3,16,1152]{4,3,2,1,0:T(8,128)(2,1)S(1)}, bf16[2,2,16,2048]{3,2,1,0:T(8,128)(2,1)S(1)}) custom-call(s32[3]{0:T(128)S(1)} %pad_add_fusion.where, ...), custom_call_target="tpu_custom_call", output_to_operand_aliasing={{0}: (1, {}), {1}: (2, {})} | custom-call | flops 8000000000 | bytes 1000000 | tf_op jit(solution)/shard_map/pallas_call | solution.py:452
  18.9 0.9 %collective-permute-start.3 = (bf16[2,2,16,2048]{3,2,1,0:T(8,128)(2,1)S(1)}, bf16[2,2,16,2048]{3,2,1,0:T(8,128)(2,1)S(1)}, u32[]{:S(2)}, u32[]{:S(2)}) collective-permute-start(bf16[2,2,16,2048]{3,2,1,0:T(8,128)(2,1)S(1)} %get-tuple-element.33.grad_b), channel_id=1, source_target_pairs={{1,2},{2,1},{3,4},{4,3},{5,6},{6,5},{9,10},{10,9},{11,12},{12,11},... | collective-permute-start | bytes 786440 | tf_op jit(solution)/shard_map/ppermute | solution.py:467
  19.8 4.0 %collective-permute-start.2 = (bf16[2,2,16,2048]{3,2,1,0:T(8,128)(2,1)S(1)}, bf16[2,2,16,2048]{3,2,1,0:T(8,128)(2,1)S(1)}, u32[]{:S(2)}, u32[]{:S(2)}) collective-permute-start(bf16[2,2,16,2048]{3,2,1,0:T(8,128)(2,1)S(1)} %get-tuple-element.33.grad_b), channel_id=1, source_target_pairs={{0,1},{1,0},{2,3},{3,2},{4,5},{5,4},{6,7},{7,6},{8,9},{9,8},{10,11... | collective-permute-start | bytes 786440 | tf_op jit(solution)/shard_map/ppermute | solution.py:467
  23.7 1.9 %shard_map.69 = (f32[1792,128]{1,0:T(8,128)S(1)}, bf16[2,6,3,16,2304]{4,3,2,1,0:T(8,128)(2,1)S(1)}, bf16[6912,256]{1,0:T(8,128)(2,1)S(1)}) custom-call(bf16[2,4,3,16,1152]{4,3,2,1,0:T(8,128)(2,1)S(1)} %get-tuple-element.32.pools, bf16[2,2,16,2048]{3,2,1,0:T(8,128)(2,1)S(1)} %get-tuple-element.33.grad_b, bf16[9,96,64]{2,1,0:T(8,128)(2,1)S(1)} %reshape.12.wa), custom_call_target="tpu_custom_call" | custom-call | flops 1000000000 | bytes 1000000 | tf_op jit(solution)/shard_map/pallas_call | solution.py:452
  25.6 7.6 %shard_map.70 = (bf16[2,6,4,16,2304]{4,3,2,1,0:T(8,128)(2,1)S(1)}, bf16[4,280,128]{2,1,0:T(8,128)(2,1)S(1)}, bf16[4,280,128]{2,1,0:T(8,128)(2,1)S(1)}, bf16[2,6,3,16,2304]{4,3,2,1,0:T(8,128)(2,1)S(1)}) custom-call(s32[3]{0:T(128)S(1)} %pad_add_fusion.where, bf16[2,6,3,16,2304]{4,3,2,1,0:T(8,128)(2,1)S(1)} %get-tuple-element.34.own, ...), custom_call_target="tpu_custom_call", output_to_operand_aliasing={{3}: (1, {})} | custom-call | flops 6000000000 | bytes 1000000 | tf_op jit(solution)/shard_map/pallas_call | solution.py:452
  33.3 2.0 %collective-permute-start.4 = (bf16[4,280,128]{2,1,0:T(8,128)(2,1)S(1)}, bf16[4,280,128]{2,1,0:T(8,128)(2,1)S(1)}, u32[]{:S(2)}, u32[]{:S(2)}) collective-permute-start(bf16[4,280,128]{2,1,0:T(8,128)(2,1)S(1)} %get-tuple-element.44), channel_id=1, source_target_pairs={{0,1},{1,0},{2,3},{3,2},{4,5},{5,4},{6,7},{7,6},{8,9},{9,8},{10,11... | collective-permute-start | bytes 860168 | tf_op jit(solution)/shard_map/ppermute | solution.py:473
  35.2 1.2 %collective-permute-done.4.recv = bf16[4,280,128]{2,1,0:T(8,128)(2,1)S(1)} collective-permute-done((bf16[4,280,128]{2,1,0:T(8,128)(2,1)S(1)}, bf16[4,280,128]{2,1,0:T(8,128)(2,1)S(1)}, u32[]{:S(2)}, u32[]{:S(2)}) %collective-permute-start.4) | collective-permute-done | bytes 286752 | tf_op jit(solution)/shard_map/ppermute | solution.py:473
  36.4 0.6 shard_map.73
  37.0 1.6 %collective-permute-start.5 = (bf16[280,128]{1,0:T(8,128)(2,1)S(1)}, bf16[280,128]{1,0:T(8,128)(2,1)S(1)}, u32[]{:S(2)}, u32[]{:S(2)}) collective-permute-start(bf16[280,128]{1,0:T(8,128)(2,1)S(1)} %get-tuple-element.46), channel_id=1, source_target_pairs={{0,8},{8,0},{16,24},{24,16},{1,9},{9,1},{17,25},{25,17},{2,10},{10... | collective-permute-start | bytes 215048 | tf_op jit(solution)/shard_map/ppermute | solution.py:473
  38.6 1.5 %collective-permute-start.6 = (bf16[280,128]{1,0:T(8,128)(2,1)S(1)}, bf16[280,128]{1,0:T(8,128)(2,1)S(1)}, u32[]{:S(2)}, u32[]{:S(2)}) collective-permute-start(bf16[280,128]{1,0:T(8,128)(2,1)S(1)} %get-tuple-element.47), channel_id=1, source_target_pairs={{0,16},{8,24},{16,0},{24,8},{1,17},{9,25},{17,1},{25,9},{2,18},{10... | collective-permute-start | bytes 215048 | tf_op jit(solution)/shard_map/ppermute | solution.py:473
  40.1 0.5 collective-permute-start.7
  40.6 2.3 %shard_map.71.rest_0_.after = bf16[4,32,1024]{2,1,0:T(8,128)(2,1)S(1)} custom-call(bf16[2,6,4,16,2304]{4,3,2,1,0:T(8,128)(2,1)S(1)} %get-tuple-element.39.ga, bf16[6912,256]{1,0:T(8,128)(2,1)S(1)} %get-tuple-element.40.tat), custom_call_target="tpu_custom_call" | custom-call | flops 2000000000 | bytes 1000000 | tf_op jit(solution)/shard_map/pallas_call | solution.py:452
  42.9 2.4 %collective-permute-done.7.refs_3_ = bf16[280,128]{1,0:T(8,128)(2,1)S(1)} collective-permute-done((bf16[280,128]{1,0:T(8,128)(2,1)S(1)}, bf16[280,128]{1,0:T(8,128)(2,1)S(1)}, u32[]{:S(2)}, u32[]{:S(2)}) %collective-permute-start.7) | collective-permute-done | bytes 71712 | tf_op jit(solution)/shard_map/ppermute | solution.py:473
  45.4 4.1 %collective-permute-start.10 = (bf16[280,128]{1,0:T(8,128)(2,1)S(1)}, bf16[280,128]{1,0:T(8,128)(2,1)S(1)}, u32[]{:S(2)}, u32[]{:S(2)}) collective-permute-start(bf16[280,128]{1,0:T(8,128)(2,1)S(1)} %shard_map.74.refs_0_), channel_id=1, source_target_pairs={{0,6},{1,7},{2,4},{3,5},{4,2},{5,3},{6,0},{7,1},{8,14},{9,15},{10,... | collective-permute-start | bytes 215048 | tf_op jit(solution)/shard_map/ppermute | solution.py:473
  49.5 0.6 collective-permute-start.8
  50.1 3.0 %shard_map.72 = (bf16[2,4,32,1024]{3,2,1,0:T(8,128)(2,1)}, f32[8,128]{1,0:T(8,128)S(1)}) custom-call(bf16[2,6,4,16,2304]{4,3,2,1,0:T(8,128)(2,1)S(1)} %get-tuple-element.39.ga, bf16[6912,256]{1,0:T(8,128)(2,1)S(1)} %get-tuple-element.40.tat, bf16[4,32,1024]{2,1,0:T(8,128)(2,1)S(1)} %shard_map.71.rest_0_.after), custom_call_target="tpu_custom_call" | custom-call | flops 2000000000 | bytes 1000000 | tf_op jit(solution)/shard_map/pallas_call | solution.py:452
  53.1 1.6 %collective-permute-done.9.refs_2_ = bf16[280,128]{1,0:T(8,128)(2,1)S(1)} collective-permute-done((bf16[280,128]{1,0:T(8,128)(2,1)S(1)}, bf16[280,128]{1,0:T(8,128)(2,1)S(1)}, u32[]{:S(2)}, u32[]{:S(2)}) %collective-permute-start.9) | collective-permute-done | bytes 71712 | tf_op jit(solution)/shard_map/ppermute | solution.py:473
  54.8 0.9 %collective-permute-start.13 = (bf16[280,128]{1,0:T(8,128)(2,1)S(1)}, bf16[280,128]{1,0:T(8,128)(2,1)S(1)}, u32[]{:S(2)}, u32[]{:S(2)}) collective-permute-start(bf16[280,128]{1,0:T(8,128)(2,1)S(1)} %shard_map.75.refs_0_), channel_id=1, source_target_pairs={{0,24},{8,16},{16,8},{24,0},{1,25},{9,17},{17,9},{25,1},{2,26},{10... | collective-permute-start | bytes 215048 | tf_op jit(solution)/shard_map/ppermute | solution.py:473
  55.7 1.3 %collective-permute-start.12 = (bf16[280,128]{1,0:T(8,128)(2,1)S(1)}, bf16[280,128]{1,0:T(8,128)(2,1)S(1)}, u32[]{:S(2)}, u32[]{:S(2)}) collective-permute-start(bf16[280,128]{1,0:T(8,128)(2,1)S(1)} %shard_map.75.refs_0_), channel_id=1, source_target_pairs={{0,16},{8,24},{16,0},{24,8},{1,17},{9,25},{17,1},{25,9},{2,18},{10... | collective-permute-start | bytes 215048 | tf_op jit(solution)/shard_map/ppermute | solution.py:473
  57.0 1.3 %collective-permute-start.11 = (bf16[280,128]{1,0:T(8,128)(2,1)S(1)}, bf16[280,128]{1,0:T(8,128)(2,1)S(1)}, u32[]{:S(2)}, u32[]{:S(2)}) collective-permute-start(bf16[280,128]{1,0:T(8,128)(2,1)S(1)} %shard_map.75.refs_0_), channel_id=1, source_target_pairs={{0,8},{8,0},{16,24},{24,16},{1,9},{9,1},{17,25},{25,17},{2,10},{10... | collective-permute-start | bytes 215048 | tf_op jit(solution)/shard_map/ppermute | solution.py:473
  58.3 1.9 %collective-permute-done.13.refs_3_ = bf16[280,128]{1,0:T(8,128)(2,1)S(1)} collective-permute-done((bf16[280,128]{1,0:T(8,128)(2,1)S(1)}, bf16[280,128]{1,0:T(8,128)(2,1)S(1)}, u32[]{:S(2)}, u32[]{:S(2)}) %collective-permute-start.13) | collective-permute-done | bytes 71712 | tf_op jit(solution)/shard_map/ppermute | solution.py:473
  60.2 0.6 collective-permute-done.12.refs_2_
  60.8 0.5 collective-permute-done.11.refs_1_
  61.3 0.6 shard_map.76.own
  62.0 1.6 %collective-permute-done.14.other = bf16[4,280,128]{2,1,0:T(8,128)(2,1)S(1)} collective-permute-done((bf16[4,280,128]{2,1,0:T(8,128)(2,1)S(1)}, bf16[4,280,128]{2,1,0:T(8,128)(2,1)S(1)}, u32[]{:S(2)}, u32[]{:S(2)}) %collective-permute-start.14) | collective-permute-done | bytes 286752 | tf_op jit(solution)/shard_map/ppermute | solution.py:473
  63.5 1.7 %shard_map.77 = (f32[27,2048]{1,0:T(8,128)}, f32[27,8192]{1,0:T(8,128)}) custom-call(s32[3]{0:T(128)S(1)} %pad_add_fusion.where, f32[1]{0:T(128)} %constant.11.clone.1.scale, bf16[4,280,128]{2,1,0:T(8,128)(2,1)S(1)} %shard_map.76.own, bf16[4,280,128]{2,1,0:T(8,128)(2,1)S(1)} %collective-permute-done.14.other), custom_call_target="tpu_custom_call" | custom-call | flops 1000000 | bytes 1000000 | tf_op jit(solution)/shard_map/pallas_call | solution.py:452
  (16 shorter events, 0.3 us)
Async XLA Ops:
  0.6 11.2 %copy-start.1 = (bf16[2,1,8,1024]{3,2,1,0:T(8,128)(2,1)S(1)}, bf16[2,1,8,1024]{3,2,1,0:T(8,128)(2,1)}, u32[]{:S(2)}) copy-start(bf16[2,1,8,1024]{3,2,1,0:T(8,128)(2,1)} %cot.1) | copy-start | bytes 98308
  0.6 11.2 %collective-permute-start.1 = (bf16[2,4,32,1024]{3,2,1,0:T(8,128)(2,1)}, bf16[2,4,32,1024]{3,2,1,0:T(8,128)(2,1)S(1)}, u32[]{:S(2)}, u32[]{:S(2)}) collective-permute-start(bf16[2,4,32,1024]{3,2,1,0:T(8,128)(2,1)} %cubes.1), channel_id=1, source_target_pairs={{1,2},{2,1},{3,4},{4,3},{5,6},{6,5},{9,10},{10,9},{11,12},{12,11},... | collective-permute-start | bytes 1572872 | tf_op jit(solution)/shard_map/ppermute | solution.py:467
  1.3 10.5 %collective-permute-start = (bf16[2,4,32,1024]{3,2,1,0:T(8,128)(2,1)}, bf16[2,4,32,1024]{3,2,1,0:T(8,128)(2,1)S(1)}, u32[]{:S(2)}, u32[]{:S(2)}) collective-permute-start(bf16[2,4,32,1024]{3,2,1,0:T(8,128)(2,1)} %cubes.1), channel_id=1, source_target_pairs={{0,1},{1,0},{2,3},{3,2},{4,5},{5,4},{6,7},{7,6},{8,9},{9,8},{10,11... | collective-permute-start | bytes 1572872 | tf_op jit(solution)/shard_map/ppermute | solution.py:467
  8.2 1.0 %copy-start = (bf16[2,4,32,1024]{3,2,1,0:T(8,128)(2,1)S(1)}, bf16[2,4,32,1024]{3,2,1,0:T(8,128)(2,1)}, u32[]{:S(2)}) copy-start(bf16[2,4,32,1024]{3,2,1,0:T(8,128)(2,1)} %cubes.1) | copy-start | bytes 1572868
  18.9 6.7 %collective-permute-start.3 = (bf16[2,2,16,2048]{3,2,1,0:T(8,128)(2,1)S(1)}, bf16[2,2,16,2048]{3,2,1,0:T(8,128)(2,1)S(1)}, u32[]{:S(2)}, u32[]{:S(2)}) collective-permute-start(bf16[2,2,16,2048]{3,2,1,0:T(8,128)(2,1)S(1)} %get-tuple-element.33.grad_b), channel_id=1, source_target_pairs={{1,2},{2,1},{3,4},{4,3},{5,6},{6,5},{9,10},{10,9},{11,12},{12,11},... | collective-permute-start | bytes 786440 | tf_op jit(solution)/shard_map/ppermute | solution.py:467
  19.8 5.8 %collective-permute-start.2 = (bf16[2,2,16,2048]{3,2,1,0:T(8,128)(2,1)S(1)}, bf16[2,2,16,2048]{3,2,1,0:T(8,128)(2,1)S(1)}, u32[]{:S(2)}, u32[]{:S(2)}) collective-permute-start(bf16[2,2,16,2048]{3,2,1,0:T(8,128)(2,1)S(1)} %get-tuple-element.33.grad_b), channel_id=1, source_target_pairs={{0,1},{1,0},{2,3},{3,2},{4,5},{5,4},{6,7},{7,6},{8,9},{9,8},{10,11... | collective-permute-start | bytes 786440 | tf_op jit(solution)/shard_map/ppermute | solution.py:467
  33.3 3.2 %collective-permute-start.4 = (bf16[4,280,128]{2,1,0:T(8,128)(2,1)S(1)}, bf16[4,280,128]{2,1,0:T(8,128)(2,1)S(1)}, u32[]{:S(2)}, u32[]{:S(2)}) collective-permute-start(bf16[4,280,128]{2,1,0:T(8,128)(2,1)S(1)} %get-tuple-element.44), channel_id=1, source_target_pairs={{0,1},{1,0},{2,3},{3,2},{4,5},{5,4},{6,7},{7,6},{8,9},{9,8},{10,11... | collective-permute-start | bytes 860168 | tf_op jit(solution)/shard_map/ppermute | solution.py:473
  37.0 5.9 %collective-permute-start.5 = (bf16[280,128]{1,0:T(8,128)(2,1)S(1)}, bf16[280,128]{1,0:T(8,128)(2,1)S(1)}, u32[]{:S(2)}, u32[]{:S(2)}) collective-permute-start(bf16[280,128]{1,0:T(8,128)(2,1)S(1)} %get-tuple-element.46), channel_id=1, source_target_pairs={{0,8},{8,0},{16,24},{24,16},{1,9},{9,1},{17,25},{25,17},{2,10},{10... | collective-permute-start | bytes 215048 | tf_op jit(solution)/shard_map/ppermute | solution.py:473
  38.6 4.3 %collective-permute-start.6 = (bf16[280,128]{1,0:T(8,128)(2,1)S(1)}, bf16[280,128]{1,0:T(8,128)(2,1)S(1)}, u32[]{:S(2)}, u32[]{:S(2)}) collective-permute-start(bf16[280,128]{1,0:T(8,128)(2,1)S(1)} %get-tuple-element.47), channel_id=1, source_target_pairs={{0,16},{8,24},{16,0},{24,8},{1,17},{9,25},{17,1},{25,9},{2,18},{10... | collective-permute-start | bytes 215048 | tf_op jit(solution)/shard_map/ppermute | solution.py:473
  40.1 5.2 %collective-permute-start.7 = (bf16[280,128]{1,0:T(8,128)(2,1)S(1)}, bf16[280,128]{1,0:T(8,128)(2,1)S(1)}, u32[]{:S(2)}, u32[]{:S(2)}) collective-permute-start(bf16[280,128]{1,0:T(8,128)(2,1)S(1)} %get-tuple-element.48), channel_id=1, source_target_pairs={{0,24},{8,16},{16,8},{24,0},{1,25},{9,17},{17,9},{25,1},{2,26},{10... | collective-permute-start | bytes 215048 | tf_op jit(solution)/shard_map/ppermute | solution.py:473
  45.4 7.7 %collective-permute-start.10 = (bf16[280,128]{1,0:T(8,128)(2,1)S(1)}, bf16[280,128]{1,0:T(8,128)(2,1)S(1)}, u32[]{:S(2)}, u32[]{:S(2)}) collective-permute-start(bf16[280,128]{1,0:T(8,128)(2,1)S(1)} %shard_map.74.refs_0_), channel_id=1, source_target_pairs={{0,6},{1,7},{2,4},{3,5},{4,2},{5,3},{6,0},{7,1},{8,14},{9,15},{10,... | collective-permute-start | bytes 215048 | tf_op jit(solution)/shard_map/ppermute | solution.py:473
  49.5 5.2 %collective-permute-start.9 = (bf16[280,128]{1,0:T(8,128)(2,1)S(1)}, bf16[280,128]{1,0:T(8,128)(2,1)S(1)}, u32[]{:S(2)}, u32[]{:S(2)}) collective-permute-start(bf16[280,128]{1,0:T(8,128)(2,1)S(1)} %shard_map.74.refs_0_), channel_id=1, source_target_pairs={{0,4},{1,5},{2,6},{3,7},{4,0},{5,1},{6,2},{7,3},{8,12},{9,13},{10,... | collective-permute-start | bytes 215048 | tf_op jit(solution)/shard_map/ppermute | solution.py:473
  49.5 5.2 %collective-permute-start.8 = (bf16[280,128]{1,0:T(8,128)(2,1)S(1)}, bf16[280,128]{1,0:T(8,128)(2,1)S(1)}, u32[]{:S(2)}, u32[]{:S(2)}) collective-permute-start(bf16[280,128]{1,0:T(8,128)(2,1)S(1)} %shard_map.74.refs_0_), channel_id=1, source_target_pairs={{0,2},{1,3},{2,0},{3,1},{4,6},{5,7},{6,4},{7,5},{8,10},{9,11},{10,... | collective-permute-start | bytes 215048 | tf_op jit(solution)/shard_map/ppermute | solution.py:473
  54.8 5.5 %collective-permute-start.13 = (bf16[280,128]{1,0:T(8,128)(2,1)S(1)}, bf16[280,128]{1,0:T(8,128)(2,1)S(1)}, u32[]{:S(2)}, u32[]{:S(2)}) collective-permute-start(bf16[280,128]{1,0:T(8,128)(2,1)S(1)} %shard_map.75.refs_0_), channel_id=1, source_target_pairs={{0,24},{8,16},{16,8},{24,0},{1,25},{9,17},{17,9},{25,1},{2,26},{10... | collective-permute-start | bytes 215048 | tf_op jit(solution)/shard_map/ppermute | solution.py:473
  55.7 5.1 %collective-permute-start.12 = (bf16[280,128]{1,0:T(8,128)(2,1)S(1)}, bf16[280,128]{1,0:T(8,128)(2,1)S(1)}, u32[]{:S(2)}, u32[]{:S(2)}) collective-permute-start(bf16[280,128]{1,0:T(8,128)(2,1)S(1)} %shard_map.75.refs_0_), channel_id=1, source_target_pairs={{0,16},{8,24},{16,0},{24,8},{1,17},{9,25},{17,1},{25,9},{2,18},{10... | collective-permute-start | bytes 215048 | tf_op jit(solution)/shard_map/ppermute | solution.py:473
  57.0 4.3 %collective-permute-start.11 = (bf16[280,128]{1,0:T(8,128)(2,1)S(1)}, bf16[280,128]{1,0:T(8,128)(2,1)S(1)}, u32[]{:S(2)}, u32[]{:S(2)}) collective-permute-start(bf16[280,128]{1,0:T(8,128)(2,1)S(1)} %shard_map.75.refs_0_), channel_id=1, source_target_pairs={{0,8},{8,0},{16,24},{24,16},{1,9},{9,1},{17,25},{25,17},{2,10},{10... | collective-permute-start | bytes 215048 | tf_op jit(solution)/shard_map/ppermute | solution.py:473
  61.9 1.6 %collective-permute-start.14 = (bf16[4,280,128]{2,1,0:T(8,128)(2,1)S(1)}, bf16[4,280,128]{2,1,0:T(8,128)(2,1)S(1)}, u32[]{:S(2)}, u32[]{:S(2)}) collective-permute-start(bf16[4,280,128]{2,1,0:T(8,128)(2,1)S(1)} %shard_map.76.own), channel_id=1, source_target_pairs={{0,1},{1,0},{2,3},{3,2},{4,5},{5,4},{6,7},{7,6},{8,9},{9,8},{10,11... | collective-permute-start | bytes 860168 | tf_op jit(solution)/shard_map/ppermute | solution.py:473

commit v6 on v5

--- a/solution.py
+++ b/solution.py
@@ -17,7 +17,7 @@
 F32 = jnp.float32
 VMEM = pl.BlockSpec(memory_space=pltpu.VMEM)
 SMEM = pl.BlockSpec(memory_space=pltpu.SMEM)
-ANY = pl.BlockSpec(memory_space=pl.ANY)
+HBM = pl.BlockSpec(memory_space=pltpu.HBM)
 
 
 def dot(a, b):
@@ -96,11 +96,10 @@
             tat[768 * d + 64 * slot : 768 * d + 64 * slot + 64, 128 * half : 128 * half + 128] = value
 
 
-def prepare_kernel(cubes, wa, wb, xs, ta, tb, tbt, dsl, inner):
+def prepare_kernel(cubes_in, wa, wb, xs, ta, tb, dsl, inner, cubes, sem):
+    arrive = pltpu.make_async_copy(cubes_in, cubes, sem)
+    arrive.start()
     picker = row_picker(4, 2, 32)
-    for b in range(cubes.shape[0]):
-        for z in range(ZD):
-            spread_input(xs, b, HALO + z, cubes[b, z], picker)
     for d in range(9):
         block = wa[d].astype(F32)
         block = jnp.concatenate([block, block], axis=1)
@@ -111,16 +110,10 @@
         block = wb[d]
         for e in range(2):
             tb[256 * d : 256 * d + 256, 128 * e : 128 * e + 128] = rows_at(block, 64 * e, 256)
-        turned = []
-        for dx in (2, 1, 0):
-            part = block[64 * dx : 64 * dx + 64].astype(F32)
-            turned.append(jnp.concatenate([part, part], axis=0).T)
-        block = jnp.concatenate(turned, axis=0)
-        to = 768 * (8 - d)
-        for e in range(2):
-            tbt[to : to + 768, 128 * e : 128 * e + 128] = halves(
-                rows_at(block, 256 * e, 768), rows_at(block, 256 * e + 128, 768)
-            )
+    arrive.wait()
+    for b in range(cubes.shape[0]):
+        for z in range(ZD):
+            spread_input(xs, b, HALO + z, cubes[b, z], picker)
 
     cube_count = cubes.shape[0]
     pre = dot(
@@ -230,7 +223,7 @@
         target[b, zz, v, :, 2176:] = jnp.zeros((16, 128), BF)
 
 
-def terms_b_kernel(pools, grad_b, wa, terms, gs, tat):
+def terms_b_kernel(pools, grad_b, wa, wb, terms, gs, tat, tbt):
     cube_count = grad_b.shape[0]
     shifter = row_picker(3, 1, 16)
     for b in range(cube_count):
@@ -240,6 +233,17 @@
         block = wa[d].astype(F32)
         block = jnp.concatenate([block, block], axis=1)
         mirror(8 - d, rows_at(block, 0, 128).T[:64], tat)
+        block = wb[d]
+        turned = []
+        for dx in (2, 1, 0):
+            part = block[64 * dx : 64 * dx + 64].astype(F32)
+            turned.append(jnp.concatenate([part, part], axis=0).T)
+        block = jnp.concatenate(turned, axis=0)
+        to = 768 * (8 - d)
+        for e in range(2):
+            tbt[to : to + 768, 128 * e : 128 * e + 128] = halves(
+                rows_at(block, 256 * e, 768), rows_at(block, 256 * e + 128, 768)
+            )
     rows_b = cube_count * 2 * 16
     grads = jnp.concatenate(
         [grad_b[:, :, :, 256 * g : 256 * g + 256].reshape(rows_b, 256) for g in range(8)], axis=0
@@ -278,23 +282,31 @@
     out[...] = tree([part[...].astype(F32) for part in parts]).astype(BF)
 
 
-def stack_kernel(where, *refs):
-    parts, out = refs[:-1], refs[-1]
-    for k, part in enumerate(parts):
-        out[where[2] ^ k] = part[...]
-
-
-def finish_kernel(where, scale, own, other, out_a, out_b, whole):
-    core = where[0] % 2
-    whole[core] = own[...].astype(F32)
-    whole[1 - core] = other[...].astype(F32)
-    count = own.shape[0]
-    for width, base, out in ((C2, 0, out_b), (C1 // 2, ROWS_B // (2 * count), out_a)):
+def finish_kernel(where, scale, *refs):
+    parts, (out_a, out_b, whole, total_a, total_b, sems) = refs[:-6], refs[-6:]
+    core, sample, count = where[0] % 2, where[2], len(parts) // 2
+    for i, part in enumerate(parts):
+        whole[core ^ (i % 2), sample ^ (i // 2)] = part[...].astype(F32)
+    copies = []
+    for width, base, total, out in (
+        (C2, 0, total_b, out_b),
+        (C1 // 2, ROWS_B // (2 * count), total_a, out_a),
+    ):
         each = width // (2 * count)
-        for i in range(width):
-            start = base + 28 * (i % each)
-            piece = whole[i // each // count, i // each % count, start : start + 27]
-            out[:, 128 * i : 128 * i + 128] = piece * scale[0]
+        for unit in range(2 * count):
+            for i in range(each):
+                piece = whole[unit // count, unit % count, base + 28 * i : base + 28 * i + 27]
+                at = 128 * (unit * each + i)
+                total[:, at : at + 128] = piece * scale[0]
+            if (unit + 1) * each % 8 == 0:
+                at = 128 * ((unit + 1) * each - 8)
+                copy = pltpu.make_async_copy(
+                    total.at[:, at : at + 1024], out.at[:, at : at + 1024], sems.at[len(copies)]
+                )
+                copy.start()
+                copies.append(copy)
+    for copy in copies:
+        copy.wait()
 
 
 def backward_kernel(where, own, recv_a, recv_b, tbt, dsl, xs, terms_b, ga, keep, send, gs, gpool, acc, term, terms):
@@ -447,16 +459,16 @@
         copy.wait()
 
 
-def call(kernel, args, outs, scratch, flops, smem=0, any_in=(), any_out=(), aliases=None):
-    specs = [SMEM if i < smem else ANY if i in any_in else VMEM for i in range(len(args))]
+def call(kernel, args, outs, scratch, flops, smem=0, any_in=(), any_out=(), aliases=None, limit=28):
+    specs = [SMEM if i < smem else HBM if i in any_in else VMEM for i in range(len(args))]
     return pl.pallas_call(
         kernel,
         out_shape=[jax.ShapeDtypeStruct(shape, dtype) for shape, dtype in outs],
         in_specs=specs,
-        out_specs=[ANY if i in any_out else VMEM for i in range(len(outs))],
+        out_specs=[HBM if i in any_out else VMEM for i in range(len(outs))],
         scratch_shapes=scratch,
         input_output_aliases=aliases or {},
-        compiler_params=pltpu.CompilerParams(vmem_limit_bytes=28 * 1024 * 1024),
+        compiler_params=pltpu.CompilerParams(vmem_limit_bytes=limit * 1024 * 1024),
         cost_estimate=pl.CostEstimate(flops=flops, bytes_accessed=1_000_000, transcendentals=0),
     )(*args)
 
@@ -482,19 +494,21 @@
     recv_a, recv_b = swap(cubes, cubes, ring)
 
     wa = weight_a.reshape(9, 96, C2)
-    own_xs, ta, tb, tbt, own_slope, inner = call(
+    wb = weight_b.reshape(9, 192, C3)
+    own_xs, ta, tb, own_slope, inner = call(
         prepare_kernel,
-        [cubes, wa, weight_b.reshape(9, 192, C3)],
+        [cubes, wa, wb],
         [
             ((cube_count, ZD + 2 * HALO, 4, 16, 1152), BF),
             ((2304, 256), BF),
             ((2304, 256), BF),
-            ((6912, 256), BF),
             ((cube_count, 6, 2, 16, 2048), BF),
             ((cube_count, 2, 16, 1024), F32),
         ],
-        [],
+        [pltpu.VMEM(cubes.shape, BF), pltpu.SemaphoreType.DMA],
         1_000_000_000,
+        any_in=(0,),
+        limit=52,
     )
     xs, dsl, pools, grad_b = call(
         forward_kernel,
@@ -512,8 +526,9 @@
     )
     back_a, back_b = swap(grad_b, grad_b, ring)
     spread = ((cube_count, 6, 3, 16, 2304), BF)
-    terms_b, own_gs, tat = call(
-        terms_b_kernel, [pools, grad_b, wa], [((ROWS_B, 128), F32), spread, ((6912, 256), BF)], [], 1_000_000_000
+    wide = ((6912, 256), BF)
+    terms_b, own_gs, tat, tbt = call(
+        terms_b_kernel, [pools, grad_b, wa, wb], [((ROWS_B, 128), F32), spread, wide, wide], [], 1_000_000_000
     )
     piece = (ROWS_A + ROWS_B) // (2 * samples)
     pieces = ((samples, piece, 128), BF)
@@ -550,18 +565,31 @@
         any_out=(0,),
     )
     (mine,) = call(add_kernel, [done, mine, *others], small, [], 1_000_000)
-    (own,) = call(
-        stack_kernel, [where, mine, *swap_along([mine] * samples, "sample", 1)], [pieces], [], 1_000_000, smem=1
-    )
-    (other,) = swap_along([own] * 2, "gz", 1)
+    gathered = [
+        lax.ppermute(
+            mine,
+            ("sample", "gz"),
+            [(i * ring + j, (i ^ k) * ring + (j ^ c)) for i in range(samples) for j in range(ring)],
+        )
+        for k in range(samples)
+        for c in range(2)
+        if k or c
+    ]
     scale = jnp.full((1,), 1.0 / (cube_count * samples), F32)
+    shape_a, shape_b = (27, C1 * C2), (27, C2 * C3)
     total_a, total_b = call(
         finish_kernel,
-        [where, scale, own, other],
-        [((27, C1 * C2), F32), ((27, C2 * C3), F32)],
-        [pltpu.VMEM((2, samples, piece, 128), F32)],
+        [where, scale, mine, *gathered],
+        [(shape_a, F32), (shape_b, F32)],
+        [
+            pltpu.VMEM((2, samples, piece, 128), F32),
+            pltpu.VMEM(shape_a, F32),
+            pltpu.VMEM(shape_b, F32),
+            pltpu.SemaphoreType.DMA((10,)),
+        ],
         1_000_000,
         smem=2,
+        any_out=(0, 1),
     )
     return input_grad, total_a, total_b
 

time: 65.6 us -> 77.4 us (1.18)
  local copies, waits for them, and re-layouts: 3.49 us -> 13.4 us
  Pallas kernels: 27.2 us -> 28.4 us
    unnamed x4 -> x20, local copies, waits for them, and re-layouts: 1.04 us -> 11 us
    ppermute x0 -> x7, starting transfers between devices: none -> 5.34 us  [shards(): lax.ppermute(mine, ('sample', 'gz'), [(i * ring + j, (i ^ k) * ring + (j...]
    ppermute x0 -> x7, waiting for transfers between devices: none -> 4.7 us  [shards(): lax.ppermute(mine, ('sample', 'gz'), [(i * ring + j, (i ^ k) * ring + (j...]
    ppermute x11 -> x7, waiting for transfers between devices: 9.85 us -> 5.36 us  [swap_along(): lax.ppermute(part, axis, [(i, i ^ k * step) for i in range(count)])]
    ppermute x11 -> x7, starting transfers between devices: 13.9 us -> 9.45 us  [swap_along(): lax.ppermute(part, axis, [(i, i ^ k * step) for i in range(count)])]
    pallas_call x11 -> x10, Pallas kernels: 27.2 us -> 28.4 us  [call(): pl.pallas_call(kernel, out_shape=[jax.ShapeDtypeStruct(shape, dtype) for...]
    ppermute x2, starting transfers between devices: 8.38 us -> 7.53 us  [swap(): lax.ppermute(first, 'gz', pairs_a)]
  transfers between devices with their start and end apart: 15 -> 18, of which waited for: 7 -> 8; matrix products, arithmetic and copies ran while one was open for 4% -> 3% of each run, Pallas kernels for 15% -> 15%
where the time goes in v6:
time: 77.4 us; the launch traced here: 77 us
  Pallas kernels  28.4 us (37%)
  starting transfers between devices  24 us (31%)
  local copies, waits for them, and re-layouts  13.4 us (17%)
  waiting for transfers between devices  10.1 us (13%)
  between operations  0.99 us (1%)
    pallas_call x10, Pallas kernels, call(): pl.pallas_call(kernel, out_shape=[jax.ShapeDtypeStruct(shape, dtype) for...  28.4 us
    unnamed x20, local copies, waits for them, and re-layouts  11 us
    ppermute x7, starting transfers between devices, swap_along(): lax.ppermute(part, axis, [(i, i ^ k * step) for i in range(count)])  9.45 us
    ppermute x2, starting transfers between devices, swap(): lax.ppermute(first, 'gz', pairs_a)  7.53 us
    ppermute x7, waiting for transfers between devices, swap_along(): lax.ppermute(part, axis, [(i, i ^ k * step) for i in range(count)])  5.36 us
    ppermute x7, starting transfers between devices, shards(): lax.ppermute(mine, ('sample', 'gz'), [(i * ring + j, (i ^ k) * ring + (j...  5.34 us
    ppermute x7, waiting for transfers between devices, shards(): lax.ppermute(mine, ('sample', 'gz'), [(i * ring + j, (i ^ k) * ring + (j...  4.7 us
    ppermute x2, starting transfers between devices, swap(): lax.ppermute(second, 'gz', pairs_b)  1.67 us
  transfers between devices with their start and end apart: 18, of which 8 were waited for; matrix products, arithmetic and copies ran while one was open for 3% of the time, Pallas kernels for 15%

profile of v6, /device:TPU:0, one launch (start us, length us, event | category | flops | bytes accessed | tf_op | source)
XLA Modules:
  0.0 77.0 jit_solution(16994822137170468431)
XLA Ops:
  1.3 4.4 %collective-permute-start = (bf16[2,4,32,1024]{3,2,1,0:T(8,128)(2,1)}, bf16[2,4,32,1024]{3,2,1,0:T(8,128)(2,1)S(1)}, u32[]{:S(2)}, u32[]{:S(2)}) collective-permute-start(bf16[2,4,32,1024]{3,2,1,0:T(8,128)(2,1)} %cubes_in.1), channel_id=1, source_target_pairs={{0,1},{1,0},{2,3},{3,2},{4,5},{5,4},{6,7},{7,6},{8,9},{9,8},{10,11... | collective-permute-start | bytes 1572872 | tf_op jit(solution)/shard_map/ppermute | solution.py:479
  5.8 1.1 %reshape.12.wa = bf16[9,96,64]{2,1,0:T(8,128)(2,1)S(1)} reshape(bf16[27,2048]{1,0:T(8,128)(2,1)} %param.5) | data formatting | bytes 221184 | tf_op jit(solution)/shard_map/reshape | solution.py:496
  6.9 1.3 %reshape.13.wb = bf16[9,192,128]{2,1,0:T(8,128)(2,1)S(1)} reshape(bf16[27,8192]{1,0:T(8,128)(2,1)} %param.6) | data formatting | bytes 884736 | tf_op jit(solution)/shard_map/reshape | solution.py:497
  8.2 1.0 %copy-done = bf16[2,4,32,1024]{3,2,1,0:T(8,128)(2,1)S(1)} copy-done((bf16[2,4,32,1024]{3,2,1,0:T(8,128)(2,1)S(1)}, bf16[2,4,32,1024]{3,2,1,0:T(8,128)(2,1)}, u32[]{:S(2)}) %copy-start) | copy-done | bytes 524312
  9.3 3.5 %shard_map.67 = (bf16[2,10,4,16,1152]{4,3,2,1,0:T(8,128)(2,1)}, bf16[2304,256]{1,0:T(8,128)(2,1)}, bf16[2304,256]{1,0:T(8,128)(2,1)}, bf16[2,6,2,16,2048]{4,3,2,1,0:T(8,128)(2,1)}, f32[2,2,16,1024]{3,2,1,0:T(8,128)S(1)}) custom-call(bf16[2,4,32,1024]{3,2,1,0:T(8,128)(2,1)S(1)} %copy-done, bf16[9,96,64]{2,1,0:T(8,128)(2,1)S(1)} %reshape.12.wa, ...), custom_call_target="tpu_custom_call" | custom-call | flops 1000000000 | bytes 1000000 | tf_op jit(solution)/shard_map/pallas_call | solution.py:464
  12.9 1.8 %copy-done.2 = bf16[2,10,4,16,1152]{4,3,2,1,0:T(8,128)(2,1)S(1)} copy-done((bf16[2,10,4,16,1152]{4,3,2,1,0:T(8,128)(2,1)S(1)}, bf16[2,10,4,16,1152]{4,3,2,1,0:T(8,128)(2,1)}, u32[]{:S(2)}) %copy-start.2) | copy-done | bytes 2949144
  14.7 1.4 %copy-done.5 = bf16[2,6,2,16,2048]{4,3,2,1,0:T(8,128)(2,1)S(1)} copy-done((bf16[2,6,2,16,2048]{4,3,2,1,0:T(8,128)(2,1)S(1)}, bf16[2,6,2,16,2048]{4,3,2,1,0:T(8,128)(2,1)}, u32[]{:S(2)}) %copy-start.5) | copy-done | bytes 1572888
  16.1 1.3 %copy-done.8 = bf16[2304,256]{1,0:T(8,128)(2,1)S(1)} copy-done((bf16[2304,256]{1,0:T(8,128)(2,1)S(1)}, bf16[2304,256]{1,0:T(8,128)(2,1)}, u32[]{:S(2)}) %copy-start.8) | copy-done | bytes 1179672
  17.4 1.3 %copy-done.9 = bf16[2304,256]{1,0:T(8,128)(2,1)S(1)} copy-done((bf16[2304,256]{1,0:T(8,128)(2,1)S(1)}, bf16[2304,256]{1,0:T(8,128)(2,1)}, u32[]{:S(2)}) %copy-start.9) | copy-done | bytes 1179672
  18.7 7.1 %shard_map.68 = (bf16[2,10,4,16,1152]{4,3,2,1,0:T(8,128)(2,1)S(1)}, bf16[2,6,2,16,2048]{4,3,2,1,0:T(8,128)(2,1)S(1)}, bf16[2,4,3,16,1152]{4,3,2,1,0:T(8,128)(2,1)S(1)}, bf16[2,2,16,2048]{3,2,1,0:T(8,128)(2,1)S(1)}) custom-call(s32[3]{0:T(128)S(1)} %pad_add_fusion.where, ...), custom_call_target="tpu_custom_call", output_to_operand_aliasing={{0}: (1, {}), {1}: (2, {})} | custom-call | flops 8000000000 | bytes 1000000 | tf_op jit(solution)/shard_map/pallas_call | solution.py:464
  25.8 1.6 %copy-done.3 = bf16[2,10,4,16,1152]{4,3,2,1,0:T(8,128)(2,1)} copy-done((bf16[2,10,4,16,1152]{4,3,2,1,0:T(8,128)(2,1)}, bf16[2,10,4,16,1152]{4,3,2,1,0:T(8,128)(2,1)S(1)}, u32[]{:S(2)}) %copy-start.3) | copy-done | bytes 2949144
  27.3 1.2 %copy-done.6 = bf16[2,6,2,16,2048]{4,3,2,1,0:T(8,128)(2,1)} copy-done((bf16[2,6,2,16,2048]{4,3,2,1,0:T(8,128)(2,1)}, bf16[2,6,2,16,2048]{4,3,2,1,0:T(8,128)(2,1)S(1)}, u32[]{:S(2)}) %copy-start.6) | copy-done | bytes 1572888
  29.5 3.1 %collective-permute-start.2 = (bf16[2,2,16,2048]{3,2,1,0:T(8,128)(2,1)S(1)}, bf16[2,2,16,2048]{3,2,1,0:T(8,128)(2,1)S(1)}, u32[]{:S(2)}, u32[]{:S(2)}) collective-permute-start(bf16[2,2,16,2048]{3,2,1,0:T(8,128)(2,1)S(1)} %get-tuple-element.33.grad_b), channel_id=1, source_target_pairs={{0,1},{1,0},{2,3},{3,2},{4,5},{5,4},{6,7},{7,6},{8,9},{9,8},{10,11... | collective-permute-start | bytes 786440 | tf_op jit(solution)/shard_map/ppermute | solution.py:479
  32.6 2.6 %shard_map.69 = (f32[1792,128]{1,0:T(8,128)S(1)}, bf16[2,6,3,16,2304]{4,3,2,1,0:T(8,128)(2,1)S(1)}, bf16[6912,256]{1,0:T(8,128)(2,1)S(1)}, bf16[6912,256]{1,0:T(8,128)(2,1)S(1)}) custom-call(bf16[2,4,3,16,1152]{4,3,2,1,0:T(8,128)(2,1)S(1)} %get-tuple-element.32.pools, bf16[2,2,16,2048]{3,2,1,0:T(8,128)(2,1)S(1)} %get-tuple-element.33.grad_b, ...), custom_call_target="tpu_custom_call" | custom-call | flops 1000000000 | bytes 1000000 | tf_op jit(solution)/shard_map/pallas_call | solution.py:464
  35.2 1.4 %copy-done.7 = bf16[2,6,2,16,2048]{4,3,2,1,0:T(8,128)(2,1)S(1)} copy-done((bf16[2,6,2,16,2048]{4,3,2,1,0:T(8,128)(2,1)S(1)}, bf16[2,6,2,16,2048]{4,3,2,1,0:T(8,128)(2,1)}, u32[]{:S(2)}) %copy-start.7) | copy-done | bytes 1572888
  36.6 7.6 %shard_map.70 = (bf16[2,6,4,16,2304]{4,3,2,1,0:T(8,128)(2,1)S(1)}, bf16[4,280,128]{2,1,0:T(8,128)(2,1)S(1)}, bf16[4,280,128]{2,1,0:T(8,128)(2,1)S(1)}, bf16[2,6,3,16,2304]{4,3,2,1,0:T(8,128)(2,1)S(1)}) custom-call(s32[3]{0:T(128)S(1)} %pad_add_fusion.where, bf16[2,6,3,16,2304]{4,3,2,1,0:T(8,128)(2,1)S(1)} %get-tuple-element.34.own, ...), custom_call_target="tpu_custom_call", output_to_operand_aliasing={{3}: (1, {})} | custom-call | flops 6000000000 | bytes 1000000 | tf_op jit(solution)/shard_map/pallas_call | solution.py:464
  44.2 1.3 %collective-permute-start.4 = (bf16[4,280,128]{2,1,0:T(8,128)(2,1)S(1)}, bf16[4,280,128]{2,1,0:T(8,128)(2,1)S(1)}, u32[]{:S(2)}, u32[]{:S(2)}) collective-permute-start(bf16[4,280,128]{2,1,0:T(8,128)(2,1)S(1)} %get-tuple-element.44), channel_id=1, source_target_pairs={{0,1},{1,0},{2,3},{3,2},{4,5},{5,4},{6,7},{7,6},{8,9},{9,8},{10,11... | collective-permute-start | bytes 860168 | tf_op jit(solution)/shard_map/ppermute | solution.py:485
  45.5 1.2 %collective-permute-done.4.recv = bf16[4,280,128]{2,1,0:T(8,128)(2,1)S(1)} collective-permute-done((bf16[4,280,128]{2,1,0:T(8,128)(2,1)S(1)}, bf16[4,280,128]{2,1,0:T(8,128)(2,1)S(1)}, u32[]{:S(2)}, u32[]{:S(2)}) %collective-permute-start.4) | collective-permute-done | bytes 286752 | tf_op jit(solution)/shard_map/ppermute | solution.py:485
  47.3 1.6 %collective-permute-start.5 = (bf16[280,128]{1,0:T(8,128)(2,1)S(1)}, bf16[280,128]{1,0:T(8,128)(2,1)S(1)}, u32[]{:S(2)}, u32[]{:S(2)}) collective-permute-start(bf16[280,128]{1,0:T(8,128)(2,1)S(1)} %get-tuple-element.46), channel_id=1, source_target_pairs={{0,8},{8,0},{16,24},{24,16},{1,9},{9,1},{17,25},{25,17},{2,10},{10... | collective-permute-start | bytes 215048 | tf_op jit(solution)/shard_map/ppermute | solution.py:485
  48.9 1.5 %collective-permute-start.6 = (bf16[280,128]{1,0:T(8,128)(2,1)S(1)}, bf16[280,128]{1,0:T(8,128)(2,1)S(1)}, u32[]{:S(2)}, u32[]{:S(2)}) collective-permute-start(bf16[280,128]{1,0:T(8,128)(2,1)S(1)} %get-tuple-element.47), channel_id=1, source_target_pairs={{0,16},{8,24},{16,0},{24,8},{1,17},{9,25},{17,1},{25,9},{2,18},{10... | collective-permute-start | bytes 215048 | tf_op jit(solution)/shard_map/ppermute | solution.py:485
  50.9 2.3 %shard_map.71.rest_0_.after = bf16[4,32,1024]{2,1,0:T(8,128)(2,1)S(1)} custom-call(bf16[2,6,4,16,2304]{4,3,2,1,0:T(8,128)(2,1)S(1)} %get-tuple-element.39.ga, bf16[6912,256]{1,0:T(8,128)(2,1)S(1)} %get-tuple-element.40.tat), custom_call_target="tpu_custom_call" | custom-call | flops 2000000000 | bytes 1000000 | tf_op jit(solution)/shard_map/pallas_call | solution.py:464
  53.2 2.4 %collective-permute-done.7.refs_3_ = bf16[280,128]{1,0:T(8,128)(2,1)S(1)} collective-permute-done((bf16[280,128]{1,0:T(8,128)(2,1)S(1)}, bf16[280,128]{1,0:T(8,128)(2,1)S(1)}, u32[]{:S(2)}, u32[]{:S(2)}) %collective-permute-start.7) | collective-permute-done | bytes 71712 | tf_op jit(solution)/shard_map/ppermute | solution.py:485
  55.7 3.9 %collective-permute-start.10 = (bf16[280,128]{1,0:T(8,128)(2,1)S(1)}, bf16[280,128]{1,0:T(8,128)(2,1)S(1)}, u32[]{:S(2)}, u32[]{:S(2)}) collective-permute-start(bf16[280,128]{1,0:T(8,128)(2,1)S(1)} %shard_map.74.refs_0_), channel_id=1, source_target_pairs={{0,6},{1,7},{2,4},{3,5},{4,2},{5,3},{6,0},{7,1},{8,14},{9,15},{10,... | collective-permute-start | bytes 215048 | tf_op jit(solution)/shard_map/ppermute | solution.py:485
  60.3 3.0 %shard_map.72 = (bf16[2,4,32,1024]{3,2,1,0:T(8,128)(2,1)}, f32[8,128]{1,0:T(8,128)S(1)}) custom-call(bf16[2,6,4,16,2304]{4,3,2,1,0:T(8,128)(2,1)S(1)} %get-tuple-element.39.ga, bf16[6912,256]{1,0:T(8,128)(2,1)S(1)} %get-tuple-element.40.tat, bf16[4,32,1024]{2,1,0:T(8,128)(2,1)S(1)} %shard_map.71.rest_0_.after), custom_call_target="tpu_custom_call" | custom-call | flops 2000000000 | bytes 1000000 | tf_op jit(solution)/shard_map/pallas_call | solution.py:464
  63.2 1.7 %collective-permute-done.9.refs_2_ = bf16[280,128]{1,0:T(8,128)(2,1)S(1)} collective-permute-done((bf16[280,128]{1,0:T(8,128)(2,1)S(1)}, bf16[280,128]{1,0:T(8,128)(2,1)S(1)}, u32[]{:S(2)}, u32[]{:S(2)}) %collective-permute-start.9) | collective-permute-done | bytes 71712 | tf_op jit(solution)/shard_map/ppermute | solution.py:485
  65.1 1.9 %collective-permute-start.16 = (bf16[280,128]{1,0:T(8,128)(2,1)S(1)}, bf16[280,128]{1,0:T(8,128)(2,1)S(1)}, u32[]{:S(2)}, u32[]{:S(2)}) collective-permute-start(bf16[280,128]{1,0:T(8,128)(2,1)S(1)} %shard_map.75.refs_0_), channel_id=1, source_target_pairs={{0,24},{1,25},{2,26},{3,27},{4,28},{5,29},{6,30},{7,31},{8,16},{9,... | collective-permute-start | bytes 215048 | tf_op jit(solution)/shard_map/ppermute | solution.py:569
  66.9 1.1 %collective-permute-start.15 = (bf16[280,128]{1,0:T(8,128)(2,1)S(1)}, bf16[280,128]{1,0:T(8,128)(2,1)S(1)}, u32[]{:S(2)}, u32[]{:S(2)}) collective-permute-start(bf16[280,128]{1,0:T(8,128)(2,1)S(1)} %shard_map.75.refs_0_), channel_id=1, source_target_pairs={{0,17},{1,16},{2,19},{3,18},{4,21},{5,20},{6,23},{7,22},{8,25},{9,... | collective-permute-start | bytes 215048 | tf_op jit(solution)/shard_map/ppermute | solution.py:569
  68.0 1.4 %collective-permute-start.14 = (bf16[280,128]{1,0:T(8,128)(2,1)S(1)}, bf16[280,128]{1,0:T(8,128)(2,1)S(1)}, u32[]{:S(2)}, u32[]{:S(2)}) collective-permute-start(bf16[280,128]{1,0:T(8,128)(2,1)S(1)} %shard_map.75.refs_0_), channel_id=1, source_target_pairs={{0,16},{1,17},{2,18},{3,19},{4,20},{5,21},{6,22},{7,23},{8,24},{9,... | collective-permute-start | bytes 215048 | tf_op jit(solution)/shard_map/ppermute | solution.py:569
  69.5 1.0 %collective-permute-done.17.refs_7_ = bf16[280,128]{1,0:T(8,128)(2,1)S(1)} collective-permute-done((bf16[280,128]{1,0:T(8,128)(2,1)S(1)}, bf16[280,128]{1,0:T(8,128)(2,1)S(1)}, u32[]{:S(2)}, u32[]{:S(2)}) %collective-permute-start.17) | collective-permute-done | bytes 71712 | tf_op jit(solution)/shard_map/ppermute | solution.py:569
  71.5 1.5 %collective-permute-done.15.refs_5_ = bf16[280,128]{1,0:T(8,128)(2,1)S(1)} collective-permute-done((bf16[280,128]{1,0:T(8,128)(2,1)S(1)}, bf16[280,128]{1,0:T(8,128)(2,1)S(1)}, u32[]{:S(2)}, u32[]{:S(2)}) %collective-permute-start.15) | collective-permute-done | bytes 71712 | tf_op jit(solution)/shard_map/ppermute | solution.py:569
  73.0 1.6 %collective-permute-done.14.refs_4_ = bf16[280,128]{1,0:T(8,128)(2,1)S(1)} collective-permute-done((bf16[280,128]{1,0:T(8,128)(2,1)S(1)}, bf16[280,128]{1,0:T(8,128)(2,1)S(1)}, u32[]{:S(2)}, u32[]{:S(2)}) %collective-permute-start.14) | collective-permute-done | bytes 71712 | tf_op jit(solution)/shard_map/ppermute | solution.py:569
  75.1 1.8 %shard_map.76 = (f32[27,2048]{1,0:T(8,128)}, f32[27,8192]{1,0:T(8,128)}) custom-call(s32[3]{0:T(128)S(1)} %pad_add_fusion.where, f32[1]{0:T(128)} %constant.11.clone.1.scale, bf16[280,128]{1,0:T(8,128)(2,1)S(1)} %shard_map.75.refs_0_, bf16[280,128]{1,0:T(8,128)(2,1)S(1)} %collective-permute-done.11.refs_1_, ...), custom_call_target="tpu_custom_call" | custom-call | flops 1000000 | bytes 1000000 | tf_op jit(solution)/shard_map/pallas_call | solution.py:464
  (37 shorter events, 5.2 us)
Async XLA Ops:
  0.6 12.2 %copy-start.1 = (bf16[2,1,8,1024]{3,2,1,0:T(8,128)(2,1)S(1)}, bf16[2,1,8,1024]{3,2,1,0:T(8,128)(2,1)}, u32[]{:S(2)}) copy-start(bf16[2,1,8,1024]{3,2,1,0:T(8,128)(2,1)} %cot.1) | copy-start | bytes 98308
  0.6 12.2 %collective-permute-start.1 = (bf16[2,4,32,1024]{3,2,1,0:T(8,128)(2,1)}, bf16[2,4,32,1024]{3,2,1,0:T(8,128)(2,1)S(1)}, u32[]{:S(2)}, u32[]{:S(2)}) collective-permute-start(bf16[2,4,32,1024]{3,2,1,0:T(8,128)(2,1)} %cubes_in.1), channel_id=1, source_target_pairs={{1,2},{2,1},{3,4},{4,3},{5,6},{6,5},{9,10},{10,9},{11,12},{12,11},... | collective-permute-start | bytes 1572872 | tf_op jit(solution)/shard_map/ppermute | solution.py:479
  1.3 11.5 %collective-permute-start = (bf16[2,4,32,1024]{3,2,1,0:T(8,128)(2,1)}, bf16[2,4,32,1024]{3,2,1,0:T(8,128)(2,1)S(1)}, u32[]{:S(2)}, u32[]{:S(2)}) collective-permute-start(bf16[2,4,32,1024]{3,2,1,0:T(8,128)(2,1)} %cubes_in.1), channel_id=1, source_target_pairs={{0,1},{1,0},{2,3},{3,2},{4,5},{5,4},{6,7},{7,6},{8,9},{9,8},{10,11... | collective-permute-start | bytes 1572872 | tf_op jit(solution)/shard_map/ppermute | solution.py:479
  8.2 1.0 %copy-start = (bf16[2,4,32,1024]{3,2,1,0:T(8,128)(2,1)S(1)}, bf16[2,4,32,1024]{3,2,1,0:T(8,128)(2,1)}, u32[]{:S(2)}) copy-start(bf16[2,4,32,1024]{3,2,1,0:T(8,128)(2,1)} %cubes_in.1) | copy-start | bytes 1572868
  12.9 1.8 %copy-start.2 = (bf16[2,10,4,16,1152]{4,3,2,1,0:T(8,128)(2,1)S(1)}, bf16[2,10,4,16,1152]{4,3,2,1,0:T(8,128)(2,1)}, u32[]{:S(2)}) copy-start(bf16[2,10,4,16,1152]{4,3,2,1,0:T(8,128)(2,1)} %get-tuple-element.27.own) | copy-start | bytes 8847364
  14.7 1.4 %copy-start.5 = (bf16[2,6,2,16,2048]{4,3,2,1,0:T(8,128)(2,1)S(1)}, bf16[2,6,2,16,2048]{4,3,2,1,0:T(8,128)(2,1)}, u32[]{:S(2)}) copy-start(bf16[2,6,2,16,2048]{4,3,2,1,0:T(8,128)(2,1)} %get-tuple-element.28.own_slope) | copy-start | bytes 4718596
  16.1 1.3 %copy-start.8 = (bf16[2304,256]{1,0:T(8,128)(2,1)S(1)}, bf16[2304,256]{1,0:T(8,128)(2,1)}, u32[]{:S(2)}) copy-start(bf16[2304,256]{1,0:T(8,128)(2,1)} %get-tuple-element.30.ta) | copy-start | bytes 3538948
  17.4 1.3 %copy-start.9 = (bf16[2304,256]{1,0:T(8,128)(2,1)S(1)}, bf16[2304,256]{1,0:T(8,128)(2,1)}, u32[]{:S(2)}) copy-start(bf16[2304,256]{1,0:T(8,128)(2,1)} %get-tuple-element.31.tb) | copy-start | bytes 3538948
  25.7 1.6 %copy-start.3 = (bf16[2,10,4,16,1152]{4,3,2,1,0:T(8,128)(2,1)}, bf16[2,10,4,16,1152]{4,3,2,1,0:T(8,128)(2,1)S(1)}, u32[]{:S(2)}) copy-start(bf16[2,10,4,16,1152]{4,3,2,1,0:T(8,128)(2,1)S(1)} %get-tuple-element.37.xs) | copy-start | bytes 8847364
  27.3 1.2 %copy-start.6 = (bf16[2,6,2,16,2048]{4,3,2,1,0:T(8,128)(2,1)}, bf16[2,6,2,16,2048]{4,3,2,1,0:T(8,128)(2,1)S(1)}, u32[]{:S(2)}) copy-start(bf16[2,6,2,16,2048]{4,3,2,1,0:T(8,128)(2,1)S(1)} %get-tuple-element.36.dsl) | copy-start | bytes 4718596
  28.5 6.7 %copy-start.4 = (bf16[2,10,4,16,1152]{4,3,2,1,0:T(8,128)(2,1)S(1)}, bf16[2,10,4,16,1152]{4,3,2,1,0:T(8,128)(2,1)}, u32[]{:S(2)}) copy-start(bf16[2,10,4,16,1152]{4,3,2,1,0:T(8,128)(2,1)} %copy-done.3) | copy-start | bytes 8847364
  28.5 6.7 %collective-permute-start.3 = (bf16[2,2,16,2048]{3,2,1,0:T(8,128)(2,1)S(1)}, bf16[2,2,16,2048]{3,2,1,0:T(8,128)(2,1)S(1)}, u32[]{:S(2)}, u32[]{:S(2)}) collective-permute-start(bf16[2,2,16,2048]{3,2,1,0:T(8,128)(2,1)S(1)} %get-tuple-element.33.grad_b), channel_id=1, source_target_pairs={{1,2},{2,1},{3,4},{4,3},{5,6},{6,5},{9,10},{10,9},{11,12},{12,11},... | collective-permute-start | bytes 786440 | tf_op jit(solution)/shard_map/ppermute | solution.py:479
  29.5 5.7 %collective-permute-start.2 = (bf16[2,2,16,2048]{3,2,1,0:T(8,128)(2,1)S(1)}, bf16[2,2,16,2048]{3,2,1,0:T(8,128)(2,1)S(1)}, u32[]{:S(2)}, u32[]{:S(2)}) collective-permute-start(bf16[2,2,16,2048]{3,2,1,0:T(8,128)(2,1)S(1)} %get-tuple-element.33.grad_b), channel_id=1, source_target_pairs={{0,1},{1,0},{2,3},{3,2},{4,5},{5,4},{6,7},{7,6},{8,9},{9,8},{10,11... | collective-permute-start | bytes 786440 | tf_op jit(solution)/shard_map/ppermute | solution.py:479
  35.2 1.4 %copy-start.7 = (bf16[2,6,2,16,2048]{4,3,2,1,0:T(8,128)(2,1)S(1)}, bf16[2,6,2,16,2048]{4,3,2,1,0:T(8,128)(2,1)}, u32[]{:S(2)}) copy-start(bf16[2,6,2,16,2048]{4,3,2,1,0:T(8,128)(2,1)} %copy-done.6) | copy-start | bytes 4718596
  44.2 2.5 %collective-permute-start.4 = (bf16[4,280,128]{2,1,0:T(8,128)(2,1)S(1)}, bf16[4,280,128]{2,1,0:T(8,128)(2,1)S(1)}, u32[]{:S(2)}, u32[]{:S(2)}) collective-permute-start(bf16[4,280,128]{2,1,0:T(8,128)(2,1)S(1)} %get-tuple-element.44), channel_id=1, source_target_pairs={{0,1},{1,0},{2,3},{3,2},{4,5},{5,4},{6,7},{7,6},{8,9},{9,8},{10,11... | collective-permute-start | bytes 860168 | tf_op jit(solution)/shard_map/ppermute | solution.py:485
  47.3 5.9 %collective-permute-start.5 = (bf16[280,128]{1,0:T(8,128)(2,1)S(1)}, bf16[280,128]{1,0:T(8,128)(2,1)S(1)}, u32[]{:S(2)}, u32[]{:S(2)}) collective-permute-start(bf16[280,128]{1,0:T(8,128)(2,1)S(1)} %get-tuple-element.46), channel_id=1, source_target_pairs={{0,8},{8,0},{16,24},{24,16},{1,9},{9,1},{17,25},{25,17},{2,10},{10... | collective-permute-start | bytes 215048 | tf_op jit(solution)/shard_map/ppermute | solution.py:485
  48.9 4.3 %collective-permute-start.6 = (bf16[280,128]{1,0:T(8,128)(2,1)S(1)}, bf16[280,128]{1,0:T(8,128)(2,1)S(1)}, u32[]{:S(2)}, u32[]{:S(2)}) collective-permute-start(bf16[280,128]{1,0:T(8,128)(2,1)S(1)} %get-tuple-element.47), channel_id=1, source_target_pairs={{0,16},{8,24},{16,0},{24,8},{1,17},{9,25},{17,1},{25,9},{2,18},{10... | collective-permute-start | bytes 215048 | tf_op jit(solution)/shard_map/ppermute | solution.py:485
  50.4 5.2 %collective-permute-start.7 = (bf16[280,128]{1,0:T(8,128)(2,1)S(1)}, bf16[280,128]{1,0:T(8,128)(2,1)S(1)}, u32[]{:S(2)}, u32[]{:S(2)}) collective-permute-start(bf16[280,128]{1,0:T(8,128)(2,1)S(1)} %get-tuple-element.48), channel_id=1, source_target_pairs={{0,24},{8,16},{16,8},{24,0},{1,25},{9,17},{17,9},{25,1},{2,26},{10... | collective-permute-start | bytes 215048 | tf_op jit(solution)/shard_map/ppermute | solution.py:485
  55.7 7.5 %collective-permute-start.10 = (bf16[280,128]{1,0:T(8,128)(2,1)S(1)}, bf16[280,128]{1,0:T(8,128)(2,1)S(1)}, u32[]{:S(2)}, u32[]{:S(2)}) collective-permute-start(bf16[280,128]{1,0:T(8,128)(2,1)S(1)} %shard_map.74.refs_0_), channel_id=1, source_target_pairs={{0,6},{1,7},{2,4},{3,5},{4,2},{5,3},{6,0},{7,1},{8,14},{9,15},{10,... | collective-permute-start | bytes 215048 | tf_op jit(solution)/shard_map/ppermute | solution.py:485
  59.6 5.3 %collective-permute-start.9 = (bf16[280,128]{1,0:T(8,128)(2,1)S(1)}, bf16[280,128]{1,0:T(8,128)(2,1)S(1)}, u32[]{:S(2)}, u32[]{:S(2)}) collective-permute-start(bf16[280,128]{1,0:T(8,128)(2,1)S(1)} %shard_map.74.refs_0_), channel_id=1, source_target_pairs={{0,4},{1,5},{2,6},{3,7},{4,0},{5,1},{6,2},{7,3},{8,12},{9,13},{10,... | collective-permute-start | bytes 215048 | tf_op jit(solution)/shard_map/ppermute | solution.py:485
  59.6 5.3 %collective-permute-start.8 = (bf16[280,128]{1,0:T(8,128)(2,1)S(1)}, bf16[280,128]{1,0:T(8,128)(2,1)S(1)}, u32[]{:S(2)}, u32[]{:S(2)}) collective-permute-start(bf16[280,128]{1,0:T(8,128)(2,1)S(1)} %shard_map.74.refs_0_), channel_id=1, source_target_pairs={{0,2},{1,3},{2,0},{3,1},{4,6},{5,7},{6,4},{7,5},{8,10},{9,11},{10,... | collective-permute-start | bytes 215048 | tf_op jit(solution)/shard_map/ppermute | solution.py:485
  65.0 5.5 %collective-permute-start.17 = (bf16[280,128]{1,0:T(8,128)(2,1)S(1)}, bf16[280,128]{1,0:T(8,128)(2,1)S(1)}, u32[]{:S(2)}, u32[]{:S(2)}) collective-permute-start(bf16[280,128]{1,0:T(8,128)(2,1)S(1)} %shard_map.75.refs_0_), channel_id=1, source_target_pairs={{0,25},{1,24},{2,27},{3,26},{4,29},{5,28},{6,31},{7,30},{8,17},{9,... | collective-permute-start | bytes 215048 | tf_op jit(solution)/shard_map/ppermute | solution.py:569
  65.1 6.2 %collective-permute-start.16 = (bf16[280,128]{1,0:T(8,128)(2,1)S(1)}, bf16[280,128]{1,0:T(8,128)(2,1)S(1)}, u32[]{:S(2)}, u32[]{:S(2)}) collective-permute-start(bf16[280,128]{1,0:T(8,128)(2,1)S(1)} %shard_map.75.refs_0_), channel_id=1, source_target_pairs={{0,24},{1,25},{2,26},{3,27},{4,28},{5,29},{6,30},{7,31},{8,16},{9,... | collective-permute-start | bytes 215048 | tf_op jit(solution)/shard_map/ppermute | solution.py:569
  66.9 6.0 %collective-permute-start.15 = (bf16[280,128]{1,0:T(8,128)(2,1)S(1)}, bf16[280,128]{1,0:T(8,128)(2,1)S(1)}, u32[]{:S(2)}, u32[]{:S(2)}) collective-permute-start(bf16[280,128]{1,0:T(8,128)(2,1)S(1)} %shard_map.75.refs_0_), channel_id=1, source_target_pairs={{0,17},{1,16},{2,19},{3,18},{4,21},{5,20},{6,23},{7,22},{8,25},{9,... | collective-permute-start | bytes 215048 | tf_op jit(solution)/shard_map/ppermute | solution.py:569
  68.0 6.6 %collective-permute-start.14 = (bf16[280,128]{1,0:T(8,128)(2,1)S(1)}, bf16[280,128]{1,0:T(8,128)(2,1)S(1)}, u32[]{:S(2)}, u32[]{:S(2)}) collective-permute-start(bf16[280,128]{1,0:T(8,128)(2,1)S(1)} %shard_map.75.refs_0_), channel_id=1, source_target_pairs={{0,16},{1,17},{2,18},{3,19},{4,20},{5,21},{6,22},{7,23},{8,24},{9,... | collective-permute-start | bytes 215048 | tf_op jit(solution)/shard_map/ppermute | solution.py:569
  69.4 5.2 %collective-permute-start.13 = (bf16[280,128]{1,0:T(8,128)(2,1)S(1)}, bf16[280,128]{1,0:T(8,128)(2,1)S(1)}, u32[]{:S(2)}, u32[]{:S(2)}) collective-permute-start(bf16[280,128]{1,0:T(8,128)(2,1)S(1)} %shard_map.75.refs_0_), channel_id=1, source_target_pairs={{0,9},{1,8},{2,11},{3,10},{4,13},{5,12},{6,15},{7,14},{8,1},{9,0},... | collective-permute-start | bytes 215048 | tf_op jit(solution)/shard_map/ppermute | solution.py:569
  70.5 4.6 %collective-permute-start.12 = (bf16[280,128]{1,0:T(8,128)(2,1)S(1)}, bf16[280,128]{1,0:T(8,128)(2,1)S(1)}, u32[]{:S(2)}, u32[]{:S(2)}) collective-permute-start(bf16[280,128]{1,0:T(8,128)(2,1)S(1)} %shard_map.75.refs_0_), channel_id=1, source_target_pairs={{0,8},{1,9},{2,10},{3,11},{4,12},{5,13},{6,14},{7,15},{8,0},{9,1},... | collective-permute-start | bytes 215048 | tf_op jit(solution)/shard_map/ppermute | solution.py:569
  71.3 3.8 %collective-permute-start.11 = (bf16[280,128]{1,0:T(8,128)(2,1)S(1)}, bf16[280,128]{1,0:T(8,128)(2,1)S(1)}, u32[]{:S(2)}, u32[]{:S(2)}) collective-permute-start(bf16[280,128]{1,0:T(8,128)(2,1)S(1)} %shard_map.75.refs_0_), channel_id=1, source_target_pairs={{0,1},{1,0},{2,3},{3,2},{4,5},{5,4},{6,7},{7,6},{8,9},{9,8},{10,11... | collective-permute-start | bytes 215048 | tf_op jit(solution)/shard_map/ppermute | solution.py:569

commit v7 on v5

--- a/solution.py
+++ b/solution.py
@@ -96,7 +96,7 @@
             tat[768 * d + 64 * slot : 768 * d + 64 * slot + 64, 128 * half : 128 * half + 128] = value
 
 
-def prepare_kernel(cubes, wa, wb, xs, ta, tb, tbt, dsl, inner):
+def prepare_kernel(cubes, wa, wb, xs, ta, tb, dsl, inner):
     picker = row_picker(4, 2, 32)
     for b in range(cubes.shape[0]):
         for z in range(ZD):
@@ -111,16 +111,6 @@
         block = wb[d]
         for e in range(2):
             tb[256 * d : 256 * d + 256, 128 * e : 128 * e + 128] = rows_at(block, 64 * e, 256)
-        turned = []
-        for dx in (2, 1, 0):
-            part = block[64 * dx : 64 * dx + 64].astype(F32)
-            turned.append(jnp.concatenate([part, part], axis=0).T)
-        block = jnp.concatenate(turned, axis=0)
-        to = 768 * (8 - d)
-        for e in range(2):
-            tbt[to : to + 768, 128 * e : 128 * e + 128] = halves(
-                rows_at(block, 256 * e, 768), rows_at(block, 256 * e + 128, 768)
-            )
 
     cube_count = cubes.shape[0]
     pre = dot(
@@ -184,7 +174,7 @@
             pooled[:, 3, :, out] = ((part[:, 4] + part[:, 5]) * high).astype(BF)
         return carry
 
-    lax.fori_loop(0, 2, groups, 0)
+    lax.fori_loop(0, 2, groups, 0, unroll=True)
 
     shifter = row_picker(3, 1, 16)
     for b in range(cube_count):
@@ -230,7 +220,7 @@
         target[b, zz, v, :, 2176:] = jnp.zeros((16, 128), BF)
 
 
-def terms_b_kernel(pools, grad_b, wa, terms, gs, tat):
+def terms_b_kernel(pools, grad_b, wa, wb, terms, gs, tat, tbt):
     cube_count = grad_b.shape[0]
     shifter = row_picker(3, 1, 16)
     for b in range(cube_count):
@@ -240,6 +230,17 @@
         block = wa[d].astype(F32)
         block = jnp.concatenate([block, block], axis=1)
         mirror(8 - d, rows_at(block, 0, 128).T[:64], tat)
+        block = wb[d]
+        turned = []
+        for dx in (2, 1, 0):
+            part = block[64 * dx : 64 * dx + 64].astype(F32)
+            turned.append(jnp.concatenate([part, part], axis=0).T)
+        block = jnp.concatenate(turned, axis=0)
+        to = 768 * (8 - d)
+        for e in range(2):
+            tbt[to : to + 768, 128 * e : 128 * e + 128] = halves(
+                rows_at(block, 256 * e, 768), rows_at(block, 256 * e + 128, 768)
+            )
     rows_b = cube_count * 2 * 16
     grads = jnp.concatenate(
         [grad_b[:, :, :, 256 * g : 256 * g + 256].reshape(rows_b, 256) for g in range(8)], axis=0
@@ -365,7 +366,7 @@
         return carry
 
     acc[...] = jnp.zeros_like(acc)
-    lax.fori_loop(0, 4, groups, 0)
+    lax.fori_loop(0, 4, groups, 0, unroll=True)
 
     terms[pl.ds(27, C1 // 2, stride=28), :] = jnp.zeros((C1 // 2, 128), F32)
     mask = lanes_below((32, 128), 64)
@@ -482,14 +483,14 @@
     recv_a, recv_b = swap(cubes, cubes, ring)
 
     wa = weight_a.reshape(9, 96, C2)
-    own_xs, ta, tb, tbt, own_slope, inner = call(
+    wb = weight_b.reshape(9, 192, C3)
+    own_xs, ta, tb, own_slope, inner = call(
         prepare_kernel,
-        [cubes, wa, weight_b.reshape(9, 192, C3)],
+        [cubes, wa, wb],
         [
             ((cube_count, ZD + 2 * HALO, 4, 16, 1152), BF),
             ((2304, 256), BF),
             ((2304, 256), BF),
-            ((6912, 256), BF),
             ((cube_count, 6, 2, 16, 2048), BF),
             ((cube_count, 2, 16, 1024), F32),
         ],
@@ -512,8 +513,9 @@
     )
     back_a, back_b = swap(grad_b, grad_b, ring)
     spread = ((cube_count, 6, 3, 16, 2304), BF)
-    terms_b, own_gs, tat = call(
-        terms_b_kernel, [pools, grad_b, wa], [((ROWS_B, 128), F32), spread, ((6912, 256), BF)], [], 1_000_000_000
+    wide = ((6912, 256), BF)
+    terms_b, own_gs, tat, tbt = call(
+        terms_b_kernel, [pools, grad_b, wa, wb], [((ROWS_B, 128), F32), spread, wide, wide], [], 1_000_000_000
     )
     piece = (ROWS_A + ROWS_B) // (2 * samples)
     pieces = ((samples, piece, 128), BF)

time: 65.6 us -> 68.4 us (1.043)
  Pallas kernels: 27.2 us -> 30.5 us
    pallas_call x11, Pallas kernels: 27.2 us -> 30.5 us  [call(): pl.pallas_call(kernel, out_shape=[jax.ShapeDtypeStruct(shape, dtype) for...]
  transfers between devices with their start and end apart: 15 -> 15, of which waited for: 7 -> 8; matrix products, arithmetic and copies ran while one was open for 4% -> 4% of each run, Pallas kernels for 15% -> 15%
where the time goes in v7:
time: 68.4 us; the launch traced here: 68.1 us
  Pallas kernels  30.5 us (45%)
  starting transfers between devices  23.4 us (34%)
  waiting for transfers between devices  9.86 us (14%)
  local copies, waits for them, and re-layouts  3.49 us (5%)
  between operations  0.79 us (1%)
    pallas_call x11, Pallas kernels, call(): pl.pallas_call(kernel, out_shape=[jax.ShapeDtypeStruct(shape, dtype) for...  30.5 us
    ppermute x11, starting transfers between devices, swap_along(): lax.ppermute(part, axis, [(i, i ^ k * step) for i in range(count)])  13.2 us
    ppermute x11, waiting for transfers between devices, swap_along(): lax.ppermute(part, axis, [(i, i ^ k * step) for i in range(count)])  9.85 us
    ppermute x2, starting transfers between devices, swap(): lax.ppermute(first, 'gz', pairs_a)  8.68 us
    ppermute x2, starting transfers between devices, swap(): lax.ppermute(second, 'gz', pairs_b)  1.55 us
  transfers between devices with their start and end apart: 15, of which 8 were waited for; matrix products, arithmetic and copies ran while one was open for 4% of the time, Pallas kernels for 15%

profile of v7, /device:TPU:0, one launch (start us, length us, event | category | flops | bytes accessed | tf_op | source)
XLA Modules:
  0.0 68.1 jit_solution(15193661213376767974)
XLA Ops:
  0.6 0.7 %collective-permute-start.1 = (bf16[2,4,32,1024]{3,2,1,0:T(8,128)(2,1)}, bf16[2,4,32,1024]{3,2,1,0:T(8,128)(2,1)S(1)}, u32[]{:S(2)}, u32[]{:S(2)}) collective-permute-start(bf16[2,4,32,1024]{3,2,1,0:T(8,128)(2,1)} %cubes.1), channel_id=1, source_target_pairs={{1,2},{2,1},{3,4},{4,3},{5,6},{6,5},{9,10},{10,9},{11,12},{12,11},... | collective-permute-start | bytes 1572872 | tf_op jit(solution)/shard_map/ppermute | solution.py:468
  1.3 4.4 %collective-permute-start = (bf16[2,4,32,1024]{3,2,1,0:T(8,128)(2,1)}, bf16[2,4,32,1024]{3,2,1,0:T(8,128)(2,1)S(1)}, u32[]{:S(2)}, u32[]{:S(2)}) collective-permute-start(bf16[2,4,32,1024]{3,2,1,0:T(8,128)(2,1)} %cubes.1), channel_id=1, source_target_pairs={{0,1},{1,0},{2,3},{3,2},{4,5},{5,4},{6,7},{7,6},{8,9},{9,8},{10,11... | collective-permute-start | bytes 1572872 | tf_op jit(solution)/shard_map/ppermute | solution.py:468
  5.8 1.1 %reshape.12.wa = bf16[9,96,64]{2,1,0:T(8,128)(2,1)S(1)} reshape(bf16[27,2048]{1,0:T(8,128)(2,1)} %param.5) | data formatting | bytes 221184 | tf_op jit(solution)/shard_map/reshape | solution.py:485
  6.9 1.3 %reshape.13.wb = bf16[9,192,128]{2,1,0:T(8,128)(2,1)S(1)} reshape(bf16[27,8192]{1,0:T(8,128)(2,1)} %param.6) | data formatting | bytes 884736 | tf_op jit(solution)/shard_map/reshape | solution.py:486
  8.2 1.0 %copy-done = bf16[2,4,32,1024]{3,2,1,0:T(8,128)(2,1)S(1)} copy-done((bf16[2,4,32,1024]{3,2,1,0:T(8,128)(2,1)S(1)}, bf16[2,4,32,1024]{3,2,1,0:T(8,128)(2,1)}, u32[]{:S(2)}) %copy-start) | copy-done | bytes 524312
  9.3 2.1 %shard_map.67 = (bf16[2,10,4,16,1152]{4,3,2,1,0:T(8,128)(2,1)S(1)}, bf16[2304,256]{1,0:T(8,128)(2,1)S(1)}, bf16[2304,256]{1,0:T(8,128)(2,1)S(1)}, bf16[2,6,2,16,...) custom-call(bf16[2,4,32,1024]{3,2,1,0:T(8,128)(2,1)S(1)} %copy-done, bf16[9,96,64]{2,1,0:T(8,128)(2,1)S(1)} %reshape.12.wa, ...), custom_call_target="tpu_custom_call" | custom-call | flops 1000000000 | bytes 1000000 | tf_op jit(solution)/shard_map/pallas_call | solution.py:453
  11.5 7.8 %shard_map.68 = (bf16[2,10,4,16,1152]{4,3,2,1,0:T(8,128)(2,1)S(1)}, bf16[2,6,2,16,2048]{4,3,2,1,0:T(8,128)(2,1)S(1)}, bf16[2,4,3,16,1152]{4,3,2,1,0:T(8,128)(2,1)S(1)}, bf16[2,2,16,2048]{3,2,1,0:T(8,128)(2,1)S(1)}) custom-call(s32[3]{0:T(128)S(1)} %pad_add_fusion.where, ...), custom_call_target="tpu_custom_call", output_to_operand_aliasing={{0}: (1, {}), {1}: (2, {})} | custom-call | flops 8000000000 | bytes 1000000 | tf_op jit(solution)/shard_map/pallas_call | solution.py:453
  19.3 0.9 %collective-permute-start.3 = (bf16[2,2,16,2048]{3,2,1,0:T(8,128)(2,1)S(1)}, bf16[2,2,16,2048]{3,2,1,0:T(8,128)(2,1)S(1)}, u32[]{:S(2)}, u32[]{:S(2)}) collective-permute-start(bf16[2,2,16,2048]{3,2,1,0:T(8,128)(2,1)S(1)} %get-tuple-element.33.grad_b), channel_id=1, source_target_pairs={{1,2},{2,1},{3,4},{4,3},{5,6},{6,5},{9,10},{10,9},{11,12},{12,11},... | collective-permute-start | bytes 786440 | tf_op jit(solution)/shard_map/ppermute | solution.py:468
  20.2 4.3 %collective-permute-start.2 = (bf16[2,2,16,2048]{3,2,1,0:T(8,128)(2,1)S(1)}, bf16[2,2,16,2048]{3,2,1,0:T(8,128)(2,1)S(1)}, u32[]{:S(2)}, u32[]{:S(2)}) collective-permute-start(bf16[2,2,16,2048]{3,2,1,0:T(8,128)(2,1)S(1)} %get-tuple-element.33.grad_b), channel_id=1, source_target_pairs={{0,1},{1,0},{2,3},{3,2},{4,5},{5,4},{6,7},{7,6},{8,9},{9,8},{10,11... | collective-permute-start | bytes 786440 | tf_op jit(solution)/shard_map/ppermute | solution.py:468
  24.5 2.5 %shard_map.69 = (f32[1792,128]{1,0:T(8,128)S(1)}, bf16[2,6,3,16,2304]{4,3,2,1,0:T(8,128)(2,1)S(1)}, bf16[6912,256]{1,0:T(8,128)(2,1)S(1)}, bf16[6912,256]{1,0:T(8,128)(2,1)S(1)}) custom-call(bf16[2,4,3,16,1152]{4,3,2,1,0:T(8,128)(2,1)S(1)} %get-tuple-element.32.pools, bf16[2,2,16,2048]{3,2,1,0:T(8,128)(2,1)S(1)} %get-tuple-element.33.grad_b, ...), custom_call_target="tpu_custom_call" | custom-call | flops 1000000000 | bytes 1000000 | tf_op jit(solution)/shard_map/pallas_call | solution.py:453
  27.0 9.7 %shard_map.70 = (bf16[2,6,4,16,2304]{4,3,2,1,0:T(8,128)(2,1)S(1)}, bf16[4,280,128]{2,1,0:T(8,128)(2,1)S(1)}, bf16[4,280,128]{2,1,0:T(8,128)(2,1)S(1)}, bf16[2,6,3,16,2304]{4,3,2,1,0:T(8,128)(2,1)S(1)}) custom-call(s32[3]{0:T(128)S(1)} %pad_add_fusion.where, bf16[2,6,3,16,2304]{4,3,2,1,0:T(8,128)(2,1)S(1)} %get-tuple-element.34.own, ...), custom_call_target="tpu_custom_call", output_to_operand_aliasing={{3}: (1, {})} | custom-call | flops 6000000000 | bytes 1000000 | tf_op jit(solution)/shard_map/pallas_call | solution.py:453
  36.8 1.3 %collective-permute-start.4 = (bf16[4,280,128]{2,1,0:T(8,128)(2,1)S(1)}, bf16[4,280,128]{2,1,0:T(8,128)(2,1)S(1)}, u32[]{:S(2)}, u32[]{:S(2)}) collective-permute-start(bf16[4,280,128]{2,1,0:T(8,128)(2,1)S(1)} %get-tuple-element.44), channel_id=1, source_target_pairs={{0,1},{1,0},{2,3},{3,2},{4,5},{5,4},{6,7},{7,6},{8,9},{9,8},{10,11... | collective-permute-start | bytes 860168 | tf_op jit(solution)/shard_map/ppermute | solution.py:474
  38.1 1.2 %collective-permute-done.4.recv = bf16[4,280,128]{2,1,0:T(8,128)(2,1)S(1)} collective-permute-done((bf16[4,280,128]{2,1,0:T(8,128)(2,1)S(1)}, bf16[4,280,128]{2,1,0:T(8,128)(2,1)S(1)}, u32[]{:S(2)}, u32[]{:S(2)}) %collective-permute-start.4) | collective-permute-done | bytes 286752 | tf_op jit(solution)/shard_map/ppermute | solution.py:474
  39.3 0.6 shard_map.73
  39.9 1.6 %collective-permute-start.5 = (bf16[280,128]{1,0:T(8,128)(2,1)S(1)}, bf16[280,128]{1,0:T(8,128)(2,1)S(1)}, u32[]{:S(2)}, u32[]{:S(2)}) collective-permute-start(bf16[280,128]{1,0:T(8,128)(2,1)S(1)} %get-tuple-element.46), channel_id=1, source_target_pairs={{0,8},{8,0},{16,24},{24,16},{1,9},{9,1},{17,25},{25,17},{2,10},{10... | collective-permute-start | bytes 215048 | tf_op jit(solution)/shard_map/ppermute | solution.py:474
  41.5 1.5 %collective-permute-start.6 = (bf16[280,128]{1,0:T(8,128)(2,1)S(1)}, bf16[280,128]{1,0:T(8,128)(2,1)S(1)}, u32[]{:S(2)}, u32[]{:S(2)}) collective-permute-start(bf16[280,128]{1,0:T(8,128)(2,1)S(1)} %get-tuple-element.47), channel_id=1, source_target_pairs={{0,16},{8,24},{16,0},{24,8},{1,17},{9,25},{17,1},{25,9},{2,18},{10... | collective-permute-start | bytes 215048 | tf_op jit(solution)/shard_map/ppermute | solution.py:474
  43.0 0.5 collective-permute-start.7
  43.4 2.3 %shard_map.71.rest_0_.after = bf16[4,32,1024]{2,1,0:T(8,128)(2,1)S(1)} custom-call(bf16[2,6,4,16,2304]{4,3,2,1,0:T(8,128)(2,1)S(1)} %get-tuple-element.39.ga, bf16[6912,256]{1,0:T(8,128)(2,1)S(1)} %get-tuple-element.40.tat), custom_call_target="tpu_custom_call" | custom-call | flops 2000000000 | bytes 1000000 | tf_op jit(solution)/shard_map/pallas_call | solution.py:453
  45.8 2.4 %collective-permute-done.7.refs_3_ = bf16[280,128]{1,0:T(8,128)(2,1)S(1)} collective-permute-done((bf16[280,128]{1,0:T(8,128)(2,1)S(1)}, bf16[280,128]{1,0:T(8,128)(2,1)S(1)}, u32[]{:S(2)}, u32[]{:S(2)}) %collective-permute-start.7) | collective-permute-done | bytes 71712 | tf_op jit(solution)/shard_map/ppermute | solution.py:474
  48.2 4.1 %collective-permute-start.10 = (bf16[280,128]{1,0:T(8,128)(2,1)S(1)}, bf16[280,128]{1,0:T(8,128)(2,1)S(1)}, u32[]{:S(2)}, u32[]{:S(2)}) collective-permute-start(bf16[280,128]{1,0:T(8,128)(2,1)S(1)} %shard_map.74.refs_0_), channel_id=1, source_target_pairs={{0,6},{1,7},{2,4},{3,5},{4,2},{5,3},{6,0},{7,1},{8,14},{9,15},{10,... | collective-permute-start | bytes 215048 | tf_op jit(solution)/shard_map/ppermute | solution.py:474
  52.3 0.6 collective-permute-start.8
  53.0 3.0 %shard_map.72 = (bf16[2,4,32,1024]{3,2,1,0:T(8,128)(2,1)}, f32[8,128]{1,0:T(8,128)S(1)}) custom-call(bf16[2,6,4,16,2304]{4,3,2,1,0:T(8,128)(2,1)S(1)} %get-tuple-element.39.ga, bf16[6912,256]{1,0:T(8,128)(2,1)S(1)} %get-tuple-element.40.tat, bf16[4,32,1024]{2,1,0:T(8,128)(2,1)S(1)} %shard_map.71.rest_0_.after), custom_call_target="tpu_custom_call" | custom-call | flops 2000000000 | bytes 1000000 | tf_op jit(solution)/shard_map/pallas_call | solution.py:453
  55.9 1.6 %collective-permute-done.9.refs_2_ = bf16[280,128]{1,0:T(8,128)(2,1)S(1)} collective-permute-done((bf16[280,128]{1,0:T(8,128)(2,1)S(1)}, bf16[280,128]{1,0:T(8,128)(2,1)S(1)}, u32[]{:S(2)}, u32[]{:S(2)}) %collective-permute-start.9) | collective-permute-done | bytes 71712 | tf_op jit(solution)/shard_map/ppermute | solution.py:474
  57.6 0.9 %collective-permute-start.13 = (bf16[280,128]{1,0:T(8,128)(2,1)S(1)}, bf16[280,128]{1,0:T(8,128)(2,1)S(1)}, u32[]{:S(2)}, u32[]{:S(2)}) collective-permute-start(bf16[280,128]{1,0:T(8,128)(2,1)S(1)} %shard_map.75.refs_0_), channel_id=1, source_target_pairs={{0,24},{8,16},{16,8},{24,0},{1,25},{9,17},{17,9},{25,1},{2,26},{10... | collective-permute-start | bytes 215048 | tf_op jit(solution)/shard_map/ppermute | solution.py:474
  58.5 1.3 %collective-permute-start.12 = (bf16[280,128]{1,0:T(8,128)(2,1)S(1)}, bf16[280,128]{1,0:T(8,128)(2,1)S(1)}, u32[]{:S(2)}, u32[]{:S(2)}) collective-permute-start(bf16[280,128]{1,0:T(8,128)(2,1)S(1)} %shard_map.75.refs_0_), channel_id=1, source_target_pairs={{0,16},{8,24},{16,0},{24,8},{1,17},{9,25},{17,1},{25,9},{2,18},{10... | collective-permute-start | bytes 215048 | tf_op jit(solution)/shard_map/ppermute | solution.py:474
  59.8 1.3 %collective-permute-start.11 = (bf16[280,128]{1,0:T(8,128)(2,1)S(1)}, bf16[280,128]{1,0:T(8,128)(2,1)S(1)}, u32[]{:S(2)}, u32[]{:S(2)}) collective-permute-start(bf16[280,128]{1,0:T(8,128)(2,1)S(1)} %shard_map.75.refs_0_), channel_id=1, source_target_pairs={{0,8},{8,0},{16,24},{24,16},{1,9},{9,1},{17,25},{25,17},{2,10},{10... | collective-permute-start | bytes 215048 | tf_op jit(solution)/shard_map/ppermute | solution.py:474
  61.2 1.8 %collective-permute-done.13.refs_3_ = bf16[280,128]{1,0:T(8,128)(2,1)S(1)} collective-permute-done((bf16[280,128]{1,0:T(8,128)(2,1)S(1)}, bf16[280,128]{1,0:T(8,128)(2,1)S(1)}, u32[]{:S(2)}, u32[]{:S(2)}) %collective-permute-start.13) | collective-permute-done | bytes 71712 | tf_op jit(solution)/shard_map/ppermute | solution.py:474
  63.0 0.6 collective-permute-done.12.refs_2_
  63.6 0.5 collective-permute-done.11.refs_1_
  64.2 0.6 shard_map.76.own
  64.8 1.6 %collective-permute-done.14.other = bf16[4,280,128]{2,1,0:T(8,128)(2,1)S(1)} collective-permute-done((bf16[4,280,128]{2,1,0:T(8,128)(2,1)S(1)}, bf16[4,280,128]{2,1,0:T(8,128)(2,1)S(1)}, u32[]{:S(2)}, u32[]{:S(2)}) %collective-permute-start.14) | collective-permute-done | bytes 286752 | tf_op jit(solution)/shard_map/ppermute | solution.py:474
  66.4 1.7 %shard_map.77 = (f32[27,2048]{1,0:T(8,128)}, f32[27,8192]{1,0:T(8,128)}) custom-call(s32[3]{0:T(128)S(1)} %pad_add_fusion.where, f32[1]{0:T(128)} %constant.11.clone.1.scale, bf16[4,280,128]{2,1,0:T(8,128)(2,1)S(1)} %shard_map.76.own, bf16[4,280,128]{2,1,0:T(8,128)(2,1)S(1)} %collective-permute-done.14.other), custom_call_target="tpu_custom_call" | custom-call | flops 1000000 | bytes 1000000 | tf_op jit(solution)/shard_map/pallas_call | solution.py:453
  (16 shorter events, 0.3 us)
Async XLA Ops:
  0.6 10.9 %copy-start.1 = (bf16[2,1,8,1024]{3,2,1,0:T(8,128)(2,1)S(1)}, bf16[2,1,8,1024]{3,2,1,0:T(8,128)(2,1)}, u32[]{:S(2)}) copy-start(bf16[2,1,8,1024]{3,2,1,0:T(8,128)(2,1)} %cot.1) | copy-start | bytes 98308
  0.6 10.9 %collective-permute-start.1 = (bf16[2,4,32,1024]{3,2,1,0:T(8,128)(2,1)}, bf16[2,4,32,1024]{3,2,1,0:T(8,128)(2,1)S(1)}, u32[]{:S(2)}, u32[]{:S(2)}) collective-permute-start(bf16[2,4,32,1024]{3,2,1,0:T(8,128)(2,1)} %cubes.1), channel_id=1, source_target_pairs={{1,2},{2,1},{3,4},{4,3},{5,6},{6,5},{9,10},{10,9},{11,12},{12,11},... | collective-permute-start | bytes 1572872 | tf_op jit(solution)/shard_map/ppermute | solution.py:468
  1.3 10.2 %collective-permute-start = (bf16[2,4,32,1024]{3,2,1,0:T(8,128)(2,1)}, bf16[2,4,32,1024]{3,2,1,0:T(8,128)(2,1)S(1)}, u32[]{:S(2)}, u32[]{:S(2)}) collective-permute-start(bf16[2,4,32,1024]{3,2,1,0:T(8,128)(2,1)} %cubes.1), channel_id=1, source_target_pairs={{0,1},{1,0},{2,3},{3,2},{4,5},{5,4},{6,7},{7,6},{8,9},{9,8},{10,11... | collective-permute-start | bytes 1572872 | tf_op jit(solution)/shard_map/ppermute | solution.py:468
  8.2 1.0 %copy-start = (bf16[2,4,32,1024]{3,2,1,0:T(8,128)(2,1)S(1)}, bf16[2,4,32,1024]{3,2,1,0:T(8,128)(2,1)}, u32[]{:S(2)}) copy-start(bf16[2,4,32,1024]{3,2,1,0:T(8,128)(2,1)} %cubes.1) | copy-start | bytes 1572868
  19.3 7.7 %collective-permute-start.3 = (bf16[2,2,16,2048]{3,2,1,0:T(8,128)(2,1)S(1)}, bf16[2,2,16,2048]{3,2,1,0:T(8,128)(2,1)S(1)}, u32[]{:S(2)}, u32[]{:S(2)}) collective-permute-start(bf16[2,2,16,2048]{3,2,1,0:T(8,128)(2,1)S(1)} %get-tuple-element.33.grad_b), channel_id=1, source_target_pairs={{1,2},{2,1},{3,4},{4,3},{5,6},{6,5},{9,10},{10,9},{11,12},{12,11},... | collective-permute-start | bytes 786440 | tf_op jit(solution)/shard_map/ppermute | solution.py:468
  20.2 6.8 %collective-permute-start.2 = (bf16[2,2,16,2048]{3,2,1,0:T(8,128)(2,1)S(1)}, bf16[2,2,16,2048]{3,2,1,0:T(8,128)(2,1)S(1)}, u32[]{:S(2)}, u32[]{:S(2)}) collective-permute-start(bf16[2,2,16,2048]{3,2,1,0:T(8,128)(2,1)S(1)} %get-tuple-element.33.grad_b), channel_id=1, source_target_pairs={{0,1},{1,0},{2,3},{3,2},{4,5},{5,4},{6,7},{7,6},{8,9},{9,8},{10,11... | collective-permute-start | bytes 786440 | tf_op jit(solution)/shard_map/ppermute | solution.py:468
  36.8 2.5 %collective-permute-start.4 = (bf16[4,280,128]{2,1,0:T(8,128)(2,1)S(1)}, bf16[4,280,128]{2,1,0:T(8,128)(2,1)S(1)}, u32[]{:S(2)}, u32[]{:S(2)}) collective-permute-start(bf16[4,280,128]{2,1,0:T(8,128)(2,1)S(1)} %get-tuple-element.44), channel_id=1, source_target_pairs={{0,1},{1,0},{2,3},{3,2},{4,5},{5,4},{6,7},{7,6},{8,9},{9,8},{10,11... | collective-permute-start | bytes 860168 | tf_op jit(solution)/shard_map/ppermute | solution.py:474
  39.9 5.9 %collective-permute-start.5 = (bf16[280,128]{1,0:T(8,128)(2,1)S(1)}, bf16[280,128]{1,0:T(8,128)(2,1)S(1)}, u32[]{:S(2)}, u32[]{:S(2)}) collective-permute-start(bf16[280,128]{1,0:T(8,128)(2,1)S(1)} %get-tuple-element.46), channel_id=1, source_target_pairs={{0,8},{8,0},{16,24},{24,16},{1,9},{9,1},{17,25},{25,17},{2,10},{10... | collective-permute-start | bytes 215048 | tf_op jit(solution)/shard_map/ppermute | solution.py:474
  41.5 4.3 %collective-permute-start.6 = (bf16[280,128]{1,0:T(8,128)(2,1)S(1)}, bf16[280,128]{1,0:T(8,128)(2,1)S(1)}, u32[]{:S(2)}, u32[]{:S(2)}) collective-permute-start(bf16[280,128]{1,0:T(8,128)(2,1)S(1)} %get-tuple-element.47), channel_id=1, source_target_pairs={{0,16},{8,24},{16,0},{24,8},{1,17},{9,25},{17,1},{25,9},{2,18},{10... | collective-permute-start | bytes 215048 | tf_op jit(solution)/shard_map/ppermute | solution.py:474
  43.0 5.2 %collective-permute-start.7 = (bf16[280,128]{1,0:T(8,128)(2,1)S(1)}, bf16[280,128]{1,0:T(8,128)(2,1)S(1)}, u32[]{:S(2)}, u32[]{:S(2)}) collective-permute-start(bf16[280,128]{1,0:T(8,128)(2,1)S(1)} %get-tuple-element.48), channel_id=1, source_target_pairs={{0,24},{8,16},{16,8},{24,0},{1,25},{9,17},{17,9},{25,1},{2,26},{10... | collective-permute-start | bytes 215048 | tf_op jit(solution)/shard_map/ppermute | solution.py:474
  48.2 7.7 %collective-permute-start.10 = (bf16[280,128]{1,0:T(8,128)(2,1)S(1)}, bf16[280,128]{1,0:T(8,128)(2,1)S(1)}, u32[]{:S(2)}, u32[]{:S(2)}) collective-permute-start(bf16[280,128]{1,0:T(8,128)(2,1)S(1)} %shard_map.74.refs_0_), channel_id=1, source_target_pairs={{0,6},{1,7},{2,4},{3,5},{4,2},{5,3},{6,0},{7,1},{8,14},{9,15},{10,... | collective-permute-start | bytes 215048 | tf_op jit(solution)/shard_map/ppermute | solution.py:474
  52.3 5.2 %collective-permute-start.9 = (bf16[280,128]{1,0:T(8,128)(2,1)S(1)}, bf16[280,128]{1,0:T(8,128)(2,1)S(1)}, u32[]{:S(2)}, u32[]{:S(2)}) collective-permute-start(bf16[280,128]{1,0:T(8,128)(2,1)S(1)} %shard_map.74.refs_0_), channel_id=1, source_target_pairs={{0,4},{1,5},{2,6},{3,7},{4,0},{5,1},{6,2},{7,3},{8,12},{9,13},{10,... | collective-permute-start | bytes 215048 | tf_op jit(solution)/shard_map/ppermute | solution.py:474
  52.3 5.2 %collective-permute-start.8 = (bf16[280,128]{1,0:T(8,128)(2,1)S(1)}, bf16[280,128]{1,0:T(8,128)(2,1)S(1)}, u32[]{:S(2)}, u32[]{:S(2)}) collective-permute-start(bf16[280,128]{1,0:T(8,128)(2,1)S(1)} %shard_map.74.refs_0_), channel_id=1, source_target_pairs={{0,2},{1,3},{2,0},{3,1},{4,6},{5,7},{6,4},{7,5},{8,10},{9,11},{10,... | collective-permute-start | bytes 215048 | tf_op jit(solution)/shard_map/ppermute | solution.py:474
  57.6 5.4 %collective-permute-start.13 = (bf16[280,128]{1,0:T(8,128)(2,1)S(1)}, bf16[280,128]{1,0:T(8,128)(2,1)S(1)}, u32[]{:S(2)}, u32[]{:S(2)}) collective-permute-start(bf16[280,128]{1,0:T(8,128)(2,1)S(1)} %shard_map.75.refs_0_), channel_id=1, source_target_pairs={{0,24},{8,16},{16,8},{24,0},{1,25},{9,17},{17,9},{25,1},{2,26},{10... | collective-permute-start | bytes 215048 | tf_op jit(solution)/shard_map/ppermute | solution.py:474
  58.5 5.1 %collective-permute-start.12 = (bf16[280,128]{1,0:T(8,128)(2,1)S(1)}, bf16[280,128]{1,0:T(8,128)(2,1)S(1)}, u32[]{:S(2)}, u32[]{:S(2)}) collective-permute-start(bf16[280,128]{1,0:T(8,128)(2,1)S(1)} %shard_map.75.refs_0_), channel_id=1, source_target_pairs={{0,16},{8,24},{16,0},{24,8},{1,17},{9,25},{17,1},{25,9},{2,18},{10... | collective-permute-start | bytes 215048 | tf_op jit(solution)/shard_map/ppermute | solution.py:474
  59.8 4.3 %collective-permute-start.11 = (bf16[280,128]{1,0:T(8,128)(2,1)S(1)}, bf16[280,128]{1,0:T(8,128)(2,1)S(1)}, u32[]{:S(2)}, u32[]{:S(2)}) collective-permute-start(bf16[280,128]{1,0:T(8,128)(2,1)S(1)} %shard_map.75.refs_0_), channel_id=1, source_target_pairs={{0,8},{8,0},{16,24},{24,16},{1,9},{9,1},{17,25},{25,17},{2,10},{10... | collective-permute-start | bytes 215048 | tf_op jit(solution)/shard_map/ppermute | solution.py:474
  64.7 1.6 %collective-permute-start.14 = (bf16[4,280,128]{2,1,0:T(8,128)(2,1)S(1)}, bf16[4,280,128]{2,1,0:T(8,128)(2,1)S(1)}, u32[]{:S(2)}, u32[]{:S(2)}) collective-permute-start(bf16[4,280,128]{2,1,0:T(8,128)(2,1)S(1)} %shard_map.76.own), channel_id=1, source_target_pairs={{0,1},{1,0},{2,3},{3,2},{4,5},{5,4},{6,7},{7,6},{8,9},{9,8},{10,11... | collective-permute-start | bytes 860168 | tf_op jit(solution)/shard_map/ppermute | solution.py:474

commit v8 on v7

--- a/solution.py
+++ b/solution.py
@@ -58,6 +58,18 @@
     return jnp.where(lanes_below(left.shape, 64), left, right).astype(BF)
 
 
+def loop(count, body):
+    def step(i, carry):
+        body(i)
+        return carry
+
+    lax.fori_loop(0, count, step, 0)
+
+
+def aligned(start, size):
+    return pl.ds(start if isinstance(start, int) else pl.multiple_of(start, size), size)
+
+
 def silu(pre):
     squash = sigmoid(pre)
     act = pre * squash
@@ -93,26 +105,31 @@
             start = 32 * (rank - 1 - 4 * half)
             keep = (lane >= start) & (lane < start + 96)
             value = jnp.where(keep, turned[(rank - 1) % 4], 0.0).astype(BF)
-            tat[768 * d + 64 * slot : 768 * d + 64 * slot + 64, 128 * half : 128 * half + 128] = value
+            tat[aligned(768 * d + 64 * slot, 64), 128 * half : 128 * half + 128] = value
 
 
 def prepare_kernel(cubes, wa, wb, xs, ta, tb, dsl, inner):
+    cube_count = cubes.shape[0]
     picker = row_picker(4, 2, 32)
-    for b in range(cubes.shape[0]):
-        for z in range(ZD):
-            spread_input(xs, b, HALO + z, cubes[b, z], picker)
-    for d in range(9):
+
+    def plane(i):
+        spread_input(xs, i // ZD, HALO + i % ZD, cubes[i // ZD, i % ZD], picker)
+
+    def weights(d):
+        rows = aligned(256 * d, 256)
         block = wa[d].astype(F32)
         block = jnp.concatenate([block, block], axis=1)
         for px in range(2):
-            ta[256 * d : 256 * d + 256, 128 * px : 128 * px + 128] = halves(
+            ta[rows, 128 * px : 128 * px + 128] = halves(
                 rows_at(block, 32 * px, 256), rows_at(block, 64 + 32 * px, 256)
             )
         block = wb[d]
         for e in range(2):
-            tb[256 * d : 256 * d + 256, 128 * e : 128 * e + 128] = rows_at(block, 64 * e, 256)
-
-    cube_count = cubes.shape[0]
+            tb[rows, 128 * e : 128 * e + 128] = rows_at(block, 64 * e, 256)
+
+    loop(cube_count * ZD, plane)
+    loop(9, weights)
+
     pre = dot(
         jnp.concatenate(
             [windows_a(xs, ((HALO, 2),), p, 128 * g) for g in range(8) for p in range(2)], axis=0
@@ -134,13 +151,16 @@
     cube_count = xs.shape[0]
     even = where[0] % 2 == 0
     picker = row_picker(4, 2, 32)
-    for b in range(cube_count):
-        for z in range(HALO):
-            far = ZD - HALO + z
-            below = jnp.where(even, recv_b[b, far].astype(F32), recv_a[b, far].astype(F32)).astype(BF)
-            above = jnp.where(even, recv_a[b, z].astype(F32), recv_b[b, z].astype(F32)).astype(BF)
-            spread_input(xs, b, z, below, picker)
-            spread_input(xs, b, HALO + ZD + z, above, picker)
+
+    def planes(i):
+        b, z = i // HALO, i % HALO
+        far = ZD - HALO + z
+        below = jnp.where(even, recv_b[b, far].astype(F32), recv_a[b, far].astype(F32)).astype(BF)
+        above = jnp.where(even, recv_a[b, z].astype(F32), recv_b[b, z].astype(F32)).astype(BF)
+        spread_input(xs, b, z, below, picker)
+        spread_input(xs, b, HALO + ZD + z, above, picker)
+
+    loop(cube_count * HALO, planes)
 
     low = jnp.where(where[0] == 0, 0.0, 0.125)
     high = jnp.where(where[0] == where[1] - 1, 0.0, 0.125)
@@ -174,15 +194,18 @@
             pooled[:, 3, :, out] = ((part[:, 4] + part[:, 5]) * high).astype(BF)
         return carry
 
-    lax.fori_loop(0, 2, groups, 0, unroll=True)
+    lax.fori_loop(0, 2, groups, 0)
 
     shifter = row_picker(3, 1, 16)
-    for b in range(cube_count):
-        for z in range(4):
-            plane = jnp.concatenate([jnp.zeros((16, 64), BF), pooled[b, z], jnp.zeros((16, 64), BF)], axis=1)
-            moved = dot(shifter, plane).astype(BF)
-            for v in range(3):
-                pools[b, z, v] = moved[16 * v : 16 * v + 16]
+
+    def pool_plane(i):
+        b, z = i // 4, i % 4
+        plane = jnp.concatenate([jnp.zeros((16, 64), BF), pooled[b, z], jnp.zeros((16, 64), BF)], axis=1)
+        moved = dot(shifter, plane).astype(BF)
+        for v in range(3):
+            pools[b, z, v] = moved[16 * v : 16 * v + 16]
+
+    loop(cube_count * 4, pool_plane)
 
     rows_b = cube_count * 2 * 16
     columns = []
@@ -223,10 +246,14 @@
 def terms_b_kernel(pools, grad_b, wa, wb, terms, gs, tat, tbt):
     cube_count = grad_b.shape[0]
     shifter = row_picker(3, 1, 16)
-    for b in range(cube_count):
-        for z in range(2):
-            spread_grad(gs, b, 2 + z, grad_b[b, z], shifter)
-    for d in range(9):
+    loop(cube_count * 2, lambda i: spread_grad(gs, i // 2, 2 + i % 2, grad_b[i // 2, i % 2], shifter))
+    rows_b = cube_count * 2 * 16
+    grads = jnp.concatenate(
+        [grad_b[:, :, :, 256 * g : 256 * g + 256].reshape(rows_b, 256) for g in range(8)], axis=0
+    )
+    terms[pl.ds(27, C2, stride=28), :] = jnp.zeros((C2, 128), F32)
+
+    def offset(d):
         block = wa[d].astype(F32)
         block = jnp.concatenate([block, block], axis=1)
         mirror(8 - d, rows_at(block, 0, 128).T[:64], tat)
@@ -236,29 +263,21 @@
             part = block[64 * dx : 64 * dx + 64].astype(F32)
             turned.append(jnp.concatenate([part, part], axis=0).T)
         block = jnp.concatenate(turned, axis=0)
-        to = 768 * (8 - d)
+        to = aligned(768 * (8 - d), 768)
         for e in range(2):
-            tbt[to : to + 768, 128 * e : 128 * e + 128] = halves(
+            tbt[to, 128 * e : 128 * e + 128] = halves(
                 rows_at(block, 256 * e, 768), rows_at(block, 256 * e + 128, 768)
             )
-    rows_b = cube_count * 2 * 16
-    grads = jnp.concatenate(
-        [grad_b[:, :, :, 256 * g : 256 * g + 256].reshape(rows_b, 256) for g in range(8)], axis=0
-    )
-    terms[pl.ds(27, C2, stride=28), :] = jnp.zeros((C2, 128), F32)
-    for dz in range(3):
-        for dy in range(3):
-            windows = jnp.concatenate(
-                [
-                    pools[:, dz : dz + 2, dy, :, 128 * g : 128 * g + 256].reshape(rows_b, 256)
-                    for g in range(8)
-                ],
-                axis=0,
-            )
-            full = dot_t(windows, grads)
-            for dx in range(3):
-                term = full[64 * dx : 64 * dx + 64, :128] + full[64 * dx + 64 : 64 * dx + 128, 128:]
-                terms[pl.ds(9 * dz + 3 * dy + dx, C2, stride=28), :] = term
+        windows = jnp.concatenate(
+            [pools[:, pl.ds(d // 3, 2), d % 3, :, 128 * g : 128 * g + 256].reshape(rows_b, 256) for g in range(8)],
+            axis=0,
+        )
+        full = dot_t(windows, grads)
+        for dx in range(3):
+            term = full[64 * dx : 64 * dx + 64, :128] + full[64 * dx + 64 : 64 * dx + 128, 128:]
+            terms[pl.ds(3 * d + dx, C2, stride=28), :] = term
+
+    loop(9, offset)
 
 
 def tree(parts):
@@ -298,31 +317,36 @@
             out[:, 128 * i : 128 * i + 128] = piece * scale[0]
 
 
-def backward_kernel(where, own, recv_a, recv_b, tbt, dsl, xs, terms_b, ga, keep, send, gs, gpool, acc, term, terms):
+def backward_kernel(where, own, recv_a, recv_b, tbt, dsl, xs, terms_b, ga, keep, send, gs, back, gpool, acc, term, terms):
     del own
     cube_count = recv_a.shape[0]
     even = where[0] % 2 == 0
     shifter = row_picker(3, 1, 16)
 
-    for b in range(cube_count):
-        for z in range(2):
-            from_a, from_b = recv_a[b, z].astype(F32), recv_b[b, z].astype(F32)
-            spread_grad(gs, b, z, jnp.where(even, from_b, from_a).astype(BF), shifter)
-            spread_grad(gs, b, 4 + z, jnp.where(even, from_a, from_b).astype(BF), shifter)
+
+    def planes(i):
+        b, z = i // 2, i % 2
+        from_a, from_b = recv_a[b, z].astype(F32), recv_b[b, z].astype(F32)
+        spread_grad(gs, b, z, jnp.where(even, from_b, from_a).astype(BF), shifter)
+        spread_grad(gs, b, 4 + z, jnp.where(even, from_a, from_b).astype(BF), shifter)
+
+    loop(cube_count * 2, planes)
 
     low = jnp.where(where[0] == 0, 0.0, 0.125)
     high = jnp.where(where[0] == where[1] - 1, 0.0, 0.125)
     rows = cube_count * 4 * 16
-    columns = []
-    for dz in range(3):
-        for dy in range(3):
-            columns.append(
-                jnp.concatenate(
-                    [gs[:, dz : dz + 4, dy, :, 512 * q : 512 * q + 768].reshape(rows, 768) for q in range(4)],
-                    axis=0,
-                )
+
+    def back_dz(dz):
+        columns = [
+            jnp.concatenate(
+                [gs[:, pl.ds(dz, 4), dy, :, 512 * q : 512 * q + 768].reshape(rows, 768) for q in range(4)], axis=0
             )
-    back = dot(jnp.concatenate(columns, axis=1), tbt[...])
+            for dy in range(3)
+        ]
+        part = dot(jnp.concatenate(columns, axis=1), tbt[aligned(2304 * dz, 2304)])
+        back[...] = jnp.where(dz == 0, part, back[...] + part)
+
+    loop(3, back_dz)
     for q in range(4):
         part = back[rows * q : rows * q + rows].reshape(cube_count, 4, 16, 256)
         for z in range(4):
@@ -366,21 +390,23 @@
         return carry
 
     acc[...] = jnp.zeros_like(acc)
-    lax.fori_loop(0, 4, groups, 0, unroll=True)
+    lax.fori_loop(0, 4, groups, 0)
 
     terms[pl.ds(27, C1 // 2, stride=28), :] = jnp.zeros((C1 // 2, 128), F32)
     mask = lanes_below((32, 128), 64)
-    for d in range(9):
-        full = acc[256 * d : 256 * d + 256]
+
+    def extract(d):
+        full = acc[aligned(256 * d, 256)]
         for dx in range(3):
             left = full[32 * dx : 32 * dx + 32, :128] + full[32 * dx + 32 : 32 * dx + 64, 128:]
             right = full[32 * dx + 64 : 32 * dx + 96, :128] + full[32 * dx + 96 : 32 * dx + 128, 128:]
             merged = jnp.where(mask, left, right)
-            slot = (3 * d + dx) % 4
-            term[slot] = merged + pltpu.roll(merged, 64, 1)
-            evens = term[slot, pl.ds(0, C1 // 2, stride=2), :]
-            odds = term[slot, pl.ds(1, C1 // 2, stride=2), :]
+            term[dx] = merged + pltpu.roll(merged, 64, 1)
+            evens = term[dx, pl.ds(0, C1 // 2, stride=2), :]
+            odds = term[dx, pl.ds(1, C1 // 2, stride=2), :]
             terms[pl.ds(3 * d + dx, C1 // 2, stride=28), :] = jnp.where(mask[:16], evens, odds)
+
+    loop(9, extract)
     low = where[0] % 2 == 0
     count = keep.shape[0]
     for part in range(count):
@@ -397,21 +423,28 @@
         send[part] = jnp.where(low, sides[1], sides[0]).astype(BF)
 
 
-def one_cube(b, ga, tat, out, landed):
+def one_cube(b, ga, tat, out, acc, landed):
     rows = ZD * 16
-    sides = []
-    for p in range(2):
-        columns = []
-        for dz in range(3):
-            for dy in range(3):
-                columns.append(
-                    jnp.concatenate(
-                        [ga[b, dz : dz + ZD, p + dy, :, 512 * q : 512 * q + 768].reshape(rows, 768) for q in range(4)],
-                        axis=0,
-                    )
+
+    def step(dz):
+        sides = []
+        for p in range(2):
+            columns = [
+                jnp.concatenate(
+                    [
+                        ga[b, pl.ds(dz, ZD), p + dy, :, 512 * q : 512 * q + 768].reshape(rows, 768)
+                        for q in range(4)
+                    ],
+                    axis=0,
                 )
-        sides.append(jnp.concatenate(columns, axis=1))
-    both = dot(jnp.concatenate(sides, axis=0), tat[...]).astype(BF).reshape(2, 4, ZD, 16, 256)
+                for dy in range(3)
+            ]
+            sides.append(jnp.concatenate(columns, axis=1))
+        part = dot(jnp.concatenate(sides, axis=0), tat[aligned(2304 * dz, 2304)])
+        acc[...] = jnp.where(dz == 0, part, acc[...] + part)
+
+    loop(3, step)
+    both = acc[...].astype(BF).reshape(2, 4, ZD, 16, 256)
     row = lax.broadcasted_iota(jnp.int32, (32, 32), 0)
     col = lax.broadcasted_iota(jnp.int32, (32, 32), 1)
     mixer = jnp.where(col == row // 2 + 16 * (row % 2), 1.0, 0.0).astype(BF)
@@ -424,14 +457,14 @@
 
 
 def early_cube_kernel(b):
-    def kernel(ga, tat, out):
-        one_cube(b, ga, tat, out, None)
+    def kernel(ga, tat, out, acc):
+        one_cube(b, ga, tat, out, acc, None)
 
     return kernel
 
 
 def last_cube_kernel(ga, tat, *rest):
-    early, (out, token, block, sems) = rest[:-4], rest[-4:]
+    early, (out, token, block, acc, sems) = rest[:-5], rest[-5:]
     last = len(early)
     copies = [pltpu.make_async_copy(cube, out.at[b], sems.at[b]) for b, cube in enumerate(early)]
     for copy in copies:
@@ -442,7 +475,7 @@
         copy.start()
         copies.append(copy)
 
-    one_cube(last, ga, tat, block, landed)
+    one_cube(last, ga, tat, block, acc, landed)
     token[...] = jnp.zeros_like(token)
     for copy in copies:
         copy.wait()
@@ -524,6 +557,7 @@
         [where, own_gs, back_a, back_b, tbt, dsl, xs, terms_b],
         [((cube_count, 6, 4, 16, 2304), BF), pieces, pieces, spread],
         [
+            pltpu.VMEM((cube_count * 256, 256), F32),
             pltpu.VMEM((cube_count, 4, 16, 1024), F32),
             pltpu.VMEM((2304, 256), F32),
             pltpu.VMEM((4, C1, 128), F32),
@@ -539,7 +573,7 @@
     others = swap_along(parts, "sample", 1)
     cube = (ZD, SIDE, SIDE * C1)
     early = [
-        call(early_cube_kernel(b), [ga, tat], [(cube, BF)], [], 2_000_000_000)[0] for b in range(cube_count - 1)
+        call(early_cube_kernel(b), [ga, tat], [(cube, BF)], [pltpu.VMEM((512, 256), F32)], 2_000_000_000)[0] for b in range(cube_count - 1)
     ]
     (mine,) = call(add_kernel, [early[0], parts[0], *others], small, [], 1_000_000)
     others = swap_along([mine] * (ring // 2), "gz", 2)
@@ -547,7 +581,11 @@
         last_cube_kernel,
         [ga, tat, *early],
         [((cube_count, *cube), BF), ((8, 128), F32)],
-        [pltpu.VMEM(cube, BF), pltpu.SemaphoreType.DMA((cube_count - 1 + ZD,))],
+        [
+            pltpu.VMEM(cube, BF),
+            pltpu.VMEM((512, 256), F32),
+            pltpu.SemaphoreType.DMA((cube_count - 1 + ZD,)),
+        ],
         2_000_000_000,
         any_out=(0,),
     )

time: 68.4 us -> 70.6 us (1.032)
  Pallas kernels: 30.5 us -> 36.4 us
  starting transfers between devices: 23.4 us -> 20.5 us
  waiting for transfers between devices: 9.86 us -> 9.05 us
    pallas_call x11, Pallas kernels: 30.5 us -> 36.4 us  [call(): pl.pallas_call(kernel, out_shape=[jax.ShapeDtypeStruct(shape, dtype) for...]
    ppermute x11, starting transfers between devices: 13.2 us -> 11.7 us  [swap_along(): lax.ppermute(part, axis, [(i, i ^ k * step) for i in range(count)])]
    ppermute x2, starting transfers between devices: 8.68 us -> 7.4 us  [swap(): lax.ppermute(first, 'gz', pairs_a)]
    ppermute x11, waiting for transfers between devices: 9.85 us -> 9.04 us  [swap_along(): lax.ppermute(part, axis, [(i, i ^ k * step) for i in range(count)])]
  transfers between devices with their start and end apart: 15 -> 15, of which waited for: 8 -> 7; matrix products, arithmetic and copies ran while one was open for 4% -> 4% of each run, Pallas kernels for 15% -> 21%
where the time goes in v8:
time: 70.6 us; the launch traced here: 70.3 us
  Pallas kernels  36.4 us (52%)
  starting transfers between devices  20.5 us (29%)
  waiting for transfers between devices  9.05 us (13%)
  local copies, waits for them, and re-layouts  3.49 us (5%)
  between operations  0.8 us (1%)
    pallas_call x11, Pallas kernels, call(): pl.pallas_call(kernel, out_shape=[jax.ShapeDtypeStruct(shape, dtype) for...  36.4 us
    ppermute x11, starting transfers between devices, swap_along(): lax.ppermute(part, axis, [(i, i ^ k * step) for i in range(count)])  11.7 us
    ppermute x11, waiting for transfers between devices, swap_along(): lax.ppermute(part, axis, [(i, i ^ k * step) for i in range(count)])  9.04 us
    ppermute x2, starting transfers between devices, swap(): lax.ppermute(first, 'gz', pairs_a)  7.4 us
  transfers between devices with their start and end apart: 15, of which 7 were waited for; matrix products, arithmetic and copies ran while one was open for 4% of the time, Pallas kernels for 21%

profile of v8, /device:TPU:0, one launch (start us, length us, event | category | flops | bytes accessed | tf_op | source)
XLA Modules:
  0.0 70.3 jit_solution(3069172379863150725)
XLA Ops:
  0.6 0.7 collective-permute-start.1
  1.3 4.4 %collective-permute-start = (bf16[2,4,32,1024]{3,2,1,0:T(8,128)(2,1)}, bf16[2,4,32,1024]{3,2,1,0:T(8,128)(2,1)S(1)}, u32[]{:S(2)}, u32[]{:S(2)}) collective-permute-start(bf16[2,4,32,1024]{3,2,1,0:T(8,128)(2,1)} %cubes.1), channel_id=1, source_target_pairs={{0,1},{1,0},{2,3},{3,2},{4,5},{5,4},{6,7},{7,6},{8,9},{9,8},{10,11... | collective-permute-start | bytes 1572872 | tf_op jit(solution)/shard_map/ppermute | solution.py:501
  5.8 1.1 %reshape.12.wa = bf16[9,96,64]{2,1,0:T(8,128)(2,1)S(1)} reshape(bf16[27,2048]{1,0:T(8,128)(2,1)} %param.5) | data formatting | bytes 221184 | tf_op jit(solution)/shard_map/reshape | solution.py:518
  6.9 1.3 %reshape.13.wb = bf16[9,192,128]{2,1,0:T(8,128)(2,1)S(1)} reshape(bf16[27,8192]{1,0:T(8,128)(2,1)} %param.6) | data formatting | bytes 884736 | tf_op jit(solution)/shard_map/reshape | solution.py:519
  8.2 1.0 %copy-done = bf16[2,4,32,1024]{3,2,1,0:T(8,128)(2,1)S(1)} copy-done((bf16[2,4,32,1024]{3,2,1,0:T(8,128)(2,1)S(1)}, bf16[2,4,32,1024]{3,2,1,0:T(8,128)(2,1)}, u32[]{:S(2)}) %copy-start) | copy-done | bytes 524312
  9.3 4.3 %shard_map.67 = (bf16[2,10,4,16,1152]{4,3,2,1,0:T(8,128)(2,1)S(1)}, bf16[2304,256]{1,0:T(8,128)(2,1)S(1)}, bf16[2304,256]{1,0:T(8,128)(2,1)S(1)}, bf16[2,6,2,16,...) custom-call(bf16[2,4,32,1024]{3,2,1,0:T(8,128)(2,1)S(1)} %copy-done, bf16[9,96,64]{2,1,0:T(8,128)(2,1)S(1)} %reshape.12.wa, ...), custom_call_target="tpu_custom_call" | custom-call | flops 1000000000 | bytes 1000000 | tf_op jit(solution)/shard_map/pallas_call | solution.py:486
  13.7 9.7 %shard_map.68 = (bf16[2,10,4,16,1152]{4,3,2,1,0:T(8,128)(2,1)S(1)}, bf16[2,6,2,16,2048]{4,3,2,1,0:T(8,128)(2,1)S(1)}, bf16[2,4,3,16,1152]{4,3,2,1,0:T(8,128)(2,1)S(1)}, bf16[2,2,16,2048]{3,2,1,0:T(8,128)(2,1)S(1)}) custom-call(s32[3]{0:T(128)S(1)} %pad_add_fusion.where, ...), custom_call_target="tpu_custom_call", output_to_operand_aliasing={{0}: (1, {}), {1}: (2, {})} | custom-call | flops 8000000000 | bytes 1000000 | tf_op jit(solution)/shard_map/pallas_call | solution.py:486
  23.4 0.7 collective-permute-start.3
  24.1 3.0 %collective-permute-start.2 = (bf16[2,2,16,2048]{3,2,1,0:T(8,128)(2,1)S(1)}, bf16[2,2,16,2048]{3,2,1,0:T(8,128)(2,1)S(1)}, u32[]{:S(2)}, u32[]{:S(2)}) collective-permute-start(bf16[2,2,16,2048]{3,2,1,0:T(8,128)(2,1)S(1)} %get-tuple-element.33.grad_b), channel_id=1, source_target_pairs={{0,1},{1,0},{2,3},{3,2},{4,5},{5,4},{6,7},{7,6},{8,9},{9,8},{10,11... | collective-permute-start | bytes 786440 | tf_op jit(solution)/shard_map/ppermute | solution.py:501
  27.1 4.5 %shard_map.69 = (f32[1792,128]{1,0:T(8,128)S(1)}, bf16[2,6,3,16,2304]{4,3,2,1,0:T(8,128)(2,1)S(1)}, bf16[6912,256]{1,0:T(8,128)(2,1)S(1)}, bf16[6912,256]{1,0:T(8,128)(2,1)S(1)}) custom-call(bf16[2,4,3,16,1152]{4,3,2,1,0:T(8,128)(2,1)S(1)} %get-tuple-element.32.pools, bf16[2,2,16,2048]{3,2,1,0:T(8,128)(2,1)S(1)} %get-tuple-element.33.grad_b, ...), custom_call_target="tpu_custom_call" | custom-call | flops 1000000000 | bytes 1000000 | tf_op jit(solution)/shard_map/pallas_call | solution.py:486
  31.6 9.1 %shard_map.70 = (bf16[2,6,4,16,2304]{4,3,2,1,0:T(8,128)(2,1)S(1)}, bf16[4,280,128]{2,1,0:T(8,128)(2,1)S(1)}, bf16[4,280,128]{2,1,0:T(8,128)(2,1)S(1)}, bf16[2,6,3,16,2304]{4,3,2,1,0:T(8,128)(2,1)S(1)}) custom-call(s32[3]{0:T(128)S(1)} %pad_add_fusion.where, bf16[2,6,3,16,2304]{4,3,2,1,0:T(8,128)(2,1)S(1)} %get-tuple-element.34.own, ...), custom_call_target="tpu_custom_call", output_to_operand_aliasing={{3}: (1, {})} | custom-call | flops 6000000000 | bytes 1000000 | tf_op jit(solution)/shard_map/pallas_call | solution.py:486
  40.8 1.6 %collective-permute-done.4.recv = bf16[4,280,128]{2,1,0:T(8,128)(2,1)S(1)} collective-permute-done((bf16[4,280,128]{2,1,0:T(8,128)(2,1)S(1)}, bf16[4,280,128]{2,1,0:T(8,128)(2,1)S(1)}, u32[]{:S(2)}, u32[]{:S(2)}) %collective-permute-start.4) | collective-permute-done | bytes 286752 | tf_op jit(solution)/shard_map/ppermute | solution.py:507
  42.4 0.6 shard_map.73
  43.0 1.6 %collective-permute-start.5 = (bf16[280,128]{1,0:T(8,128)(2,1)S(1)}, bf16[280,128]{1,0:T(8,128)(2,1)S(1)}, u32[]{:S(2)}, u32[]{:S(2)}) collective-permute-start(bf16[280,128]{1,0:T(8,128)(2,1)S(1)} %get-tuple-element.46), channel_id=1, source_target_pairs={{0,8},{8,0},{16,24},{24,16},{1,9},{9,1},{17,25},{25,17},{2,10},{10... | collective-permute-start | bytes 215048 | tf_op jit(solution)/shard_map/ppermute | solution.py:507
  44.5 1.5 %collective-permute-start.6 = (bf16[280,128]{1,0:T(8,128)(2,1)S(1)}, bf16[280,128]{1,0:T(8,128)(2,1)S(1)}, u32[]{:S(2)}, u32[]{:S(2)}) collective-permute-start(bf16[280,128]{1,0:T(8,128)(2,1)S(1)} %get-tuple-element.47), channel_id=1, source_target_pairs={{0,16},{8,24},{16,0},{24,8},{1,17},{9,25},{17,1},{25,9},{2,18},{10... | collective-permute-start | bytes 215048 | tf_op jit(solution)/shard_map/ppermute | solution.py:507
  46.1 0.5 collective-permute-start.7
  46.5 2.5 %shard_map.71.rest_0_.after = bf16[4,32,1024]{2,1,0:T(8,128)(2,1)S(1)} custom-call(bf16[2,6,4,16,2304]{4,3,2,1,0:T(8,128)(2,1)S(1)} %get-tuple-element.39.ga, bf16[6912,256]{1,0:T(8,128)(2,1)S(1)} %get-tuple-element.40.tat), custom_call_target="tpu_custom_call" | custom-call | flops 2000000000 | bytes 1000000 | tf_op jit(solution)/shard_map/pallas_call | solution.py:486
  49.1 2.2 %collective-permute-done.7.refs_3_ = bf16[280,128]{1,0:T(8,128)(2,1)S(1)} collective-permute-done((bf16[280,128]{1,0:T(8,128)(2,1)S(1)}, bf16[280,128]{1,0:T(8,128)(2,1)S(1)}, u32[]{:S(2)}, u32[]{:S(2)}) %collective-permute-start.7) | collective-permute-done | bytes 71712 | tf_op jit(solution)/shard_map/ppermute | solution.py:507
  51.3 2.3 %collective-permute-start.10 = (bf16[280,128]{1,0:T(8,128)(2,1)S(1)}, bf16[280,128]{1,0:T(8,128)(2,1)S(1)}, u32[]{:S(2)}, u32[]{:S(2)}) collective-permute-start(bf16[280,128]{1,0:T(8,128)(2,1)S(1)} %shard_map.74.refs_0_), channel_id=1, source_target_pairs={{0,6},{1,7},{2,4},{3,5},{4,2},{5,3},{6,0},{7,1},{8,14},{9,15},{10,... | collective-permute-start | bytes 215048 | tf_op jit(solution)/shard_map/ppermute | solution.py:507
  53.6 0.8 %collective-permute-start.9 = (bf16[280,128]{1,0:T(8,128)(2,1)S(1)}, bf16[280,128]{1,0:T(8,128)(2,1)S(1)}, u32[]{:S(2)}, u32[]{:S(2)}) collective-permute-start(bf16[280,128]{1,0:T(8,128)(2,1)S(1)} %shard_map.74.refs_0_), channel_id=1, source_target_pairs={{0,4},{1,5},{2,6},{3,7},{4,0},{5,1},{6,2},{7,3},{8,12},{9,13},{10,... | collective-permute-start | bytes 215048 | tf_op jit(solution)/shard_map/ppermute | solution.py:507
  54.4 1.3 %collective-permute-start.8 = (bf16[280,128]{1,0:T(8,128)(2,1)S(1)}, bf16[280,128]{1,0:T(8,128)(2,1)S(1)}, u32[]{:S(2)}, u32[]{:S(2)}) collective-permute-start(bf16[280,128]{1,0:T(8,128)(2,1)S(1)} %shard_map.74.refs_0_), channel_id=1, source_target_pairs={{0,2},{1,3},{2,0},{3,1},{4,6},{5,7},{6,4},{7,5},{8,10},{9,11},{10,... | collective-permute-start | bytes 215048 | tf_op jit(solution)/shard_map/ppermute | solution.py:507
  55.8 3.2 %shard_map.72 = (bf16[2,4,32,1024]{3,2,1,0:T(8,128)(2,1)}, f32[8,128]{1,0:T(8,128)S(1)}) custom-call(bf16[2,6,4,16,2304]{4,3,2,1,0:T(8,128)(2,1)S(1)} %get-tuple-element.39.ga, bf16[6912,256]{1,0:T(8,128)(2,1)S(1)} %get-tuple-element.40.tat, bf16[4,32,1024]{2,1,0:T(8,128)(2,1)S(1)} %shard_map.71.rest_0_.after), custom_call_target="tpu_custom_call" | custom-call | flops 2000000000 | bytes 1000000 | tf_op jit(solution)/shard_map/pallas_call | solution.py:486
  59.0 0.7 %collective-permute-done.9.refs_2_ = bf16[280,128]{1,0:T(8,128)(2,1)S(1)} collective-permute-done((bf16[280,128]{1,0:T(8,128)(2,1)S(1)}, bf16[280,128]{1,0:T(8,128)(2,1)S(1)}, u32[]{:S(2)}, u32[]{:S(2)}) %collective-permute-start.9) | collective-permute-done | bytes 71712 | tf_op jit(solution)/shard_map/ppermute | solution.py:507
  59.8 1.2 %collective-permute-start.13 = (bf16[280,128]{1,0:T(8,128)(2,1)S(1)}, bf16[280,128]{1,0:T(8,128)(2,1)S(1)}, u32[]{:S(2)}, u32[]{:S(2)}) collective-permute-start(bf16[280,128]{1,0:T(8,128)(2,1)S(1)} %shard_map.75.refs_0_), channel_id=1, source_target_pairs={{0,24},{8,16},{16,8},{24,0},{1,25},{9,17},{17,9},{25,1},{2,26},{10... | collective-permute-start | bytes 215048 | tf_op jit(solution)/shard_map/ppermute | solution.py:507
  61.0 1.0 %collective-permute-start.12 = (bf16[280,128]{1,0:T(8,128)(2,1)S(1)}, bf16[280,128]{1,0:T(8,128)(2,1)S(1)}, u32[]{:S(2)}, u32[]{:S(2)}) collective-permute-start(bf16[280,128]{1,0:T(8,128)(2,1)S(1)} %shard_map.75.refs_0_), channel_id=1, source_target_pairs={{0,16},{8,24},{16,0},{24,8},{1,17},{9,25},{17,1},{25,9},{2,18},{10... | collective-permute-start | bytes 215048 | tf_op jit(solution)/shard_map/ppermute | solution.py:507
  62.0 1.3 %collective-permute-start.11 = (bf16[280,128]{1,0:T(8,128)(2,1)S(1)}, bf16[280,128]{1,0:T(8,128)(2,1)S(1)}, u32[]{:S(2)}, u32[]{:S(2)}) collective-permute-start(bf16[280,128]{1,0:T(8,128)(2,1)S(1)} %shard_map.75.refs_0_), channel_id=1, source_target_pairs={{0,8},{8,0},{16,24},{24,16},{1,9},{9,1},{17,25},{25,17},{2,10},{10... | collective-permute-start | bytes 215048 | tf_op jit(solution)/shard_map/ppermute | solution.py:507
  63.4 1.8 %collective-permute-done.13.refs_3_ = bf16[280,128]{1,0:T(8,128)(2,1)S(1)} collective-permute-done((bf16[280,128]{1,0:T(8,128)(2,1)S(1)}, bf16[280,128]{1,0:T(8,128)(2,1)S(1)}, u32[]{:S(2)}, u32[]{:S(2)}) %collective-permute-start.13) | collective-permute-done | bytes 71712 | tf_op jit(solution)/shard_map/ppermute | solution.py:507
  65.2 0.7 %collective-permute-done.12.refs_2_ = bf16[280,128]{1,0:T(8,128)(2,1)S(1)} collective-permute-done((bf16[280,128]{1,0:T(8,128)(2,1)S(1)}, bf16[280,128]{1,0:T(8,128)(2,1)S(1)}, u32[]{:S(2)}, u32[]{:S(2)}) %collective-permute-start.12) | collective-permute-done | bytes 71712 | tf_op jit(solution)/shard_map/ppermute | solution.py:507
  65.9 0.5 collective-permute-done.11.refs_1_
  66.4 0.6 shard_map.76.own
  67.0 1.6 %collective-permute-done.14.other = bf16[4,280,128]{2,1,0:T(8,128)(2,1)S(1)} collective-permute-done((bf16[4,280,128]{2,1,0:T(8,128)(2,1)S(1)}, bf16[4,280,128]{2,1,0:T(8,128)(2,1)S(1)}, u32[]{:S(2)}, u32[]{:S(2)}) %collective-permute-start.14) | collective-permute-done | bytes 286752 | tf_op jit(solution)/shard_map/ppermute | solution.py:507
  68.6 1.7 %shard_map.77 = (f32[27,2048]{1,0:T(8,128)}, f32[27,8192]{1,0:T(8,128)}) custom-call(s32[3]{0:T(128)S(1)} %pad_add_fusion.where, f32[1]{0:T(128)} %constant.11.clone.1.scale, bf16[4,280,128]{2,1,0:T(8,128)(2,1)S(1)} %shard_map.76.own, bf16[4,280,128]{2,1,0:T(8,128)(2,1)S(1)} %collective-permute-done.14.other), custom_call_target="tpu_custom_call" | custom-call | flops 1000000 | bytes 1000000 | tf_op jit(solution)/shard_map/pallas_call | solution.py:486
  (16 shorter events, 0.3 us)
Async XLA Ops:
  0.6 13.1 %copy-start.1 = (bf16[2,1,8,1024]{3,2,1,0:T(8,128)(2,1)S(1)}, bf16[2,1,8,1024]{3,2,1,0:T(8,128)(2,1)}, u32[]{:S(2)}) copy-start(bf16[2,1,8,1024]{3,2,1,0:T(8,128)(2,1)} %cot.1) | copy-start | bytes 98308
  0.6 13.0 %collective-permute-start.1 = (bf16[2,4,32,1024]{3,2,1,0:T(8,128)(2,1)}, bf16[2,4,32,1024]{3,2,1,0:T(8,128)(2,1)S(1)}, u32[]{:S(2)}, u32[]{:S(2)}) collective-permute-start(bf16[2,4,32,1024]{3,2,1,0:T(8,128)(2,1)} %cubes.1), channel_id=1, source_target_pairs={{1,2},{2,1},{3,4},{4,3},{5,6},{6,5},{9,10},{10,9},{11,12},{12,11},... | collective-permute-start | bytes 1572872 | tf_op jit(solution)/shard_map/ppermute | solution.py:501
  1.3 12.3 %collective-permute-start = (bf16[2,4,32,1024]{3,2,1,0:T(8,128)(2,1)}, bf16[2,4,32,1024]{3,2,1,0:T(8,128)(2,1)S(1)}, u32[]{:S(2)}, u32[]{:S(2)}) collective-permute-start(bf16[2,4,32,1024]{3,2,1,0:T(8,128)(2,1)} %cubes.1), channel_id=1, source_target_pairs={{0,1},{1,0},{2,3},{3,2},{4,5},{5,4},{6,7},{7,6},{8,9},{9,8},{10,11... | collective-permute-start | bytes 1572872 | tf_op jit(solution)/shard_map/ppermute | solution.py:501
  8.2 1.0 %copy-start = (bf16[2,4,32,1024]{3,2,1,0:T(8,128)(2,1)S(1)}, bf16[2,4,32,1024]{3,2,1,0:T(8,128)(2,1)}, u32[]{:S(2)}) copy-start(bf16[2,4,32,1024]{3,2,1,0:T(8,128)(2,1)} %cubes.1) | copy-start | bytes 1572868
  23.4 8.1 %collective-permute-start.3 = (bf16[2,2,16,2048]{3,2,1,0:T(8,128)(2,1)S(1)}, bf16[2,2,16,2048]{3,2,1,0:T(8,128)(2,1)S(1)}, u32[]{:S(2)}, u32[]{:S(2)}) collective-permute-start(bf16[2,2,16,2048]{3,2,1,0:T(8,128)(2,1)S(1)} %get-tuple-element.33.grad_b), channel_id=1, source_target_pairs={{1,2},{2,1},{3,4},{4,3},{5,6},{6,5},{9,10},{10,9},{11,12},{12,11},... | collective-permute-start | bytes 786440 | tf_op jit(solution)/shard_map/ppermute | solution.py:501
  24.1 7.5 %collective-permute-start.2 = (bf16[2,2,16,2048]{3,2,1,0:T(8,128)(2,1)S(1)}, bf16[2,2,16,2048]{3,2,1,0:T(8,128)(2,1)S(1)}, u32[]{:S(2)}, u32[]{:S(2)}) collective-permute-start(bf16[2,2,16,2048]{3,2,1,0:T(8,128)(2,1)S(1)} %get-tuple-element.33.grad_b), channel_id=1, source_target_pairs={{0,1},{1,0},{2,3},{3,2},{4,5},{5,4},{6,7},{7,6},{8,9},{9,8},{10,11... | collective-permute-start | bytes 786440 | tf_op jit(solution)/shard_map/ppermute | solution.py:501
  40.7 1.6 %collective-permute-start.4 = (bf16[4,280,128]{2,1,0:T(8,128)(2,1)S(1)}, bf16[4,280,128]{2,1,0:T(8,128)(2,1)S(1)}, u32[]{:S(2)}, u32[]{:S(2)}) collective-permute-start(bf16[4,280,128]{2,1,0:T(8,128)(2,1)S(1)} %get-tuple-element.44), channel_id=1, source_target_pairs={{0,1},{1,0},{2,3},{3,2},{4,5},{5,4},{6,7},{7,6},{8,9},{9,8},{10,11... | collective-permute-start | bytes 860168 | tf_op jit(solution)/shard_map/ppermute | solution.py:507
  43.0 6.1 %collective-permute-start.5 = (bf16[280,128]{1,0:T(8,128)(2,1)S(1)}, bf16[280,128]{1,0:T(8,128)(2,1)S(1)}, u32[]{:S(2)}, u32[]{:S(2)}) collective-permute-start(bf16[280,128]{1,0:T(8,128)(2,1)S(1)} %get-tuple-element.46), channel_id=1, source_target_pairs={{0,8},{8,0},{16,24},{24,16},{1,9},{9,1},{17,25},{25,17},{2,10},{10... | collective-permute-start | bytes 215048 | tf_op jit(solution)/shard_map/ppermute | solution.py:507
  44.5 4.6 %collective-permute-start.6 = (bf16[280,128]{1,0:T(8,128)(2,1)S(1)}, bf16[280,128]{1,0:T(8,128)(2,1)S(1)}, u32[]{:S(2)}, u32[]{:S(2)}) collective-permute-start(bf16[280,128]{1,0:T(8,128)(2,1)S(1)} %get-tuple-element.47), channel_id=1, source_target_pairs={{0,16},{8,24},{16,0},{24,8},{1,17},{9,25},{17,1},{25,9},{2,18},{10... | collective-permute-start | bytes 215048 | tf_op jit(solution)/shard_map/ppermute | solution.py:507
  46.1 5.2 %collective-permute-start.7 = (bf16[280,128]{1,0:T(8,128)(2,1)S(1)}, bf16[280,128]{1,0:T(8,128)(2,1)S(1)}, u32[]{:S(2)}, u32[]{:S(2)}) collective-permute-start(bf16[280,128]{1,0:T(8,128)(2,1)S(1)} %get-tuple-element.48), channel_id=1, source_target_pairs={{0,24},{8,16},{16,8},{24,0},{1,25},{9,17},{17,9},{25,1},{2,26},{10... | collective-permute-start | bytes 215048 | tf_op jit(solution)/shard_map/ppermute | solution.py:507
  51.3 7.7 %collective-permute-start.10 = (bf16[280,128]{1,0:T(8,128)(2,1)S(1)}, bf16[280,128]{1,0:T(8,128)(2,1)S(1)}, u32[]{:S(2)}, u32[]{:S(2)}) collective-permute-start(bf16[280,128]{1,0:T(8,128)(2,1)S(1)} %shard_map.74.refs_0_), channel_id=1, source_target_pairs={{0,6},{1,7},{2,4},{3,5},{4,2},{5,3},{6,0},{7,1},{8,14},{9,15},{10,... | collective-permute-start | bytes 215048 | tf_op jit(solution)/shard_map/ppermute | solution.py:507
  53.6 6.1 %collective-permute-start.9 = (bf16[280,128]{1,0:T(8,128)(2,1)S(1)}, bf16[280,128]{1,0:T(8,128)(2,1)S(1)}, u32[]{:S(2)}, u32[]{:S(2)}) collective-permute-start(bf16[280,128]{1,0:T(8,128)(2,1)S(1)} %shard_map.74.refs_0_), channel_id=1, source_target_pairs={{0,4},{1,5},{2,6},{3,7},{4,0},{5,1},{6,2},{7,3},{8,12},{9,13},{10,... | collective-permute-start | bytes 215048 | tf_op jit(solution)/shard_map/ppermute | solution.py:507
  54.4 5.3 %collective-permute-start.8 = (bf16[280,128]{1,0:T(8,128)(2,1)S(1)}, bf16[280,128]{1,0:T(8,128)(2,1)S(1)}, u32[]{:S(2)}, u32[]{:S(2)}) collective-permute-start(bf16[280,128]{1,0:T(8,128)(2,1)S(1)} %shard_map.74.refs_0_), channel_id=1, source_target_pairs={{0,2},{1,3},{2,0},{3,1},{4,6},{5,7},{6,4},{7,5},{8,10},{9,11},{10,... | collective-permute-start | bytes 215048 | tf_op jit(solution)/shard_map/ppermute | solution.py:507
  59.8 5.4 %collective-permute-start.13 = (bf16[280,128]{1,0:T(8,128)(2,1)S(1)}, bf16[280,128]{1,0:T(8,128)(2,1)S(1)}, u32[]{:S(2)}, u32[]{:S(2)}) collective-permute-start(bf16[280,128]{1,0:T(8,128)(2,1)S(1)} %shard_map.75.refs_0_), channel_id=1, source_target_pairs={{0,24},{8,16},{16,8},{24,0},{1,25},{9,17},{17,9},{25,1},{2,26},{10... | collective-permute-start | bytes 215048 | tf_op jit(solution)/shard_map/ppermute | solution.py:507
  61.0 4.9 %collective-permute-start.12 = (bf16[280,128]{1,0:T(8,128)(2,1)S(1)}, bf16[280,128]{1,0:T(8,128)(2,1)S(1)}, u32[]{:S(2)}, u32[]{:S(2)}) collective-permute-start(bf16[280,128]{1,0:T(8,128)(2,1)S(1)} %shard_map.75.refs_0_), channel_id=1, source_target_pairs={{0,16},{8,24},{16,0},{24,8},{1,17},{9,25},{17,1},{25,9},{2,18},{10... | collective-permute-start | bytes 215048 | tf_op jit(solution)/shard_map/ppermute | solution.py:507
  62.0 4.3 %collective-permute-start.11 = (bf16[280,128]{1,0:T(8,128)(2,1)S(1)}, bf16[280,128]{1,0:T(8,128)(2,1)S(1)}, u32[]{:S(2)}, u32[]{:S(2)}) collective-permute-start(bf16[280,128]{1,0:T(8,128)(2,1)S(1)} %shard_map.75.refs_0_), channel_id=1, source_target_pairs={{0,8},{8,0},{16,24},{24,16},{1,9},{9,1},{17,25},{25,17},{2,10},{10... | collective-permute-start | bytes 215048 | tf_op jit(solution)/shard_map/ppermute | solution.py:507
  66.9 1.6 %collective-permute-start.14 = (bf16[4,280,128]{2,1,0:T(8,128)(2,1)S(1)}, bf16[4,280,128]{2,1,0:T(8,128)(2,1)S(1)}, u32[]{:S(2)}, u32[]{:S(2)}) collective-permute-start(bf16[4,280,128]{2,1,0:T(8,128)(2,1)S(1)} %shard_map.76.own), channel_id=1, source_target_pairs={{0,1},{1,0},{2,3},{3,2},{4,5},{5,4},{6,7},{7,6},{8,9},{9,8},{10,11... | collective-permute-start | bytes 860168 | tf_op jit(solution)/shard_map/ppermute | solution.py:507

commit v9 on v7

--- a/solution.py
+++ b/solution.py
@@ -64,10 +64,10 @@
     return act, (squash + act * (1.0 - squash)).astype(BF)
 
 
-def windows_a(xs, spans, p, start):
+def windows_a(xs, spans, p, start, offsets=(0, 1, 2)):
     lanes = pl.ds(start if isinstance(start, int) else pl.multiple_of(start, 128), 256)
     columns = []
-    for dz in range(3):
+    for dz in offsets:
         for dy in range(3):
             parts = [xs[:, first + dz : first + dz + planes, p + dy, :, lanes] for first, planes in spans]
             whole = jnp.concatenate(parts, axis=1) if len(parts) > 1 else parts[0]
@@ -96,19 +96,26 @@
             tat[768 * d + 64 * slot : 768 * d + 64 * slot + 64, 128 * half : 128 * half + 128] = value
 
 
-def prepare_kernel(cubes, wa, wb, xs, ta, tb, dsl, inner):
+def prepare_kernel(cubes, weight_a, weight_b, xs, ta, tb, dsl, inner, edge_low, edge_high, wa, wb):
+    mask = lanes_below((27, 128), 64)
+    for j in range(C1 // 2):
+        both = weight_a[:, 128 * j : 128 * j + 128].astype(F32)
+        other = pltpu.roll(both, 64, 1)
+        wa[pl.ds(2 * j, 27, stride=C1), :] = jnp.where(mask, both, other)
+        wa[pl.ds(2 * j + 1, 27, stride=C1), :] = jnp.where(mask, other, both)
+    for i in range(C2):
+        wb[pl.ds(i, 27, stride=C2), :] = weight_b[:, 128 * i : 128 * i + 128].astype(F32)
     picker = row_picker(4, 2, 32)
     for b in range(cubes.shape[0]):
         for z in range(ZD):
             spread_input(xs, b, HALO + z, cubes[b, z], picker)
     for d in range(9):
-        block = wa[d].astype(F32)
-        block = jnp.concatenate([block, block], axis=1)
+        block = wa[96 * d : 96 * d + 96]
         for px in range(2):
             ta[256 * d : 256 * d + 256, 128 * px : 128 * px + 128] = halves(
                 rows_at(block, 32 * px, 256), rows_at(block, 64 + 32 * px, 256)
             )
-        block = wb[d]
+        block = wb[192 * d : 192 * d + 192].astype(BF)
         for e in range(2):
             tb[256 * d : 256 * d + 256, 128 * e : 128 * e + 128] = rows_at(block, 64 * e, 256)
 
@@ -127,9 +134,14 @@
             dsl[:, 2:4, p, :, 256 * g : 256 * g + 256] = slope[g, p]
         part = act[g, 0] + act[g, 1]
         inner[:, :, :, 128 * g : 128 * g + 128] = part[..., :128] + part[..., 128:]
-
-
-def forward_kernel(where, own, own_slope, inner, recv_a, recv_b, ta, tb, cot, xs, dsl, pools, grad_b, pooled):
+    for edge, first, offsets in ((edge_low, HALO - 1, (1, 2)), (edge_high, HALO + 2, (0, 1))):
+        rows = jnp.concatenate(
+            [windows_a(xs, ((first, 1),), p, 128 * g, offsets) for g in range(8) for p in range(2)], axis=0
+        )
+        edge[...] = dot(rows, ta[768 * offsets[0] : 768 * offsets[0] + 1536])
+
+
+def forward_kernel(where, own, own_slope, inner, edge_low, edge_high, recv_a, recv_b, ta, tb, cot, xs, dsl, pools, grad_b, pooled):
     del own, own_slope
     cube_count = xs.shape[0]
     even = where[0] % 2 == 0
@@ -146,35 +158,41 @@
     high = jnp.where(where[0] == where[1] - 1, 0.0, 0.125)
 
     def groups(i, carry):
-        pre = dot(
-            jnp.concatenate(
-                [
-                    windows_a(xs, ((0, 3), (HALO + ZD - 2, 3)), p, 512 * i + 128 * j)
-                    for j in range(4)
-                    for p in range(2)
-                ],
-                axis=0,
-            ),
-            ta[...],
-        )
-        act, slope = silu(pre)
-        slope = slope.reshape(4, 2, cube_count, 6, 16, 256)
-        act = act.reshape(4, 2, cube_count, 6, 16, 256)
+        def stack(spans, offsets=(0, 1, 2)):
+            return jnp.concatenate(
+                [windows_a(xs, spans, p, 512 * i + 128 * j, offsets) for j in range(4) for p in range(2)], axis=0
+            )
+
+        act, slope = silu(dot(stack(((0, 2), (HALO + ZD - 1, 2))), ta[...]))
+        slope = slope.reshape(4, 2, cube_count, 4, 16, 256)
+        act = act.reshape(4, 2, cube_count, 4, 16, 256)
+        rows = cube_count * 128
+        here = pl.ds(pl.multiple_of(rows * i, rows), rows)
+        sides = []
+        for edge, first, dz in ((edge_low, HALO - 1, 0), (edge_high, HALO + 2, 2)):
+            pre = edge[here] + dot(stack(((first, 1),), (dz,)), ta[768 * dz : 768 * dz + 768])
+            edge_act, edge_slope = silu(pre)
+            edge_act = edge_act.reshape(4, 2, cube_count, 16, 256)
+            sides.append((edge_act, edge_slope.reshape(4, 2, cube_count, 16, 256)))
         for j in range(4):
             for p in range(2):
                 to = pl.ds(pl.multiple_of(1024 * i + 256 * j, 256), 256)
-                dsl[:, 0:2, p, :, to] = slope[j, p][:, 1:3]
-                dsl[:, 4:6, p, :, to] = slope[j, p][:, 3:5]
+                dsl[:, 0, p, :, to] = slope[j, p][:, 1]
+                dsl[:, 1, p, :, to] = sides[0][1][j, p]
+                dsl[:, 4, p, :, to] = sides[1][1][j, p]
+                dsl[:, 5, p, :, to] = slope[j, p][:, 2]
             part = act[j, 0] + act[j, 1]
             part = part[..., :128] + part[..., 128:]
+            ends = [side[0][j, 0] + side[0][j, 1] for side in sides]
+            ends = [end[..., :128] + end[..., 128:] for end in ends]
             out = pl.ds(pl.multiple_of(512 * i + 128 * j, 128), 128)
             pooled[:, 0, :, out] = ((part[:, 0] + part[:, 1]) * low).astype(BF)
-            pooled[:, 1, :, out] = ((part[:, 2] + inner[:, 0, :, out]) * 0.125).astype(BF)
-            pooled[:, 2, :, out] = ((part[:, 3] + inner[:, 1, :, out]) * 0.125).astype(BF)
-            pooled[:, 3, :, out] = ((part[:, 4] + part[:, 5]) * high).astype(BF)
+            pooled[:, 1, :, out] = ((ends[0] + inner[:, 0, :, out]) * 0.125).astype(BF)
+            pooled[:, 2, :, out] = ((ends[1] + inner[:, 1, :, out]) * 0.125).astype(BF)
+            pooled[:, 3, :, out] = ((part[:, 2] + part[:, 3]) * high).astype(BF)
         return carry
 
-    lax.fori_loop(0, 2, groups, 0, unroll=True)
+    lax.fori_loop(0, 2, groups, 0)
 
     shifter = row_picker(3, 1, 16)
     for b in range(cube_count):
@@ -227,13 +245,11 @@
         for z in range(2):
             spread_grad(gs, b, 2 + z, grad_b[b, z], shifter)
     for d in range(9):
-        block = wa[d].astype(F32)
-        block = jnp.concatenate([block, block], axis=1)
-        mirror(8 - d, rows_at(block, 0, 128).T[:64], tat)
-        block = wb[d]
+        mirror(8 - d, rows_at(wa[96 * d : 96 * d + 96], 0, 128).T[:64], tat)
+        block = wb[192 * d : 192 * d + 192]
         turned = []
         for dx in (2, 1, 0):
-            part = block[64 * dx : 64 * dx + 64].astype(F32)
+            part = block[64 * dx : 64 * dx + 64]
             turned.append(jnp.concatenate([part, part], axis=0).T)
         block = jnp.concatenate(turned, axis=0)
         to = 768 * (8 - d)
@@ -366,7 +382,7 @@
         return carry
 
     acc[...] = jnp.zeros_like(acc)
-    lax.fori_loop(0, 4, groups, 0, unroll=True)
+    lax.fori_loop(0, 4, groups, 0)
 
     terms[pl.ds(27, C1 // 2, stride=28), :] = jnp.zeros((C1 // 2, 128), F32)
     mask = lanes_below((32, 128), 64)
@@ -482,24 +498,26 @@
     where = jnp.stack([lax.axis_index("gz"), jnp.int32(ring), lax.axis_index("sample")]).astype(jnp.int32)
     recv_a, recv_b = swap(cubes, cubes, ring)
 
-    wa = weight_a.reshape(9, 96, C2)
-    wb = weight_b.reshape(9, 192, C3)
-    own_xs, ta, tb, own_slope, inner = call(
+    own_xs, ta, tb, own_slope, inner, edge_low, edge_high, wa, wb = call(
         prepare_kernel,
-        [cubes, wa, wb],
+        [cubes, weight_a, weight_b],
         [
             ((cube_count, ZD + 2 * HALO, 4, 16, 1152), BF),
             ((2304, 256), BF),
             ((2304, 256), BF),
             ((cube_count, 6, 2, 16, 2048), BF),
             ((cube_count, 2, 16, 1024), F32),
+            ((cube_count * 256, 256), F32),
+            ((cube_count * 256, 256), F32),
+            ((27 * C1, 128), F32),
+            ((27 * C2, 128), F32),
         ],
         [],
         1_000_000_000,
     )
     xs, dsl, pools, grad_b = call(
         forward_kernel,
-        [where, own_xs, own_slope, inner, recv_a, recv_b, ta, tb, cotangent],
+        [where, own_xs, own_slope, inner, edge_low, edge_high, recv_a, recv_b, ta, tb, cotangent],
         [
             ((cube_count, ZD + 2 * HALO, 4, 16, 1152), BF),
             ((cube_count, 6, 2, 16, 2048), BF),

time: 68.4 us -> 64.8 us (0.947)
  Pallas kernels: 30.5 us -> 27.9 us
    pallas_call x11, Pallas kernels: 30.5 us -> 27.9 us  [call(): pl.pallas_call(kernel, out_shape=[jax.ShapeDtypeStruct(shape, dtype) for...]
    reshape x2 -> x0, local copies, waits for them, and re-layouts: 2.45 us -> none  [the longest x1 1.3 us: shards(): wb = weight_b.reshape(9, 192, C3)]
    unnamed x4 -> x8, local copies, waits for them, and re-layouts: 1.04 us -> 2.99 us
    ppermute x2, starting transfers between devices: 8.68 us -> 7.41 us  [swap(): lax.ppermute(first, 'gz', pairs_a)]
    ppermute x11, starting transfers between devices: 13.2 us -> 14 us  [swap_along(): lax.ppermute(part, axis, [(i, i ^ k * step) for i in range(count)])]
  transfers between devices with their start and end apart: 15 -> 15, of which waited for: 8 -> 7; matrix products, arithmetic and copies ran while one was open for 4% -> 0% of each run, Pallas kernels for 15% -> 17%
where the time goes in v9:
time: 64.8 us; the launch traced here: 64.6 us
  Pallas kernels  27.9 us (43%)
  starting transfers between devices  22.9 us (35%)
  waiting for transfers between devices  9.89 us (15%)
  local copies, waits for them, and re-layouts  2.99 us (5%)
  between operations  0.77 us (1%)
    pallas_call x11, Pallas kernels, call(): pl.pallas_call(kernel, out_shape=[jax.ShapeDtypeStruct(shape, dtype) for...  27.9 us
    ppermute x11, starting transfers between devices, swap_along(): lax.ppermute(part, axis, [(i, i ^ k * step) for i in range(count)])  14 us
    ppermute x11, waiting for transfers between devices, swap_along(): lax.ppermute(part, axis, [(i, i ^ k * step) for i in range(count)])  9.88 us
    ppermute x2, starting transfers between devices, swap(): lax.ppermute(first, 'gz', pairs_a)  7.41 us
    unnamed x8, local copies, waits for them, and re-layouts  2.99 us
    ppermute x2, starting transfers between devices, swap(): lax.ppermute(second, 'gz', pairs_b)  1.55 us
  transfers between devices with their start and end apart: 15, of which 7 were waited for; matrix products, arithmetic and copies ran while one was open for 0% of the time, Pallas kernels for 17%

profile of v9, /device:TPU:0, one launch (start us, length us, event | category | flops | bytes accessed | tf_op | source)
XLA Modules:
  0.0 64.6 jit_solution(6746978924062127070)
XLA Ops:
  0.6 0.7 %collective-permute-start.1 = (bf16[2,4,32,1024]{3,2,1,0:T(8,128)(2,1)}, bf16[2,4,32,1024]{3,2,1,0:T(8,128)(2,1)S(1)}, u32[]{:S(2)}, u32[]{:S(2)}) collective-permute-start(bf16[2,4,32,1024]{3,2,1,0:T(8,128)(2,1)} %cubes.1), channel_id=1, source_target_pairs={{1,2},{2,1},{3,4},{4,3},{5,6},{6,5},{9,10},{10,9},{11,12},{12,11},... | collective-permute-start | bytes 1572872 | tf_op jit(solution)/shard_map/ppermute | solution.py:484
  1.3 4.4 %collective-permute-start = (bf16[2,4,32,1024]{3,2,1,0:T(8,128)(2,1)}, bf16[2,4,32,1024]{3,2,1,0:T(8,128)(2,1)S(1)}, u32[]{:S(2)}, u32[]{:S(2)}) collective-permute-start(bf16[2,4,32,1024]{3,2,1,0:T(8,128)(2,1)} %cubes.1), channel_id=1, source_target_pairs={{0,1},{1,0},{2,3},{3,2},{4,5},{5,4},{6,7},{7,6},{8,9},{9,8},{10,11... | collective-permute-start | bytes 1572872 | tf_op jit(solution)/shard_map/ppermute | solution.py:484
  5.8 1.0 %copy-done = bf16[27,8192]{1,0:T(8,128)(2,1)S(1)} copy-done((bf16[27,8192]{1,0:T(8,128)(2,1)S(1)}, bf16[27,8192]{1,0:T(8,128)(2,1)}, u32[]{:S(2)}) %copy-start) | copy-done | bytes 442392
  6.8 1.0 %copy-done.1 = bf16[2,4,32,1024]{3,2,1,0:T(8,128)(2,1)S(1)} copy-done((bf16[2,4,32,1024]{3,2,1,0:T(8,128)(2,1)S(1)}, bf16[2,4,32,1024]{3,2,1,0:T(8,128)(2,1)}, u32[]{:S(2)}) %copy-start.1) | copy-done | bytes 524312
  7.8 0.9 %copy-done.2 = bf16[27,2048]{1,0:T(8,128)(2,1)S(1)} copy-done((bf16[27,2048]{1,0:T(8,128)(2,1)S(1)}, bf16[27,2048]{1,0:T(8,128)(2,1)}, u32[]{:S(2)}) %copy-start.2) | copy-done | bytes 110616
  8.7 4.0 %shard_map.67 = (bf16[2,10,4,16,1152]{4,3,2,1,0:T(8,128)(2,1)S(1)}, bf16[2304,256]{1,0:T(8,128)(2,1)S(1)}, bf16[2304,256]{1,0:T(8,128)(2,1)S(1)}, bf16[2,6,2,16,...) custom-call(bf16[2,4,32,1024]{3,2,1,0:T(8,128)(2,1)S(1)} %copy-done., ...), custom_call_target="tpu_custom_call" | custom-call | flops 1000000000 | bytes 1000000 | tf_op jit(solution)/shard_map/pallas_call | solution.py:469
  12.8 6.4 %shard_map.68 = (bf16[2,10,4,16,1152]{4,3,2,1,0:T(8,128)(2,1)S(1)}, bf16[2,6,2,16,2048]{4,3,2,1,0:T(8,128)(2,1)S(1)}, bf16[2,4,3,16,1152]{4,3,2,1,0:T(8,128)(2,1)S(1)}, bf16[2,2,16,2048]{3,2,1,0:T(8,128)(2,1)S(1)}) custom-call(s32[3]{0:T(128)S(1)} %pad_add_fusion.where, ...), custom_call_target="tpu_custom_call", output_to_operand_aliasing={{0}: (1, {}), {1}: (2, {})} | custom-call | flops 8000000000 | bytes 1000000 | tf_op jit(solution)/shard_map/pallas_call | solution.py:469
  19.2 0.9 %collective-permute-start.3 = (bf16[2,2,16,2048]{3,2,1,0:T(8,128)(2,1)S(1)}, bf16[2,2,16,2048]{3,2,1,0:T(8,128)(2,1)S(1)}, u32[]{:S(2)}, u32[]{:S(2)}) collective-permute-start(bf16[2,2,16,2048]{3,2,1,0:T(8,128)(2,1)S(1)} %get-tuple-element.39.grad_b), channel_id=1, source_target_pairs={{1,2},{2,1},{3,4},{4,3},{5,6},{6,5},{9,10},{10,9},{11,12},{12,11},... | collective-permute-start | bytes 786440 | tf_op jit(solution)/shard_map/ppermute | solution.py:484
  20.1 3.0 %collective-permute-start.2 = (bf16[2,2,16,2048]{3,2,1,0:T(8,128)(2,1)S(1)}, bf16[2,2,16,2048]{3,2,1,0:T(8,128)(2,1)S(1)}, u32[]{:S(2)}, u32[]{:S(2)}) collective-permute-start(bf16[2,2,16,2048]{3,2,1,0:T(8,128)(2,1)S(1)} %get-tuple-element.39.grad_b), channel_id=1, source_target_pairs={{0,1},{1,0},{2,3},{3,2},{4,5},{5,4},{6,7},{7,6},{8,9},{9,8},{10,11... | collective-permute-start | bytes 786440 | tf_op jit(solution)/shard_map/ppermute | solution.py:484
  23.1 1.7 %shard_map.69 = (f32[1792,128]{1,0:T(8,128)S(1)}, bf16[2,6,3,16,2304]{4,3,2,1,0:T(8,128)(2,1)S(1)}, bf16[6912,256]{1,0:T(8,128)(2,1)S(1)}, bf16[6912,256]{1,0:T(8,128)(2,1)S(1)}) custom-call(bf16[2,4,3,16,1152]{4,3,2,1,0:T(8,128)(2,1)S(1)} %get-tuple-element.38.pools, bf16[2,2,16,2048]{3,2,1,0:T(8,128)(2,1)S(1)} %get-tuple-element.39.grad_b, ...), custom_call_target="tpu_custom_call" | custom-call | flops 1000000000 | bytes 1000000 | tf_op jit(solution)/shard_map/pallas_call | solution.py:469
  24.8 7.6 %shard_map.70 = (bf16[2,6,4,16,2304]{4,3,2,1,0:T(8,128)(2,1)S(1)}, bf16[4,280,128]{2,1,0:T(8,128)(2,1)S(1)}, bf16[4,280,128]{2,1,0:T(8,128)(2,1)S(1)}, bf16[2,6,3,16,2304]{4,3,2,1,0:T(8,128)(2,1)S(1)}) custom-call(s32[3]{0:T(128)S(1)} %pad_add_fusion.where, bf16[2,6,3,16,2304]{4,3,2,1,0:T(8,128)(2,1)S(1)} %get-tuple-element.42.own, ...), custom_call_target="tpu_custom_call", output_to_operand_aliasing={{3}: (1, {})} | custom-call | flops 6000000000 | bytes 1000000 | tf_op jit(solution)/shard_map/pallas_call | solution.py:469
  32.4 2.2 %collective-permute-start.4 = (bf16[4,280,128]{2,1,0:T(8,128)(2,1)S(1)}, bf16[4,280,128]{2,1,0:T(8,128)(2,1)S(1)}, u32[]{:S(2)}, u32[]{:S(2)}) collective-permute-start(bf16[4,280,128]{2,1,0:T(8,128)(2,1)S(1)} %get-tuple-element.52), channel_id=1, source_target_pairs={{0,1},{1,0},{2,3},{3,2},{4,5},{5,4},{6,7},{7,6},{8,9},{9,8},{10,11... | collective-permute-start | bytes 860168 | tf_op jit(solution)/shard_map/ppermute | solution.py:490
  34.6 1.2 %collective-permute-done.4.recv = bf16[4,280,128]{2,1,0:T(8,128)(2,1)S(1)} collective-permute-done((bf16[4,280,128]{2,1,0:T(8,128)(2,1)S(1)}, bf16[4,280,128]{2,1,0:T(8,128)(2,1)S(1)}, u32[]{:S(2)}, u32[]{:S(2)}) %collective-permute-start.4) | collective-permute-done | bytes 286752 | tf_op jit(solution)/shard_map/ppermute | solution.py:490
  35.8 0.6 shard_map.73
  36.4 1.6 %collective-permute-start.5 = (bf16[280,128]{1,0:T(8,128)(2,1)S(1)}, bf16[280,128]{1,0:T(8,128)(2,1)S(1)}, u32[]{:S(2)}, u32[]{:S(2)}) collective-permute-start(bf16[280,128]{1,0:T(8,128)(2,1)S(1)} %get-tuple-element.54), channel_id=1, source_target_pairs={{0,8},{8,0},{16,24},{24,16},{1,9},{9,1},{17,25},{25,17},{2,10},{10... | collective-permute-start | bytes 215048 | tf_op jit(solution)/shard_map/ppermute | solution.py:490
  38.0 1.5 %collective-permute-start.6 = (bf16[280,128]{1,0:T(8,128)(2,1)S(1)}, bf16[280,128]{1,0:T(8,128)(2,1)S(1)}, u32[]{:S(2)}, u32[]{:S(2)}) collective-permute-start(bf16[280,128]{1,0:T(8,128)(2,1)S(1)} %get-tuple-element.55), channel_id=1, source_target_pairs={{0,16},{8,24},{16,0},{24,8},{1,17},{9,25},{17,1},{25,9},{2,18},{10... | collective-permute-start | bytes 215048 | tf_op jit(solution)/shard_map/ppermute | solution.py:490
  39.5 0.5 collective-permute-start.7
  40.0 2.3 %shard_map.71.rest_0_.after = bf16[4,32,1024]{2,1,0:T(8,128)(2,1)S(1)} custom-call(bf16[2,6,4,16,2304]{4,3,2,1,0:T(8,128)(2,1)S(1)} %get-tuple-element.47.ga, bf16[6912,256]{1,0:T(8,128)(2,1)S(1)} %get-tuple-element.48.tat), custom_call_target="tpu_custom_call" | custom-call | flops 2000000000 | bytes 1000000 | tf_op jit(solution)/shard_map/pallas_call | solution.py:469
  42.3 2.4 %collective-permute-done.7.refs_3_ = bf16[280,128]{1,0:T(8,128)(2,1)S(1)} collective-permute-done((bf16[280,128]{1,0:T(8,128)(2,1)S(1)}, bf16[280,128]{1,0:T(8,128)(2,1)S(1)}, u32[]{:S(2)}, u32[]{:S(2)}) %collective-permute-start.7) | collective-permute-done | bytes 71712 | tf_op jit(solution)/shard_map/ppermute | solution.py:490
  44.8 4.0 %collective-permute-start.10 = (bf16[280,128]{1,0:T(8,128)(2,1)S(1)}, bf16[280,128]{1,0:T(8,128)(2,1)S(1)}, u32[]{:S(2)}, u32[]{:S(2)}) collective-permute-start(bf16[280,128]{1,0:T(8,128)(2,1)S(1)} %shard_map.74.refs_0_), channel_id=1, source_target_pairs={{0,6},{1,7},{2,4},{3,5},{4,2},{5,3},{6,0},{7,1},{8,14},{9,15},{10,... | collective-permute-start | bytes 215048 | tf_op jit(solution)/shard_map/ppermute | solution.py:490
  48.7 0.6 collective-permute-start.8
  49.4 3.0 %shard_map.72 = (bf16[2,4,32,1024]{3,2,1,0:T(8,128)(2,1)}, f32[8,128]{1,0:T(8,128)S(1)}) custom-call(bf16[2,6,4,16,2304]{4,3,2,1,0:T(8,128)(2,1)S(1)} %get-tuple-element.47.ga, bf16[6912,256]{1,0:T(8,128)(2,1)S(1)} %get-tuple-element.48.tat, bf16[4,32,1024]{2,1,0:T(8,128)(2,1)S(1)} %shard_map.71.rest_0_.after), custom_call_target="tpu_custom_call" | custom-call | flops 2000000000 | bytes 1000000 | tf_op jit(solution)/shard_map/pallas_call | solution.py:469
  52.3 1.7 %collective-permute-done.9.refs_2_ = bf16[280,128]{1,0:T(8,128)(2,1)S(1)} collective-permute-done((bf16[280,128]{1,0:T(8,128)(2,1)S(1)}, bf16[280,128]{1,0:T(8,128)(2,1)S(1)}, u32[]{:S(2)}, u32[]{:S(2)}) %collective-permute-start.9) | collective-permute-done | bytes 71712 | tf_op jit(solution)/shard_map/ppermute | solution.py:490
  54.0 1.0 %collective-permute-start.13 = (bf16[280,128]{1,0:T(8,128)(2,1)S(1)}, bf16[280,128]{1,0:T(8,128)(2,1)S(1)}, u32[]{:S(2)}, u32[]{:S(2)}) collective-permute-start(bf16[280,128]{1,0:T(8,128)(2,1)S(1)} %shard_map.75.refs_0_), channel_id=1, source_target_pairs={{0,24},{8,16},{16,8},{24,0},{1,25},{9,17},{17,9},{25,1},{2,26},{10... | collective-permute-start | bytes 215048 | tf_op jit(solution)/shard_map/ppermute | solution.py:490
  55.0 1.3 %collective-permute-start.12 = (bf16[280,128]{1,0:T(8,128)(2,1)S(1)}, bf16[280,128]{1,0:T(8,128)(2,1)S(1)}, u32[]{:S(2)}, u32[]{:S(2)}) collective-permute-start(bf16[280,128]{1,0:T(8,128)(2,1)S(1)} %shard_map.75.refs_0_), channel_id=1, source_target_pairs={{0,16},{8,24},{16,0},{24,8},{1,17},{9,25},{17,1},{25,9},{2,18},{10... | collective-permute-start | bytes 215048 | tf_op jit(solution)/shard_map/ppermute | solution.py:490
  56.3 1.3 %collective-permute-start.11 = (bf16[280,128]{1,0:T(8,128)(2,1)S(1)}, bf16[280,128]{1,0:T(8,128)(2,1)S(1)}, u32[]{:S(2)}, u32[]{:S(2)}) collective-permute-start(bf16[280,128]{1,0:T(8,128)(2,1)S(1)} %shard_map.75.refs_0_), channel_id=1, source_target_pairs={{0,8},{8,0},{16,24},{24,16},{1,9},{9,1},{17,25},{25,17},{2,10},{10... | collective-permute-start | bytes 215048 | tf_op jit(solution)/shard_map/ppermute | solution.py:490
  57.6 1.9 %collective-permute-done.13.refs_3_ = bf16[280,128]{1,0:T(8,128)(2,1)S(1)} collective-permute-done((bf16[280,128]{1,0:T(8,128)(2,1)S(1)}, bf16[280,128]{1,0:T(8,128)(2,1)S(1)}, u32[]{:S(2)}, u32[]{:S(2)}) %collective-permute-start.13) | collective-permute-done | bytes 71712 | tf_op jit(solution)/shard_map/ppermute | solution.py:490
  59.5 0.6 collective-permute-done.12.refs_2_
  60.1 0.5 collective-permute-done.11.refs_1_
  60.6 0.6 shard_map.76.own
  61.3 1.6 %collective-permute-done.14.other = bf16[4,280,128]{2,1,0:T(8,128)(2,1)S(1)} collective-permute-done((bf16[4,280,128]{2,1,0:T(8,128)(2,1)S(1)}, bf16[4,280,128]{2,1,0:T(8,128)(2,1)S(1)}, u32[]{:S(2)}, u32[]{:S(2)}) %collective-permute-start.14) | collective-permute-done | bytes 286752 | tf_op jit(solution)/shard_map/ppermute | solution.py:490
  62.8 1.7 %shard_map.77 = (f32[27,2048]{1,0:T(8,128)}, f32[27,8192]{1,0:T(8,128)}) custom-call(s32[3]{0:T(128)S(1)} %pad_add_fusion.where, f32[1]{0:T(128)} %constant.11.clone.1.scale, bf16[4,280,128]{2,1,0:T(8,128)(2,1)S(1)} %shard_map.76.own, bf16[4,280,128]{2,1,0:T(8,128)(2,1)S(1)} %collective-permute-done.14.other), custom_call_target="tpu_custom_call" | custom-call | flops 1000000 | bytes 1000000 | tf_op jit(solution)/shard_map/pallas_call | solution.py:469
  (18 shorter events, 0.3 us)
Async XLA Ops:
  0.6 12.2 %collective-permute-start.1 = (bf16[2,4,32,1024]{3,2,1,0:T(8,128)(2,1)}, bf16[2,4,32,1024]{3,2,1,0:T(8,128)(2,1)S(1)}, u32[]{:S(2)}, u32[]{:S(2)}) collective-permute-start(bf16[2,4,32,1024]{3,2,1,0:T(8,128)(2,1)} %cubes.1), channel_id=1, source_target_pairs={{1,2},{2,1},{3,4},{4,3},{5,6},{6,5},{9,10},{10,9},{11,12},{12,11},... | collective-permute-start | bytes 1572872 | tf_op jit(solution)/shard_map/ppermute | solution.py:484
  1.3 11.5 %collective-permute-start = (bf16[2,4,32,1024]{3,2,1,0:T(8,128)(2,1)}, bf16[2,4,32,1024]{3,2,1,0:T(8,128)(2,1)S(1)}, u32[]{:S(2)}, u32[]{:S(2)}) collective-permute-start(bf16[2,4,32,1024]{3,2,1,0:T(8,128)(2,1)} %cubes.1), channel_id=1, source_target_pairs={{0,1},{1,0},{2,3},{3,2},{4,5},{5,4},{6,7},{7,6},{8,9},{9,8},{10,11... | collective-permute-start | bytes 1572872 | tf_op jit(solution)/shard_map/ppermute | solution.py:484
  5.8 1.0 %copy-start = (bf16[27,8192]{1,0:T(8,128)(2,1)S(1)}, bf16[27,8192]{1,0:T(8,128)(2,1)}, u32[]{:S(2)}) copy-start(bf16[27,8192]{1,0:T(8,128)(2,1)} %weight_b.1) | copy-start | bytes 1327108
  6.8 1.0 %copy-start.1 = (bf16[2,4,32,1024]{3,2,1,0:T(8,128)(2,1)S(1)}, bf16[2,4,32,1024]{3,2,1,0:T(8,128)(2,1)}, u32[]{:S(2)}) copy-start(bf16[2,4,32,1024]{3,2,1,0:T(8,128)(2,1)} %cubes.1) | copy-start | bytes 1572868
  7.8 0.9 %copy-start.2 = (bf16[27,2048]{1,0:T(8,128)(2,1)S(1)}, bf16[27,2048]{1,0:T(8,128)(2,1)}, u32[]{:S(2)}) copy-start(bf16[27,2048]{1,0:T(8,128)(2,1)} %weight_a.1) | copy-start | bytes 331780
  8.7 4.1 %copy-start.3 = (bf16[2,1,8,1024]{3,2,1,0:T(8,128)(2,1)S(1)}, bf16[2,1,8,1024]{3,2,1,0:T(8,128)(2,1)}, u32[]{:S(2)}) copy-start(bf16[2,1,8,1024]{3,2,1,0:T(8,128)(2,1)} %cot.1) | copy-start | bytes 98308
  19.2 5.6 %collective-permute-start.3 = (bf16[2,2,16,2048]{3,2,1,0:T(8,128)(2,1)S(1)}, bf16[2,2,16,2048]{3,2,1,0:T(8,128)(2,1)S(1)}, u32[]{:S(2)}, u32[]{:S(2)}) collective-permute-start(bf16[2,2,16,2048]{3,2,1,0:T(8,128)(2,1)S(1)} %get-tuple-element.39.grad_b), channel_id=1, source_target_pairs={{1,2},{2,1},{3,4},{4,3},{5,6},{6,5},{9,10},{10,9},{11,12},{12,11},... | collective-permute-start | bytes 786440 | tf_op jit(solution)/shard_map/ppermute | solution.py:484
  20.1 4.8 %collective-permute-start.2 = (bf16[2,2,16,2048]{3,2,1,0:T(8,128)(2,1)S(1)}, bf16[2,2,16,2048]{3,2,1,0:T(8,128)(2,1)S(1)}, u32[]{:S(2)}, u32[]{:S(2)}) collective-permute-start(bf16[2,2,16,2048]{3,2,1,0:T(8,128)(2,1)S(1)} %get-tuple-element.39.grad_b), channel_id=1, source_target_pairs={{0,1},{1,0},{2,3},{3,2},{4,5},{5,4},{6,7},{7,6},{8,9},{9,8},{10,11... | collective-permute-start | bytes 786440 | tf_op jit(solution)/shard_map/ppermute | solution.py:484
  32.4 3.4 %collective-permute-start.4 = (bf16[4,280,128]{2,1,0:T(8,128)(2,1)S(1)}, bf16[4,280,128]{2,1,0:T(8,128)(2,1)S(1)}, u32[]{:S(2)}, u32[]{:S(2)}) collective-permute-start(bf16[4,280,128]{2,1,0:T(8,128)(2,1)S(1)} %get-tuple-element.52), channel_id=1, source_target_pairs={{0,1},{1,0},{2,3},{3,2},{4,5},{5,4},{6,7},{7,6},{8,9},{9,8},{10,11... | collective-permute-start | bytes 860168 | tf_op jit(solution)/shard_map/ppermute | solution.py:490
  36.4 5.9 %collective-permute-start.5 = (bf16[280,128]{1,0:T(8,128)(2,1)S(1)}, bf16[280,128]{1,0:T(8,128)(2,1)S(1)}, u32[]{:S(2)}, u32[]{:S(2)}) collective-permute-start(bf16[280,128]{1,0:T(8,128)(2,1)S(1)} %get-tuple-element.54), channel_id=1, source_target_pairs={{0,8},{8,0},{16,24},{24,16},{1,9},{9,1},{17,25},{25,17},{2,10},{10... | collective-permute-start | bytes 215048 | tf_op jit(solution)/shard_map/ppermute | solution.py:490
  38.0 4.3 %collective-permute-start.6 = (bf16[280,128]{1,0:T(8,128)(2,1)S(1)}, bf16[280,128]{1,0:T(8,128)(2,1)S(1)}, u32[]{:S(2)}, u32[]{:S(2)}) collective-permute-start(bf16[280,128]{1,0:T(8,128)(2,1)S(1)} %get-tuple-element.55), channel_id=1, source_target_pairs={{0,16},{8,24},{16,0},{24,8},{1,17},{9,25},{17,1},{25,9},{2,18},{10... | collective-permute-start | bytes 215048 | tf_op jit(solution)/shard_map/ppermute | solution.py:490
  39.5 5.2 %collective-permute-start.7 = (bf16[280,128]{1,0:T(8,128)(2,1)S(1)}, bf16[280,128]{1,0:T(8,128)(2,1)S(1)}, u32[]{:S(2)}, u32[]{:S(2)}) collective-permute-start(bf16[280,128]{1,0:T(8,128)(2,1)S(1)} %get-tuple-element.56), channel_id=1, source_target_pairs={{0,24},{8,16},{16,8},{24,0},{1,25},{9,17},{17,9},{25,1},{2,26},{10... | collective-permute-start | bytes 215048 | tf_op jit(solution)/shard_map/ppermute | solution.py:490
  44.8 7.6 %collective-permute-start.10 = (bf16[280,128]{1,0:T(8,128)(2,1)S(1)}, bf16[280,128]{1,0:T(8,128)(2,1)S(1)}, u32[]{:S(2)}, u32[]{:S(2)}) collective-permute-start(bf16[280,128]{1,0:T(8,128)(2,1)S(1)} %shard_map.74.refs_0_), channel_id=1, source_target_pairs={{0,6},{1,7},{2,4},{3,5},{4,2},{5,3},{6,0},{7,1},{8,14},{9,15},{10,... | collective-permute-start | bytes 215048 | tf_op jit(solution)/shard_map/ppermute | solution.py:490
  48.7 5.3 %collective-permute-start.9 = (bf16[280,128]{1,0:T(8,128)(2,1)S(1)}, bf16[280,128]{1,0:T(8,128)(2,1)S(1)}, u32[]{:S(2)}, u32[]{:S(2)}) collective-permute-start(bf16[280,128]{1,0:T(8,128)(2,1)S(1)} %shard_map.74.refs_0_), channel_id=1, source_target_pairs={{0,4},{1,5},{2,6},{3,7},{4,0},{5,1},{6,2},{7,3},{8,12},{9,13},{10,... | collective-permute-start | bytes 215048 | tf_op jit(solution)/shard_map/ppermute | solution.py:490
  48.7 5.3 %collective-permute-start.8 = (bf16[280,128]{1,0:T(8,128)(2,1)S(1)}, bf16[280,128]{1,0:T(8,128)(2,1)S(1)}, u32[]{:S(2)}, u32[]{:S(2)}) collective-permute-start(bf16[280,128]{1,0:T(8,128)(2,1)S(1)} %shard_map.74.refs_0_), channel_id=1, source_target_pairs={{0,2},{1,3},{2,0},{3,1},{4,6},{5,7},{6,4},{7,5},{8,10},{9,11},{10,... | collective-permute-start | bytes 215048 | tf_op jit(solution)/shard_map/ppermute | solution.py:490
  54.0 5.5 %collective-permute-start.13 = (bf16[280,128]{1,0:T(8,128)(2,1)S(1)}, bf16[280,128]{1,0:T(8,128)(2,1)S(1)}, u32[]{:S(2)}, u32[]{:S(2)}) collective-permute-start(bf16[280,128]{1,0:T(8,128)(2,1)S(1)} %shard_map.75.refs_0_), channel_id=1, source_target_pairs={{0,24},{8,16},{16,8},{24,0},{1,25},{9,17},{17,9},{25,1},{2,26},{10... | collective-permute-start | bytes 215048 | tf_op jit(solution)/shard_map/ppermute | solution.py:490
  55.0 5.1 %collective-permute-start.12 = (bf16[280,128]{1,0:T(8,128)(2,1)S(1)}, bf16[280,128]{1,0:T(8,128)(2,1)S(1)}, u32[]{:S(2)}, u32[]{:S(2)}) collective-permute-start(bf16[280,128]{1,0:T(8,128)(2,1)S(1)} %shard_map.75.refs_0_), channel_id=1, source_target_pairs={{0,16},{8,24},{16,0},{24,8},{1,17},{9,25},{17,1},{25,9},{2,18},{10... | collective-permute-start | bytes 215048 | tf_op jit(solution)/shard_map/ppermute | solution.py:490
  56.3 4.3 %collective-permute-start.11 = (bf16[280,128]{1,0:T(8,128)(2,1)S(1)}, bf16[280,128]{1,0:T(8,128)(2,1)S(1)}, u32[]{:S(2)}, u32[]{:S(2)}) collective-permute-start(bf16[280,128]{1,0:T(8,128)(2,1)S(1)} %shard_map.75.refs_0_), channel_id=1, source_target_pairs={{0,8},{8,0},{16,24},{24,16},{1,9},{9,1},{17,25},{25,17},{2,10},{10... | collective-permute-start | bytes 215048 | tf_op jit(solution)/shard_map/ppermute | solution.py:490
  61.2 1.6 %collective-permute-start.14 = (bf16[4,280,128]{2,1,0:T(8,128)(2,1)S(1)}, bf16[4,280,128]{2,1,0:T(8,128)(2,1)S(1)}, u32[]{:S(2)}, u32[]{:S(2)}) collective-permute-start(bf16[4,280,128]{2,1,0:T(8,128)(2,1)S(1)} %shard_map.76.own), channel_id=1, source_target_pairs={{0,1},{1,0},{2,3},{3,2},{4,5},{5,4},{6,7},{7,6},{8,9},{9,8},{10,11... | collective-permute-start | bytes 860168 | tf_op jit(solution)/shard_map/ppermute | solution.py:490

commit v10 on v9

--- a/solution.py
+++ b/solution.py
@@ -149,7 +149,7 @@
     for b in range(cube_count):
         for z in range(HALO):
             far = ZD - HALO + z
-            below = jnp.where(even, recv_b[b, far].astype(F32), recv_a[b, far].astype(F32)).astype(BF)
+            below = jnp.where(even, recv_b[b, z].astype(F32), recv_a[b, far].astype(F32)).astype(BF)
             above = jnp.where(even, recv_a[b, z].astype(F32), recv_b[b, z].astype(F32)).astype(BF)
             spread_input(xs, b, z, below, picker)
             spread_input(xs, b, HALO + ZD + z, above, picker)
@@ -238,7 +238,7 @@
         target[b, zz, v, :, 2176:] = jnp.zeros((16, 128), BF)
 
 
-def terms_b_kernel(pools, grad_b, wa, wb, terms, gs, tat, tbt):
+def terms_b_kernel(pools, grad_b, wa, wb, terms, gs, tat, tbt, back):
     cube_count = grad_b.shape[0]
     shifter = row_picker(3, 1, 16)
     for b in range(cube_count):
@@ -276,6 +276,27 @@
                 term = full[64 * dx : 64 * dx + 64, :128] + full[64 * dx + 64 : 64 * dx + 128, 128:]
                 terms[pl.ds(9 * dz + 3 * dy + dx, C2, stride=28), :] = term
 
+    sources = windows_b(gs, ((2, 2),))
+    given = [
+        dot(sources, tbt[2304 * dz : 2304 * dz + 2304]).reshape(4, cube_count, 2, 16, 256) for dz in range(3)
+    ]
+    back[:, :, 0] = given[2][:, :, 0]
+    back[:, :, 1] = given[1][:, :, 0] + given[2][:, :, 1]
+    back[:, :, 2] = given[0][:, :, 0] + given[1][:, :, 1]
+    back[:, :, 3] = given[0][:, :, 1]
+
+
+def windows_b(gs, spans):
+    columns = []
+    for dy in range(3):
+        stacks = []
+        for q in range(4):
+            parts = [gs[:, first : first + planes, dy, :, 512 * q : 512 * q + 768] for first, planes in spans]
+            whole = jnp.concatenate(parts, axis=1) if len(parts) > 1 else parts[0]
+            stacks.append(whole.reshape(whole.shape[0] * whole.shape[1] * 16, 768))
+        columns.append(jnp.concatenate(stacks, axis=0))
+    return jnp.concatenate(columns, axis=1)
+
 
 def tree(parts):
     while len(parts) > 1:
@@ -301,20 +322,31 @@
         out[where[2] ^ k] = part[...]
 
 
-def finish_kernel(where, scale, own, other, out_a, out_b, whole):
-    core = where[0] % 2
-    whole[core] = own[...].astype(F32)
-    whole[1 - core] = other[...].astype(F32)
-    count = own.shape[0]
+def lay_out(pieces, scale, out_a, out_b, whole):
+    whole[...] = pieces[...].astype(F32) * scale
+    count = pieces.shape[0]
     for width, base, out in ((C2, 0, out_b), (C1 // 2, ROWS_B // (2 * count), out_a)):
         each = width // (2 * count)
-        for i in range(width):
+        for i in range(width // 2):
             start = base + 28 * (i % each)
-            piece = whole[i // each // count, i // each % count, start : start + 27]
-            out[:, 128 * i : 128 * i + 128] = piece * scale[0]
-
-
-def backward_kernel(where, own, recv_a, recv_b, tbt, dsl, xs, terms_b, ga, keep, send, gs, gpool, acc, term, terms):
+            out[:, 128 * i : 128 * i + 128] = whole[i // each, start : start + 27]
+
+
+def first_half_kernel(scale, pieces, out_a, out_b, whole):
+    lay_out(pieces, scale[0], out_a, out_b, whole)
+
+
+def finish_kernel(where, scale, pieces, own_a, own_b, out_a, out_b, whole, other_a, other_b):
+    lay_out(pieces, scale[0], other_a, other_b, whole)
+    low = where[0] % 2 == 0
+    for own, other, out in ((own_a, other_a, out_a), (own_b, other_b, out_b)):
+        width = own.shape[1]
+        mine, theirs = own[...], other[...]
+        out[:, :width] = jnp.where(low, mine, theirs)
+        out[:, width:] = jnp.where(low, theirs, mine)
+
+
+def backward_kernel(where, own, recv_a, recv_b, tbt, dsl, xs, terms_b, back, ga, keep, send, gs, gpool, acc, term, terms):
     del own
     cube_count = recv_a.shape[0]
     even = where[0] % 2 == 0
@@ -328,22 +360,21 @@
 
     low = jnp.where(where[0] == 0, 0.0, 0.125)
     high = jnp.where(where[0] == where[1] - 1, 0.0, 0.125)
-    rows = cube_count * 4 * 16
-    columns = []
-    for dz in range(3):
-        for dy in range(3):
-            columns.append(
-                jnp.concatenate(
-                    [gs[:, dz : dz + 4, dy, :, 512 * q : 512 * q + 768].reshape(rows, 768) for q in range(4)],
-                    axis=0,
-                )
-            )
-    back = dot(jnp.concatenate(columns, axis=1), tbt[...])
-    for q in range(4):
-        part = back[rows * q : rows * q + rows].reshape(cube_count, 4, 16, 256)
-        for z in range(4):
-            scale = low if z == 0 else high if z == 3 else 0.125
-            gpool[:, z, :, 256 * q : 256 * q + 256] = part[:, z] * scale
+    parts = [
+        dot(windows_b(gs, spans), tbt[2304 * dz : 2304 * dz + 2304]).reshape(4, cube_count, 2, 16, 256)
+        for dz, spans in enumerate((((0, 2),), ((1, 1), (4, 1)), ((4, 2),)))
+    ]
+    extra = (
+        parts[0][:, :, 0] + parts[1][:, :, 0],
+        parts[0][:, :, 1],
+        parts[2][:, :, 0],
+        parts[1][:, :, 1] + parts[2][:, :, 1],
+    )
+    for z in range(4):
+        scale = low if z == 0 else high if z == 3 else 0.125
+        total = (back[:, :, z] + extra[z]) * scale
+        for q in range(4):
+            gpool[:, z, :, 256 * q : 256 * q + 256] = total[q]
 
     ga[:, :, :, :, :128] = jnp.zeros((cube_count, 6, 4, 16, 128), BF)
     ga[:, :, :, :, 2176:] = jnp.zeros((cube_count, 6, 4, 16, 128), BF)
@@ -496,7 +527,8 @@
     ring = lax.axis_size("gz")
     samples = lax.axis_size("sample")
     where = jnp.stack([lax.axis_index("gz"), jnp.int32(ring), lax.axis_index("sample")]).astype(jnp.int32)
-    recv_a, recv_b = swap(cubes, cubes, ring)
+    outer = lax.dynamic_slice_in_dim(cubes, lax.axis_index("gz") % 2, HALO, axis=1)
+    recv_a, recv_b = swap(cubes, outer, ring)
 
     own_xs, ta, tb, own_slope, inner, edge_low, edge_high, wa, wb = call(
         prepare_kernel,
@@ -532,14 +564,18 @@
     back_a, back_b = swap(grad_b, grad_b, ring)
     spread = ((cube_count, 6, 3, 16, 2304), BF)
     wide = ((6912, 256), BF)
-    terms_b, own_gs, tat, tbt = call(
-        terms_b_kernel, [pools, grad_b, wa, wb], [((ROWS_B, 128), F32), spread, wide, wide], [], 1_000_000_000
+    terms_b, own_gs, tat, tbt, back = call(
+        terms_b_kernel,
+        [pools, grad_b, wa, wb],
+        [((ROWS_B, 128), F32), spread, wide, wide, ((4, cube_count, 4, 16, 256), F32)],
+        [],
+        1_000_000_000,
     )
     piece = (ROWS_A + ROWS_B) // (2 * samples)
     pieces = ((samples, piece, 128), BF)
     ga, keep, send, _ = call(
         backward_kernel,
-        [where, own_gs, back_a, back_b, tbt, dsl, xs, terms_b],
+        [where, own_gs, back_a, back_b, tbt, dsl, xs, terms_b, back],
         [((cube_count, 6, 4, 16, 2304), BF), pieces, pieces, spread],
         [
             pltpu.VMEM((cube_count, 4, 16, 1024), F32),
@@ -575,11 +611,14 @@
     )
     (other,) = swap_along([own] * 2, "gz", 1)
     scale = jnp.full((1,), 1.0 / (cube_count * samples), F32)
+    half_a, half_b = (27, C1 * C2 // 2), (27, C2 * C3 // 2)
+    whole = pltpu.VMEM((samples, piece, 128), F32)
+    own_a, own_b = call(first_half_kernel, [scale, own], [(half_a, F32), (half_b, F32)], [whole], 1_000_000, smem=1)
     total_a, total_b = call(
         finish_kernel,
-        [where, scale, own, other],
+        [where, scale, other, own_a, own_b],
         [((27, C1 * C2), F32), ((27, C2 * C3), F32)],
-        [pltpu.VMEM((2, samples, piece, 128), F32)],
+        [whole, pltpu.VMEM(half_a, F32), pltpu.VMEM(half_b, F32)],
         1_000_000,
         smem=2,
     )

time: 64.8 us -> 64.7 us (level)
  local copies, waits for them, and re-layouts: 2.99 us -> 4.01 us
  starting transfers between devices: 22.9 us -> 22 us
    ppermute x2, starting transfers between devices: 7.41 us -> 5.86 us  [swap(): lax.ppermute(first, 'gz', pairs_a)]
    dynamic_slice x0 -> x1, local copies, waits for them, and re-layouts: none -> 1.02 us  [shards(): lax.dynamic_slice_in_dim(cubes, lax.axis_index('gz') % 2, HALO, axis=1)]
    pallas_call x11 -> x12, Pallas kernels: 27.9 us -> 27.8 us  [call(): pl.pallas_call(kernel, out_shape=[jax.ShapeDtypeStruct(shape, dtype) for...]
  transfers between devices with their start and end apart: 15 -> 15, of which waited for: 7 -> 7; matrix products, arithmetic and copies ran while one was open for 0% -> 2% of each run, Pallas kernels for 17% -> 18%
where the time goes in v10:
time: 64.7 us; the launch traced here: 64.5 us
  Pallas kernels  27.8 us (43%)
  starting transfers between devices  22 us (34%)
  waiting for transfers between devices  9.77 us (15%)
  local copies, waits for them, and re-layouts  4.01 us (6%)
  between operations  0.79 us (1%)
    pallas_call x12, Pallas kernels, call(): pl.pallas_call(kernel, out_shape=[jax.ShapeDtypeStruct(shape, dtype) for...  27.8 us
    ppermute x11, starting transfers between devices, swap_along(): lax.ppermute(part, axis, [(i, i ^ k * step) for i in range(count)])  14.6 us
    ppermute x11, waiting for transfers between devices, swap_along(): lax.ppermute(part, axis, [(i, i ^ k * step) for i in range(count)])  9.76 us
    ppermute x2, starting transfers between devices, swap(): lax.ppermute(first, 'gz', pairs_a)  5.86 us
    unnamed x8, local copies, waits for them, and re-layouts  2.99 us
    ppermute x2, starting transfers between devices, swap(): lax.ppermute(second, 'gz', pairs_b)  1.54 us
  transfers between devices with their start and end apart: 15, of which 7 were waited for; matrix products, arithmetic and copies ran while one was open for 2% of the time, Pallas kernels for 18%

profile of v10, /device:TPU:0, one launch (start us, length us, event | category | flops | bytes accessed | tf_op | source)
XLA Modules:
  0.0 64.5 jit_solution(7528242846036125767)
XLA Ops:
  0.6 0.5 collective-permute-start
  1.2 1.0 %constant_dynamic-slice_fusion = bf16[2,3,32,1024]{3,2,1,0:T(8,128)(2,1)S(1)} fusion(bf16[2,4,32,1024]{3,2,1,0:T(8,128)(2,1)} %cubes.1, s32[]{:T(128)S(6)} %select_n.11), kind=kLoop, calls=%fused_computation.1 | loop fusion | bytes 786436 | tf_op jit(solution)/shard_map/dynamic_slice | solution.py:530
  2.2 0.7 %collective-permute-start.1 = (bf16[2,3,32,1024]{3,2,1,0:T(8,128)(2,1)S(1)}, bf16[2,3,32,1024]{3,2,1,0:T(8,128)(2,1)S(1)}, u32[]{:S(2)}, u32[]{:S(2)}) collective-permute-start(bf16[2,3,32,1024]{3,2,1,0:T(8,128)(2,1)S(1)} %constant_dynamic-slice_fusion), channel_id=1, source_target_pairs={{1,2},{2,1},{3,4},{4,3},{5,6},{6,5},{9,10},{10,9},{11,12},{12,11},... | collective-permute-start | bytes 1179656 | tf_op jit(solution)/shard_map/ppermute | solution.py:515
  2.9 1.0 %copy-done = bf16[2,4,32,1024]{3,2,1,0:T(8,128)(2,1)S(1)} copy-done((bf16[2,4,32,1024]{3,2,1,0:T(8,128)(2,1)S(1)}, bf16[2,4,32,1024]{3,2,1,0:T(8,128)(2,1)}, u32[]{:S(2)}) %copy-start) | copy-done | bytes 524312
  3.9 1.0 %copy-done.1 = bf16[27,8192]{1,0:T(8,128)(2,1)S(1)} copy-done((bf16[27,8192]{1,0:T(8,128)(2,1)S(1)}, bf16[27,8192]{1,0:T(8,128)(2,1)}, u32[]{:S(2)}) %copy-start.1) | copy-done | bytes 442392
  5.0 0.9 %copy-done.2 = bf16[27,2048]{1,0:T(8,128)(2,1)S(1)} copy-done((bf16[27,2048]{1,0:T(8,128)(2,1)S(1)}, bf16[27,2048]{1,0:T(8,128)(2,1)}, u32[]{:S(2)}) %copy-start.2) | copy-done | bytes 110616
  5.9 4.0 %shard_map.67 = (bf16[2,10,4,16,1152]{4,3,2,1,0:T(8,128)(2,1)S(1)}, bf16[2304,256]{1,0:T(8,128)(2,1)S(1)}, bf16[2304,256]{1,0:T(8,128)(2,1)S(1)}, bf16[2,6,2,16,...) custom-call(bf16[2,4,32,1024]{3,2,1,0:T(8,128)(2,1)S(1)} %copy-done,, ...), custom_call_target="tpu_custom_call" | custom-call | flops 1000000000 | bytes 1000000 | tf_op jit(solution)/shard_map/pallas_call | solution.py:500
  10.0 6.4 %shard_map.68 = (bf16[2,10,4,16,1152]{4,3,2,1,0:T(8,128)(2,1)S(1)}, bf16[2,6,2,16,2048]{4,3,2,1,0:T(8,128)(2,1)S(1)}, bf16[2,4,3,16,1152]{4,3,2,1,0:T(8,128)(2,1)S(1)}, bf16[2,2,16,2048]{3,2,1,0:T(8,128)(2,1)S(1)}) custom-call(s32[3]{0:T(128)S(1)} %pad_add_fusion.where, ...), custom_call_target="tpu_custom_call", output_to_operand_aliasing={{0}: (1, {}), {1}: (2, {})} | custom-call | flops 8000000000 | bytes 1000000 | tf_op jit(solution)/shard_map/pallas_call | solution.py:500
  16.3 0.9 %collective-permute-start.3 = (bf16[2,2,16,2048]{3,2,1,0:T(8,128)(2,1)S(1)}, bf16[2,2,16,2048]{3,2,1,0:T(8,128)(2,1)S(1)}, u32[]{:S(2)}, u32[]{:S(2)}) collective-permute-start(bf16[2,2,16,2048]{3,2,1,0:T(8,128)(2,1)S(1)} %get-tuple-element.42.grad_b), channel_id=1, source_target_pairs={{1,2},{2,1},{3,4},{4,3},{5,6},{6,5},{9,10},{10,9},{11,12},{12,11},... | collective-permute-start | bytes 786440 | tf_op jit(solution)/shard_map/ppermute | solution.py:515
  17.2 5.3 %collective-permute-start.2 = (bf16[2,2,16,2048]{3,2,1,0:T(8,128)(2,1)S(1)}, bf16[2,2,16,2048]{3,2,1,0:T(8,128)(2,1)S(1)}, u32[]{:S(2)}, u32[]{:S(2)}) collective-permute-start(bf16[2,2,16,2048]{3,2,1,0:T(8,128)(2,1)S(1)} %get-tuple-element.42.grad_b), channel_id=1, source_target_pairs={{0,1},{1,0},{2,3},{3,2},{4,5},{5,4},{6,7},{7,6},{8,9},{9,8},{10,11... | collective-permute-start | bytes 786440 | tf_op jit(solution)/shard_map/ppermute | solution.py:515
  22.5 2.5 %shard_map.69 = (f32[1792,128]{1,0:T(8,128)S(1)}, bf16[2,6,3,16,2304]{4,3,2,1,0:T(8,128)(2,1)S(1)}, bf16[6912,256]{1,0:T(8,128)(2,1)S(1)}, bf16[6912,256]{1,0:T(8,128)(2,1)S(1)}, f32[4,2,4,16,256]{4,3,2,1,0:T(8,128)S(1)}) custom-call(bf16[2,4,3,16,1152]{4,3,2,1,0:T(8,128)(2,1)S(1)} %get-tuple-element.41.pools, ...), custom_call_target="tpu_custom_call" | custom-call | flops 1000000000 | bytes 1000000 | tf_op jit(solution)/shard_map/pallas_call | solution.py:500
  25.1 6.6 %shard_map.70 = (bf16[2,6,4,16,2304]{4,3,2,1,0:T(8,128)(2,1)S(1)}, bf16[4,280,128]{2,1,0:T(8,128)(2,1)S(1)}, bf16[4,280,128]{2,1,0:T(8,128)(2,1)S(1)}, bf16[2,6,3,16,2304]{4,3,2,1,0:T(8,128)(2,1)S(1)}) custom-call(s32[3]{0:T(128)S(1)} %pad_add_fusion.where, bf16[2,6,3,16,2304]{4,3,2,1,0:T(8,128)(2,1)S(1)} %get-tuple-element.45.own, ...), custom_call_target="tpu_custom_call", output_to_operand_aliasing={{3}: (1, {})} | custom-call | flops 6000000000 | bytes 1000000 | tf_op jit(solution)/shard_map/pallas_call | solution.py:500
  31.7 3.0 %collective-permute-start.4 = (bf16[4,280,128]{2,1,0:T(8,128)(2,1)S(1)}, bf16[4,280,128]{2,1,0:T(8,128)(2,1)S(1)}, u32[]{:S(2)}, u32[]{:S(2)}) collective-permute-start(bf16[4,280,128]{2,1,0:T(8,128)(2,1)S(1)} %get-tuple-element.56), channel_id=1, source_target_pairs={{0,1},{1,0},{2,3},{3,2},{4,5},{5,4},{6,7},{7,6},{8,9},{9,8},{10,11... | collective-permute-start | bytes 860168 | tf_op jit(solution)/shard_map/ppermute | solution.py:521
  34.7 1.2 %collective-permute-done.4.recv = bf16[4,280,128]{2,1,0:T(8,128)(2,1)S(1)} collective-permute-done((bf16[4,280,128]{2,1,0:T(8,128)(2,1)S(1)}, bf16[4,280,128]{2,1,0:T(8,128)(2,1)S(1)}, u32[]{:S(2)}, u32[]{:S(2)}) %collective-permute-start.4) | collective-permute-done | bytes 286752 | tf_op jit(solution)/shard_map/ppermute | solution.py:521
  35.9 0.6 shard_map.73
  36.5 1.6 %collective-permute-start.5 = (bf16[280,128]{1,0:T(8,128)(2,1)S(1)}, bf16[280,128]{1,0:T(8,128)(2,1)S(1)}, u32[]{:S(2)}, u32[]{:S(2)}) collective-permute-start(bf16[280,128]{1,0:T(8,128)(2,1)S(1)} %get-tuple-element.58), channel_id=1, source_target_pairs={{0,8},{8,0},{16,24},{24,16},{1,9},{9,1},{17,25},{25,17},{2,10},{10... | collective-permute-start | bytes 215048 | tf_op jit(solution)/shard_map/ppermute | solution.py:521
  38.1 1.5 %collective-permute-start.6 = (bf16[280,128]{1,0:T(8,128)(2,1)S(1)}, bf16[280,128]{1,0:T(8,128)(2,1)S(1)}, u32[]{:S(2)}, u32[]{:S(2)}) collective-permute-start(bf16[280,128]{1,0:T(8,128)(2,1)S(1)} %get-tuple-element.59), channel_id=1, source_target_pairs={{0,16},{8,24},{16,0},{24,8},{1,17},{9,25},{17,1},{25,9},{2,18},{10... | collective-permute-start | bytes 215048 | tf_op jit(solution)/shard_map/ppermute | solution.py:521
  40.1 2.3 %shard_map.71.rest_0_.after = bf16[4,32,1024]{2,1,0:T(8,128)(2,1)S(1)} custom-call(bf16[2,6,4,16,2304]{4,3,2,1,0:T(8,128)(2,1)S(1)} %get-tuple-element.51.ga, bf16[6912,256]{1,0:T(8,128)(2,1)S(1)} %get-tuple-element.52.tat), custom_call_target="tpu_custom_call" | custom-call | flops 2000000000 | bytes 1000000 | tf_op jit(solution)/shard_map/pallas_call | solution.py:500
  42.4 2.4 %collective-permute-done.7.refs_3_ = bf16[280,128]{1,0:T(8,128)(2,1)S(1)} collective-permute-done((bf16[280,128]{1,0:T(8,128)(2,1)S(1)}, bf16[280,128]{1,0:T(8,128)(2,1)S(1)}, u32[]{:S(2)}, u32[]{:S(2)}) %collective-permute-start.7) | collective-permute-done | bytes 71712 | tf_op jit(solution)/shard_map/ppermute | solution.py:521
  44.9 2.9 %collective-permute-start.10 = (bf16[280,128]{1,0:T(8,128)(2,1)S(1)}, bf16[280,128]{1,0:T(8,128)(2,1)S(1)}, u32[]{:S(2)}, u32[]{:S(2)}) collective-permute-start(bf16[280,128]{1,0:T(8,128)(2,1)S(1)} %shard_map.74.refs_0_), channel_id=1, source_target_pairs={{0,6},{1,7},{2,4},{3,5},{4,2},{5,3},{6,0},{7,1},{8,14},{9,15},{10,... | collective-permute-start | bytes 215048 | tf_op jit(solution)/shard_map/ppermute | solution.py:521
  48.0 1.3 %collective-permute-start.8 = (bf16[280,128]{1,0:T(8,128)(2,1)S(1)}, bf16[280,128]{1,0:T(8,128)(2,1)S(1)}, u32[]{:S(2)}, u32[]{:S(2)}) collective-permute-start(bf16[280,128]{1,0:T(8,128)(2,1)S(1)} %shard_map.74.refs_0_), channel_id=1, source_target_pairs={{0,2},{1,3},{2,0},{3,1},{4,6},{5,7},{6,4},{7,5},{8,10},{9,11},{10,... | collective-permute-start | bytes 215048 | tf_op jit(solution)/shard_map/ppermute | solution.py:521
  49.3 3.0 %shard_map.72 = (bf16[2,4,32,1024]{3,2,1,0:T(8,128)(2,1)}, f32[8,128]{1,0:T(8,128)S(1)}) custom-call(bf16[2,6,4,16,2304]{4,3,2,1,0:T(8,128)(2,1)S(1)} %get-tuple-element.51.ga, bf16[6912,256]{1,0:T(8,128)(2,1)S(1)} %get-tuple-element.52.tat, bf16[4,32,1024]{2,1,0:T(8,128)(2,1)S(1)} %shard_map.71.rest_0_.after), custom_call_target="tpu_custom_call" | custom-call | flops 2000000000 | bytes 1000000 | tf_op jit(solution)/shard_map/pallas_call | solution.py:500
  52.3 1.7 %collective-permute-done.9.refs_2_ = bf16[280,128]{1,0:T(8,128)(2,1)S(1)} collective-permute-done((bf16[280,128]{1,0:T(8,128)(2,1)S(1)}, bf16[280,128]{1,0:T(8,128)(2,1)S(1)}, u32[]{:S(2)}, u32[]{:S(2)}) %collective-permute-start.9) | collective-permute-done | bytes 71712 | tf_op jit(solution)/shard_map/ppermute | solution.py:521
  54.0 0.8 %collective-permute-start.13 = (bf16[280,128]{1,0:T(8,128)(2,1)S(1)}, bf16[280,128]{1,0:T(8,128)(2,1)S(1)}, u32[]{:S(2)}, u32[]{:S(2)}) collective-permute-start(bf16[280,128]{1,0:T(8,128)(2,1)S(1)} %shard_map.75.refs_0_), channel_id=1, source_target_pairs={{0,24},{8,16},{16,8},{24,0},{1,25},{9,17},{17,9},{25,1},{2,26},{10... | collective-permute-start | bytes 215048 | tf_op jit(solution)/shard_map/ppermute | solution.py:521
  54.8 1.4 %collective-permute-start.12 = (bf16[280,128]{1,0:T(8,128)(2,1)S(1)}, bf16[280,128]{1,0:T(8,128)(2,1)S(1)}, u32[]{:S(2)}, u32[]{:S(2)}) collective-permute-start(bf16[280,128]{1,0:T(8,128)(2,1)S(1)} %shard_map.75.refs_0_), channel_id=1, source_target_pairs={{0,16},{8,24},{16,0},{24,8},{1,17},{9,25},{17,1},{25,9},{2,18},{10... | collective-permute-start | bytes 215048 | tf_op jit(solution)/shard_map/ppermute | solution.py:521
  56.2 1.4 %collective-permute-start.11 = (bf16[280,128]{1,0:T(8,128)(2,1)S(1)}, bf16[280,128]{1,0:T(8,128)(2,1)S(1)}, u32[]{:S(2)}, u32[]{:S(2)}) collective-permute-start(bf16[280,128]{1,0:T(8,128)(2,1)S(1)} %shard_map.75.refs_0_), channel_id=1, source_target_pairs={{0,8},{8,0},{16,24},{24,16},{1,9},{9,1},{17,25},{25,17},{2,10},{10... | collective-permute-start | bytes 215048 | tf_op jit(solution)/shard_map/ppermute | solution.py:521
  57.6 1.8 %collective-permute-done.13.refs_3_ = bf16[280,128]{1,0:T(8,128)(2,1)S(1)} collective-permute-done((bf16[280,128]{1,0:T(8,128)(2,1)S(1)}, bf16[280,128]{1,0:T(8,128)(2,1)S(1)}, u32[]{:S(2)}, u32[]{:S(2)}) %collective-permute-start.13) | collective-permute-done | bytes 71712 | tf_op jit(solution)/shard_map/ppermute | solution.py:521
  59.4 0.5 collective-permute-done.12.refs_2_
  59.9 0.6 collective-permute-done.11.refs_1_
  60.5 0.6 shard_map.76.pieces
  61.3 1.5 %collective-permute-done.14.pieces = bf16[4,280,128]{2,1,0:T(8,128)(2,1)S(1)} collective-permute-done((bf16[4,280,128]{2,1,0:T(8,128)(2,1)S(1)}, bf16[4,280,128]{2,1,0:T(8,128)(2,1)S(1)}, u32[]{:S(2)}, u32[]{:S(2)}) %collective-permute-start.14) | collective-permute-done | bytes 286752 | tf_op jit(solution)/shard_map/ppermute | solution.py:521
  62.7 1.7 %shard_map.78 = (f32[27,2048]{1,0:T(8,128)}, f32[27,8192]{1,0:T(8,128)}) custom-call(s32[3]{0:T(128)S(1)} %pad_add_fusion.where, f32[1]{0:T(128)} %constant.27.clone.1.scale, bf16[4,280,128]{2,1,0:T(8,128)(2,1)S(1)} %collective-permute-done.14.pieces, f32[27,1024]{1,0:T(8,128)S(1)} %get-tuple-element.61.own_a, f32[27,4096]{1,0:T(8,128)S(1)} %get-tuple-element.62.own_b), custom_call_target="tpu_custom_call" | custom-call | flops 1000000 | bytes 1000000 | tf_op jit(solution)/shard_map/pallas_call | solution.py:500
  (20 shorter events, 1.1 us)
Async XLA Ops:
  0.6 9.3 %copy-start.3 = (bf16[2,1,8,1024]{3,2,1,0:T(8,128)(2,1)S(1)}, bf16[2,1,8,1024]{3,2,1,0:T(8,128)(2,1)}, u32[]{:S(2)}) copy-start(bf16[2,1,8,1024]{3,2,1,0:T(8,128)(2,1)} %cot.1) | copy-start | bytes 98308
  0.6 9.3 %collective-permute-start = (bf16[2,4,32,1024]{3,2,1,0:T(8,128)(2,1)}, bf16[2,4,32,1024]{3,2,1,0:T(8,128)(2,1)S(1)}, u32[]{:S(2)}, u32[]{:S(2)}) collective-permute-start(bf16[2,4,32,1024]{3,2,1,0:T(8,128)(2,1)} %cubes.1), channel_id=1, source_target_pairs={{0,1},{1,0},{2,3},{3,2},{4,5},{5,4},{6,7},{7,6},{8,9},{9,8},{10,11... | collective-permute-start | bytes 1572872 | tf_op jit(solution)/shard_map/ppermute | solution.py:515
  2.2 7.8 %collective-permute-start.1 = (bf16[2,3,32,1024]{3,2,1,0:T(8,128)(2,1)S(1)}, bf16[2,3,32,1024]{3,2,1,0:T(8,128)(2,1)S(1)}, u32[]{:S(2)}, u32[]{:S(2)}) collective-permute-start(bf16[2,3,32,1024]{3,2,1,0:T(8,128)(2,1)S(1)} %constant_dynamic-slice_fusion), channel_id=1, source_target_pairs={{1,2},{2,1},{3,4},{4,3},{5,6},{6,5},{9,10},{10,9},{11,12},{12,11},... | collective-permute-start | bytes 1179656 | tf_op jit(solution)/shard_map/ppermute | solution.py:515
  2.9 1.0 %copy-start = (bf16[2,4,32,1024]{3,2,1,0:T(8,128)(2,1)S(1)}, bf16[2,4,32,1024]{3,2,1,0:T(8,128)(2,1)}, u32[]{:S(2)}) copy-start(bf16[2,4,32,1024]{3,2,1,0:T(8,128)(2,1)} %cubes.1) | copy-start | bytes 1572868
  3.9 1.0 %copy-start.1 = (bf16[27,8192]{1,0:T(8,128)(2,1)S(1)}, bf16[27,8192]{1,0:T(8,128)(2,1)}, u32[]{:S(2)}) copy-start(bf16[27,8192]{1,0:T(8,128)(2,1)} %weight_b.1) | copy-start | bytes 1327108
  5.0 0.9 %copy-start.2 = (bf16[27,2048]{1,0:T(8,128)(2,1)S(1)}, bf16[27,2048]{1,0:T(8,128)(2,1)}, u32[]{:S(2)}) copy-start(bf16[27,2048]{1,0:T(8,128)(2,1)} %weight_a.1) | copy-start | bytes 331780
  16.3 8.7 %collective-permute-start.3 = (bf16[2,2,16,2048]{3,2,1,0:T(8,128)(2,1)S(1)}, bf16[2,2,16,2048]{3,2,1,0:T(8,128)(2,1)S(1)}, u32[]{:S(2)}, u32[]{:S(2)}) collective-permute-start(bf16[2,2,16,2048]{3,2,1,0:T(8,128)(2,1)S(1)} %get-tuple-element.42.grad_b), channel_id=1, source_target_pairs={{1,2},{2,1},{3,4},{4,3},{5,6},{6,5},{9,10},{10,9},{11,12},{12,11},... | collective-permute-start | bytes 786440 | tf_op jit(solution)/shard_map/ppermute | solution.py:515
  17.2 7.9 %collective-permute-start.2 = (bf16[2,2,16,2048]{3,2,1,0:T(8,128)(2,1)S(1)}, bf16[2,2,16,2048]{3,2,1,0:T(8,128)(2,1)S(1)}, u32[]{:S(2)}, u32[]{:S(2)}) collective-permute-start(bf16[2,2,16,2048]{3,2,1,0:T(8,128)(2,1)S(1)} %get-tuple-element.42.grad_b), channel_id=1, source_target_pairs={{0,1},{1,0},{2,3},{3,2},{4,5},{5,4},{6,7},{7,6},{8,9},{9,8},{10,11... | collective-permute-start | bytes 786440 | tf_op jit(solution)/shard_map/ppermute | solution.py:515
  31.7 4.2 %collective-permute-start.4 = (bf16[4,280,128]{2,1,0:T(8,128)(2,1)S(1)}, bf16[4,280,128]{2,1,0:T(8,128)(2,1)S(1)}, u32[]{:S(2)}, u32[]{:S(2)}) collective-permute-start(bf16[4,280,128]{2,1,0:T(8,128)(2,1)S(1)} %get-tuple-element.56), channel_id=1, source_target_pairs={{0,1},{1,0},{2,3},{3,2},{4,5},{5,4},{6,7},{7,6},{8,9},{9,8},{10,11... | collective-permute-start | bytes 860168 | tf_op jit(solution)/shard_map/ppermute | solution.py:521
  36.5 5.9 %collective-permute-start.5 = (bf16[280,128]{1,0:T(8,128)(2,1)S(1)}, bf16[280,128]{1,0:T(8,128)(2,1)S(1)}, u32[]{:S(2)}, u32[]{:S(2)}) collective-permute-start(bf16[280,128]{1,0:T(8,128)(2,1)S(1)} %get-tuple-element.58), channel_id=1, source_target_pairs={{0,8},{8,0},{16,24},{24,16},{1,9},{9,1},{17,25},{25,17},{2,10},{10... | collective-permute-start | bytes 215048 | tf_op jit(solution)/shard_map/ppermute | solution.py:521
  38.1 4.3 %collective-permute-start.6 = (bf16[280,128]{1,0:T(8,128)(2,1)S(1)}, bf16[280,128]{1,0:T(8,128)(2,1)S(1)}, u32[]{:S(2)}, u32[]{:S(2)}) collective-permute-start(bf16[280,128]{1,0:T(8,128)(2,1)S(1)} %get-tuple-element.59), channel_id=1, source_target_pairs={{0,16},{8,24},{16,0},{24,8},{1,17},{9,25},{17,1},{25,9},{2,18},{10... | collective-permute-start | bytes 215048 | tf_op jit(solution)/shard_map/ppermute | solution.py:521
  39.6 5.2 %collective-permute-start.7 = (bf16[280,128]{1,0:T(8,128)(2,1)S(1)}, bf16[280,128]{1,0:T(8,128)(2,1)S(1)}, u32[]{:S(2)}, u32[]{:S(2)}) collective-permute-start(bf16[280,128]{1,0:T(8,128)(2,1)S(1)} %get-tuple-element.60), channel_id=1, source_target_pairs={{0,24},{8,16},{16,8},{24,0},{1,25},{9,17},{17,9},{25,1},{2,26},{10... | collective-permute-start | bytes 215048 | tf_op jit(solution)/shard_map/ppermute | solution.py:521
  44.9 7.4 %collective-permute-start.10 = (bf16[280,128]{1,0:T(8,128)(2,1)S(1)}, bf16[280,128]{1,0:T(8,128)(2,1)S(1)}, u32[]{:S(2)}, u32[]{:S(2)}) collective-permute-start(bf16[280,128]{1,0:T(8,128)(2,1)S(1)} %shard_map.74.refs_0_), channel_id=1, source_target_pairs={{0,6},{1,7},{2,4},{3,5},{4,2},{5,3},{6,0},{7,1},{8,14},{9,15},{10,... | collective-permute-start | bytes 215048 | tf_op jit(solution)/shard_map/ppermute | solution.py:521
  47.7 6.2 %collective-permute-start.9 = (bf16[280,128]{1,0:T(8,128)(2,1)S(1)}, bf16[280,128]{1,0:T(8,128)(2,1)S(1)}, u32[]{:S(2)}, u32[]{:S(2)}) collective-permute-start(bf16[280,128]{1,0:T(8,128)(2,1)S(1)} %shard_map.74.refs_0_), channel_id=1, source_target_pairs={{0,4},{1,5},{2,6},{3,7},{4,0},{5,1},{6,2},{7,3},{8,12},{9,13},{10,... | collective-permute-start | bytes 215048 | tf_op jit(solution)/shard_map/ppermute | solution.py:521
  48.0 6.0 %collective-permute-start.8 = (bf16[280,128]{1,0:T(8,128)(2,1)S(1)}, bf16[280,128]{1,0:T(8,128)(2,1)S(1)}, u32[]{:S(2)}, u32[]{:S(2)}) collective-permute-start(bf16[280,128]{1,0:T(8,128)(2,1)S(1)} %shard_map.74.refs_0_), channel_id=1, source_target_pairs={{0,2},{1,3},{2,0},{3,1},{4,6},{5,7},{6,4},{7,5},{8,10},{9,11},{10,... | collective-permute-start | bytes 215048 | tf_op jit(solution)/shard_map/ppermute | solution.py:521
  54.0 5.4 %collective-permute-start.13 = (bf16[280,128]{1,0:T(8,128)(2,1)S(1)}, bf16[280,128]{1,0:T(8,128)(2,1)S(1)}, u32[]{:S(2)}, u32[]{:S(2)}) collective-permute-start(bf16[280,128]{1,0:T(8,128)(2,1)S(1)} %shard_map.75.refs_0_), channel_id=1, source_target_pairs={{0,24},{8,16},{16,8},{24,0},{1,25},{9,17},{17,9},{25,1},{2,26},{10... | collective-permute-start | bytes 215048 | tf_op jit(solution)/shard_map/ppermute | solution.py:521
  54.8 5.1 %collective-permute-start.12 = (bf16[280,128]{1,0:T(8,128)(2,1)S(1)}, bf16[280,128]{1,0:T(8,128)(2,1)S(1)}, u32[]{:S(2)}, u32[]{:S(2)}) collective-permute-start(bf16[280,128]{1,0:T(8,128)(2,1)S(1)} %shard_map.75.refs_0_), channel_id=1, source_target_pairs={{0,16},{8,24},{16,0},{24,8},{1,17},{9,25},{17,1},{25,9},{2,18},{10... | collective-permute-start | bytes 215048 | tf_op jit(solution)/shard_map/ppermute | solution.py:521
  56.2 4.3 %collective-permute-start.11 = (bf16[280,128]{1,0:T(8,128)(2,1)S(1)}, bf16[280,128]{1,0:T(8,128)(2,1)S(1)}, u32[]{:S(2)}, u32[]{:S(2)}) collective-permute-start(bf16[280,128]{1,0:T(8,128)(2,1)S(1)} %shard_map.75.refs_0_), channel_id=1, source_target_pairs={{0,8},{8,0},{16,24},{24,16},{1,9},{9,1},{17,25},{25,17},{2,10},{10... | collective-permute-start | bytes 215048 | tf_op jit(solution)/shard_map/ppermute | solution.py:521
  61.1 1.6 %collective-permute-start.14 = (bf16[4,280,128]{2,1,0:T(8,128)(2,1)S(1)}, bf16[4,280,128]{2,1,0:T(8,128)(2,1)S(1)}, u32[]{:S(2)}, u32[]{:S(2)}) collective-permute-start(bf16[4,280,128]{2,1,0:T(8,128)(2,1)S(1)} %shard_map.76.pieces), channel_id=1, source_target_pairs={{0,1},{1,0},{2,3},{3,2},{4,5},{5,4},{6,7},{7,6},{8,9},{9,8},{10,11... | collective-permute-start | bytes 860168 | tf_op jit(solution)/shard_map/ppermute | solution.py:521

commit v11 on v10

--- a/solution.py
+++ b/solution.py
@@ -96,15 +96,13 @@
             tat[768 * d + 64 * slot : 768 * d + 64 * slot + 64, 128 * half : 128 * half + 128] = value
 
 
-def prepare_kernel(cubes, weight_a, weight_b, xs, ta, tb, dsl, inner, edge_low, edge_high, wa, wb):
+def prepare_kernel(cubes, weight_a, xs, ta, dsl, inner, edge_low, edge_high, wa):
     mask = lanes_below((27, 128), 64)
     for j in range(C1 // 2):
         both = weight_a[:, 128 * j : 128 * j + 128].astype(F32)
         other = pltpu.roll(both, 64, 1)
         wa[pl.ds(2 * j, 27, stride=C1), :] = jnp.where(mask, both, other)
         wa[pl.ds(2 * j + 1, 27, stride=C1), :] = jnp.where(mask, other, both)
-    for i in range(C2):
-        wb[pl.ds(i, 27, stride=C2), :] = weight_b[:, 128 * i : 128 * i + 128].astype(F32)
     picker = row_picker(4, 2, 32)
     for b in range(cubes.shape[0]):
         for z in range(ZD):
@@ -115,9 +113,6 @@
             ta[256 * d : 256 * d + 256, 128 * px : 128 * px + 128] = halves(
                 rows_at(block, 32 * px, 256), rows_at(block, 64 + 32 * px, 256)
             )
-        block = wb[192 * d : 192 * d + 192].astype(BF)
-        for e in range(2):
-            tb[256 * d : 256 * d + 256, 128 * e : 128 * e + 128] = rows_at(block, 64 * e, 256)
 
     cube_count = cubes.shape[0]
     pre = dot(
@@ -139,6 +134,15 @@
             [windows_a(xs, ((first, 1),), p, 128 * g, offsets) for g in range(8) for p in range(2)], axis=0
         )
         edge[...] = dot(rows, ta[768 * offsets[0] : 768 * offsets[0] + 1536])
+
+
+def prepare_b_kernel(weight_b, tb, wb):
+    for i in range(C2):
+        wb[pl.ds(i, 27, stride=C2), :] = weight_b[:, 128 * i : 128 * i + 128].astype(F32)
+    for d in range(9):
+        block = wb[192 * d : 192 * d + 192].astype(BF)
+        for e in range(2):
+            tb[256 * d : 256 * d + 256, 128 * e : 128 * e + 128] = rows_at(block, 64 * e, 256)
 
 
 def forward_kernel(where, own, own_slope, inner, edge_low, edge_high, recv_a, recv_b, ta, tb, cot, xs, dsl, pools, grad_b, pooled):
@@ -332,18 +336,26 @@
             out[:, 128 * i : 128 * i + 128] = whole[i // each, start : start + 27]
 
 
-def first_half_kernel(scale, pieces, out_a, out_b, whole):
-    lay_out(pieces, scale[0], out_a, out_b, whole)
-
-
-def finish_kernel(where, scale, pieces, own_a, own_b, out_a, out_b, whole, other_a, other_b):
-    lay_out(pieces, scale[0], other_a, other_b, whole)
-    low = where[0] % 2 == 0
-    for own, other, out in ((own_a, other_a, out_a), (own_b, other_b, out_b)):
-        width = own.shape[1]
-        mine, theirs = own[...], other[...]
-        out[:, :width] = jnp.where(low, mine, theirs)
-        out[:, width:] = jnp.where(low, theirs, mine)
+def send_half(core, pieces, scale, outs, halves_out, whole, sems):
+    lay_out(pieces, scale, *halves_out, whole)
+    copies = []
+    for i, (out, half) in enumerate(zip(outs, halves_out)):
+        width = half.shape[1]
+        copies.append(
+            pltpu.make_async_copy(half, out.at[:, pl.ds(pl.multiple_of(core * width, width), width)], sems.at[i])
+        )
+        copies[-1].start()
+    for copy in copies:
+        copy.wait()
+
+
+def first_half_kernel(where, scale, pieces, out_a, out_b, whole, half_a, half_b, sems):
+    send_half(where[0] % 2, pieces, scale[0], (out_a, out_b), (half_a, half_b), whole, sems)
+
+
+def finish_kernel(where, scale, pieces, before_a, before_b, out_a, out_b, whole, half_a, half_b, sems):
+    del before_a, before_b
+    send_half(1 - where[0] % 2, pieces, scale[0], (out_a, out_b), (half_a, half_b), whole, sems)
 
 
 def backward_kernel(where, own, recv_a, recv_b, tbt, dsl, xs, terms_b, back, ga, keep, send, gs, gpool, acc, term, terms):
@@ -530,22 +542,23 @@
     outer = lax.dynamic_slice_in_dim(cubes, lax.axis_index("gz") % 2, HALO, axis=1)
     recv_a, recv_b = swap(cubes, outer, ring)
 
-    own_xs, ta, tb, own_slope, inner, edge_low, edge_high, wa, wb = call(
+    own_xs, ta, own_slope, inner, edge_low, edge_high, wa = call(
         prepare_kernel,
-        [cubes, weight_a, weight_b],
+        [cubes, weight_a],
         [
             ((cube_count, ZD + 2 * HALO, 4, 16, 1152), BF),
-            ((2304, 256), BF),
             ((2304, 256), BF),
             ((cube_count, 6, 2, 16, 2048), BF),
             ((cube_count, 2, 16, 1024), F32),
             ((cube_count * 256, 256), F32),
             ((cube_count * 256, 256), F32),
             ((27 * C1, 128), F32),
-            ((27 * C2, 128), F32),
         ],
         [],
         1_000_000_000,
+    )
+    tb, wb = call(
+        prepare_b_kernel, [weight_b], [((2304, 256), BF), ((27 * C2, 128), F32)], [], 500_000_000
     )
     xs, dsl, pools, grad_b = call(
         forward_kernel,
@@ -611,16 +624,24 @@
     )
     (other,) = swap_along([own] * 2, "gz", 1)
     scale = jnp.full((1,), 1.0 / (cube_count * samples), F32)
-    half_a, half_b = (27, C1 * C2 // 2), (27, C2 * C3 // 2)
-    whole = pltpu.VMEM((samples, piece, 128), F32)
-    own_a, own_b = call(first_half_kernel, [scale, own], [(half_a, F32), (half_b, F32)], [whole], 1_000_000, smem=1)
+    shapes = [((27, C1 * C2), F32), ((27, C2 * C3), F32)]
+    scratch = [
+        pltpu.VMEM((samples, piece, 128), F32),
+        pltpu.VMEM((27, C1 * C2 // 2), F32),
+        pltpu.VMEM((27, C2 * C3 // 2), F32),
+        pltpu.SemaphoreType.DMA((2,)),
+    ]
+    totals = call(first_half_kernel, [where, scale, own], shapes, scratch, 1_000_000, smem=2, any_out=(0, 1))
     total_a, total_b = call(
         finish_kernel,
-        [where, scale, other, own_a, own_b],
-        [((27, C1 * C2), F32), ((27, C2 * C3), F32)],
-        [whole, pltpu.VMEM(half_a, F32), pltpu.VMEM(half_b, F32)],
+        [where, scale, other, *totals],
+        shapes,
+        scratch,
         1_000_000,
         smem=2,
+        any_in=(3, 4),
+        any_out=(0, 1),
+        aliases={3: 0, 4: 1},
     )
     return input_grad, total_a, total_b
 

time: 64.7 us -> 63.5 us (0.981)
  local copies, waits for them, and re-layouts: 4.01 us -> 2.07 us
  Pallas kernels: 27.8 us -> 29 us
  waiting for transfers between devices: 9.77 us -> 8.81 us
    unnamed x8, local copies, waits for them, and re-layouts: 2.99 us -> 1.05 us
    ppermute x2, starting transfers between devices: 5.86 us -> 7.8 us  [swap(): lax.ppermute(first, 'gz', pairs_a)]
    ppermute x11, starting transfers between devices: 14.6 us -> 13 us  [swap_along(): lax.ppermute(part, axis, [(i, i ^ k * step) for i in range(count)])]
    pallas_call x12 -> x13, Pallas kernels: 27.8 us -> 29 us  [call(): pl.pallas_call(kernel, out_shape=[jax.ShapeDtypeStruct(shape, dtype) for...]
    ppermute x11, waiting for transfers between devices: 9.76 us -> 8.8 us  [swap_along(): lax.ppermute(part, axis, [(i, i ^ k * step) for i in range(count)])]
  transfers between devices with their start and end apart: 15 -> 15, of which waited for: 7 -> 8; matrix products, arithmetic and copies ran while one was open for 2% -> 2% of each run, Pallas kernels for 18% -> 21%
where the time goes in v11:
time: 63.5 us; the launch traced here: 63.3 us
  Pallas kernels  29 us (46%)
  starting transfers between devices  22.3 us (35%)
  waiting for transfers between devices  8.81 us (14%)
  local copies, waits for them, and re-layouts  2.07 us (3%)
  between operations  0.98 us (2%)
    pallas_call x13, Pallas kernels, call(): pl.pallas_call(kernel, out_shape=[jax.ShapeDtypeStruct(shape, dtype) for...  29 us
    ppermute x11, starting transfers between devices, swap_along(): lax.ppermute(part, axis, [(i, i ^ k * step) for i in range(count)])  13 us
    ppermute x11, waiting for transfers between devices, swap_along(): lax.ppermute(part, axis, [(i, i ^ k * step) for i in range(count)])  8.8 us
    ppermute x2, starting transfers between devices, swap(): lax.ppermute(first, 'gz', pairs_a)  7.8 us
    ppermute x2, starting transfers between devices, swap(): lax.ppermute(second, 'gz', pairs_b)  1.54 us
  transfers between devices with their start and end apart: 15, of which 8 were waited for; matrix products, arithmetic and copies ran while one was open for 2% of the time, Pallas kernels for 21%

profile of v11, /device:TPU:0, one launch (start us, length us, event | category | flops | bytes accessed | tf_op | source)
XLA Modules:
  0.0 63.3 jit_solution(80467964301082018)
XLA Ops:
  0.6 0.5 collective-permute-start
  1.2 1.0 %constant_dynamic-slice_fusion = bf16[2,3,32,1024]{3,2,1,0:T(8,128)(2,1)S(1)} fusion(bf16[2,4,32,1024]{3,2,1,0:T(8,128)(2,1)} %cubes.1, s32[]{:T(128)S(6)} %select_n.11), kind=kLoop, calls=%fused_computation.1 | loop fusion | bytes 786436 | tf_op jit(solution)/shard_map/dynamic_slice | solution.py:542
  2.2 0.7 %collective-permute-start.1 = (bf16[2,3,32,1024]{3,2,1,0:T(8,128)(2,1)S(1)}, bf16[2,3,32,1024]{3,2,1,0:T(8,128)(2,1)S(1)}, u32[]{:S(2)}, u32[]{:S(2)}) collective-permute-start(bf16[2,3,32,1024]{3,2,1,0:T(8,128)(2,1)S(1)} %constant_dynamic-slice_fusion), channel_id=1, source_target_pairs={{1,2},{2,1},{3,4},{4,3},{5,6},{6,5},{9,10},{10,9},{11,12},{12,11},... | collective-permute-start | bytes 1179656 | tf_op jit(solution)/shard_map/ppermute | solution.py:527
  2.9 1.0 %copy-done.1 = bf16[27,8192]{1,0:T(8,128)(2,1)S(1)} copy-done((bf16[27,8192]{1,0:T(8,128)(2,1)S(1)}, bf16[27,8192]{1,0:T(8,128)(2,1)}, u32[]{:S(2)}) %copy-start.1) | copy-done | bytes 442392
  3.9 1.0 %shard_map.68 = (bf16[2304,256]{1,0:T(8,128)(2,1)S(1)}, f32[1728,128]{1,0:T(8,128)S(1)}) custom-call(bf16[27,8192]{1,0:T(8,128)(2,1)S(1)} %copy-done.1), custom_call_target="tpu_custom_call" | custom-call | flops 500000000 | bytes 1000000 | tf_op jit(solution)/shard_map/pallas_call | solution.py:512
  4.9 3.1 %shard_map.67 = (bf16[2,10,4,16,1152]{4,3,2,1,0:T(8,128)(2,1)S(1)}, bf16[2304,256]{1,0:T(8,128)(2,1)S(1)}, bf16[2,6,2,16,2048]{4,3,2,1,0:T(8,128)(2,1)S(1)}, f32...) custom-call(bf16[2,4,32,1024]{3,2,1,0:T(8,128)(2,1)S(1)} %copy-done, ...), custom_call_target="tpu_custom_call" | custom-call | flops 1000000000 | bytes 1000000 | tf_op jit(solution)/shard_map/pallas_call | solution.py:512
  8.1 6.4 %shard_map.69 = (bf16[2,10,4,16,1152]{4,3,2,1,0:T(8,128)(2,1)S(1)}, bf16[2,6,2,16,2048]{4,3,2,1,0:T(8,128)(2,1)S(1)}, bf16[2,4,3,16,1152]{4,3,2,1,0:T(8,128)(2,1)S(1)}, bf16[2,2,16,2048]{3,2,1,0:T(8,128)(2,1)S(1)}) custom-call(s32[3]{0:T(128)S(1)} %pad_add_fusion.where, ...), custom_call_target="tpu_custom_call", output_to_operand_aliasing={{0}: (1, {}), {1}: (2, {})} | custom-call | flops 8000000000 | bytes 1000000 | tf_op jit(solution)/shard_map/pallas_call | solution.py:512
  14.5 0.9 %collective-permute-start.3 = (bf16[2,2,16,2048]{3,2,1,0:T(8,128)(2,1)S(1)}, bf16[2,2,16,2048]{3,2,1,0:T(8,128)(2,1)S(1)}, u32[]{:S(2)}, u32[]{:S(2)}) collective-permute-start(bf16[2,2,16,2048]{3,2,1,0:T(8,128)(2,1)S(1)} %get-tuple-element.42.grad_b), channel_id=1, source_target_pairs={{1,2},{2,1},{3,4},{4,3},{5,6},{6,5},{9,10},{10,9},{11,12},{12,11},... | collective-permute-start | bytes 786440 | tf_op jit(solution)/shard_map/ppermute | solution.py:527
  15.3 7.3 %collective-permute-start.2 = (bf16[2,2,16,2048]{3,2,1,0:T(8,128)(2,1)S(1)}, bf16[2,2,16,2048]{3,2,1,0:T(8,128)(2,1)S(1)}, u32[]{:S(2)}, u32[]{:S(2)}) collective-permute-start(bf16[2,2,16,2048]{3,2,1,0:T(8,128)(2,1)S(1)} %get-tuple-element.42.grad_b), channel_id=1, source_target_pairs={{0,1},{1,0},{2,3},{3,2},{4,5},{5,4},{6,7},{7,6},{8,9},{9,8},{10,11... | collective-permute-start | bytes 786440 | tf_op jit(solution)/shard_map/ppermute | solution.py:527
  22.6 2.5 %shard_map.70 = (f32[1792,128]{1,0:T(8,128)S(1)}, bf16[2,6,3,16,2304]{4,3,2,1,0:T(8,128)(2,1)S(1)}, bf16[6912,256]{1,0:T(8,128)(2,1)S(1)}, bf16[6912,256]{1,0:T(8,128)(2,1)S(1)}, f32[4,2,4,16,256]{4,3,2,1,0:T(8,128)S(1)}) custom-call(bf16[2,4,3,16,1152]{4,3,2,1,0:T(8,128)(2,1)S(1)} %get-tuple-element.41.pools, ...), custom_call_target="tpu_custom_call" | custom-call | flops 1000000000 | bytes 1000000 | tf_op jit(solution)/shard_map/pallas_call | solution.py:512
  25.1 6.7 %shard_map.71 = (bf16[2,6,4,16,2304]{4,3,2,1,0:T(8,128)(2,1)S(1)}, bf16[4,280,128]{2,1,0:T(8,128)(2,1)S(1)}, bf16[4,280,128]{2,1,0:T(8,128)(2,1)S(1)}, bf16[2,6,3,16,2304]{4,3,2,1,0:T(8,128)(2,1)S(1)}) custom-call(s32[3]{0:T(128)S(1)} %pad_add_fusion.where, bf16[2,6,3,16,2304]{4,3,2,1,0:T(8,128)(2,1)S(1)} %get-tuple-element.45.own, ...), custom_call_target="tpu_custom_call", output_to_operand_aliasing={{3}: (1, {})} | custom-call | flops 6000000000 | bytes 1000000 | tf_op jit(solution)/shard_map/pallas_call | solution.py:512
  31.8 1.3 %collective-permute-start.4 = (bf16[4,280,128]{2,1,0:T(8,128)(2,1)S(1)}, bf16[4,280,128]{2,1,0:T(8,128)(2,1)S(1)}, u32[]{:S(2)}, u32[]{:S(2)}) collective-permute-start(bf16[4,280,128]{2,1,0:T(8,128)(2,1)S(1)} %get-tuple-element.56), channel_id=1, source_target_pairs={{0,1},{1,0},{2,3},{3,2},{4,5},{5,4},{6,7},{7,6},{8,9},{9,8},{10,11... | collective-permute-start | bytes 860168 | tf_op jit(solution)/shard_map/ppermute | solution.py:533
  33.1 1.2 %collective-permute-done.4.recv = bf16[4,280,128]{2,1,0:T(8,128)(2,1)S(1)} collective-permute-done((bf16[4,280,128]{2,1,0:T(8,128)(2,1)S(1)}, bf16[4,280,128]{2,1,0:T(8,128)(2,1)S(1)}, u32[]{:S(2)}, u32[]{:S(2)}) %collective-permute-start.4) | collective-permute-done | bytes 286752 | tf_op jit(solution)/shard_map/ppermute | solution.py:533
  34.3 0.6 shard_map.74
  35.0 2.0 %collective-permute-start.5 = (bf16[280,128]{1,0:T(8,128)(2,1)S(1)}, bf16[280,128]{1,0:T(8,128)(2,1)S(1)}, u32[]{:S(2)}, u32[]{:S(2)}) collective-permute-start(bf16[280,128]{1,0:T(8,128)(2,1)S(1)} %get-tuple-element.58), channel_id=1, source_target_pairs={{0,8},{8,0},{16,24},{24,16},{1,9},{9,1},{17,25},{25,17},{2,10},{10... | collective-permute-start | bytes 215048 | tf_op jit(solution)/shard_map/ppermute | solution.py:533
  37.0 1.5 %collective-permute-start.6 = (bf16[280,128]{1,0:T(8,128)(2,1)S(1)}, bf16[280,128]{1,0:T(8,128)(2,1)S(1)}, u32[]{:S(2)}, u32[]{:S(2)}) collective-permute-start(bf16[280,128]{1,0:T(8,128)(2,1)S(1)} %get-tuple-element.59), channel_id=1, source_target_pairs={{0,16},{8,24},{16,0},{24,8},{1,17},{9,25},{17,1},{25,9},{2,18},{10... | collective-permute-start | bytes 215048 | tf_op jit(solution)/shard_map/ppermute | solution.py:533
  38.5 2.3 %shard_map.72.rest_0_.after = bf16[4,32,1024]{2,1,0:T(8,128)(2,1)S(1)} custom-call(bf16[2,6,4,16,2304]{4,3,2,1,0:T(8,128)(2,1)S(1)} %get-tuple-element.51.ga, bf16[6912,256]{1,0:T(8,128)(2,1)S(1)} %get-tuple-element.52.tat), custom_call_target="tpu_custom_call" | custom-call | flops 2000000000 | bytes 1000000 | tf_op jit(solution)/shard_map/pallas_call | solution.py:512
  40.8 0.5 collective-permute-done.6.refs_2_
  41.3 2.4 %collective-permute-done.7.refs_3_ = bf16[280,128]{1,0:T(8,128)(2,1)S(1)} collective-permute-done((bf16[280,128]{1,0:T(8,128)(2,1)S(1)}, bf16[280,128]{1,0:T(8,128)(2,1)S(1)}, u32[]{:S(2)}, u32[]{:S(2)}) %collective-permute-start.7) | collective-permute-done | bytes 71712 | tf_op jit(solution)/shard_map/ppermute | solution.py:533
  43.8 3.6 %collective-permute-start.10 = (bf16[280,128]{1,0:T(8,128)(2,1)S(1)}, bf16[280,128]{1,0:T(8,128)(2,1)S(1)}, u32[]{:S(2)}, u32[]{:S(2)}) collective-permute-start(bf16[280,128]{1,0:T(8,128)(2,1)S(1)} %shard_map.75.refs_0_), channel_id=1, source_target_pairs={{0,6},{1,7},{2,4},{3,5},{4,2},{5,3},{6,0},{7,1},{8,14},{9,15},{10,... | collective-permute-start | bytes 215048 | tf_op jit(solution)/shard_map/ppermute | solution.py:533
  47.4 0.8 %collective-permute-start.8 = (bf16[280,128]{1,0:T(8,128)(2,1)S(1)}, bf16[280,128]{1,0:T(8,128)(2,1)S(1)}, u32[]{:S(2)}, u32[]{:S(2)}) collective-permute-start(bf16[280,128]{1,0:T(8,128)(2,1)S(1)} %shard_map.75.refs_0_), channel_id=1, source_target_pairs={{0,2},{1,3},{2,0},{3,1},{4,6},{5,7},{6,4},{7,5},{8,10},{9,11},{10,... | collective-permute-start | bytes 215048 | tf_op jit(solution)/shard_map/ppermute | solution.py:533
  48.2 3.0 %shard_map.73 = (bf16[2,4,32,1024]{3,2,1,0:T(8,128)(2,1)}, f32[8,128]{1,0:T(8,128)S(1)}) custom-call(bf16[2,6,4,16,2304]{4,3,2,1,0:T(8,128)(2,1)S(1)} %get-tuple-element.51.ga, bf16[6912,256]{1,0:T(8,128)(2,1)S(1)} %get-tuple-element.52.tat, bf16[4,32,1024]{2,1,0:T(8,128)(2,1)S(1)} %shard_map.72.rest_0_.after), custom_call_target="tpu_custom_call" | custom-call | flops 2000000000 | bytes 1000000 | tf_op jit(solution)/shard_map/pallas_call | solution.py:512
  51.2 1.7 %collective-permute-done.9.refs_2_ = bf16[280,128]{1,0:T(8,128)(2,1)S(1)} collective-permute-done((bf16[280,128]{1,0:T(8,128)(2,1)S(1)}, bf16[280,128]{1,0:T(8,128)(2,1)S(1)}, u32[]{:S(2)}, u32[]{:S(2)}) %collective-permute-start.9) | collective-permute-done | bytes 71712 | tf_op jit(solution)/shard_map/ppermute | solution.py:533
  52.9 0.8 %collective-permute-start.13 = (bf16[280,128]{1,0:T(8,128)(2,1)S(1)}, bf16[280,128]{1,0:T(8,128)(2,1)S(1)}, u32[]{:S(2)}, u32[]{:S(2)}) collective-permute-start(bf16[280,128]{1,0:T(8,128)(2,1)S(1)} %shard_map.76.refs_0_), channel_id=1, source_target_pairs={{0,24},{8,16},{16,8},{24,0},{1,25},{9,17},{17,9},{25,1},{2,26},{10... | collective-permute-start | bytes 215048 | tf_op jit(solution)/shard_map/ppermute | solution.py:533
  53.7 1.4 %collective-permute-start.12 = (bf16[280,128]{1,0:T(8,128)(2,1)S(1)}, bf16[280,128]{1,0:T(8,128)(2,1)S(1)}, u32[]{:S(2)}, u32[]{:S(2)}) collective-permute-start(bf16[280,128]{1,0:T(8,128)(2,1)S(1)} %shard_map.76.refs_0_), channel_id=1, source_target_pairs={{0,16},{8,24},{16,0},{24,8},{1,17},{9,25},{17,1},{25,9},{2,18},{10... | collective-permute-start | bytes 215048 | tf_op jit(solution)/shard_map/ppermute | solution.py:533
  55.1 1.4 %collective-permute-start.11 = (bf16[280,128]{1,0:T(8,128)(2,1)S(1)}, bf16[280,128]{1,0:T(8,128)(2,1)S(1)}, u32[]{:S(2)}, u32[]{:S(2)}) collective-permute-start(bf16[280,128]{1,0:T(8,128)(2,1)S(1)} %shard_map.76.refs_0_), channel_id=1, source_target_pairs={{0,8},{8,0},{16,24},{24,16},{1,9},{9,1},{17,25},{25,17},{2,10},{10... | collective-permute-start | bytes 215048 | tf_op jit(solution)/shard_map/ppermute | solution.py:533
  56.5 1.9 %collective-permute-done.13.refs_3_ = bf16[280,128]{1,0:T(8,128)(2,1)S(1)} collective-permute-done((bf16[280,128]{1,0:T(8,128)(2,1)S(1)}, bf16[280,128]{1,0:T(8,128)(2,1)S(1)}, u32[]{:S(2)}, u32[]{:S(2)}) %collective-permute-start.13) | collective-permute-done | bytes 71712 | tf_op jit(solution)/shard_map/ppermute | solution.py:533
  58.4 0.5 collective-permute-done.12.refs_2_
  58.8 0.6 collective-permute-done.11.refs_1_
  59.4 0.6 shard_map.77.pieces
  60.1 1.5 %shard_map.78 = (f32[27,2048]{1,0:T(8,128)}, f32[27,8192]{1,0:T(8,128)}) custom-call(s32[3]{0:T(128)S(1)} %pad_add_fusion.where, f32[1]{0:T(128)} %constant.27.clone.1.scale, bf16[4,280,128]{2,1,0:T(8,128)(2,1)S(1)} %shard_map.77.pieces), custom_call_target="tpu_custom_call" | custom-call | flops 1000000 | bytes 1000000 | tf_op jit(solution)/shard_map/pallas_call | solution.py:512
  61.6 1.5 %shard_map.79 = (f32[27,2048]{1,0:T(8,128)}, f32[27,8192]{1,0:T(8,128)}) custom-call(s32[3]{0:T(128)S(1)} %pad_add_fusion.where, f32[1]{0:T(128)} %constant.27.clone.1.scale, bf16[4,280,128]{2,1,0:T(8,128)(2,1)S(1)} %collective-permute-done.14.pieces, f32[27,2048]{1,0:T(8,128)} %get-tuple-element.61.before_a, ...), custom_call_target="tpu_custom_call", output_to_operand_aliasing={{0}: (3, {}), {1}: (4, {})} | custom-call | flops 1000000 | bytes 1000000 | tf_op jit(solution)/shard_map/pallas_call | solution.py:512
  (21 shorter events, 0.4 us)
Async XLA Ops:
  0.6 4.3 %copy-start = (bf16[2,4,32,1024]{3,2,1,0:T(8,128)(2,1)S(1)}, bf16[2,4,32,1024]{3,2,1,0:T(8,128)(2,1)}, u32[]{:S(2)}) copy-start(bf16[2,4,32,1024]{3,2,1,0:T(8,128)(2,1)} %cubes.1) | copy-start | bytes 1572868
  0.6 4.3 %copy-start.2 = (bf16[27,2048]{1,0:T(8,128)(2,1)S(1)}, bf16[27,2048]{1,0:T(8,128)(2,1)}, u32[]{:S(2)}) copy-start(bf16[27,2048]{1,0:T(8,128)(2,1)} %weight_a.1) | copy-start | bytes 331780
  0.6 7.4 %collective-permute-start = (bf16[2,4,32,1024]{3,2,1,0:T(8,128)(2,1)}, bf16[2,4,32,1024]{3,2,1,0:T(8,128)(2,1)S(1)}, u32[]{:S(2)}, u32[]{:S(2)}) collective-permute-start(bf16[2,4,32,1024]{3,2,1,0:T(8,128)(2,1)} %cubes.1), channel_id=1, source_target_pairs={{0,1},{1,0},{2,3},{3,2},{4,5},{5,4},{6,7},{7,6},{8,9},{9,8},{10,11... | collective-permute-start | bytes 1572872 | tf_op jit(solution)/shard_map/ppermute | solution.py:527
  2.2 5.9 %collective-permute-start.1 = (bf16[2,3,32,1024]{3,2,1,0:T(8,128)(2,1)S(1)}, bf16[2,3,32,1024]{3,2,1,0:T(8,128)(2,1)S(1)}, u32[]{:S(2)}, u32[]{:S(2)}) collective-permute-start(bf16[2,3,32,1024]{3,2,1,0:T(8,128)(2,1)S(1)} %constant_dynamic-slice_fusion), channel_id=1, source_target_pairs={{1,2},{2,1},{3,4},{4,3},{5,6},{6,5},{9,10},{10,9},{11,12},{12,11},... | collective-permute-start | bytes 1179656 | tf_op jit(solution)/shard_map/ppermute | solution.py:527
  2.9 1.0 %copy-start.1 = (bf16[27,8192]{1,0:T(8,128)(2,1)S(1)}, bf16[27,8192]{1,0:T(8,128)(2,1)}, u32[]{:S(2)}) copy-start(bf16[27,8192]{1,0:T(8,128)(2,1)} %weight_b.1) | copy-start | bytes 1327108
  3.9 4.1 %copy-start.3 = (bf16[2,1,8,1024]{3,2,1,0:T(8,128)(2,1)S(1)}, bf16[2,1,8,1024]{3,2,1,0:T(8,128)(2,1)}, u32[]{:S(2)}) copy-start(bf16[2,1,8,1024]{3,2,1,0:T(8,128)(2,1)} %cot.1) | copy-start | bytes 98308
  14.5 10.7 %collective-permute-start.3 = (bf16[2,2,16,2048]{3,2,1,0:T(8,128)(2,1)S(1)}, bf16[2,2,16,2048]{3,2,1,0:T(8,128)(2,1)S(1)}, u32[]{:S(2)}, u32[]{:S(2)}) collective-permute-start(bf16[2,2,16,2048]{3,2,1,0:T(8,128)(2,1)S(1)} %get-tuple-element.42.grad_b), channel_id=1, source_target_pairs={{1,2},{2,1},{3,4},{4,3},{5,6},{6,5},{9,10},{10,9},{11,12},{12,11},... | collective-permute-start | bytes 786440 | tf_op jit(solution)/shard_map/ppermute | solution.py:527
  15.3 9.8 %collective-permute-start.2 = (bf16[2,2,16,2048]{3,2,1,0:T(8,128)(2,1)S(1)}, bf16[2,2,16,2048]{3,2,1,0:T(8,128)(2,1)S(1)}, u32[]{:S(2)}, u32[]{:S(2)}) collective-permute-start(bf16[2,2,16,2048]{3,2,1,0:T(8,128)(2,1)S(1)} %get-tuple-element.42.grad_b), channel_id=1, source_target_pairs={{0,1},{1,0},{2,3},{3,2},{4,5},{5,4},{6,7},{7,6},{8,9},{9,8},{10,11... | collective-permute-start | bytes 786440 | tf_op jit(solution)/shard_map/ppermute | solution.py:527
  31.8 2.5 %collective-permute-start.4 = (bf16[4,280,128]{2,1,0:T(8,128)(2,1)S(1)}, bf16[4,280,128]{2,1,0:T(8,128)(2,1)S(1)}, u32[]{:S(2)}, u32[]{:S(2)}) collective-permute-start(bf16[4,280,128]{2,1,0:T(8,128)(2,1)S(1)} %get-tuple-element.56), channel_id=1, source_target_pairs={{0,1},{1,0},{2,3},{3,2},{4,5},{5,4},{6,7},{7,6},{8,9},{9,8},{10,11... | collective-permute-start | bytes 860168 | tf_op jit(solution)/shard_map/ppermute | solution.py:533
  35.0 5.9 %collective-permute-start.5 = (bf16[280,128]{1,0:T(8,128)(2,1)S(1)}, bf16[280,128]{1,0:T(8,128)(2,1)S(1)}, u32[]{:S(2)}, u32[]{:S(2)}) collective-permute-start(bf16[280,128]{1,0:T(8,128)(2,1)S(1)} %get-tuple-element.58), channel_id=1, source_target_pairs={{0,8},{8,0},{16,24},{24,16},{1,9},{9,1},{17,25},{25,17},{2,10},{10... | collective-permute-start | bytes 215048 | tf_op jit(solution)/shard_map/ppermute | solution.py:533
  37.0 4.3 %collective-permute-start.6 = (bf16[280,128]{1,0:T(8,128)(2,1)S(1)}, bf16[280,128]{1,0:T(8,128)(2,1)S(1)}, u32[]{:S(2)}, u32[]{:S(2)}) collective-permute-start(bf16[280,128]{1,0:T(8,128)(2,1)S(1)} %get-tuple-element.59), channel_id=1, source_target_pairs={{0,16},{8,24},{16,0},{24,8},{1,17},{9,25},{17,1},{25,9},{2,18},{10... | collective-permute-start | bytes 215048 | tf_op jit(solution)/shard_map/ppermute | solution.py:533
  38.5 5.2 %collective-permute-start.7 = (bf16[280,128]{1,0:T(8,128)(2,1)S(1)}, bf16[280,128]{1,0:T(8,128)(2,1)S(1)}, u32[]{:S(2)}, u32[]{:S(2)}) collective-permute-start(bf16[280,128]{1,0:T(8,128)(2,1)S(1)} %get-tuple-element.60), channel_id=1, source_target_pairs={{0,24},{8,16},{16,8},{24,0},{1,25},{9,17},{17,9},{25,1},{2,26},{10... | collective-permute-start | bytes 215048 | tf_op jit(solution)/shard_map/ppermute | solution.py:533
  43.8 7.4 %collective-permute-start.10 = (bf16[280,128]{1,0:T(8,128)(2,1)S(1)}, bf16[280,128]{1,0:T(8,128)(2,1)S(1)}, u32[]{:S(2)}, u32[]{:S(2)}) collective-permute-start(bf16[280,128]{1,0:T(8,128)(2,1)S(1)} %shard_map.75.refs_0_), channel_id=1, source_target_pairs={{0,6},{1,7},{2,4},{3,5},{4,2},{5,3},{6,0},{7,1},{8,14},{9,15},{10,... | collective-permute-start | bytes 215048 | tf_op jit(solution)/shard_map/ppermute | solution.py:533
  47.4 5.5 %collective-permute-start.9 = (bf16[280,128]{1,0:T(8,128)(2,1)S(1)}, bf16[280,128]{1,0:T(8,128)(2,1)S(1)}, u32[]{:S(2)}, u32[]{:S(2)}) collective-permute-start(bf16[280,128]{1,0:T(8,128)(2,1)S(1)} %shard_map.75.refs_0_), channel_id=1, source_target_pairs={{0,4},{1,5},{2,6},{3,7},{4,0},{5,1},{6,2},{7,3},{8,12},{9,13},{10,... | collective-permute-start | bytes 215048 | tf_op jit(solution)/shard_map/ppermute | solution.py:533
  47.4 5.5 %collective-permute-start.8 = (bf16[280,128]{1,0:T(8,128)(2,1)S(1)}, bf16[280,128]{1,0:T(8,128)(2,1)S(1)}, u32[]{:S(2)}, u32[]{:S(2)}) collective-permute-start(bf16[280,128]{1,0:T(8,128)(2,1)S(1)} %shard_map.75.refs_0_), channel_id=1, source_target_pairs={{0,2},{1,3},{2,0},{3,1},{4,6},{5,7},{6,4},{7,5},{8,10},{9,11},{10,... | collective-permute-start | bytes 215048 | tf_op jit(solution)/shard_map/ppermute | solution.py:533
  52.9 5.4 %collective-permute-start.13 = (bf16[280,128]{1,0:T(8,128)(2,1)S(1)}, bf16[280,128]{1,0:T(8,128)(2,1)S(1)}, u32[]{:S(2)}, u32[]{:S(2)}) collective-permute-start(bf16[280,128]{1,0:T(8,128)(2,1)S(1)} %shard_map.76.refs_0_), channel_id=1, source_target_pairs={{0,24},{8,16},{16,8},{24,0},{1,25},{9,17},{17,9},{25,1},{2,26},{10... | collective-permute-start | bytes 215048 | tf_op jit(solution)/shard_map/ppermute | solution.py:533
  53.7 5.1 %collective-permute-start.12 = (bf16[280,128]{1,0:T(8,128)(2,1)S(1)}, bf16[280,128]{1,0:T(8,128)(2,1)S(1)}, u32[]{:S(2)}, u32[]{:S(2)}) collective-permute-start(bf16[280,128]{1,0:T(8,128)(2,1)S(1)} %shard_map.76.refs_0_), channel_id=1, source_target_pairs={{0,16},{8,24},{16,0},{24,8},{1,17},{9,25},{17,1},{25,9},{2,18},{10... | collective-permute-start | bytes 215048 | tf_op jit(solution)/shard_map/ppermute | solution.py:533
  55.1 4.3 %collective-permute-start.11 = (bf16[280,128]{1,0:T(8,128)(2,1)S(1)}, bf16[280,128]{1,0:T(8,128)(2,1)S(1)}, u32[]{:S(2)}, u32[]{:S(2)}) collective-permute-start(bf16[280,128]{1,0:T(8,128)(2,1)S(1)} %shard_map.76.refs_0_), channel_id=1, source_target_pairs={{0,8},{8,0},{16,24},{24,16},{1,9},{9,1},{17,25},{25,17},{2,10},{10... | collective-permute-start | bytes 215048 | tf_op jit(solution)/shard_map/ppermute | solution.py:533
  60.0 1.6 %collective-permute-start.14 = (bf16[4,280,128]{2,1,0:T(8,128)(2,1)S(1)}, bf16[4,280,128]{2,1,0:T(8,128)(2,1)S(1)}, u32[]{:S(2)}, u32[]{:S(2)}) collective-permute-start(bf16[4,280,128]{2,1,0:T(8,128)(2,1)S(1)} %shard_map.77.pieces), channel_id=1, source_target_pairs={{0,1},{1,0},{2,3},{3,2},{4,5},{5,4},{6,7},{7,6},{8,9},{9,8},{10,11... | collective-permute-start | bytes 860168 | tf_op jit(solution)/shard_map/ppermute | solution.py:533

commit v12 on v11

--- a/solution.py
+++ b/solution.py
@@ -32,11 +32,14 @@
     return pl.reciprocal(1.0 + jnp.exp(-v), approx=True)
 
 
-def row_picker(variants, stride, columns):
-    shape = (variants * 16, columns)
+def row_picker(variants, stride, planes):
+    size = 16 * stride
+    shape = (planes * variants * 16, planes * size)
     row = lax.broadcasted_iota(jnp.int32, shape, 0)
     col = lax.broadcasted_iota(jnp.int32, shape, 1)
-    return jnp.where(col == stride * (row % 16) + row // 16 - 1, 1.0, 0.0).astype(BF)
+    want = stride * (row % 16) + row // 16 % variants - 1
+    hit = (col == row // (16 * variants) * size + want) & (want >= 0) & (want < size)
+    return jnp.where(hit, 1.0, 0.0).astype(BF)
 
 
 def rows_at(block, before, total):
@@ -75,11 +78,14 @@
     return jnp.concatenate(columns, axis=1)
 
 
-def spread_input(target, b, zz, plane, picker):
-    plane = jnp.concatenate([jnp.zeros((32, 32), BF), plane, jnp.zeros((32, 96), BF)], axis=1)
-    moved = dot(picker, plane).astype(BF)
-    for v in range(4):
-        target[b, zz, v] = moved[16 * v : 16 * v + 16]
+def spread_input(target, b, zz, planes, picker):
+    rows = 32 * len(planes)
+    block = jnp.concatenate(planes, axis=0)
+    block = jnp.concatenate([jnp.zeros((rows, 32), BF), block, jnp.zeros((rows, 96), BF)], axis=1)
+    moved = dot(picker, block).astype(BF)
+    for i in range(len(planes)):
+        for v in range(4):
+            target[b, zz + i, v] = moved[64 * i + 16 * v : 64 * i + 16 * v + 16]
 
 
 RANKS = (-3, -1, 0, 2, 1, 3, 4, 6, 5, 7, 8, 10)
@@ -103,10 +109,9 @@
         other = pltpu.roll(both, 64, 1)
         wa[pl.ds(2 * j, 27, stride=C1), :] = jnp.where(mask, both, other)
         wa[pl.ds(2 * j + 1, 27, stride=C1), :] = jnp.where(mask, other, both)
-    picker = row_picker(4, 2, 32)
+    picker = row_picker(4, 2, ZD)
     for b in range(cubes.shape[0]):
-        for z in range(ZD):
-            spread_input(xs, b, HALO + z, cubes[b, z], picker)
+        spread_input(xs, b, HALO, [cubes[b, z] for z in range(ZD)], picker)
     for d in range(9):
         block = wa[96 * d : 96 * d + 96]
         for px in range(2):
@@ -149,14 +154,15 @@
     del own, own_slope
     cube_count = xs.shape[0]
     even = where[0] % 2 == 0
-    picker = row_picker(4, 2, 32)
+    picker = row_picker(4, 2, HALO)
     for b in range(cube_count):
+        below, above = [], []
         for z in range(HALO):
             far = ZD - HALO + z
-            below = jnp.where(even, recv_b[b, z].astype(F32), recv_a[b, far].astype(F32)).astype(BF)
-            above = jnp.where(even, recv_a[b, z].astype(F32), recv_b[b, z].astype(F32)).astype(BF)
-            spread_input(xs, b, z, below, picker)
-            spread_input(xs, b, HALO + ZD + z, above, picker)
+            below.append(jnp.where(even, recv_b[b, z].astype(F32), recv_a[b, far].astype(F32)).astype(BF))
+            above.append(jnp.where(even, recv_a[b, z].astype(F32), recv_b[b, z].astype(F32)).astype(BF))
+        spread_input(xs, b, 0, below, picker)
+        spread_input(xs, b, HALO + ZD, above, picker)
 
     low = jnp.where(where[0] == 0, 0.0, 0.125)
     high = jnp.where(where[0] == where[1] - 1, 0.0, 0.125)
@@ -198,13 +204,14 @@
 
     lax.fori_loop(0, 2, groups, 0)
 
-    shifter = row_picker(3, 1, 16)
+    shifter = row_picker(3, 1, 4)
     for b in range(cube_count):
+        block = pooled[b].reshape(64, 1024)
+        block = jnp.concatenate([jnp.zeros((64, 64), BF), block, jnp.zeros((64, 64), BF)], axis=1)
+        moved = dot(shifter, block).astype(BF)
         for z in range(4):
-            plane = jnp.concatenate([jnp.zeros((16, 64), BF), pooled[b, z], jnp.zeros((16, 64), BF)], axis=1)
-            moved = dot(shifter, plane).astype(BF)
             for v in range(3):
-                pools[b, z, v] = moved[16 * v : 16 * v + 16]
+                pools[b, z, v] = moved[48 * z + 16 * v : 48 * z + 16 * v + 16]
 
     rows_b = cube_count * 2 * 16
     columns = []
@@ -234,20 +241,20 @@
                 grad_b[:, z, :, at : at + 128] = (up * part[:, z, :, 128 * e : 128 * e + 128]).astype(BF)
 
 
-def spread_grad(target, b, zz, plane, shifter):
-    moved = dot(shifter, plane).astype(BF)
-    for v in range(3):
-        target[b, zz, v, :, 128:2176] = moved[16 * v : 16 * v + 16]
-        target[b, zz, v, :, :128] = jnp.zeros((16, 128), BF)
-        target[b, zz, v, :, 2176:] = jnp.zeros((16, 128), BF)
+def spread_grad(target, b, zz, pair, shifter):
+    moved = dot(shifter, pair.reshape(32, 2048)).astype(BF)
+    for i in range(2):
+        for v in range(3):
+            target[b, zz + i, v, :, 128:2176] = moved[48 * i + 16 * v : 48 * i + 16 * v + 16]
+            target[b, zz + i, v, :, :128] = jnp.zeros((16, 128), BF)
+            target[b, zz + i, v, :, 2176:] = jnp.zeros((16, 128), BF)
 
 
 def terms_b_kernel(pools, grad_b, wa, wb, terms, gs, tat, tbt, back):
     cube_count = grad_b.shape[0]
-    shifter = row_picker(3, 1, 16)
+    shifter = row_picker(3, 1, 2)
     for b in range(cube_count):
-        for z in range(2):
-            spread_grad(gs, b, 2 + z, grad_b[b, z], shifter)
+        spread_grad(gs, b, 2, grad_b[b], shifter)
     for d in range(9):
         mirror(8 - d, rows_at(wa[96 * d : 96 * d + 96], 0, 128).T[:64], tat)
         block = wb[192 * d : 192 * d + 192]
@@ -362,13 +369,11 @@
     del own
     cube_count = recv_a.shape[0]
     even = where[0] % 2 == 0
-    shifter = row_picker(3, 1, 16)
-
+    shifter = row_picker(3, 1, 2)
     for b in range(cube_count):
-        for z in range(2):
-            from_a, from_b = recv_a[b, z].astype(F32), recv_b[b, z].astype(F32)
-            spread_grad(gs, b, z, jnp.where(even, from_b, from_a).astype(BF), shifter)
-            spread_grad(gs, b, 4 + z, jnp.where(even, from_a, from_b).astype(BF), shifter)
+        from_a, from_b = recv_a[b].astype(F32), recv_b[b].astype(F32)
+        spread_grad(gs, b, 0, jnp.where(even, from_b, from_a).astype(BF), shifter)
+        spread_grad(gs, b, 4, jnp.where(even, from_a, from_b).astype(BF), shifter)
 
     low = jnp.where(where[0] == 0, 0.0, 0.125)
     high = jnp.where(where[0] == where[1] - 1, 0.0, 0.125)

time: 63.5 us -> 63.5 us (level)
  no operation moved by 1% of the time
where the time goes in v12:
time: 63.5 us; the launch traced here: 63.3 us
  Pallas kernels  29 us (46%)
  starting transfers between devices  22.3 us (35%)
  waiting for transfers between devices  8.81 us (14%)
  local copies, waits for them, and re-layouts  2.07 us (3%)
  between operations  0.98 us (2%)
    pallas_call x13, Pallas kernels, call(): pl.pallas_call(kernel, out_shape=[jax.ShapeDtypeStruct(shape, dtype) for...  29 us
    ppermute x11, starting transfers between devices, swap_along(): lax.ppermute(part, axis, [(i, i ^ k * step) for i in range(count)])  13 us
    ppermute x11, waiting for transfers between devices, swap_along(): lax.ppermute(part, axis, [(i, i ^ k * step) for i in range(count)])  8.8 us
    ppermute x2, starting transfers between devices, swap(): lax.ppermute(first, 'gz', pairs_a)  7.8 us
    ppermute x2, starting transfers between devices, swap(): lax.ppermute(second, 'gz', pairs_b)  1.54 us
  transfers between devices with their start and end apart: 15, of which 8 were waited for; matrix products, arithmetic and copies ran while one was open for 2% of the time, Pallas kernels for 21%

profile of v12, /device:TPU:0, one launch (start us, length us, event | category | flops | bytes accessed | tf_op | source)
XLA Modules:
  0.0 63.3 jit_solution(15674709363916610192)
XLA Ops:
  0.6 0.5 collective-permute-start
  1.2 1.0 %constant_dynamic-slice_fusion = bf16[2,3,32,1024]{3,2,1,0:T(8,128)(2,1)S(1)} fusion(bf16[2,4,32,1024]{3,2,1,0:T(8,128)(2,1)} %cubes.1, s32[]{:T(128)S(6)} %select_n.11), kind=kLoop, calls=%fused_computation.1 | loop fusion | bytes 786436 | tf_op jit(solution)/shard_map/dynamic_slice | solution.py:547
  2.2 0.7 %collective-permute-start.1 = (bf16[2,3,32,1024]{3,2,1,0:T(8,128)(2,1)S(1)}, bf16[2,3,32,1024]{3,2,1,0:T(8,128)(2,1)S(1)}, u32[]{:S(2)}, u32[]{:S(2)}) collective-permute-start(bf16[2,3,32,1024]{3,2,1,0:T(8,128)(2,1)S(1)} %constant_dynamic-slice_fusion), channel_id=1, source_target_pairs={{1,2},{2,1},{3,4},{4,3},{5,6},{6,5},{9,10},{10,9},{11,12},{12,11},... | collective-permute-start | bytes 1179656 | tf_op jit(solution)/shard_map/ppermute | solution.py:532
  2.9 1.0 %copy-done.1 = bf16[27,8192]{1,0:T(8,128)(2,1)S(1)} copy-done((bf16[27,8192]{1,0:T(8,128)(2,1)S(1)}, bf16[27,8192]{1,0:T(8,128)(2,1)}, u32[]{:S(2)}) %copy-start.1) | copy-done | bytes 442392
  3.9 1.0 %shard_map.68 = (bf16[2304,256]{1,0:T(8,128)(2,1)S(1)}, f32[1728,128]{1,0:T(8,128)S(1)}) custom-call(bf16[27,8192]{1,0:T(8,128)(2,1)S(1)} %copy-done.1), custom_call_target="tpu_custom_call" | custom-call | flops 500000000 | bytes 1000000 | tf_op jit(solution)/shard_map/pallas_call | solution.py:517
  4.9 3.1 %shard_map.67 = (bf16[2,10,4,16,1152]{4,3,2,1,0:T(8,128)(2,1)S(1)}, bf16[2304,256]{1,0:T(8,128)(2,1)S(1)}, bf16[2,6,2,16,2048]{4,3,2,1,0:T(8,128)(2,1)S(1)}, f32...) custom-call(bf16[2,4,32,1024]{3,2,1,0:T(8,128)(2,1)S(1)} %copy-done, ...), custom_call_target="tpu_custom_call" | custom-call | flops 1000000000 | bytes 1000000 | tf_op jit(solution)/shard_map/pallas_call | solution.py:517
  8.1 6.4 %shard_map.69 = (bf16[2,10,4,16,1152]{4,3,2,1,0:T(8,128)(2,1)S(1)}, bf16[2,6,2,16,2048]{4,3,2,1,0:T(8,128)(2,1)S(1)}, bf16[2,4,3,16,1152]{4,3,2,1,0:T(8,128)(2,1)S(1)}, bf16[2,2,16,2048]{3,2,1,0:T(8,128)(2,1)S(1)}) custom-call(s32[3]{0:T(128)S(1)} %pad_add_fusion.where, ...), custom_call_target="tpu_custom_call", output_to_operand_aliasing={{0}: (1, {}), {1}: (2, {})} | custom-call | flops 8000000000 | bytes 1000000 | tf_op jit(solution)/shard_map/pallas_call | solution.py:517
  14.5 0.9 %collective-permute-start.3 = (bf16[2,2,16,2048]{3,2,1,0:T(8,128)(2,1)S(1)}, bf16[2,2,16,2048]{3,2,1,0:T(8,128)(2,1)S(1)}, u32[]{:S(2)}, u32[]{:S(2)}) collective-permute-start(bf16[2,2,16,2048]{3,2,1,0:T(8,128)(2,1)S(1)} %get-tuple-element.42.grad_b), channel_id=1, source_target_pairs={{1,2},{2,1},{3,4},{4,3},{5,6},{6,5},{9,10},{10,9},{11,12},{12,11},... | collective-permute-start | bytes 786440 | tf_op jit(solution)/shard_map/ppermute | solution.py:532
  15.3 7.3 %collective-permute-start.2 = (bf16[2,2,16,2048]{3,2,1,0:T(8,128)(2,1)S(1)}, bf16[2,2,16,2048]{3,2,1,0:T(8,128)(2,1)S(1)}, u32[]{:S(2)}, u32[]{:S(2)}) collective-permute-start(bf16[2,2,16,2048]{3,2,1,0:T(8,128)(2,1)S(1)} %get-tuple-element.42.grad_b), channel_id=1, source_target_pairs={{0,1},{1,0},{2,3},{3,2},{4,5},{5,4},{6,7},{7,6},{8,9},{9,8},{10,11... | collective-permute-start | bytes 786440 | tf_op jit(solution)/shard_map/ppermute | solution.py:532
  22.6 2.5 %shard_map.70 = (f32[1792,128]{1,0:T(8,128)S(1)}, bf16[2,6,3,16,2304]{4,3,2,1,0:T(8,128)(2,1)S(1)}, bf16[6912,256]{1,0:T(8,128)(2,1)S(1)}, bf16[6912,256]{1,0:T(8,128)(2,1)S(1)}, f32[4,2,4,16,256]{4,3,2,1,0:T(8,128)S(1)}) custom-call(bf16[2,4,3,16,1152]{4,3,2,1,0:T(8,128)(2,1)S(1)} %get-tuple-element.41.pools, ...), custom_call_target="tpu_custom_call" | custom-call | flops 1000000000 | bytes 1000000 | tf_op jit(solution)/shard_map/pallas_call | solution.py:517
  25.1 6.7 %shard_map.71 = (bf16[2,6,4,16,2304]{4,3,2,1,0:T(8,128)(2,1)S(1)}, bf16[4,280,128]{2,1,0:T(8,128)(2,1)S(1)}, bf16[4,280,128]{2,1,0:T(8,128)(2,1)S(1)}, bf16[2,6,3,16,2304]{4,3,2,1,0:T(8,128)(2,1)S(1)}) custom-call(s32[3]{0:T(128)S(1)} %pad_add_fusion.where, bf16[2,6,3,16,2304]{4,3,2,1,0:T(8,128)(2,1)S(1)} %get-tuple-element.45.own, ...), custom_call_target="tpu_custom_call", output_to_operand_aliasing={{3}: (1, {})} | custom-call | flops 6000000000 | bytes 1000000 | tf_op jit(solution)/shard_map/pallas_call | solution.py:517
  31.8 1.3 %collective-permute-start.4 = (bf16[4,280,128]{2,1,0:T(8,128)(2,1)S(1)}, bf16[4,280,128]{2,1,0:T(8,128)(2,1)S(1)}, u32[]{:S(2)}, u32[]{:S(2)}) collective-permute-start(bf16[4,280,128]{2,1,0:T(8,128)(2,1)S(1)} %get-tuple-element.56), channel_id=1, source_target_pairs={{0,1},{1,0},{2,3},{3,2},{4,5},{5,4},{6,7},{7,6},{8,9},{9,8},{10,11... | collective-permute-start | bytes 860168 | tf_op jit(solution)/shard_map/ppermute | solution.py:538
  33.2 1.2 %collective-permute-done.4.recv = bf16[4,280,128]{2,1,0:T(8,128)(2,1)S(1)} collective-permute-done((bf16[4,280,128]{2,1,0:T(8,128)(2,1)S(1)}, bf16[4,280,128]{2,1,0:T(8,128)(2,1)S(1)}, u32[]{:S(2)}, u32[]{:S(2)}) %collective-permute-start.4) | collective-permute-done | bytes 286752 | tf_op jit(solution)/shard_map/ppermute | solution.py:538
  34.4 0.6 shard_map.74
  35.0 2.0 %collective-permute-start.5 = (bf16[280,128]{1,0:T(8,128)(2,1)S(1)}, bf16[280,128]{1,0:T(8,128)(2,1)S(1)}, u32[]{:S(2)}, u32[]{:S(2)}) collective-permute-start(bf16[280,128]{1,0:T(8,128)(2,1)S(1)} %get-tuple-element.58), channel_id=1, source_target_pairs={{0,8},{8,0},{16,24},{24,16},{1,9},{9,1},{17,25},{25,17},{2,10},{10... | collective-permute-start | bytes 215048 | tf_op jit(solution)/shard_map/ppermute | solution.py:538
  37.0 1.5 %collective-permute-start.6 = (bf16[280,128]{1,0:T(8,128)(2,1)S(1)}, bf16[280,128]{1,0:T(8,128)(2,1)S(1)}, u32[]{:S(2)}, u32[]{:S(2)}) collective-permute-start(bf16[280,128]{1,0:T(8,128)(2,1)S(1)} %get-tuple-element.59), channel_id=1, source_target_pairs={{0,16},{8,24},{16,0},{24,8},{1,17},{9,25},{17,1},{25,9},{2,18},{10... | collective-permute-start | bytes 215048 | tf_op jit(solution)/shard_map/ppermute | solution.py:538
  38.6 2.3 %shard_map.72.rest_0_.after = bf16[4,32,1024]{2,1,0:T(8,128)(2,1)S(1)} custom-call(bf16[2,6,4,16,2304]{4,3,2,1,0:T(8,128)(2,1)S(1)} %get-tuple-element.51.ga, bf16[6912,256]{1,0:T(8,128)(2,1)S(1)} %get-tuple-element.52.tat), custom_call_target="tpu_custom_call" | custom-call | flops 2000000000 | bytes 1000000 | tf_op jit(solution)/shard_map/pallas_call | solution.py:517
  40.8 0.5 collective-permute-done.6.refs_2_
  41.3 2.4 %collective-permute-done.7.refs_3_ = bf16[280,128]{1,0:T(8,128)(2,1)S(1)} collective-permute-done((bf16[280,128]{1,0:T(8,128)(2,1)S(1)}, bf16[280,128]{1,0:T(8,128)(2,1)S(1)}, u32[]{:S(2)}, u32[]{:S(2)}) %collective-permute-start.7) | collective-permute-done | bytes 71712 | tf_op jit(solution)/shard_map/ppermute | solution.py:538
  43.8 3.6 %collective-permute-start.10 = (bf16[280,128]{1,0:T(8,128)(2,1)S(1)}, bf16[280,128]{1,0:T(8,128)(2,1)S(1)}, u32[]{:S(2)}, u32[]{:S(2)}) collective-permute-start(bf16[280,128]{1,0:T(8,128)(2,1)S(1)} %shard_map.75.refs_0_), channel_id=1, source_target_pairs={{0,6},{1,7},{2,4},{3,5},{4,2},{5,3},{6,0},{7,1},{8,14},{9,15},{10,... | collective-permute-start | bytes 215048 | tf_op jit(solution)/shard_map/ppermute | solution.py:538
  47.4 0.8 %collective-permute-start.8 = (bf16[280,128]{1,0:T(8,128)(2,1)S(1)}, bf16[280,128]{1,0:T(8,128)(2,1)S(1)}, u32[]{:S(2)}, u32[]{:S(2)}) collective-permute-start(bf16[280,128]{1,0:T(8,128)(2,1)S(1)} %shard_map.75.refs_0_), channel_id=1, source_target_pairs={{0,2},{1,3},{2,0},{3,1},{4,6},{5,7},{6,4},{7,5},{8,10},{9,11},{10,... | collective-permute-start | bytes 215048 | tf_op jit(solution)/shard_map/ppermute | solution.py:538
  48.2 3.0 %shard_map.73 = (bf16[2,4,32,1024]{3,2,1,0:T(8,128)(2,1)}, f32[8,128]{1,0:T(8,128)S(1)}) custom-call(bf16[2,6,4,16,2304]{4,3,2,1,0:T(8,128)(2,1)S(1)} %get-tuple-element.51.ga, bf16[6912,256]{1,0:T(8,128)(2,1)S(1)} %get-tuple-element.52.tat, bf16[4,32,1024]{2,1,0:T(8,128)(2,1)S(1)} %shard_map.72.rest_0_.after), custom_call_target="tpu_custom_call" | custom-call | flops 2000000000 | bytes 1000000 | tf_op jit(solution)/shard_map/pallas_call | solution.py:517
  51.2 1.7 %collective-permute-done.9.refs_2_ = bf16[280,128]{1,0:T(8,128)(2,1)S(1)} collective-permute-done((bf16[280,128]{1,0:T(8,128)(2,1)S(1)}, bf16[280,128]{1,0:T(8,128)(2,1)S(1)}, u32[]{:S(2)}, u32[]{:S(2)}) %collective-permute-start.9) | collective-permute-done | bytes 71712 | tf_op jit(solution)/shard_map/ppermute | solution.py:538
  53.0 0.8 %collective-permute-start.13 = (bf16[280,128]{1,0:T(8,128)(2,1)S(1)}, bf16[280,128]{1,0:T(8,128)(2,1)S(1)}, u32[]{:S(2)}, u32[]{:S(2)}) collective-permute-start(bf16[280,128]{1,0:T(8,128)(2,1)S(1)} %shard_map.76.refs_0_), channel_id=1, source_target_pairs={{0,24},{8,16},{16,8},{24,0},{1,25},{9,17},{17,9},{25,1},{2,26},{10... | collective-permute-start | bytes 215048 | tf_op jit(solution)/shard_map/ppermute | solution.py:538
  53.8 1.4 %collective-permute-start.12 = (bf16[280,128]{1,0:T(8,128)(2,1)S(1)}, bf16[280,128]{1,0:T(8,128)(2,1)S(1)}, u32[]{:S(2)}, u32[]{:S(2)}) collective-permute-start(bf16[280,128]{1,0:T(8,128)(2,1)S(1)} %shard_map.76.refs_0_), channel_id=1, source_target_pairs={{0,16},{8,24},{16,0},{24,8},{1,17},{9,25},{17,1},{25,9},{2,18},{10... | collective-permute-start | bytes 215048 | tf_op jit(solution)/shard_map/ppermute | solution.py:538
  55.1 1.4 %collective-permute-start.11 = (bf16[280,128]{1,0:T(8,128)(2,1)S(1)}, bf16[280,128]{1,0:T(8,128)(2,1)S(1)}, u32[]{:S(2)}, u32[]{:S(2)}) collective-permute-start(bf16[280,128]{1,0:T(8,128)(2,1)S(1)} %shard_map.76.refs_0_), channel_id=1, source_target_pairs={{0,8},{8,0},{16,24},{24,16},{1,9},{9,1},{17,25},{25,17},{2,10},{10... | collective-permute-start | bytes 215048 | tf_op jit(solution)/shard_map/ppermute | solution.py:538
  56.5 1.9 %collective-permute-done.13.refs_3_ = bf16[280,128]{1,0:T(8,128)(2,1)S(1)} collective-permute-done((bf16[280,128]{1,0:T(8,128)(2,1)S(1)}, bf16[280,128]{1,0:T(8,128)(2,1)S(1)}, u32[]{:S(2)}, u32[]{:S(2)}) %collective-permute-start.13) | collective-permute-done | bytes 71712 | tf_op jit(solution)/shard_map/ppermute | solution.py:538
  58.4 0.5 collective-permute-done.12.refs_2_
  58.9 0.6 collective-permute-done.11.refs_1_
  59.5 0.6 shard_map.77.pieces
  60.1 1.5 %shard_map.78 = (f32[27,2048]{1,0:T(8,128)}, f32[27,8192]{1,0:T(8,128)}) custom-call(s32[3]{0:T(128)S(1)} %pad_add_fusion.where, f32[1]{0:T(128)} %constant.27.clone.1.scale, bf16[4,280,128]{2,1,0:T(8,128)(2,1)S(1)} %shard_map.77.pieces), custom_call_target="tpu_custom_call" | custom-call | flops 1000000 | bytes 1000000 | tf_op jit(solution)/shard_map/pallas_call | solution.py:517
  61.7 1.5 %shard_map.79 = (f32[27,2048]{1,0:T(8,128)}, f32[27,8192]{1,0:T(8,128)}) custom-call(s32[3]{0:T(128)S(1)} %pad_add_fusion.where, f32[1]{0:T(128)} %constant.27.clone.1.scale, bf16[4,280,128]{2,1,0:T(8,128)(2,1)S(1)} %collective-permute-done.14.pieces, f32[27,2048]{1,0:T(8,128)} %get-tuple-element.61.before_a, ...), custom_call_target="tpu_custom_call", output_to_operand_aliasing={{0}: (3, {}), {1}: (4, {})} | custom-call | flops 1000000 | bytes 1000000 | tf_op jit(solution)/shard_map/pallas_call | solution.py:517
  (21 shorter events, 0.4 us)
Async XLA Ops:
  0.6 4.3 %copy-start = (bf16[2,4,32,1024]{3,2,1,0:T(8,128)(2,1)S(1)}, bf16[2,4,32,1024]{3,2,1,0:T(8,128)(2,1)}, u32[]{:S(2)}) copy-start(bf16[2,4,32,1024]{3,2,1,0:T(8,128)(2,1)} %cubes.1) | copy-start | bytes 1572868
  0.6 4.3 %copy-start.2 = (bf16[27,2048]{1,0:T(8,128)(2,1)S(1)}, bf16[27,2048]{1,0:T(8,128)(2,1)}, u32[]{:S(2)}) copy-start(bf16[27,2048]{1,0:T(8,128)(2,1)} %weight_a.1) | copy-start | bytes 331780
  0.6 7.4 %collective-permute-start = (bf16[2,4,32,1024]{3,2,1,0:T(8,128)(2,1)}, bf16[2,4,32,1024]{3,2,1,0:T(8,128)(2,1)S(1)}, u32[]{:S(2)}, u32[]{:S(2)}) collective-permute-start(bf16[2,4,32,1024]{3,2,1,0:T(8,128)(2,1)} %cubes.1), channel_id=1, source_target_pairs={{0,1},{1,0},{2,3},{3,2},{4,5},{5,4},{6,7},{7,6},{8,9},{9,8},{10,11... | collective-permute-start | bytes 1572872 | tf_op jit(solution)/shard_map/ppermute | solution.py:532
  2.2 5.9 %collective-permute-start.1 = (bf16[2,3,32,1024]{3,2,1,0:T(8,128)(2,1)S(1)}, bf16[2,3,32,1024]{3,2,1,0:T(8,128)(2,1)S(1)}, u32[]{:S(2)}, u32[]{:S(2)}) collective-permute-start(bf16[2,3,32,1024]{3,2,1,0:T(8,128)(2,1)S(1)} %constant_dynamic-slice_fusion), channel_id=1, source_target_pairs={{1,2},{2,1},{3,4},{4,3},{5,6},{6,5},{9,10},{10,9},{11,12},{12,11},... | collective-permute-start | bytes 1179656 | tf_op jit(solution)/shard_map/ppermute | solution.py:532
  2.9 1.0 %copy-start.1 = (bf16[27,8192]{1,0:T(8,128)(2,1)S(1)}, bf16[27,8192]{1,0:T(8,128)(2,1)}, u32[]{:S(2)}) copy-start(bf16[27,8192]{1,0:T(8,128)(2,1)} %weight_b.1) | copy-start | bytes 1327108
  3.9 4.1 %copy-start.3 = (bf16[2,1,8,1024]{3,2,1,0:T(8,128)(2,1)S(1)}, bf16[2,1,8,1024]{3,2,1,0:T(8,128)(2,1)}, u32[]{:S(2)}) copy-start(bf16[2,1,8,1024]{3,2,1,0:T(8,128)(2,1)} %cot.1) | copy-start | bytes 98308
  14.5 10.7 %collective-permute-start.3 = (bf16[2,2,16,2048]{3,2,1,0:T(8,128)(2,1)S(1)}, bf16[2,2,16,2048]{3,2,1,0:T(8,128)(2,1)S(1)}, u32[]{:S(2)}, u32[]{:S(2)}) collective-permute-start(bf16[2,2,16,2048]{3,2,1,0:T(8,128)(2,1)S(1)} %get-tuple-element.42.grad_b), channel_id=1, source_target_pairs={{1,2},{2,1},{3,4},{4,3},{5,6},{6,5},{9,10},{10,9},{11,12},{12,11},... | collective-permute-start | bytes 786440 | tf_op jit(solution)/shard_map/ppermute | solution.py:532
  15.3 9.8 %collective-permute-start.2 = (bf16[2,2,16,2048]{3,2,1,0:T(8,128)(2,1)S(1)}, bf16[2,2,16,2048]{3,2,1,0:T(8,128)(2,1)S(1)}, u32[]{:S(2)}, u32[]{:S(2)}) collective-permute-start(bf16[2,2,16,2048]{3,2,1,0:T(8,128)(2,1)S(1)} %get-tuple-element.42.grad_b), channel_id=1, source_target_pairs={{0,1},{1,0},{2,3},{3,2},{4,5},{5,4},{6,7},{7,6},{8,9},{9,8},{10,11... | collective-permute-start | bytes 786440 | tf_op jit(solution)/shard_map/ppermute | solution.py:532
  31.8 2.5 %collective-permute-start.4 = (bf16[4,280,128]{2,1,0:T(8,128)(2,1)S(1)}, bf16[4,280,128]{2,1,0:T(8,128)(2,1)S(1)}, u32[]{:S(2)}, u32[]{:S(2)}) collective-permute-start(bf16[4,280,128]{2,1,0:T(8,128)(2,1)S(1)} %get-tuple-element.56), channel_id=1, source_target_pairs={{0,1},{1,0},{2,3},{3,2},{4,5},{5,4},{6,7},{7,6},{8,9},{9,8},{10,11... | collective-permute-start | bytes 860168 | tf_op jit(solution)/shard_map/ppermute | solution.py:538
  35.0 5.9 %collective-permute-start.5 = (bf16[280,128]{1,0:T(8,128)(2,1)S(1)}, bf16[280,128]{1,0:T(8,128)(2,1)S(1)}, u32[]{:S(2)}, u32[]{:S(2)}) collective-permute-start(bf16[280,128]{1,0:T(8,128)(2,1)S(1)} %get-tuple-element.58), channel_id=1, source_target_pairs={{0,8},{8,0},{16,24},{24,16},{1,9},{9,1},{17,25},{25,17},{2,10},{10... | collective-permute-start | bytes 215048 | tf_op jit(solution)/shard_map/ppermute | solution.py:538
  37.0 4.3 %collective-permute-start.6 = (bf16[280,128]{1,0:T(8,128)(2,1)S(1)}, bf16[280,128]{1,0:T(8,128)(2,1)S(1)}, u32[]{:S(2)}, u32[]{:S(2)}) collective-permute-start(bf16[280,128]{1,0:T(8,128)(2,1)S(1)} %get-tuple-element.59), channel_id=1, source_target_pairs={{0,16},{8,24},{16,0},{24,8},{1,17},{9,25},{17,1},{25,9},{2,18},{10... | collective-permute-start | bytes 215048 | tf_op jit(solution)/shard_map/ppermute | solution.py:538
  38.5 5.2 %collective-permute-start.7 = (bf16[280,128]{1,0:T(8,128)(2,1)S(1)}, bf16[280,128]{1,0:T(8,128)(2,1)S(1)}, u32[]{:S(2)}, u32[]{:S(2)}) collective-permute-start(bf16[280,128]{1,0:T(8,128)(2,1)S(1)} %get-tuple-element.60), channel_id=1, source_target_pairs={{0,24},{8,16},{16,8},{24,0},{1,25},{9,17},{17,9},{25,1},{2,26},{10... | collective-permute-start | bytes 215048 | tf_op jit(solution)/shard_map/ppermute | solution.py:538
  43.8 7.4 %collective-permute-start.10 = (bf16[280,128]{1,0:T(8,128)(2,1)S(1)}, bf16[280,128]{1,0:T(8,128)(2,1)S(1)}, u32[]{:S(2)}, u32[]{:S(2)}) collective-permute-start(bf16[280,128]{1,0:T(8,128)(2,1)S(1)} %shard_map.75.refs_0_), channel_id=1, source_target_pairs={{0,6},{1,7},{2,4},{3,5},{4,2},{5,3},{6,0},{7,1},{8,14},{9,15},{10,... | collective-permute-start | bytes 215048 | tf_op jit(solution)/shard_map/ppermute | solution.py:538
  47.4 5.5 %collective-permute-start.9 = (bf16[280,128]{1,0:T(8,128)(2,1)S(1)}, bf16[280,128]{1,0:T(8,128)(2,1)S(1)}, u32[]{:S(2)}, u32[]{:S(2)}) collective-permute-start(bf16[280,128]{1,0:T(8,128)(2,1)S(1)} %shard_map.75.refs_0_), channel_id=1, source_target_pairs={{0,4},{1,5},{2,6},{3,7},{4,0},{5,1},{6,2},{7,3},{8,12},{9,13},{10,... | collective-permute-start | bytes 215048 | tf_op jit(solution)/shard_map/ppermute | solution.py:538
  47.4 5.5 %collective-permute-start.8 = (bf16[280,128]{1,0:T(8,128)(2,1)S(1)}, bf16[280,128]{1,0:T(8,128)(2,1)S(1)}, u32[]{:S(2)}, u32[]{:S(2)}) collective-permute-start(bf16[280,128]{1,0:T(8,128)(2,1)S(1)} %shard_map.75.refs_0_), channel_id=1, source_target_pairs={{0,2},{1,3},{2,0},{3,1},{4,6},{5,7},{6,4},{7,5},{8,10},{9,11},{10,... | collective-permute-start | bytes 215048 | tf_op jit(solution)/shard_map/ppermute | solution.py:538
  53.0 5.4 %collective-permute-start.13 = (bf16[280,128]{1,0:T(8,128)(2,1)S(1)}, bf16[280,128]{1,0:T(8,128)(2,1)S(1)}, u32[]{:S(2)}, u32[]{:S(2)}) collective-permute-start(bf16[280,128]{1,0:T(8,128)(2,1)S(1)} %shard_map.76.refs_0_), channel_id=1, source_target_pairs={{0,24},{8,16},{16,8},{24,0},{1,25},{9,17},{17,9},{25,1},{2,26},{10... | collective-permute-start | bytes 215048 | tf_op jit(solution)/shard_map/ppermute | solution.py:538
  53.8 5.1 %collective-permute-start.12 = (bf16[280,128]{1,0:T(8,128)(2,1)S(1)}, bf16[280,128]{1,0:T(8,128)(2,1)S(1)}, u32[]{:S(2)}, u32[]{:S(2)}) collective-permute-start(bf16[280,128]{1,0:T(8,128)(2,1)S(1)} %shard_map.76.refs_0_), channel_id=1, source_target_pairs={{0,16},{8,24},{16,0},{24,8},{1,17},{9,25},{17,1},{25,9},{2,18},{10... | collective-permute-start | bytes 215048 | tf_op jit(solution)/shard_map/ppermute | solution.py:538
  55.1 4.3 %collective-permute-start.11 = (bf16[280,128]{1,0:T(8,128)(2,1)S(1)}, bf16[280,128]{1,0:T(8,128)(2,1)S(1)}, u32[]{:S(2)}, u32[]{:S(2)}) collective-permute-start(bf16[280,128]{1,0:T(8,128)(2,1)S(1)} %shard_map.76.refs_0_), channel_id=1, source_target_pairs={{0,8},{8,0},{16,24},{24,16},{1,9},{9,1},{17,25},{25,17},{2,10},{10... | collective-permute-start | bytes 215048 | tf_op jit(solution)/shard_map/ppermute | solution.py:538
  60.0 1.6 %collective-permute-start.14 = (bf16[4,280,128]{2,1,0:T(8,128)(2,1)S(1)}, bf16[4,280,128]{2,1,0:T(8,128)(2,1)S(1)}, u32[]{:S(2)}, u32[]{:S(2)}) collective-permute-start(bf16[4,280,128]{2,1,0:T(8,128)(2,1)S(1)} %shard_map.77.pieces), channel_id=1, source_target_pairs={{0,1},{1,0},{2,3},{3,2},{4,5},{5,4},{6,7},{7,6},{8,9},{9,8},{10,11... | collective-permute-start | bytes 860168 | tf_op jit(solution)/shard_map/ppermute | solution.py:538

commit v13 on v12

--- a/solution.py
+++ b/solution.py
@@ -1,3 +1,5 @@
+import functools
+
 import jax
 import jax.numpy as jnp
 from jax import lax
@@ -16,8 +18,11 @@
 BF = jnp.bfloat16
 F32 = jnp.float32
 VMEM = pl.BlockSpec(memory_space=pltpu.VMEM)
-SMEM = pl.BlockSpec(memory_space=pltpu.SMEM)
 ANY = pl.BlockSpec(memory_space=pl.ANY)
+
+
+def position():
+    return lax.axis_index("gz"), lax.axis_size("gz"), lax.axis_index("sample")
 
 
 def dot(a, b):
@@ -150,8 +155,9 @@
             tb[256 * d : 256 * d + 256, 128 * e : 128 * e + 128] = rows_at(block, 64 * e, 256)
 
 
-def forward_kernel(where, own, own_slope, inner, edge_low, edge_high, recv_a, recv_b, ta, tb, cot, xs, dsl, pools, grad_b, pooled):
+def forward_kernel(own, own_slope, inner, edge_low, edge_high, recv_a, recv_b, ta, tb, cot, xs, dsl, pools, grad_b, pooled):
     del own, own_slope
+    where = position()
     cube_count = xs.shape[0]
     even = where[0] % 2 == 0
     picker = row_picker(4, 2, HALO)
@@ -315,7 +321,8 @@
     return parts[0]
 
 
-def scatter_kernel(where, keep, recv, *outs):
+def scatter_kernel(keep, recv, *outs):
+    where = position()
     for k, out in enumerate(outs):
         part = where[2] ^ k
         out[...] = (keep[part].astype(F32) + recv[part].astype(F32)).astype(BF)
@@ -327,7 +334,8 @@
     out[...] = tree([part[...].astype(F32) for part in parts]).astype(BF)
 
 
-def stack_kernel(where, *refs):
+def stack_kernel(*refs):
+    where = position()
     parts, out = refs[:-1], refs[-1]
     for k, part in enumerate(parts):
         out[where[2] ^ k] = part[...]
@@ -356,17 +364,18 @@
         copy.wait()
 
 
-def first_half_kernel(where, scale, pieces, out_a, out_b, whole, half_a, half_b, sems):
-    send_half(where[0] % 2, pieces, scale[0], (out_a, out_b), (half_a, half_b), whole, sems)
-
-
-def finish_kernel(where, scale, pieces, before_a, before_b, out_a, out_b, whole, half_a, half_b, sems):
+def first_half_kernel(scale, pieces, out_a, out_b, whole, half_a, half_b, sems):
+    send_half(position()[0] % 2, pieces, scale, (out_a, out_b), (half_a, half_b), whole, sems)
+
+
+def finish_kernel(scale, pieces, before_a, before_b, out_a, out_b, whole, half_a, half_b, sems):
     del before_a, before_b
-    send_half(1 - where[0] % 2, pieces, scale[0], (out_a, out_b), (half_a, half_b), whole, sems)
-
-
-def backward_kernel(where, own, recv_a, recv_b, tbt, dsl, xs, terms_b, back, ga, keep, send, gs, gpool, acc, term, terms):
+    send_half(1 - position()[0] % 2, pieces, scale, (out_a, out_b), (half_a, half_b), whole, sems)
+
+
+def backward_kernel(own, recv_a, recv_b, tbt, dsl, xs, terms_b, back, ga, keep, send, gs, gpool, acc, term, terms):
     del own
+    where = position()
     cube_count = recv_a.shape[0]
     even = where[0] % 2 == 0
     shifter = row_picker(3, 1, 2)
@@ -512,8 +521,8 @@
         copy.wait()
 
 
-def call(kernel, args, outs, scratch, flops, smem=0, any_in=(), any_out=(), aliases=None):
-    specs = [SMEM if i < smem else ANY if i in any_in else VMEM for i in range(len(args))]
+def call(kernel, args, outs, scratch, flops, any_in=(), any_out=(), aliases=None):
+    specs = [ANY if i in any_in else VMEM for i in range(len(args))]
     return pl.pallas_call(
         kernel,
         out_shape=[jax.ShapeDtypeStruct(shape, dtype) for shape, dtype in outs],
@@ -543,7 +552,6 @@
     cube_count = cubes.shape[0]
     ring = lax.axis_size("gz")
     samples = lax.axis_size("sample")
-    where = jnp.stack([lax.axis_index("gz"), jnp.int32(ring), lax.axis_index("sample")]).astype(jnp.int32)
     outer = lax.dynamic_slice_in_dim(cubes, lax.axis_index("gz") % 2, HALO, axis=1)
     recv_a, recv_b = swap(cubes, outer, ring)
 
@@ -567,7 +575,7 @@
     )
     xs, dsl, pools, grad_b = call(
         forward_kernel,
-        [where, own_xs, own_slope, inner, edge_low, edge_high, recv_a, recv_b, ta, tb, cotangent],
+        [own_xs, own_slope, inner, edge_low, edge_high, recv_a, recv_b, ta, tb, cotangent],
         [
             ((cube_count, ZD + 2 * HALO, 4, 16, 1152), BF),
             ((cube_count, 6, 2, 16, 2048), BF),
@@ -576,8 +584,7 @@
         ],
         [pltpu.VMEM((cube_count, 4, 16, 1024), BF)],
         8_000_000_000,
-        smem=1,
-        aliases={1: 0, 2: 1},
+        aliases={0: 0, 1: 1},
     )
     back_a, back_b = swap(grad_b, grad_b, ring)
     spread = ((cube_count, 6, 3, 16, 2304), BF)
@@ -593,7 +600,7 @@
     pieces = ((samples, piece, 128), BF)
     ga, keep, send, _ = call(
         backward_kernel,
-        [where, own_gs, back_a, back_b, tbt, dsl, xs, terms_b, back],
+        [own_gs, back_a, back_b, tbt, dsl, xs, terms_b, back],
         [((cube_count, 6, 4, 16, 2304), BF), pieces, pieces, spread],
         [
             pltpu.VMEM((cube_count, 4, 16, 1024), F32),
@@ -602,12 +609,11 @@
             pltpu.VMEM((ROWS_A, 128), F32),
         ],
         6_000_000_000,
-        smem=1,
-        aliases={1: 3},
+        aliases={0: 3},
     )
     small = [((piece, 128), BF)]
     (recv,) = swap_along([send] * 2, "gz", 1)
-    parts = call(scatter_kernel, [where, keep, recv], small * samples, [], 1_000_000, smem=1)
+    parts = call(scatter_kernel, [keep, recv], small * samples, [], 1_000_000)
     others = swap_along(parts, "sample", 1)
     cube = (ZD, SIDE, SIDE * C1)
     early = [
@@ -625,10 +631,10 @@
     )
     (mine,) = call(add_kernel, [done, mine, *others], small, [], 1_000_000)
     (own,) = call(
-        stack_kernel, [where, mine, *swap_along([mine] * samples, "sample", 1)], [pieces], [], 1_000_000, smem=1
+        stack_kernel, [mine, *swap_along([mine] * samples, "sample", 1)], [pieces], [], 1_000_000
     )
     (other,) = swap_along([own] * 2, "gz", 1)
-    scale = jnp.full((1,), 1.0 / (cube_count * samples), F32)
+    scale = 1.0 / (cube_count * samples)
     shapes = [((27, C1 * C2), F32), ((27, C2 * C3), F32)]
     scratch = [
         pltpu.VMEM((samples, piece, 128), F32),
@@ -636,17 +642,16 @@
         pltpu.VMEM((27, C2 * C3 // 2), F32),
         pltpu.SemaphoreType.DMA((2,)),
     ]
-    totals = call(first_half_kernel, [where, scale, own], shapes, scratch, 1_000_000, smem=2, any_out=(0, 1))
+    totals = call(functools.partial(first_half_kernel, scale), [own], shapes, scratch, 1_000_000, any_out=(0, 1))
     total_a, total_b = call(
-        finish_kernel,
-        [where, scale, other, *totals],
+        functools.partial(finish_kernel, scale),
+        [other, *totals],
         shapes,
         scratch,
         1_000_000,
-        smem=2,
-        any_in=(3, 4),
+        any_in=(1, 2),
         any_out=(0, 1),
-        aliases={3: 0, 4: 1},
+        aliases={1: 0, 2: 1},
     )
     return input_grad, total_a, total_b
 

time: 63.5 us -> 60.8 us (0.957)
  Pallas kernels: 29 us -> 25.6 us
    pallas_call x13, Pallas kernels: 29 us -> 25.6 us  [call(): pl.pallas_call(kernel, out_shape=[jax.ShapeDtypeStruct(shape, dtype) for...]
where the time goes in v13:
time: 60.8 us; the launch traced here: 60.6 us
  Pallas kernels  25.6 us (42%)
  starting transfers between devices  22.5 us (37%)
  waiting for transfers between devices  9.39 us (15%)
  local copies, waits for them, and re-layouts  2.07 us (3%)
  between operations  0.99 us (2%)
    pallas_call x13, Pallas kernels, call(): pl.pallas_call(kernel, out_shape=[jax.ShapeDtypeStruct(shape, dtype) for...  25.6 us
    ppermute x11, starting transfers between devices, swap_along(): lax.ppermute(part, axis, [(i, i ^ k * step) for i in range(count)])  13.1 us
    ppermute x11, waiting for transfers between devices, swap_along(): lax.ppermute(part, axis, [(i, i ^ k * step) for i in range(count)])  9.38 us
    ppermute x2, starting transfers between devices, swap(): lax.ppermute(first, 'gz', pairs_a)  7.91 us
    ppermute x2, starting transfers between devices, swap(): lax.ppermute(second, 'gz', pairs_b)  1.54 us
  transfers between devices with their start and end apart: 15, of which 8 were waited for; matrix products, arithmetic and copies ran while one was open for 2% of the time, Pallas kernels for 21%

profile of v13, /device:TPU:0, one launch (start us, length us, event | category | flops | bytes accessed | tf_op | source)
XLA Modules:
  0.0 60.6 jit_solution(12275121581897197145)
XLA Ops:
  0.6 0.5 collective-permute-start
  1.2 1.0 %constant_dynamic-slice_fusion = bf16[2,3,32,1024]{3,2,1,0:T(8,128)(2,1)S(1)} fusion(bf16[2,4,32,1024]{3,2,1,0:T(8,128)(2,1)} %cubes.1, s32[]{:T(128)S(6)} %select_n.11), kind=kLoop, calls=%fused_computation | loop fusion | bytes 786436 | tf_op jit(solution)/shard_map/dynamic_slice | solution.py:555
  2.2 0.7 %collective-permute-start.1 = (bf16[2,3,32,1024]{3,2,1,0:T(8,128)(2,1)S(1)}, bf16[2,3,32,1024]{3,2,1,0:T(8,128)(2,1)S(1)}, u32[]{:S(2)}, u32[]{:S(2)}) collective-permute-start(bf16[2,3,32,1024]{3,2,1,0:T(8,128)(2,1)S(1)} %constant_dynamic-slice_fusion), channel_id=1, source_target_pairs={{1,2},{2,1},{3,4},{4,3},{5,6},{6,5},{9,10},{10,9},{11,12},{12,11},... | collective-permute-start | bytes 1179656 | tf_op jit(solution)/shard_map/ppermute | solution.py:541
  2.9 1.0 %copy-done.1 = bf16[27,8192]{1,0:T(8,128)(2,1)S(1)} copy-done((bf16[27,8192]{1,0:T(8,128)(2,1)S(1)}, bf16[27,8192]{1,0:T(8,128)(2,1)}, u32[]{:S(2)}) %copy-start.1) | copy-done | bytes 442392
  3.9 1.0 %shard_map.68 = (bf16[2304,256]{1,0:T(8,128)(2,1)S(1)}, f32[1728,128]{1,0:T(8,128)S(1)}) custom-call(bf16[27,8192]{1,0:T(8,128)(2,1)S(1)} %copy-done.1), custom_call_target="tpu_custom_call" | custom-call | flops 500000000 | bytes 1000000 | tf_op jit(solution)/shard_map/pallas_call | solution.py:526
  4.9 3.0 %shard_map.67 = (bf16[2,10,4,16,1152]{4,3,2,1,0:T(8,128)(2,1)S(1)}, bf16[2304,256]{1,0:T(8,128)(2,1)S(1)}, bf16[2,6,2,16,2048]{4,3,2,1,0:T(8,128)(2,1)S(1)}, f32...) custom-call(bf16[2,4,32,1024]{3,2,1,0:T(8,128)(2,1)S(1)} %copy-done, ...), custom_call_target="tpu_custom_call" | custom-call | flops 1000000000 | bytes 1000000 | tf_op jit(solution)/shard_map/pallas_call | solution.py:526
  8.0 5.8 %shard_map.69 = (bf16[2,10,4,16,1152]{4,3,2,1,0:T(8,128)(2,1)S(1)}, bf16[2,6,2,16,2048]{4,3,2,1,0:T(8,128)(2,1)S(1)}, bf16[2,4,3,16,1152]{4,3,2,1,0:T(8,128)(2,1)S(1)}, bf16[2,2,16,2048]{3,2,1,0:T(8,128)(2,1)S(1)}) custom-call(bf16[2,10,4,16,1152]{4,3,2,1,0:T(8,128)(2,1)S(1)} %get-tuple-element.34.own, ...), custom_call_target="tpu_custom_call", output_to_operand_aliasing={{0}: (0, {}), {1}: (1, {})} | custom-call | flops 8000000000 | bytes 1000000 | tf_op jit(solution)/shard_map/pallas_call | solution.py:526
  13.8 0.9 %collective-permute-start.3 = (bf16[2,2,16,2048]{3,2,1,0:T(8,128)(2,1)S(1)}, bf16[2,2,16,2048]{3,2,1,0:T(8,128)(2,1)S(1)}, u32[]{:S(2)}, u32[]{:S(2)}) collective-permute-start(bf16[2,2,16,2048]{3,2,1,0:T(8,128)(2,1)S(1)} %get-tuple-element.42.grad_b), channel_id=1, source_target_pairs={{1,2},{2,1},{3,4},{4,3},{5,6},{6,5},{9,10},{10,9},{11,12},{12,11},... | collective-permute-start | bytes 786440 | tf_op jit(solution)/shard_map/ppermute | solution.py:541
  14.7 7.4 %collective-permute-start.2 = (bf16[2,2,16,2048]{3,2,1,0:T(8,128)(2,1)S(1)}, bf16[2,2,16,2048]{3,2,1,0:T(8,128)(2,1)S(1)}, u32[]{:S(2)}, u32[]{:S(2)}) collective-permute-start(bf16[2,2,16,2048]{3,2,1,0:T(8,128)(2,1)S(1)} %get-tuple-element.42.grad_b), channel_id=1, source_target_pairs={{0,1},{1,0},{2,3},{3,2},{4,5},{5,4},{6,7},{7,6},{8,9},{9,8},{10,11... | collective-permute-start | bytes 786440 | tf_op jit(solution)/shard_map/ppermute | solution.py:541
  22.1 2.4 %shard_map.70 = (f32[1792,128]{1,0:T(8,128)S(1)}, bf16[2,6,3,16,2304]{4,3,2,1,0:T(8,128)(2,1)S(1)}, bf16[6912,256]{1,0:T(8,128)(2,1)S(1)}, bf16[6912,256]{1,0:T(8,128)(2,1)S(1)}, f32[4,2,4,16,256]{4,3,2,1,0:T(8,128)S(1)}) custom-call(bf16[2,4,3,16,1152]{4,3,2,1,0:T(8,128)(2,1)S(1)} %get-tuple-element.41.pools, ...), custom_call_target="tpu_custom_call" | custom-call | flops 1000000000 | bytes 1000000 | tf_op jit(solution)/shard_map/pallas_call | solution.py:526
  24.5 6.1 %shard_map.71 = (bf16[2,6,4,16,2304]{4,3,2,1,0:T(8,128)(2,1)S(1)}, bf16[4,280,128]{2,1,0:T(8,128)(2,1)S(1)}, bf16[4,280,128]{2,1,0:T(8,128)(2,1)S(1)}, bf16[2,6,3,16,2304]{4,3,2,1,0:T(8,128)(2,1)S(1)}) custom-call(bf16[2,6,3,16,2304]{4,3,2,1,0:T(8,128)(2,1)S(1)} %get-tuple-element.45.own, ...), custom_call_target="tpu_custom_call", output_to_operand_aliasing={{3}: (0, {})} | custom-call | flops 6000000000 | bytes 1000000 | tf_op jit(solution)/shard_map/pallas_call | solution.py:526
  30.7 1.4 %collective-permute-start.4 = (bf16[4,280,128]{2,1,0:T(8,128)(2,1)S(1)}, bf16[4,280,128]{2,1,0:T(8,128)(2,1)S(1)}, u32[]{:S(2)}, u32[]{:S(2)}) collective-permute-start(bf16[4,280,128]{2,1,0:T(8,128)(2,1)S(1)} %get-tuple-element.56), channel_id=1, source_target_pairs={{0,1},{1,0},{2,3},{3,2},{4,5},{5,4},{6,7},{7,6},{8,9},{9,8},{10,11... | collective-permute-start | bytes 860168 | tf_op jit(solution)/shard_map/ppermute | solution.py:547
  32.1 1.2 %collective-permute-done.4.recv = bf16[4,280,128]{2,1,0:T(8,128)(2,1)S(1)} collective-permute-done((bf16[4,280,128]{2,1,0:T(8,128)(2,1)S(1)}, bf16[4,280,128]{2,1,0:T(8,128)(2,1)S(1)}, u32[]{:S(2)}, u32[]{:S(2)}) %collective-permute-start.4) | collective-permute-done | bytes 286752 | tf_op jit(solution)/shard_map/ppermute | solution.py:547
  33.3 2.0 %collective-permute-start.5 = (bf16[280,128]{1,0:T(8,128)(2,1)S(1)}, bf16[280,128]{1,0:T(8,128)(2,1)S(1)}, u32[]{:S(2)}, u32[]{:S(2)}) collective-permute-start(bf16[280,128]{1,0:T(8,128)(2,1)S(1)} %get-tuple-element.58), channel_id=1, source_target_pairs={{0,8},{8,0},{16,24},{24,16},{1,9},{9,1},{17,25},{25,17},{2,10},{10... | collective-permute-start | bytes 215048 | tf_op jit(solution)/shard_map/ppermute | solution.py:547
  35.4 1.5 %collective-permute-start.6 = (bf16[280,128]{1,0:T(8,128)(2,1)S(1)}, bf16[280,128]{1,0:T(8,128)(2,1)S(1)}, u32[]{:S(2)}, u32[]{:S(2)}) collective-permute-start(bf16[280,128]{1,0:T(8,128)(2,1)S(1)} %get-tuple-element.59), channel_id=1, source_target_pairs={{0,16},{8,24},{16,0},{24,8},{1,17},{9,25},{17,1},{25,9},{2,18},{10... | collective-permute-start | bytes 215048 | tf_op jit(solution)/shard_map/ppermute | solution.py:547
  36.9 2.3 %shard_map.72.rest_0_.after = bf16[4,32,1024]{2,1,0:T(8,128)(2,1)S(1)} custom-call(bf16[2,6,4,16,2304]{4,3,2,1,0:T(8,128)(2,1)S(1)} %get-tuple-element.51.ga, bf16[6912,256]{1,0:T(8,128)(2,1)S(1)} %get-tuple-element.52.tat), custom_call_target="tpu_custom_call" | custom-call | flops 2000000000 | bytes 1000000 | tf_op jit(solution)/shard_map/pallas_call | solution.py:526
  39.2 0.5 collective-permute-done.6.refs_2_
  39.7 2.4 %collective-permute-done.7.refs_3_ = bf16[280,128]{1,0:T(8,128)(2,1)S(1)} collective-permute-done((bf16[280,128]{1,0:T(8,128)(2,1)S(1)}, bf16[280,128]{1,0:T(8,128)(2,1)S(1)}, u32[]{:S(2)}, u32[]{:S(2)}) %collective-permute-start.7) | collective-permute-done | bytes 71712 | tf_op jit(solution)/shard_map/ppermute | solution.py:547
  42.1 3.6 %collective-permute-start.10 = (bf16[280,128]{1,0:T(8,128)(2,1)S(1)}, bf16[280,128]{1,0:T(8,128)(2,1)S(1)}, u32[]{:S(2)}, u32[]{:S(2)}) collective-permute-start(bf16[280,128]{1,0:T(8,128)(2,1)S(1)} %shard_map.75.refs_0_), channel_id=1, source_target_pairs={{0,6},{1,7},{2,4},{3,5},{4,2},{5,3},{6,0},{7,1},{8,14},{9,15},{10,... | collective-permute-start | bytes 215048 | tf_op jit(solution)/shard_map/ppermute | solution.py:547
  45.8 0.8 %collective-permute-start.8 = (bf16[280,128]{1,0:T(8,128)(2,1)S(1)}, bf16[280,128]{1,0:T(8,128)(2,1)S(1)}, u32[]{:S(2)}, u32[]{:S(2)}) collective-permute-start(bf16[280,128]{1,0:T(8,128)(2,1)S(1)} %shard_map.75.refs_0_), channel_id=1, source_target_pairs={{0,2},{1,3},{2,0},{3,1},{4,6},{5,7},{6,4},{7,5},{8,10},{9,11},{10,... | collective-permute-start | bytes 215048 | tf_op jit(solution)/shard_map/ppermute | solution.py:547
  46.6 2.9 %shard_map.73 = (bf16[2,4,32,1024]{3,2,1,0:T(8,128)(2,1)}, f32[8,128]{1,0:T(8,128)S(1)}) custom-call(bf16[2,6,4,16,2304]{4,3,2,1,0:T(8,128)(2,1)S(1)} %get-tuple-element.51.ga, bf16[6912,256]{1,0:T(8,128)(2,1)S(1)} %get-tuple-element.52.tat, bf16[4,32,1024]{2,1,0:T(8,128)(2,1)S(1)} %shard_map.72.rest_0_.after), custom_call_target="tpu_custom_call" | custom-call | flops 2000000000 | bytes 1000000 | tf_op jit(solution)/shard_map/pallas_call | solution.py:526
  49.6 1.7 %collective-permute-done.9.refs_2_ = bf16[280,128]{1,0:T(8,128)(2,1)S(1)} collective-permute-done((bf16[280,128]{1,0:T(8,128)(2,1)S(1)}, bf16[280,128]{1,0:T(8,128)(2,1)S(1)}, u32[]{:S(2)}, u32[]{:S(2)}) %collective-permute-start.9) | collective-permute-done | bytes 71712 | tf_op jit(solution)/shard_map/ppermute | solution.py:547
  51.3 0.8 %collective-permute-start.13 = (bf16[280,128]{1,0:T(8,128)(2,1)S(1)}, bf16[280,128]{1,0:T(8,128)(2,1)S(1)}, u32[]{:S(2)}, u32[]{:S(2)}) collective-permute-start(bf16[280,128]{1,0:T(8,128)(2,1)S(1)} %shard_map.76.refs_0_), channel_id=1, source_target_pairs={{0,24},{8,16},{16,8},{24,0},{1,25},{9,17},{17,9},{25,1},{2,26},{10... | collective-permute-start | bytes 215048 | tf_op jit(solution)/shard_map/ppermute | solution.py:547
  52.1 1.4 %collective-permute-start.12 = (bf16[280,128]{1,0:T(8,128)(2,1)S(1)}, bf16[280,128]{1,0:T(8,128)(2,1)S(1)}, u32[]{:S(2)}, u32[]{:S(2)}) collective-permute-start(bf16[280,128]{1,0:T(8,128)(2,1)S(1)} %shard_map.76.refs_0_), channel_id=1, source_target_pairs={{0,16},{8,24},{16,0},{24,8},{1,17},{9,25},{17,1},{25,9},{2,18},{10... | collective-permute-start | bytes 215048 | tf_op jit(solution)/shard_map/ppermute | solution.py:547
  53.5 1.4 %collective-permute-start.11 = (bf16[280,128]{1,0:T(8,128)(2,1)S(1)}, bf16[280,128]{1,0:T(8,128)(2,1)S(1)}, u32[]{:S(2)}, u32[]{:S(2)}) collective-permute-start(bf16[280,128]{1,0:T(8,128)(2,1)S(1)} %shard_map.76.refs_0_), channel_id=1, source_target_pairs={{0,8},{8,0},{16,24},{24,16},{1,9},{9,1},{17,25},{25,17},{2,10},{10... | collective-permute-start | bytes 215048 | tf_op jit(solution)/shard_map/ppermute | solution.py:547
  54.9 1.9 %collective-permute-done.13.refs_3_ = bf16[280,128]{1,0:T(8,128)(2,1)S(1)} collective-permute-done((bf16[280,128]{1,0:T(8,128)(2,1)S(1)}, bf16[280,128]{1,0:T(8,128)(2,1)S(1)}, u32[]{:S(2)}, u32[]{:S(2)}) %collective-permute-start.13) | collective-permute-done | bytes 71712 | tf_op jit(solution)/shard_map/ppermute | solution.py:547
  56.8 0.4 collective-permute-done.12.refs_2_
  57.2 0.6 collective-permute-done.11.refs_1_
  57.9 0.1 collective-permute-start.14
  57.9 0.9 %shard_map.78 = (f32[27,2048]{1,0:T(8,128)}, f32[27,8192]{1,0:T(8,128)}) custom-call(bf16[4,280,128]{2,1,0:T(8,128)(2,1)S(1)} %shard_map.77.pieces), custom_call_target="tpu_custom_call" | custom-call | flops 1000000 | bytes 1000000 | tf_op jit(solution)/shard_map/pallas_call | solution.py:526
  58.9 0.6 %collective-permute-done.14.pieces = bf16[4,280,128]{2,1,0:T(8,128)(2,1)S(1)} collective-permute-done((bf16[4,280,128]{2,1,0:T(8,128)(2,1)S(1)}, bf16[4,280,128]{2,1,0:T(8,128)(2,1)S(1)}, u32[]{:S(2)}, u32[]{:S(2)}) %collective-permute-start.14) | collective-permute-done | bytes 286752 | tf_op jit(solution)/shard_map/ppermute | solution.py:547
  59.5 0.9 %shard_map.79 = (f32[27,2048]{1,0:T(8,128)}, f32[27,8192]{1,0:T(8,128)}) custom-call(bf16[4,280,128]{2,1,0:T(8,128)(2,1)S(1)} %collective-permute-done.14.pieces, f32[27,2048]{1,0:T(8,128)} %get-tuple-element.61.before_a, f32[27,8192]{1,0:T(8,128)} %get-tuple-element.62.before_b), custom_call_target="tpu_custom_call", output_to_operand_aliasing={{0}: (1, {}), {1}: (2, {})} | custom-call | flops 1000000 | bytes 1000000 | tf_op jit(solution)/shard_map/pallas_call | solution.py:526
  (20 shorter events, 0.3 us)
Async XLA Ops:
  0.6 4.3 %copy-start = (bf16[2,4,32,1024]{3,2,1,0:T(8,128)(2,1)S(1)}, bf16[2,4,32,1024]{3,2,1,0:T(8,128)(2,1)}, u32[]{:S(2)}) copy-start(bf16[2,4,32,1024]{3,2,1,0:T(8,128)(2,1)} %cubes.1) | copy-start | bytes 1572868
  0.6 4.3 %copy-start.2 = (bf16[27,2048]{1,0:T(8,128)(2,1)S(1)}, bf16[27,2048]{1,0:T(8,128)(2,1)}, u32[]{:S(2)}) copy-start(bf16[27,2048]{1,0:T(8,128)(2,1)} %weight_a.1) | copy-start | bytes 331780
  0.6 7.3 %collective-permute-start = (bf16[2,4,32,1024]{3,2,1,0:T(8,128)(2,1)}, bf16[2,4,32,1024]{3,2,1,0:T(8,128)(2,1)S(1)}, u32[]{:S(2)}, u32[]{:S(2)}) collective-permute-start(bf16[2,4,32,1024]{3,2,1,0:T(8,128)(2,1)} %cubes.1), channel_id=1, source_target_pairs={{0,1},{1,0},{2,3},{3,2},{4,5},{5,4},{6,7},{7,6},{8,9},{9,8},{10,11... | collective-permute-start | bytes 1572872 | tf_op jit(solution)/shard_map/ppermute | solution.py:541
  2.2 5.7 %collective-permute-start.1 = (bf16[2,3,32,1024]{3,2,1,0:T(8,128)(2,1)S(1)}, bf16[2,3,32,1024]{3,2,1,0:T(8,128)(2,1)S(1)}, u32[]{:S(2)}, u32[]{:S(2)}) collective-permute-start(bf16[2,3,32,1024]{3,2,1,0:T(8,128)(2,1)S(1)} %constant_dynamic-slice_fusion), channel_id=1, source_target_pairs={{1,2},{2,1},{3,4},{4,3},{5,6},{6,5},{9,10},{10,9},{11,12},{12,11},... | collective-permute-start | bytes 1179656 | tf_op jit(solution)/shard_map/ppermute | solution.py:541
  2.9 1.0 %copy-start.1 = (bf16[27,8192]{1,0:T(8,128)(2,1)S(1)}, bf16[27,8192]{1,0:T(8,128)(2,1)}, u32[]{:S(2)}) copy-start(bf16[27,8192]{1,0:T(8,128)(2,1)} %weight_b.1) | copy-start | bytes 1327108
  3.9 4.0 %copy-start.3 = (bf16[2,1,8,1024]{3,2,1,0:T(8,128)(2,1)S(1)}, bf16[2,1,8,1024]{3,2,1,0:T(8,128)(2,1)}, u32[]{:S(2)}) copy-start(bf16[2,1,8,1024]{3,2,1,0:T(8,128)(2,1)} %cot.1) | copy-start | bytes 98308
  13.8 10.7 %collective-permute-start.3 = (bf16[2,2,16,2048]{3,2,1,0:T(8,128)(2,1)S(1)}, bf16[2,2,16,2048]{3,2,1,0:T(8,128)(2,1)S(1)}, u32[]{:S(2)}, u32[]{:S(2)}) collective-permute-start(bf16[2,2,16,2048]{3,2,1,0:T(8,128)(2,1)S(1)} %get-tuple-element.42.grad_b), channel_id=1, source_target_pairs={{1,2},{2,1},{3,4},{4,3},{5,6},{6,5},{9,10},{10,9},{11,12},{12,11},... | collective-permute-start | bytes 786440 | tf_op jit(solution)/shard_map/ppermute | solution.py:541
  14.7 9.8 %collective-permute-start.2 = (bf16[2,2,16,2048]{3,2,1,0:T(8,128)(2,1)S(1)}, bf16[2,2,16,2048]{3,2,1,0:T(8,128)(2,1)S(1)}, u32[]{:S(2)}, u32[]{:S(2)}) collective-permute-start(bf16[2,2,16,2048]{3,2,1,0:T(8,128)(2,1)S(1)} %get-tuple-element.42.grad_b), channel_id=1, source_target_pairs={{0,1},{1,0},{2,3},{3,2},{4,5},{5,4},{6,7},{7,6},{8,9},{9,8},{10,11... | collective-permute-start | bytes 786440 | tf_op jit(solution)/shard_map/ppermute | solution.py:541
  30.7 2.6 %collective-permute-start.4 = (bf16[4,280,128]{2,1,0:T(8,128)(2,1)S(1)}, bf16[4,280,128]{2,1,0:T(8,128)(2,1)S(1)}, u32[]{:S(2)}, u32[]{:S(2)}) collective-permute-start(bf16[4,280,128]{2,1,0:T(8,128)(2,1)S(1)} %get-tuple-element.56), channel_id=1, source_target_pairs={{0,1},{1,0},{2,3},{3,2},{4,5},{5,4},{6,7},{7,6},{8,9},{9,8},{10,11... | collective-permute-start | bytes 860168 | tf_op jit(solution)/shard_map/ppermute | solution.py:547
  33.3 5.9 %collective-permute-start.5 = (bf16[280,128]{1,0:T(8,128)(2,1)S(1)}, bf16[280,128]{1,0:T(8,128)(2,1)S(1)}, u32[]{:S(2)}, u32[]{:S(2)}) collective-permute-start(bf16[280,128]{1,0:T(8,128)(2,1)S(1)} %get-tuple-element.58), channel_id=1, source_target_pairs={{0,8},{8,0},{16,24},{24,16},{1,9},{9,1},{17,25},{25,17},{2,10},{10... | collective-permute-start | bytes 215048 | tf_op jit(solution)/shard_map/ppermute | solution.py:547
  35.4 4.3 %collective-permute-start.6 = (bf16[280,128]{1,0:T(8,128)(2,1)S(1)}, bf16[280,128]{1,0:T(8,128)(2,1)S(1)}, u32[]{:S(2)}, u32[]{:S(2)}) collective-permute-start(bf16[280,128]{1,0:T(8,128)(2,1)S(1)} %get-tuple-element.59), channel_id=1, source_target_pairs={{0,16},{8,24},{16,0},{24,8},{1,17},{9,25},{17,1},{25,9},{2,18},{10... | collective-permute-start | bytes 215048 | tf_op jit(solution)/shard_map/ppermute | solution.py:547
  36.9 5.2 %collective-permute-start.7 = (bf16[280,128]{1,0:T(8,128)(2,1)S(1)}, bf16[280,128]{1,0:T(8,128)(2,1)S(1)}, u32[]{:S(2)}, u32[]{:S(2)}) collective-permute-start(bf16[280,128]{1,0:T(8,128)(2,1)S(1)} %get-tuple-element.60), channel_id=1, source_target_pairs={{0,24},{8,16},{16,8},{24,0},{1,25},{9,17},{17,9},{25,1},{2,26},{10... | collective-permute-start | bytes 215048 | tf_op jit(solution)/shard_map/ppermute | solution.py:547
  42.1 7.4 %collective-permute-start.10 = (bf16[280,128]{1,0:T(8,128)(2,1)S(1)}, bf16[280,128]{1,0:T(8,128)(2,1)S(1)}, u32[]{:S(2)}, u32[]{:S(2)}) collective-permute-start(bf16[280,128]{1,0:T(8,128)(2,1)S(1)} %shard_map.75.refs_0_), channel_id=1, source_target_pairs={{0,6},{1,7},{2,4},{3,5},{4,2},{5,3},{6,0},{7,1},{8,14},{9,15},{10,... | collective-permute-start | bytes 215048 | tf_op jit(solution)/shard_map/ppermute | solution.py:547
  45.8 5.5 %collective-permute-start.9 = (bf16[280,128]{1,0:T(8,128)(2,1)S(1)}, bf16[280,128]{1,0:T(8,128)(2,1)S(1)}, u32[]{:S(2)}, u32[]{:S(2)}) collective-permute-start(bf16[280,128]{1,0:T(8,128)(2,1)S(1)} %shard_map.75.refs_0_), channel_id=1, source_target_pairs={{0,4},{1,5},{2,6},{3,7},{4,0},{5,1},{6,2},{7,3},{8,12},{9,13},{10,... | collective-permute-start | bytes 215048 | tf_op jit(solution)/shard_map/ppermute | solution.py:547
  45.8 5.5 %collective-permute-start.8 = (bf16[280,128]{1,0:T(8,128)(2,1)S(1)}, bf16[280,128]{1,0:T(8,128)(2,1)S(1)}, u32[]{:S(2)}, u32[]{:S(2)}) collective-permute-start(bf16[280,128]{1,0:T(8,128)(2,1)S(1)} %shard_map.75.refs_0_), channel_id=1, source_target_pairs={{0,2},{1,3},{2,0},{3,1},{4,6},{5,7},{6,4},{7,5},{8,10},{9,11},{10,... | collective-permute-start | bytes 215048 | tf_op jit(solution)/shard_map/ppermute | solution.py:547
  51.3 5.5 %collective-permute-start.13 = (bf16[280,128]{1,0:T(8,128)(2,1)S(1)}, bf16[280,128]{1,0:T(8,128)(2,1)S(1)}, u32[]{:S(2)}, u32[]{:S(2)}) collective-permute-start(bf16[280,128]{1,0:T(8,128)(2,1)S(1)} %shard_map.76.refs_0_), channel_id=1, source_target_pairs={{0,24},{8,16},{16,8},{24,0},{1,25},{9,17},{17,9},{25,1},{2,26},{10... | collective-permute-start | bytes 215048 | tf_op jit(solution)/shard_map/ppermute | solution.py:547
  52.1 5.1 %collective-permute-start.12 = (bf16[280,128]{1,0:T(8,128)(2,1)S(1)}, bf16[280,128]{1,0:T(8,128)(2,1)S(1)}, u32[]{:S(2)}, u32[]{:S(2)}) collective-permute-start(bf16[280,128]{1,0:T(8,128)(2,1)S(1)} %shard_map.76.refs_0_), channel_id=1, source_target_pairs={{0,16},{8,24},{16,0},{24,8},{1,17},{9,25},{17,1},{25,9},{2,18},{10... | collective-permute-start | bytes 215048 | tf_op jit(solution)/shard_map/ppermute | solution.py:547
  53.5 4.3 %collective-permute-start.11 = (bf16[280,128]{1,0:T(8,128)(2,1)S(1)}, bf16[280,128]{1,0:T(8,128)(2,1)S(1)}, u32[]{:S(2)}, u32[]{:S(2)}) collective-permute-start(bf16[280,128]{1,0:T(8,128)(2,1)S(1)} %shard_map.76.refs_0_), channel_id=1, source_target_pairs={{0,8},{8,0},{16,24},{24,16},{1,9},{9,1},{17,25},{25,17},{2,10},{10... | collective-permute-start | bytes 215048 | tf_op jit(solution)/shard_map/ppermute | solution.py:547
  57.9 1.6 %collective-permute-start.14 = (bf16[4,280,128]{2,1,0:T(8,128)(2,1)S(1)}, bf16[4,280,128]{2,1,0:T(8,128)(2,1)S(1)}, u32[]{:S(2)}, u32[]{:S(2)}) collective-permute-start(bf16[4,280,128]{2,1,0:T(8,128)(2,1)S(1)} %shard_map.77.pieces), channel_id=1, source_target_pairs={{0,1},{1,0},{2,3},{3,2},{4,5},{5,4},{6,7},{7,6},{8,9},{9,8},{10,11... | collective-permute-start | bytes 860168 | tf_op jit(solution)/shard_map/ppermute | solution.py:547

commit v14 on v13

--- a/solution.py
+++ b/solution.py
@@ -565,13 +565,13 @@
             ((cube_count, 2, 16, 1024), F32),
             ((cube_count * 256, 256), F32),
             ((cube_count * 256, 256), F32),
-            ((27 * C1, 128), F32),
+            ((32 * C1, 128), F32),
         ],
         [],
         1_000_000_000,
     )
     tb, wb = call(
-        prepare_b_kernel, [weight_b], [((2304, 256), BF), ((27 * C2, 128), F32)], [], 500_000_000
+        prepare_b_kernel, [weight_b], [((2304, 256), BF), ((32 * C2, 128), F32)], [], 500_000_000
     )
     xs, dsl, pools, grad_b = call(
         forward_kernel,

time: 60.8 us -> 60.8 us (level)
  no operation moved by 1% of the time
where the time goes in v14:
time: 60.8 us; the launch traced here: 60.6 us
  Pallas kernels  25.6 us (42%)
  starting transfers between devices  22.5 us (37%)
  waiting for transfers between devices  9.39 us (15%)
  local copies, waits for them, and re-layouts  2.07 us (3%)
  between operations  0.99 us (2%)
    pallas_call x13, Pallas kernels, call(): pl.pallas_call(kernel, out_shape=[jax.ShapeDtypeStruct(shape, dtype) for...  25.6 us
    ppermute x11, starting transfers between devices, swap_along(): lax.ppermute(part, axis, [(i, i ^ k * step) for i in range(count)])  13.1 us
    ppermute x11, waiting for transfers between devices, swap_along(): lax.ppermute(part, axis, [(i, i ^ k * step) for i in range(count)])  9.38 us
    ppermute x2, starting transfers between devices, swap(): lax.ppermute(first, 'gz', pairs_a)  7.91 us
    ppermute x2, starting transfers between devices, swap(): lax.ppermute(second, 'gz', pairs_b)  1.54 us
  transfers between devices with their start and end apart: 15, of which 8 were waited for; matrix products, arithmetic and copies ran while one was open for 2% of the time, Pallas kernels for 21%

profile of v14, /device:TPU:0, one launch (start us, length us, event | category | flops | bytes accessed | tf_op | source)
XLA Modules:
  0.0 60.6 jit_solution(11955637169241487588)
XLA Ops:
  0.6 0.5 collective-permute-start
  1.2 1.0 %constant_dynamic-slice_fusion = bf16[2,3,32,1024]{3,2,1,0:T(8,128)(2,1)S(1)} fusion(bf16[2,4,32,1024]{3,2,1,0:T(8,128)(2,1)} %cubes.1, s32[]{:T(128)S(6)} %select_n.11), kind=kLoop, calls=%fused_computation | loop fusion | bytes 786436 | tf_op jit(solution)/shard_map/dynamic_slice | solution.py:555
  2.2 0.7 %collective-permute-start.1 = (bf16[2,3,32,1024]{3,2,1,0:T(8,128)(2,1)S(1)}, bf16[2,3,32,1024]{3,2,1,0:T(8,128)(2,1)S(1)}, u32[]{:S(2)}, u32[]{:S(2)}) collective-permute-start(bf16[2,3,32,1024]{3,2,1,0:T(8,128)(2,1)S(1)} %constant_dynamic-slice_fusion), channel_id=1, source_target_pairs={{1,2},{2,1},{3,4},{4,3},{5,6},{6,5},{9,10},{10,9},{11,12},{12,11},... | collective-permute-start | bytes 1179656 | tf_op jit(solution)/shard_map/ppermute | solution.py:541
  2.9 1.0 %copy-done.1 = bf16[27,8192]{1,0:T(8,128)(2,1)S(1)} copy-done((bf16[27,8192]{1,0:T(8,128)(2,1)S(1)}, bf16[27,8192]{1,0:T(8,128)(2,1)}, u32[]{:S(2)}) %copy-start.1) | copy-done | bytes 442392
  3.9 1.0 %shard_map.68 = (bf16[2304,256]{1,0:T(8,128)(2,1)S(1)}, f32[2048,128]{1,0:T(8,128)S(1)}) custom-call(bf16[27,8192]{1,0:T(8,128)(2,1)S(1)} %copy-done.1), custom_call_target="tpu_custom_call" | custom-call | flops 500000000 | bytes 1000000 | tf_op jit(solution)/shard_map/pallas_call | solution.py:526
  4.9 3.0 %shard_map.67 = (bf16[2,10,4,16,1152]{4,3,2,1,0:T(8,128)(2,1)S(1)}, bf16[2304,256]{1,0:T(8,128)(2,1)S(1)}, bf16[2,6,2,16,2048]{4,3,2,1,0:T(8,128)(2,1)S(1)}, f32...) custom-call(bf16[2,4,32,1024]{3,2,1,0:T(8,128)(2,1)S(1)} %copy-done, ...), custom_call_target="tpu_custom_call" | custom-call | flops 1000000000 | bytes 1000000 | tf_op jit(solution)/shard_map/pallas_call | solution.py:526
  8.0 5.8 %shard_map.69 = (bf16[2,10,4,16,1152]{4,3,2,1,0:T(8,128)(2,1)S(1)}, bf16[2,6,2,16,2048]{4,3,2,1,0:T(8,128)(2,1)S(1)}, bf16[2,4,3,16,1152]{4,3,2,1,0:T(8,128)(2,1)S(1)}, bf16[2,2,16,2048]{3,2,1,0:T(8,128)(2,1)S(1)}) custom-call(bf16[2,10,4,16,1152]{4,3,2,1,0:T(8,128)(2,1)S(1)} %get-tuple-element.34.own, ...), custom_call_target="tpu_custom_call", output_to_operand_aliasing={{0}: (0, {}), {1}: (1, {})} | custom-call | flops 8000000000 | bytes 1000000 | tf_op jit(solution)/shard_map/pallas_call | solution.py:526
  13.8 0.9 %collective-permute-start.3 = (bf16[2,2,16,2048]{3,2,1,0:T(8,128)(2,1)S(1)}, bf16[2,2,16,2048]{3,2,1,0:T(8,128)(2,1)S(1)}, u32[]{:S(2)}, u32[]{:S(2)}) collective-permute-start(bf16[2,2,16,2048]{3,2,1,0:T(8,128)(2,1)S(1)} %get-tuple-element.42.grad_b), channel_id=1, source_target_pairs={{1,2},{2,1},{3,4},{4,3},{5,6},{6,5},{9,10},{10,9},{11,12},{12,11},... | collective-permute-start | bytes 786440 | tf_op jit(solution)/shard_map/ppermute | solution.py:541
  14.7 7.4 %collective-permute-start.2 = (bf16[2,2,16,2048]{3,2,1,0:T(8,128)(2,1)S(1)}, bf16[2,2,16,2048]{3,2,1,0:T(8,128)(2,1)S(1)}, u32[]{:S(2)}, u32[]{:S(2)}) collective-permute-start(bf16[2,2,16,2048]{3,2,1,0:T(8,128)(2,1)S(1)} %get-tuple-element.42.grad_b), channel_id=1, source_target_pairs={{0,1},{1,0},{2,3},{3,2},{4,5},{5,4},{6,7},{7,6},{8,9},{9,8},{10,11... | collective-permute-start | bytes 786440 | tf_op jit(solution)/shard_map/ppermute | solution.py:541
  22.1 2.4 %shard_map.70 = (f32[1792,128]{1,0:T(8,128)S(1)}, bf16[2,6,3,16,2304]{4,3,2,1,0:T(8,128)(2,1)S(1)}, bf16[6912,256]{1,0:T(8,128)(2,1)S(1)}, bf16[6912,256]{1,0:T(8,128)(2,1)S(1)}, f32[4,2,4,16,256]{4,3,2,1,0:T(8,128)S(1)}) custom-call(bf16[2,4,3,16,1152]{4,3,2,1,0:T(8,128)(2,1)S(1)} %get-tuple-element.41.pools, ...), custom_call_target="tpu_custom_call" | custom-call | flops 1000000000 | bytes 1000000 | tf_op jit(solution)/shard_map/pallas_call | solution.py:526
  24.5 6.1 %shard_map.71 = (bf16[2,6,4,16,2304]{4,3,2,1,0:T(8,128)(2,1)S(1)}, bf16[4,280,128]{2,1,0:T(8,128)(2,1)S(1)}, bf16[4,280,128]{2,1,0:T(8,128)(2,1)S(1)}, bf16[2,6,3,16,2304]{4,3,2,1,0:T(8,128)(2,1)S(1)}) custom-call(bf16[2,6,3,16,2304]{4,3,2,1,0:T(8,128)(2,1)S(1)} %get-tuple-element.45.own, ...), custom_call_target="tpu_custom_call", output_to_operand_aliasing={{3}: (0, {})} | custom-call | flops 6000000000 | bytes 1000000 | tf_op jit(solution)/shard_map/pallas_call | solution.py:526
  30.7 1.4 %collective-permute-start.4 = (bf16[4,280,128]{2,1,0:T(8,128)(2,1)S(1)}, bf16[4,280,128]{2,1,0:T(8,128)(2,1)S(1)}, u32[]{:S(2)}, u32[]{:S(2)}) collective-permute-start(bf16[4,280,128]{2,1,0:T(8,128)(2,1)S(1)} %get-tuple-element.56), channel_id=1, source_target_pairs={{0,1},{1,0},{2,3},{3,2},{4,5},{5,4},{6,7},{7,6},{8,9},{9,8},{10,11... | collective-permute-start | bytes 860168 | tf_op jit(solution)/shard_map/ppermute | solution.py:547
  32.1 1.2 %collective-permute-done.4.recv = bf16[4,280,128]{2,1,0:T(8,128)(2,1)S(1)} collective-permute-done((bf16[4,280,128]{2,1,0:T(8,128)(2,1)S(1)}, bf16[4,280,128]{2,1,0:T(8,128)(2,1)S(1)}, u32[]{:S(2)}, u32[]{:S(2)}) %collective-permute-start.4) | collective-permute-done | bytes 286752 | tf_op jit(solution)/shard_map/ppermute | solution.py:547
  33.3 2.0 %collective-permute-start.5 = (bf16[280,128]{1,0:T(8,128)(2,1)S(1)}, bf16[280,128]{1,0:T(8,128)(2,1)S(1)}, u32[]{:S(2)}, u32[]{:S(2)}) collective-permute-start(bf16[280,128]{1,0:T(8,128)(2,1)S(1)} %get-tuple-element.58), channel_id=1, source_target_pairs={{0,8},{8,0},{16,24},{24,16},{1,9},{9,1},{17,25},{25,17},{2,10},{10... | collective-permute-start | bytes 215048 | tf_op jit(solution)/shard_map/ppermute | solution.py:547
  35.4 1.5 %collective-permute-start.6 = (bf16[280,128]{1,0:T(8,128)(2,1)S(1)}, bf16[280,128]{1,0:T(8,128)(2,1)S(1)}, u32[]{:S(2)}, u32[]{:S(2)}) collective-permute-start(bf16[280,128]{1,0:T(8,128)(2,1)S(1)} %get-tuple-element.59), channel_id=1, source_target_pairs={{0,16},{8,24},{16,0},{24,8},{1,17},{9,25},{17,1},{25,9},{2,18},{10... | collective-permute-start | bytes 215048 | tf_op jit(solution)/shard_map/ppermute | solution.py:547
  36.9 2.3 %shard_map.72.rest_0_.after = bf16[4,32,1024]{2,1,0:T(8,128)(2,1)S(1)} custom-call(bf16[2,6,4,16,2304]{4,3,2,1,0:T(8,128)(2,1)S(1)} %get-tuple-element.51.ga, bf16[6912,256]{1,0:T(8,128)(2,1)S(1)} %get-tuple-element.52.tat), custom_call_target="tpu_custom_call" | custom-call | flops 2000000000 | bytes 1000000 | tf_op jit(solution)/shard_map/pallas_call | solution.py:526
  39.2 0.5 collective-permute-done.6.refs_2_
  39.7 2.4 %collective-permute-done.7.refs_3_ = bf16[280,128]{1,0:T(8,128)(2,1)S(1)} collective-permute-done((bf16[280,128]{1,0:T(8,128)(2,1)S(1)}, bf16[280,128]{1,0:T(8,128)(2,1)S(1)}, u32[]{:S(2)}, u32[]{:S(2)}) %collective-permute-start.7) | collective-permute-done | bytes 71712 | tf_op jit(solution)/shard_map/ppermute | solution.py:547
  42.1 3.6 %collective-permute-start.10 = (bf16[280,128]{1,0:T(8,128)(2,1)S(1)}, bf16[280,128]{1,0:T(8,128)(2,1)S(1)}, u32[]{:S(2)}, u32[]{:S(2)}) collective-permute-start(bf16[280,128]{1,0:T(8,128)(2,1)S(1)} %shard_map.75.refs_0_), channel_id=1, source_target_pairs={{0,6},{1,7},{2,4},{3,5},{4,2},{5,3},{6,0},{7,1},{8,14},{9,15},{10,... | collective-permute-start | bytes 215048 | tf_op jit(solution)/shard_map/ppermute | solution.py:547
  45.8 0.8 %collective-permute-start.8 = (bf16[280,128]{1,0:T(8,128)(2,1)S(1)}, bf16[280,128]{1,0:T(8,128)(2,1)S(1)}, u32[]{:S(2)}, u32[]{:S(2)}) collective-permute-start(bf16[280,128]{1,0:T(8,128)(2,1)S(1)} %shard_map.75.refs_0_), channel_id=1, source_target_pairs={{0,2},{1,3},{2,0},{3,1},{4,6},{5,7},{6,4},{7,5},{8,10},{9,11},{10,... | collective-permute-start | bytes 215048 | tf_op jit(solution)/shard_map/ppermute | solution.py:547
  46.6 2.9 %shard_map.73 = (bf16[2,4,32,1024]{3,2,1,0:T(8,128)(2,1)}, f32[8,128]{1,0:T(8,128)S(1)}) custom-call(bf16[2,6,4,16,2304]{4,3,2,1,0:T(8,128)(2,1)S(1)} %get-tuple-element.51.ga, bf16[6912,256]{1,0:T(8,128)(2,1)S(1)} %get-tuple-element.52.tat, bf16[4,32,1024]{2,1,0:T(8,128)(2,1)S(1)} %shard_map.72.rest_0_.after), custom_call_target="tpu_custom_call" | custom-call | flops 2000000000 | bytes 1000000 | tf_op jit(solution)/shard_map/pallas_call | solution.py:526
  49.6 1.7 %collective-permute-done.9.refs_2_ = bf16[280,128]{1,0:T(8,128)(2,1)S(1)} collective-permute-done((bf16[280,128]{1,0:T(8,128)(2,1)S(1)}, bf16[280,128]{1,0:T(8,128)(2,1)S(1)}, u32[]{:S(2)}, u32[]{:S(2)}) %collective-permute-start.9) | collective-permute-done | bytes 71712 | tf_op jit(solution)/shard_map/ppermute | solution.py:547
  51.3 0.8 %collective-permute-start.13 = (bf16[280,128]{1,0:T(8,128)(2,1)S(1)}, bf16[280,128]{1,0:T(8,128)(2,1)S(1)}, u32[]{:S(2)}, u32[]{:S(2)}) collective-permute-start(bf16[280,128]{1,0:T(8,128)(2,1)S(1)} %shard_map.76.refs_0_), channel_id=1, source_target_pairs={{0,24},{8,16},{16,8},{24,0},{1,25},{9,17},{17,9},{25,1},{2,26},{10... | collective-permute-start | bytes 215048 | tf_op jit(solution)/shard_map/ppermute | solution.py:547
  52.1 1.4 %collective-permute-start.12 = (bf16[280,128]{1,0:T(8,128)(2,1)S(1)}, bf16[280,128]{1,0:T(8,128)(2,1)S(1)}, u32[]{:S(2)}, u32[]{:S(2)}) collective-permute-start(bf16[280,128]{1,0:T(8,128)(2,1)S(1)} %shard_map.76.refs_0_), channel_id=1, source_target_pairs={{0,16},{8,24},{16,0},{24,8},{1,17},{9,25},{17,1},{25,9},{2,18},{10... | collective-permute-start | bytes 215048 | tf_op jit(solution)/shard_map/ppermute | solution.py:547
  53.5 1.4 %collective-permute-start.11 = (bf16[280,128]{1,0:T(8,128)(2,1)S(1)}, bf16[280,128]{1,0:T(8,128)(2,1)S(1)}, u32[]{:S(2)}, u32[]{:S(2)}) collective-permute-start(bf16[280,128]{1,0:T(8,128)(2,1)S(1)} %shard_map.76.refs_0_), channel_id=1, source_target_pairs={{0,8},{8,0},{16,24},{24,16},{1,9},{9,1},{17,25},{25,17},{2,10},{10... | collective-permute-start | bytes 215048 | tf_op jit(solution)/shard_map/ppermute | solution.py:547
  54.9 1.9 %collective-permute-done.13.refs_3_ = bf16[280,128]{1,0:T(8,128)(2,1)S(1)} collective-permute-done((bf16[280,128]{1,0:T(8,128)(2,1)S(1)}, bf16[280,128]{1,0:T(8,128)(2,1)S(1)}, u32[]{:S(2)}, u32[]{:S(2)}) %collective-permute-start.13) | collective-permute-done | bytes 71712 | tf_op jit(solution)/shard_map/ppermute | solution.py:547
  56.8 0.4 collective-permute-done.12.refs_2_
  57.2 0.6 collective-permute-done.11.refs_1_
  57.9 0.1 collective-permute-start.14
  57.9 0.9 %shard_map.78 = (f32[27,2048]{1,0:T(8,128)}, f32[27,8192]{1,0:T(8,128)}) custom-call(bf16[4,280,128]{2,1,0:T(8,128)(2,1)S(1)} %shard_map.77.pieces), custom_call_target="tpu_custom_call" | custom-call | flops 1000000 | bytes 1000000 | tf_op jit(solution)/shard_map/pallas_call | solution.py:526
  58.9 0.6 %collective-permute-done.14.pieces = bf16[4,280,128]{2,1,0:T(8,128)(2,1)S(1)} collective-permute-done((bf16[4,280,128]{2,1,0:T(8,128)(2,1)S(1)}, bf16[4,280,128]{2,1,0:T(8,128)(2,1)S(1)}, u32[]{:S(2)}, u32[]{:S(2)}) %collective-permute-start.14) | collective-permute-done | bytes 286752 | tf_op jit(solution)/shard_map/ppermute | solution.py:547
  59.5 0.9 %shard_map.79 = (f32[27,2048]{1,0:T(8,128)}, f32[27,8192]{1,0:T(8,128)}) custom-call(bf16[4,280,128]{2,1,0:T(8,128)(2,1)S(1)} %collective-permute-done.14.pieces, f32[27,2048]{1,0:T(8,128)} %get-tuple-element.61.before_a, f32[27,8192]{1,0:T(8,128)} %get-tuple-element.62.before_b), custom_call_target="tpu_custom_call", output_to_operand_aliasing={{0}: (1, {}), {1}: (2, {})} | custom-call | flops 1000000 | bytes 1000000 | tf_op jit(solution)/shard_map/pallas_call | solution.py:526
  (20 shorter events, 0.3 us)
Async XLA Ops:
  0.6 4.3 %copy-start = (bf16[2,4,32,1024]{3,2,1,0:T(8,128)(2,1)S(1)}, bf16[2,4,32,1024]{3,2,1,0:T(8,128)(2,1)}, u32[]{:S(2)}) copy-start(bf16[2,4,32,1024]{3,2,1,0:T(8,128)(2,1)} %cubes.1) | copy-start | bytes 1572868
  0.6 4.3 %copy-start.2 = (bf16[27,2048]{1,0:T(8,128)(2,1)S(1)}, bf16[27,2048]{1,0:T(8,128)(2,1)}, u32[]{:S(2)}) copy-start(bf16[27,2048]{1,0:T(8,128)(2,1)} %weight_a.1) | copy-start | bytes 331780
  0.6 7.3 %collective-permute-start = (bf16[2,4,32,1024]{3,2,1,0:T(8,128)(2,1)}, bf16[2,4,32,1024]{3,2,1,0:T(8,128)(2,1)S(1)}, u32[]{:S(2)}, u32[]{:S(2)}) collective-permute-start(bf16[2,4,32,1024]{3,2,1,0:T(8,128)(2,1)} %cubes.1), channel_id=1, source_target_pairs={{0,1},{1,0},{2,3},{3,2},{4,5},{5,4},{6,7},{7,6},{8,9},{9,8},{10,11... | collective-permute-start | bytes 1572872 | tf_op jit(solution)/shard_map/ppermute | solution.py:541
  2.2 5.7 %collective-permute-start.1 = (bf16[2,3,32,1024]{3,2,1,0:T(8,128)(2,1)S(1)}, bf16[2,3,32,1024]{3,2,1,0:T(8,128)(2,1)S(1)}, u32[]{:S(2)}, u32[]{:S(2)}) collective-permute-start(bf16[2,3,32,1024]{3,2,1,0:T(8,128)(2,1)S(1)} %constant_dynamic-slice_fusion), channel_id=1, source_target_pairs={{1,2},{2,1},{3,4},{4,3},{5,6},{6,5},{9,10},{10,9},{11,12},{12,11},... | collective-permute-start | bytes 1179656 | tf_op jit(solution)/shard_map/ppermute | solution.py:541
  2.9 1.0 %copy-start.1 = (bf16[27,8192]{1,0:T(8,128)(2,1)S(1)}, bf16[27,8192]{1,0:T(8,128)(2,1)}, u32[]{:S(2)}) copy-start(bf16[27,8192]{1,0:T(8,128)(2,1)} %weight_b.1) | copy-start | bytes 1327108
  3.9 4.0 %copy-start.3 = (bf16[2,1,8,1024]{3,2,1,0:T(8,128)(2,1)S(1)}, bf16[2,1,8,1024]{3,2,1,0:T(8,128)(2,1)}, u32[]{:S(2)}) copy-start(bf16[2,1,8,1024]{3,2,1,0:T(8,128)(2,1)} %cot.1) | copy-start | bytes 98308
  13.8 10.7 %collective-permute-start.3 = (bf16[2,2,16,2048]{3,2,1,0:T(8,128)(2,1)S(1)}, bf16[2,2,16,2048]{3,2,1,0:T(8,128)(2,1)S(1)}, u32[]{:S(2)}, u32[]{:S(2)}) collective-permute-start(bf16[2,2,16,2048]{3,2,1,0:T(8,128)(2,1)S(1)} %get-tuple-element.42.grad_b), channel_id=1, source_target_pairs={{1,2},{2,1},{3,4},{4,3},{5,6},{6,5},{9,10},{10,9},{11,12},{12,11},... | collective-permute-start | bytes 786440 | tf_op jit(solution)/shard_map/ppermute | solution.py:541
  14.7 9.8 %collective-permute-start.2 = (bf16[2,2,16,2048]{3,2,1,0:T(8,128)(2,1)S(1)}, bf16[2,2,16,2048]{3,2,1,0:T(8,128)(2,1)S(1)}, u32[]{:S(2)}, u32[]{:S(2)}) collective-permute-start(bf16[2,2,16,2048]{3,2,1,0:T(8,128)(2,1)S(1)} %get-tuple-element.42.grad_b), channel_id=1, source_target_pairs={{0,1},{1,0},{2,3},{3,2},{4,5},{5,4},{6,7},{7,6},{8,9},{9,8},{10,11... | collective-permute-start | bytes 786440 | tf_op jit(solution)/shard_map/ppermute | solution.py:541
  30.7 2.6 %collective-permute-start.4 = (bf16[4,280,128]{2,1,0:T(8,128)(2,1)S(1)}, bf16[4,280,128]{2,1,0:T(8,128)(2,1)S(1)}, u32[]{:S(2)}, u32[]{:S(2)}) collective-permute-start(bf16[4,280,128]{2,1,0:T(8,128)(2,1)S(1)} %get-tuple-element.56), channel_id=1, source_target_pairs={{0,1},{1,0},{2,3},{3,2},{4,5},{5,4},{6,7},{7,6},{8,9},{9,8},{10,11... | collective-permute-start | bytes 860168 | tf_op jit(solution)/shard_map/ppermute | solution.py:547
  33.3 5.9 %collective-permute-start.5 = (bf16[280,128]{1,0:T(8,128)(2,1)S(1)}, bf16[280,128]{1,0:T(8,128)(2,1)S(1)}, u32[]{:S(2)}, u32[]{:S(2)}) collective-permute-start(bf16[280,128]{1,0:T(8,128)(2,1)S(1)} %get-tuple-element.58), channel_id=1, source_target_pairs={{0,8},{8,0},{16,24},{24,16},{1,9},{9,1},{17,25},{25,17},{2,10},{10... | collective-permute-start | bytes 215048 | tf_op jit(solution)/shard_map/ppermute | solution.py:547
  35.4 4.3 %collective-permute-start.6 = (bf16[280,128]{1,0:T(8,128)(2,1)S(1)}, bf16[280,128]{1,0:T(8,128)(2,1)S(1)}, u32[]{:S(2)}, u32[]{:S(2)}) collective-permute-start(bf16[280,128]{1,0:T(8,128)(2,1)S(1)} %get-tuple-element.59), channel_id=1, source_target_pairs={{0,16},{8,24},{16,0},{24,8},{1,17},{9,25},{17,1},{25,9},{2,18},{10... | collective-permute-start | bytes 215048 | tf_op jit(solution)/shard_map/ppermute | solution.py:547
  36.9 5.2 %collective-permute-start.7 = (bf16[280,128]{1,0:T(8,128)(2,1)S(1)}, bf16[280,128]{1,0:T(8,128)(2,1)S(1)}, u32[]{:S(2)}, u32[]{:S(2)}) collective-permute-start(bf16[280,128]{1,0:T(8,128)(2,1)S(1)} %get-tuple-element.60), channel_id=1, source_target_pairs={{0,24},{8,16},{16,8},{24,0},{1,25},{9,17},{17,9},{25,1},{2,26},{10... | collective-permute-start | bytes 215048 | tf_op jit(solution)/shard_map/ppermute | solution.py:547
  42.1 7.4 %collective-permute-start.10 = (bf16[280,128]{1,0:T(8,128)(2,1)S(1)}, bf16[280,128]{1,0:T(8,128)(2,1)S(1)}, u32[]{:S(2)}, u32[]{:S(2)}) collective-permute-start(bf16[280,128]{1,0:T(8,128)(2,1)S(1)} %shard_map.75.refs_0_), channel_id=1, source_target_pairs={{0,6},{1,7},{2,4},{3,5},{4,2},{5,3},{6,0},{7,1},{8,14},{9,15},{10,... | collective-permute-start | bytes 215048 | tf_op jit(solution)/shard_map/ppermute | solution.py:547
  45.8 5.5 %collective-permute-start.9 = (bf16[280,128]{1,0:T(8,128)(2,1)S(1)}, bf16[280,128]{1,0:T(8,128)(2,1)S(1)}, u32[]{:S(2)}, u32[]{:S(2)}) collective-permute-start(bf16[280,128]{1,0:T(8,128)(2,1)S(1)} %shard_map.75.refs_0_), channel_id=1, source_target_pairs={{0,4},{1,5},{2,6},{3,7},{4,0},{5,1},{6,2},{7,3},{8,12},{9,13},{10,... | collective-permute-start | bytes 215048 | tf_op jit(solution)/shard_map/ppermute | solution.py:547
  45.8 5.5 %collective-permute-start.8 = (bf16[280,128]{1,0:T(8,128)(2,1)S(1)}, bf16[280,128]{1,0:T(8,128)(2,1)S(1)}, u32[]{:S(2)}, u32[]{:S(2)}) collective-permute-start(bf16[280,128]{1,0:T(8,128)(2,1)S(1)} %shard_map.75.refs_0_), channel_id=1, source_target_pairs={{0,2},{1,3},{2,0},{3,1},{4,6},{5,7},{6,4},{7,5},{8,10},{9,11},{10,... | collective-permute-start | bytes 215048 | tf_op jit(solution)/shard_map/ppermute | solution.py:547
  51.3 5.5 %collective-permute-start.13 = (bf16[280,128]{1,0:T(8,128)(2,1)S(1)}, bf16[280,128]{1,0:T(8,128)(2,1)S(1)}, u32[]{:S(2)}, u32[]{:S(2)}) collective-permute-start(bf16[280,128]{1,0:T(8,128)(2,1)S(1)} %shard_map.76.refs_0_), channel_id=1, source_target_pairs={{0,24},{8,16},{16,8},{24,0},{1,25},{9,17},{17,9},{25,1},{2,26},{10... | collective-permute-start | bytes 215048 | tf_op jit(solution)/shard_map/ppermute | solution.py:547
  52.1 5.1 %collective-permute-start.12 = (bf16[280,128]{1,0:T(8,128)(2,1)S(1)}, bf16[280,128]{1,0:T(8,128)(2,1)S(1)}, u32[]{:S(2)}, u32[]{:S(2)}) collective-permute-start(bf16[280,128]{1,0:T(8,128)(2,1)S(1)} %shard_map.76.refs_0_), channel_id=1, source_target_pairs={{0,16},{8,24},{16,0},{24,8},{1,17},{9,25},{17,1},{25,9},{2,18},{10... | collective-permute-start | bytes 215048 | tf_op jit(solution)/shard_map/ppermute | solution.py:547
  53.5 4.3 %collective-permute-start.11 = (bf16[280,128]{1,0:T(8,128)(2,1)S(1)}, bf16[280,128]{1,0:T(8,128)(2,1)S(1)}, u32[]{:S(2)}, u32[]{:S(2)}) collective-permute-start(bf16[280,128]{1,0:T(8,128)(2,1)S(1)} %shard_map.76.refs_0_), channel_id=1, source_target_pairs={{0,8},{8,0},{16,24},{24,16},{1,9},{9,1},{17,25},{25,17},{2,10},{10... | collective-permute-start | bytes 215048 | tf_op jit(solution)/shard_map/ppermute | solution.py:547
  57.9 1.6 %collective-permute-start.14 = (bf16[4,280,128]{2,1,0:T(8,128)(2,1)S(1)}, bf16[4,280,128]{2,1,0:T(8,128)(2,1)S(1)}, u32[]{:S(2)}, u32[]{:S(2)}) collective-permute-start(bf16[4,280,128]{2,1,0:T(8,128)(2,1)S(1)} %shard_map.77.pieces), channel_id=1, source_target_pairs={{0,1},{1,0},{2,3},{3,2},{4,5},{5,4},{6,7},{7,6},{8,9},{9,8},{10,11... | collective-permute-start | bytes 860168 | tf_op jit(solution)/shard_map/ppermute | solution.py:547
